TPU v7x, 32 devices: a whole 2x2x4 slice. The times are simulated.
32 devices in a mesh: lat: 4 (over x, core), lon: 8 (over z, y).
Axes of the slice: x: 2, y: 2, z: 4, core: 2. Of those that a mesh axis runs over, the one named last changes fastest.
Arguments:
- fields: bfloat16 [4, 16, 72, 1024], P(None, 'lat', 'lon'), may hold values from -6 to 6
- conv_first: float32 [9, 1024], replicated, may hold values from -2 to 2
- w_qkv: bfloat16 [1024, 3072], replicated, may hold values from -2 to 2
- w_out: bfloat16 [1024, 1024], replicated, may hold values from -0.1875 to 0.1875
- conv_second: float32 [9, 1024], replicated, may hold values from -2 to 2
- key_list: int32 [4, 8, 8], P('lat', 'lon'), may hold values from 0 to 7, as said below
- key_count: int32 [4, 8], P('lat', 'lon'), may hold values from 1 to 8, as said below
Outputs:
- attended: bfloat16 [4, 16, 72, 1024], P(None, 'lat', 'lon')
- mixed: bfloat16 [4, 16, 72, 1024], P(None, 'lat', 'lon')
Inputs may be any that keep to these rules, and one draw needn't show every extreme that they name: Entry 0 of key_list[p, q] is q; entries 1 to key_count[p, q] - 1 are distinct longitude band indices other than q; the remaining entries are q. key_count[p, q] is 8 in the first and the last latitude band.
All inputs are finite; a program needn't handle non-finite values.
Results may differ from a plain program's by a relative error of at most 0.034.
Values may be sent and summed in bfloat16 or wider, within the bound.
No kernel may reach another device: no remote copies, remote signals or barrier semaphores. Data moves between devices by JAX's collectives and lax.ppermute only.
A program may use at most 128 MiB of HBM per device.

v0:
```python
import jax
import jax.numpy as jnp
from jax import lax
from jax.sharding import PartitionSpec as P

HEADS = 16


NEG_FILL = -1e30
EPSILON = 1e-05


def with_halo(cells, sides, width, closed):
    for axis, dim in sides:
        count = lax.axis_size(axis)
        ends = count if closed else count - 1
        head = lax.slice_in_dim(cells, 0, width, axis=dim)
        tail = lax.slice_in_dim(cells, cells.shape[dim] - width, cells.shape[dim], axis=dim)
        cells = jnp.concatenate(
            [
                lax.ppermute(tail, axis, [(i, (i + 1) % count) for i in range(ends)]),
                cells,
                lax.ppermute(head, axis, [((i + 1) % count, i) for i in range(ends)]),
            ],
            axis=dim,
        )
    return cells


def from_behind(x, axis, by):
    size = lax.axis_size(axis)
    return lax.ppermute(x, axis, [(i, (i + by) % size) for i in range(size)])


def depthwise(field, weights):
    row_count = field.shape[1]
    column_count = field.shape[2]
    widened = with_halo(field, (("lon", 2),), 1, True)
    widened = with_halo(widened, (("lat", 1),), 1, False)
    result = jnp.zeros(field.shape, jnp.float32)
    for offset_lat in range(3):
        for offset_lon in range(3):
            window = widened[
                :, offset_lat : offset_lat + row_count, offset_lon : offset_lon + column_count
            ]
            result = result + weights[3 * offset_lat + offset_lon] * window.astype(jnp.float32)
    return result


def attend(state, query, keyvals, valid, scale):
    highest, summed, accum = state
    width = keyvals.shape[1] // 2
    heads = query.shape[1]
    head_size = query.shape[2]
    keys_part = keyvals[:, :width].reshape(-1, heads, head_size)
    values_part = keyvals[:, width:].reshape(-1, heads, head_size)
    scores = (
        jnp.einsum("qhd,khd->qhk", query, keys_part, preferred_element_type=jnp.float32) * scale
    )
    scores = jnp.where(valid[None, None, :], scores, NEG_FILL)
    new_highest = jnp.maximum(highest, jnp.max(scores, axis=-1))
    weights = jnp.where(valid[None, None, :], jnp.exp(scores - new_highest[..., None]), 0.0)
    factor = jnp.exp(highest - new_highest)
    summed = summed * factor + jnp.sum(weights, axis=-1)
    accum = accum * factor[..., None] + jnp.einsum(
        "qhk,khd->qhd",
        weights.astype(jnp.bfloat16),
        values_part,
        preferred_element_type=jnp.float32,
    )
    return (new_highest, summed, accum)


def local(fields, conv_first, w_qkv, w_out, conv_second, key_list, key_count):
    level_count, row_count, column_count, width = fields.shape
    tokens = level_count * row_count * column_count
    heads = HEADS
    head_size = width // heads
    scale = head_size ** (-0.5)
    stream = (fields.astype(jnp.float32) + depthwise(fields, conv_first)).astype(jnp.bfloat16)
    stream_flat = stream.reshape(tokens, width).astype(jnp.float32)
    normed = (
        stream_flat
        * lax.rsqrt(jnp.mean(stream_flat * stream_flat, axis=-1, keepdims=True) + EPSILON)
    ).astype(jnp.bfloat16)
    query = (
        jnp.dot(normed, w_qkv[:, :width], preferred_element_type=jnp.float32)
        .astype(jnp.bfloat16)
        .reshape(tokens, heads, head_size)
    )
    w_pair = w_qkv[:, width:]
    keyvals = jnp.dot(normed, w_pair, preferred_element_type=jnp.float32).astype(jnp.bfloat16)
    lat_here = lax.axis_index("lat")
    lat_total = lax.axis_size("lat")
    lon_here = lax.axis_index("lon")
    lon_total = lax.axis_size("lon")
    slot_index = jnp.arange(lon_total, dtype=jnp.int32)
    listed = key_list.reshape(lon_total)
    count = key_count.reshape(())
    linked = jnp.any(
        (listed[None, :] == slot_index[:, None]) & (slot_index < count)[None, :], axis=1
    )

    def spread(flag):
        return jnp.broadcast_to(flag, (tokens,))

    grid = keyvals.reshape(level_count, row_count, column_count, keyvals.shape[1])
    band = with_halo(grid, (("lat", 1),), row_count, False)
    upper = band[:, :row_count].reshape(tokens, keyvals.shape[1])
    lower = band[:, 2 * row_count :].reshape(tokens, keyvals.shape[1])
    near_keys = jnp.concatenate([upper, keyvals, lower], axis=0)
    near_valid = jnp.concatenate(
        [spread(lat_here > 0), jnp.ones((tokens,), jnp.bool_), spread(lat_here < lat_total - 1)]
    )
    state = (
        jnp.full((tokens, heads), NEG_FILL, jnp.float32),
        jnp.zeros((tokens, heads), jnp.float32),
        jnp.zeros((tokens, heads, head_size), jnp.float32),
    )
    state = attend(state, query, near_keys, near_valid, scale)

    def visit(current, piece, valid):
        return attend(current, query, piece, valid, scale)

    def turn(step, carry):
        buffer, current = carry
        buffer = from_behind(buffer, "lon", 1)
        source = (lon_here - step) % lon_total
        return (buffer, visit(current, buffer, spread(linked[source])))

    state = lax.fori_loop(1, lon_total, turn, (keyvals, state))[1]
    highest, summed, accum = state
    attended = (accum / summed[..., None]).astype(jnp.bfloat16).reshape(tokens, width)
    projected = jnp.dot(attended, w_out, preferred_element_type=jnp.float32)
    after = (stream_flat + projected).astype(jnp.bfloat16).reshape(fields.shape)
    mixed = (after.astype(jnp.float32) + depthwise(after, conv_second)).astype(jnp.bfloat16)
    return (attended.reshape(fields.shape), mixed)


def solution(mesh):
    return jax.shard_map(
        local,
        mesh=mesh,
        in_specs=(
            P(None, "lat", "lon", None),
            P(),
            P(),
            P(),
            P(),
            P("lat", "lon", None),
            P("lat", "lon"),
        ),
        out_specs=(P(None, "lat", "lon", None), P(None, "lat", "lon", None)),
        check_vma=False,
    )
```

profile of v0, /device:TPU:0, one launch (start us, length us, event | category | flops | bytes accessed | tf_op | source)
XLA Modules:
  0.0 266.2 jit_solution(8671068724025023925)
XLA Ops:
  1.6 3.0 %collective-permute-start.1 = (bf16[4,4,1,1024]{3,1,2,0:T(4,128)(2,1)S(1)}, bf16[4,4,1,1024]{3,1,2,0:T(4,128)(2,1)S(1)}, u32[]{:S(2)}, u32[]{:S(2)}) collective-permute-start(bf16[4,4,1,1024]{3,1,2,0:T(4,128)(2,1)S(1)} %get-tuple-element.297), channel_id=1, source_target_pairs={{0,1},{1,2},{2,3},{3,4},{4,5},{5,6},{6,7},{7,0},{8,9},{9,10},{10,1... | collective-permute-start | bytes 98312 | tf_op jit(solution)/shard_map/ppermute | solution.py:21
  4.6 3.1 %collective-permute-start.2 = (bf16[4,4,1,1024]{3,1,2,0:T(4,128)(2,1)S(1)}, bf16[4,4,1,1024]{3,1,2,0:T(4,128)(2,1)S(1)}, u32[]{:S(2)}, u32[]{:S(2)}) collective-permute-start(bf16[4,4,1,1024]{3,1,2,0:T(4,128)(2,1)S(1)} %get-tuple-element.296), channel_id=1, source_target_pairs={{1,0},{2,1},{3,2},{4,3},{5,4},{6,5},{7,6},{0,7},{9,8},{10,9},{11,1... | collective-permute-start | bytes 98312 | tf_op jit(solution)/shard_map/ppermute | solution.py:23
  7.7 1.8 collective-permute-done.1
  15.3 2.1 collective-permute-done.4
  17.5 4.1 %multiply_reduce_fusion = (f32[4,4,9]{1,2,0:T(8,128)S(1)}, f32[4,4,9,1024]{3,1,2,0:T(4,128)S(1)}) fusion(bf16[4,1,11,1024]{3,1,2,0:T(2,128)(2,1)S(1)} %collective-permute-done.4, bf16[4,4,11,1024]{3,1,2,0:T(4,128)(2,1)S(1)} %constant_dynamic-update-slice_fusion, f32[1024]{0:T(1024)S(1)} %bitcast.104, f32[1024]{0:T(1024)S(1)} %bitcast.105, ...), kind=kLoop, calls=%fused_computation.68 | loop fusion | flops 8109936 | bytes 1528384 | tf_op jit(solution)/shard_map/reduce_sum | solution.py:84
  21.6 1.4 copy.82
  23.0 1.3 reshape.114
  24.5 3.0 %fusion.21 = bf16[144,2048]{1,0:T(8,128)(2,1)S(1)} fusion(bf16[1024,3072]{1,0:T(8,128)(2,1)} %param.11, f32[144,1024]{1,0:T(8,128)S(1)} %reshape.114, f32[144]{0:T(256)S(1)} %rsqrt.12), kind=kOutput, calls=%fused_computation.29 | convolution fusion | flops 604569600 | bytes 5374528 | tf_op jit(solution)/shard_map/dot_general | solution.py:92
  28.8 2.6 copy.84
  31.3 6.7 %collective-permute-start.5 = (bf16[4,4,9,2048]{3,1,2,0:T(4,128)(2,1)}, bf16[4,4,9,2048]{3,1,2,0:T(4,128)(2,1)}, u32[]{:S(2)}, u32[]{:S(2)}) collective-permute-start(bf16[4,4,9,2048]{3,1,2,0:T(4,128)(2,1)} %copy.84), channel_id=1, source_target_pairs={{0,8},{8,16},{16,24},{1,9},{9,17},{17,25},{2,10},{10,18},{18,26},{... | collective-permute-start | bytes 1769480 | tf_op jit(solution)/shard_map/ppermute | solution.py:21
  38.1 1.5 collective-permute-start.6
  39.8 2.8 %fusion.37 = bf16[144,1024]{1,0:T(8,128)(2,1)} fusion(bf16[1024,3072]{1,0:T(8,128)(2,1)} %param.11, f32[144,1024]{1,0:T(8,128)S(1)} %reshape.114, f32[144]{0:T(256)S(1)} %rsqrt.12), kind=kOutput, calls=%fused_computation.42 | convolution fusion | flops 302432256 | bytes 2982464 | tf_op jit(solution)/shard_map/dot_general | solution.py:87
  42.6 2.0 copy.96
  44.6 1.4 copy.85
  47.2 1.4 copy.87
  49.7 1.5 pad_maximum_fusion
  51.2 1.4 fusion.65
  52.6 1.5 copy.88
  54.1 2.0 bitcast_reduce_fusion.1
  56.1 1.6 fusion.20
  58.3 1.3 copy.90
  59.6 4.9 %fusion.33 = f32[144,16,64]{0,2,1:T(8,128)} fusion(bf16[432,16,64]{0,2,1:T(8,128)(2,1)} %bitcast.96, f32[16,432,144]{1,2,0:T(8,128)} %copy-done.1, f32[144,16]{0,1:T(8,128)S(1)} %broadcast_maximum_fusion, pred[432]{0:T(512)(128)(4,1)S(1)} %pad_add_fusion, f32[144,16]{0,1:T(8,128)S(1)} %get-tuple-element.316), kind=kOutput, calls=%fused_computation.37 | convolution fusion | flops 132526080 | bytes 5474736 | tf_op jit(solution)/shard_map/qhk,khd->qhd/dot_general | solution.py:65
  64.5 176.4 %while.21 = (s32[]{:T(128)}, bf16[144,2048]{1,0:T(8,128)(2,1)S(1)}, f32[144,16]{0,1:T(8,128)S(1)}, f32[144,16]{0,1:T(8,128)S(1)}, f32[144,16,64]{0,2,1:T(8,128)}...) while((s32[]{:T(128)}, bf16[144,2048]{1,0:T(8,128)(2,1)S(1)}, ...), condition=%wide.region_7.8_spmd, body=%wide.region_4.7_spmd.sunk | while | flops 89547280 | bytes 17990036 | solution.py:131
  65.2 17.6 %collective-permute-done = bf16[144,2048]{1,0:T(8,128)(2,1)S(1)} collective-permute-done((bf16[144,2048]{1,0:T(8,128)(2,1)S(1)}, bf16[144,2048]{1,0:T(8,128)(2,1)S(1)}, u32[]{:S(2)}, u32[]{:S(2)}) %collective-permute-start) | collective-permute-done | bytes 589856 | tf_op jit(solution)/shard_map/while/body/eval_jaxpr/ppermute | solution.py:32
  85.8 2.3 bitcast_reduce_fusion.3
  92.2 17.7 %collective-permute-done = bf16[144,2048]{1,0:T(8,128)(2,1)S(1)} collective-permute-done((bf16[144,2048]{1,0:T(8,128)(2,1)S(1)}, bf16[144,2048]{1,0:T(8,128)(2,1)S(1)}, u32[]{:S(2)}, u32[]{:S(2)}) %collective-permute-start) | collective-permute-done | bytes 589856 | tf_op jit(solution)/shard_map/while/body/eval_jaxpr/ppermute | solution.py:32
  112.9 2.3 bitcast_reduce_fusion.3
  119.3 16.9 %collective-permute-done = bf16[144,2048]{1,0:T(8,128)(2,1)S(1)} collective-permute-done((bf16[144,2048]{1,0:T(8,128)(2,1)S(1)}, bf16[144,2048]{1,0:T(8,128)(2,1)S(1)}, u32[]{:S(2)}, u32[]{:S(2)}) %collective-permute-start) | collective-permute-done | bytes 589856 | tf_op jit(solution)/shard_map/while/body/eval_jaxpr/ppermute | solution.py:32
  139.2 2.3 bitcast_reduce_fusion.3
  142.7 1.3 fusion.92
  145.6 16.0 %collective-permute-done = bf16[144,2048]{1,0:T(8,128)(2,1)S(1)} collective-permute-done((bf16[144,2048]{1,0:T(8,128)(2,1)S(1)}, bf16[144,2048]{1,0:T(8,128)(2,1)S(1)}, u32[]{:S(2)}, u32[]{:S(2)}) %collective-permute-start) | collective-permute-done | bytes 589856 | tf_op jit(solution)/shard_map/while/body/eval_jaxpr/ppermute | solution.py:32
  164.5 2.3 bitcast_reduce_fusion.3
  171.0 15.1 %collective-permute-done = bf16[144,2048]{1,0:T(8,128)(2,1)S(1)} collective-permute-done((bf16[144,2048]{1,0:T(8,128)(2,1)S(1)}, bf16[144,2048]{1,0:T(8,128)(2,1)S(1)}, u32[]{:S(2)}, u32[]{:S(2)}) %collective-permute-start) | collective-permute-done | bytes 589856 | tf_op jit(solution)/shard_map/while/body/eval_jaxpr/ppermute | solution.py:32
  189.0 2.3 bitcast_reduce_fusion.3
  195.4 14.1 %collective-permute-done = bf16[144,2048]{1,0:T(8,128)(2,1)S(1)} collective-permute-done((bf16[144,2048]{1,0:T(8,128)(2,1)S(1)}, bf16[144,2048]{1,0:T(8,128)(2,1)S(1)}, u32[]{:S(2)}, u32[]{:S(2)}) %collective-permute-start) | collective-permute-done | bytes 589856 | tf_op jit(solution)/shard_map/while/body/eval_jaxpr/ppermute | solution.py:32
  212.5 2.3 bitcast_reduce_fusion.3
  218.9 13.2 %collective-permute-done = bf16[144,2048]{1,0:T(8,128)(2,1)S(1)} collective-permute-done((bf16[144,2048]{1,0:T(8,128)(2,1)S(1)}, bf16[144,2048]{1,0:T(8,128)(2,1)S(1)}, u32[]{:S(2)}, u32[]{:S(2)}) %collective-permute-start) | collective-permute-done | bytes 589856 | tf_op jit(solution)/shard_map/while/body/eval_jaxpr/ppermute | solution.py:32
  235.1 2.3 bitcast_reduce_fusion.3
  240.9 1.3 divide_convert_fusion
  242.3 1.6 fusion.36
  244.1 4.7 %collective-permute-start.8 = (bf16[4,4,1,1024]{3,2,1,0:T(2,128)(2,1)S(1)}, bf16[4,4,1,1024]{3,2,1,0:T(2,128)(2,1)S(1)}, u32[]{:S(2)}, u32[]{:S(2)}) collective-permute-start(bf16[4,4,1,1024]{3,2,1,0:T(2,128)(2,1)S(1)} %get-tuple-element.293), channel_id=1, source_target_pairs={{1,0},{2,1},{3,2},{4,3},{5,4},{6,5},{7,6},{0,7},{9,8},{10,9},{11,1... | collective-permute-start | bytes 98312 | tf_op jit(solution)/shard_map/ppermute | solution.py:23
  248.8 2.2 collective-permute-done.7
  253.2 3.7 %collective-permute-start.9 = (bf16[4,1,11,1024]{3,2,1,0:T(8,128)(2,1)S(1)}, bf16[4,1,11,1024]{3,2,1,0:T(8,128)(2,1)}, u32[]{:S(2)}, u32[]{:S(2)}) collective-permute-start(bf16[4,1,11,1024]{3,2,1,0:T(8,128)(2,1)S(1)} %get-tuple-element.290), channel_id=1, source_target_pairs={{0,8},{8,16},{16,24},{1,9},{9,17},{17,25},{2,10},{10,18},{18,26},{... | collective-permute-start | bytes 270344 | tf_op jit(solution)/shard_map/ppermute | solution.py:21
  256.8 1.7 fusion.69
  258.5 1.3 copy.92
  259.8 1.6 reshape_reshape.3
  262.4 1.4 maximum_maximum_fusion
  263.9 1.4 fusion.45
  (178 shorter events, 62.5 us)
Async XLA Ops:
  0.6 241.6 %copy-start = (bf16[1024,1024]{1,0:T(8,128)(2,1)S(1)}, bf16[1024,1024]{1,0:T(8,128)(2,1)}, u32[]{:S(2)}) copy-start(bf16[1024,1024]{1,0:T(8,128)(2,1)} %param.12) | copy-start | bytes 6291460
  1.6 8.0 %collective-permute-start.1 = (bf16[4,4,1,1024]{3,1,2,0:T(4,128)(2,1)S(1)}, bf16[4,4,1,1024]{3,1,2,0:T(4,128)(2,1)S(1)}, u32[]{:S(2)}, u32[]{:S(2)}) collective-permute-start(bf16[4,4,1,1024]{3,1,2,0:T(4,128)(2,1)S(1)} %get-tuple-element.297), channel_id=1, source_target_pairs={{0,1},{1,2},{2,3},{3,4},{4,5},{5,6},{6,7},{7,0},{8,9},{9,10},{10,1... | collective-permute-start | bytes 98312 | tf_op jit(solution)/shard_map/ppermute | solution.py:21
  4.6 6.0 %collective-permute-start.2 = (bf16[4,4,1,1024]{3,1,2,0:T(4,128)(2,1)S(1)}, bf16[4,4,1,1024]{3,1,2,0:T(4,128)(2,1)S(1)}, u32[]{:S(2)}, u32[]{:S(2)}) collective-permute-start(bf16[4,4,1,1024]{3,1,2,0:T(4,128)(2,1)S(1)} %get-tuple-element.296), channel_id=1, source_target_pairs={{1,0},{2,1},{3,2},{4,3},{5,4},{6,5},{7,6},{0,7},{9,8},{10,9},{11,1... | collective-permute-start | bytes 98312 | tf_op jit(solution)/shard_map/ppermute | solution.py:23
  11.0 4.4 %collective-permute-start.3 = (bf16[4,1,11,1024]{3,1,2,0:T(2,128)(2,1)S(1)}, bf16[4,1,11,1024]{3,1,2,0:T(2,128)(2,1)S(1)}, u32[]{:S(2)}, u32[]{:S(2)}) collective-permute-start(bf16[4,1,11,1024]{3,1,2,0:T(2,128)(2,1)S(1)} %get-tuple-element.294), channel_id=1, source_target_pairs={{0,8},{8,16},{16,24},{1,9},{9,17},{17,25},{2,10},{10,18},{18,26},{... | collective-permute-start | bytes 270344 | tf_op jit(solution)/shard_map/ppermute | solution.py:21
  12.3 5.2 %collective-permute-start.4 = (bf16[4,1,11,1024]{3,1,2,0:T(2,128)(2,1)S(1)}, bf16[4,1,11,1024]{3,1,2,0:T(2,128)(2,1)S(1)}, u32[]{:S(2)}, u32[]{:S(2)}) collective-permute-start(bf16[4,1,11,1024]{3,1,2,0:T(2,128)(2,1)S(1)} %get-tuple-element.295), channel_id=1, source_target_pairs={{8,0},{16,8},{24,16},{9,1},{17,9},{25,17},{10,2},{18,10},{26,18},{... | collective-permute-start | bytes 270344 | tf_op jit(solution)/shard_map/ppermute | solution.py:23
  24.3 15.5 %copy-start.3 = (f32[144,1024]{1,0:T(8,128)}, f32[144,1024]{1,0:T(8,128)S(1)}, u32[]{:S(2)}) copy-start(f32[144,1024]{1,0:T(8,128)S(1)} %reshape.114) | copy-start | bytes 1769476
  27.5 15.1 %copy-start.5 = (bf16[144,2048]{1,0:T(8,128)(2,1)}, bf16[144,2048]{1,0:T(8,128)(2,1)S(1)}, u32[]{:S(2)}) copy-start(bf16[144,2048]{1,0:T(8,128)(2,1)S(1)} %fusion.21) | copy-start | bytes 1769476
  27.5 12.1 %copy-start.14 = (s32[1,1,8]{2,1,0:T(1,128)S(1)}, s32[1,1,8]{2,1,0:T(1,128)}, u32[]{:S(2)}) copy-start(s32[1,1,8]{2,1,0:T(1,128)} %param.14) | copy-start | bytes 100
  31.3 13.3 %collective-permute-start.5 = (bf16[4,4,9,2048]{3,1,2,0:T(4,128)(2,1)}, bf16[4,4,9,2048]{3,1,2,0:T(4,128)(2,1)}, u32[]{:S(2)}, u32[]{:S(2)}) collective-permute-start(bf16[4,4,9,2048]{3,1,2,0:T(4,128)(2,1)} %copy.84), channel_id=1, source_target_pairs={{0,8},{8,16},{16,24},{1,9},{9,17},{17,25},{2,10},{10,18},{18,26},{... | collective-permute-start | bytes 1769480 | tf_op jit(solution)/shard_map/ppermute | solution.py:21
  38.1 9.1 %collective-permute-start.6 = (bf16[4,4,9,2048]{3,1,2,0:T(4,128)(2,1)}, bf16[4,4,9,2048]{3,1,2,0:T(4,128)(2,1)}, u32[]{:S(2)}, u32[]{:S(2)}) collective-permute-start(bf16[4,4,9,2048]{3,1,2,0:T(4,128)(2,1)} %copy.84), channel_id=1, source_target_pairs={{8,0},{16,8},{24,16},{9,1},{17,9},{25,17},{10,2},{18,10},{26,18},{... | collective-permute-start | bytes 1769480 | tf_op jit(solution)/shard_map/ppermute | solution.py:23
  56.1 2.1 copy-start.1
  56.1 2.1 copy-start.4
  59.6 4.9 %copy-start.6 = (bf16[144,2048]{1,0:T(8,128)(2,1)S(1)}, bf16[144,2048]{1,0:T(8,128)(2,1)}, u32[]{:S(2)}) copy-start(bf16[144,2048]{1,0:T(8,128)(2,1)} %copy-done.5) | copy-start | bytes 1769476
  64.5 18.3 %collective-permute-start = (bf16[144,2048]{1,0:T(8,128)(2,1)S(1)}, bf16[144,2048]{1,0:T(8,128)(2,1)S(1)}, u32[]{:S(2)}, u32[]{:S(2)}) collective-permute-start(bf16[144,2048]{1,0:T(8,128)(2,1)S(1)} %get-tuple-element.394), channel_id=1, source_target_pairs={{0,1},{1,2},{2,3},{3,4},{4,5},{5,6},{6,7},{7,0},{8,9},{9,10},{10,1... | collective-permute-start | bytes 1769480 | tf_op jit(solution)/shard_map/while/body/eval_jaxpr/ppermute | solution.py:32
  85.8 3.5 %copy-start.2 = (bf16[144,1024]{0,1:T(8,128)(2,1)S(1)}, bf16[144,1024]{0,1:T(8,128)(2,1)}, u32[]{:S(2)}) copy-start(bf16[144,1024]{0,1:T(8,128)(2,1)} %copy.101) | copy-start | bytes 884740 | tf_op jit(solution)/shard_map/while
  85.8 3.6 %copy-start.7 = (f32[144,16,64]{0,2,1:T(8,128)S(1)}, f32[144,16,64]{0,2,1:T(8,128)}, u32[]{:S(2)}) copy-start(f32[144,16,64]{0,2,1:T(8,128)} %get-tuple-element.397) | copy-start | bytes 1769476 | tf_op jit(solution)/shard_map/while
  90.6 1.0 copy-start.8
  91.6 18.3 %collective-permute-start = (bf16[144,2048]{1,0:T(8,128)(2,1)S(1)}, bf16[144,2048]{1,0:T(8,128)(2,1)S(1)}, u32[]{:S(2)}, u32[]{:S(2)}) collective-permute-start(bf16[144,2048]{1,0:T(8,128)(2,1)S(1)} %get-tuple-element.394), channel_id=1, source_target_pairs={{0,1},{1,2},{2,3},{3,4},{4,5},{5,6},{6,7},{7,0},{8,9},{9,10},{10,1... | collective-permute-start | bytes 1769480 | tf_op jit(solution)/shard_map/while/body/eval_jaxpr/ppermute | solution.py:32
  112.9 3.5 %copy-start.2 = (bf16[144,1024]{0,1:T(8,128)(2,1)S(1)}, bf16[144,1024]{0,1:T(8,128)(2,1)}, u32[]{:S(2)}) copy-start(bf16[144,1024]{0,1:T(8,128)(2,1)} %copy.101) | copy-start | bytes 884740 | tf_op jit(solution)/shard_map/while
  112.9 3.6 %copy-start.7 = (f32[144,16,64]{0,2,1:T(8,128)S(1)}, f32[144,16,64]{0,2,1:T(8,128)}, u32[]{:S(2)}) copy-start(f32[144,16,64]{0,2,1:T(8,128)} %get-tuple-element.397) | copy-start | bytes 1769476 | tf_op jit(solution)/shard_map/while
  117.7 1.0 copy-start.8
  118.7 17.5 %collective-permute-start = (bf16[144,2048]{1,0:T(8,128)(2,1)S(1)}, bf16[144,2048]{1,0:T(8,128)(2,1)S(1)}, u32[]{:S(2)}, u32[]{:S(2)}) collective-permute-start(bf16[144,2048]{1,0:T(8,128)(2,1)S(1)} %get-tuple-element.394), channel_id=1, source_target_pairs={{0,1},{1,2},{2,3},{3,4},{4,5},{5,6},{6,7},{7,0},{8,9},{9,10},{10,1... | collective-permute-start | bytes 1769480 | tf_op jit(solution)/shard_map/while/body/eval_jaxpr/ppermute | solution.py:32
  139.2 3.5 %copy-start.2 = (bf16[144,1024]{0,1:T(8,128)(2,1)S(1)}, bf16[144,1024]{0,1:T(8,128)(2,1)}, u32[]{:S(2)}) copy-start(bf16[144,1024]{0,1:T(8,128)(2,1)} %copy.101) | copy-start | bytes 884740 | tf_op jit(solution)/shard_map/while
  139.2 3.5 %copy-start.7 = (f32[144,16,64]{0,2,1:T(8,128)S(1)}, f32[144,16,64]{0,2,1:T(8,128)}, u32[]{:S(2)}) copy-start(f32[144,16,64]{0,2,1:T(8,128)} %get-tuple-element.397) | copy-start | bytes 1769476 | tf_op jit(solution)/shard_map/while
  144.0 1.0 copy-start.8
  145.0 16.6 %collective-permute-start = (bf16[144,2048]{1,0:T(8,128)(2,1)S(1)}, bf16[144,2048]{1,0:T(8,128)(2,1)S(1)}, u32[]{:S(2)}, u32[]{:S(2)}) collective-permute-start(bf16[144,2048]{1,0:T(8,128)(2,1)S(1)} %get-tuple-element.394), channel_id=1, source_target_pairs={{0,1},{1,2},{2,3},{3,4},{4,5},{5,6},{6,7},{7,0},{8,9},{9,10},{10,1... | collective-permute-start | bytes 1769480 | tf_op jit(solution)/shard_map/while/body/eval_jaxpr/ppermute | solution.py:32
  164.5 3.5 %copy-start.2 = (bf16[144,1024]{0,1:T(8,128)(2,1)S(1)}, bf16[144,1024]{0,1:T(8,128)(2,1)}, u32[]{:S(2)}) copy-start(bf16[144,1024]{0,1:T(8,128)(2,1)} %copy.101) | copy-start | bytes 884740 | tf_op jit(solution)/shard_map/while
  164.5 3.6 %copy-start.7 = (f32[144,16,64]{0,2,1:T(8,128)S(1)}, f32[144,16,64]{0,2,1:T(8,128)}, u32[]{:S(2)}) copy-start(f32[144,16,64]{0,2,1:T(8,128)} %get-tuple-element.397) | copy-start | bytes 1769476 | tf_op jit(solution)/shard_map/while
  169.4 1.0 copy-start.8
  170.4 15.7 %collective-permute-start = (bf16[144,2048]{1,0:T(8,128)(2,1)S(1)}, bf16[144,2048]{1,0:T(8,128)(2,1)S(1)}, u32[]{:S(2)}, u32[]{:S(2)}) collective-permute-start(bf16[144,2048]{1,0:T(8,128)(2,1)S(1)} %get-tuple-element.394), channel_id=1, source_target_pairs={{0,1},{1,2},{2,3},{3,4},{4,5},{5,6},{6,7},{7,0},{8,9},{9,10},{10,1... | collective-permute-start | bytes 1769480 | tf_op jit(solution)/shard_map/while/body/eval_jaxpr/ppermute | solution.py:32
  189.0 3.5 %copy-start.2 = (bf16[144,1024]{0,1:T(8,128)(2,1)S(1)}, bf16[144,1024]{0,1:T(8,128)(2,1)}, u32[]{:S(2)}) copy-start(bf16[144,1024]{0,1:T(8,128)(2,1)} %copy.101) | copy-start | bytes 884740 | tf_op jit(solution)/shard_map/while
  189.0 3.6 %copy-start.7 = (f32[144,16,64]{0,2,1:T(8,128)S(1)}, f32[144,16,64]{0,2,1:T(8,128)}, u32[]{:S(2)}) copy-start(f32[144,16,64]{0,2,1:T(8,128)} %get-tuple-element.397) | copy-start | bytes 1769476 | tf_op jit(solution)/shard_map/while
  193.8 1.0 copy-start.8
  194.8 14.7 %collective-permute-start = (bf16[144,2048]{1,0:T(8,128)(2,1)S(1)}, bf16[144,2048]{1,0:T(8,128)(2,1)S(1)}, u32[]{:S(2)}, u32[]{:S(2)}) collective-permute-start(bf16[144,2048]{1,0:T(8,128)(2,1)S(1)} %get-tuple-element.394), channel_id=1, source_target_pairs={{0,1},{1,2},{2,3},{3,4},{4,5},{5,6},{6,7},{7,0},{8,9},{9,10},{10,1... | collective-permute-start | bytes 1769480 | tf_op jit(solution)/shard_map/while/body/eval_jaxpr/ppermute | solution.py:32
  212.5 3.5 %copy-start.2 = (bf16[144,1024]{0,1:T(8,128)(2,1)S(1)}, bf16[144,1024]{0,1:T(8,128)(2,1)}, u32[]{:S(2)}) copy-start(bf16[144,1024]{0,1:T(8,128)(2,1)} %copy.101) | copy-start | bytes 884740 | tf_op jit(solution)/shard_map/while
  212.5 3.5 %copy-start.7 = (f32[144,16,64]{0,2,1:T(8,128)S(1)}, f32[144,16,64]{0,2,1:T(8,128)}, u32[]{:S(2)}) copy-start(f32[144,16,64]{0,2,1:T(8,128)} %get-tuple-element.397) | copy-start | bytes 1769476 | tf_op jit(solution)/shard_map/while
  218.3 13.8 %collective-permute-start = (bf16[144,2048]{1,0:T(8,128)(2,1)S(1)}, bf16[144,2048]{1,0:T(8,128)(2,1)S(1)}, u32[]{:S(2)}, u32[]{:S(2)}) collective-permute-start(bf16[144,2048]{1,0:T(8,128)(2,1)S(1)} %get-tuple-element.394), channel_id=1, source_target_pairs={{0,1},{1,2},{2,3},{3,4},{4,5},{5,6},{6,7},{7,0},{8,9},{9,10},{10,1... | collective-permute-start | bytes 1769480 | tf_op jit(solution)/shard_map/while/body/eval_jaxpr/ppermute | solution.py:32
  235.1 3.5 %copy-start.2 = (bf16[144,1024]{0,1:T(8,128)(2,1)S(1)}, bf16[144,1024]{0,1:T(8,128)(2,1)}, u32[]{:S(2)}) copy-start(bf16[144,1024]{0,1:T(8,128)(2,1)} %copy.101) | copy-start | bytes 884740 | tf_op jit(solution)/shard_map/while
  235.1 3.6 %copy-start.7 = (f32[144,16,64]{0,2,1:T(8,128)S(1)}, f32[144,16,64]{0,2,1:T(8,128)}, u32[]{:S(2)}) copy-start(f32[144,16,64]{0,2,1:T(8,128)} %get-tuple-element.397) | copy-start | bytes 1769476 | tf_op jit(solution)/shard_map/while
  244.1 7.0 %collective-permute-start.7 = (bf16[4,4,1,1024]{3,2,1,0:T(2,128)(2,1)S(1)}, bf16[4,4,1,1024]{3,2,1,0:T(2,128)(2,1)S(1)}, u32[]{:S(2)}, u32[]{:S(2)}) collective-permute-start(bf16[4,4,1,1024]{3,2,1,0:T(2,128)(2,1)S(1)} %get-tuple-element.292), channel_id=1, source_target_pairs={{0,1},{1,2},{2,3},{3,4},{4,5},{5,6},{6,7},{7,0},{8,9},{9,10},{10,1... | collective-permute-start | bytes 98312 | tf_op jit(solution)/shard_map/ppermute | solution.py:21
  244.1 7.0 %collective-permute-start.8 = (bf16[4,4,1,1024]{3,2,1,0:T(2,128)(2,1)S(1)}, bf16[4,4,1,1024]{3,2,1,0:T(2,128)(2,1)S(1)}, u32[]{:S(2)}, u32[]{:S(2)}) collective-permute-start(bf16[4,4,1,1024]{3,2,1,0:T(2,128)(2,1)S(1)} %get-tuple-element.293), channel_id=1, source_target_pairs={{1,0},{2,1},{3,2},{4,3},{5,4},{6,5},{7,6},{0,7},{9,8},{10,9},{11,1... | collective-permute-start | bytes 98312 | tf_op jit(solution)/shard_map/ppermute | solution.py:23
  251.9 10.6 %collective-permute-start.10 = (bf16[4,1,11,1024]{3,2,1,0:T(8,128)(2,1)}, bf16[4,1,11,1024]{3,2,1,0:T(8,128)(2,1)S(1)}, u32[]{:S(2)}, u32[]{:S(2)}) collective-permute-start(bf16[4,1,11,1024]{3,2,1,0:T(8,128)(2,1)} %get-tuple-element.291), channel_id=1, source_target_pairs={{8,0},{16,8},{24,16},{9,1},{17,9},{25,17},{10,2},{18,10},{26,18},{... | collective-permute-start | bytes 270344 | tf_op jit(solution)/shard_map/ppermute | solution.py:23
  253.2 9.3 %collective-permute-start.9 = (bf16[4,1,11,1024]{3,2,1,0:T(8,128)(2,1)S(1)}, bf16[4,1,11,1024]{3,2,1,0:T(8,128)(2,1)}, u32[]{:S(2)}, u32[]{:S(2)}) collective-permute-start(bf16[4,1,11,1024]{3,2,1,0:T(8,128)(2,1)S(1)} %get-tuple-element.290), channel_id=1, source_target_pairs={{0,8},{8,16},{16,24},{1,9},{9,17},{17,25},{2,10},{10,18},{18,26},{... | collective-permute-start | bytes 270344 | tf_op jit(solution)/shard_map/ppermute | solution.py:21
  261.4 2.4 copy-start.9
  261.4 2.4 copy-start.10
  261.4 2.4 copy-start.11
  261.4 2.4 copy-start.12
  261.4 2.4 copy-start.13
  (2 other events, 2.0 us)
where the time goes:
time: 268 us; the launch traced here: 266 us
  waiting for transfers between devices  117 us (44%)
  local copies, waits for them, and re-layouts  60 us (22%)
  matrix products  39.6 us (15%)
  starting transfers between devices  26.8 us (10%)
  other arithmetic  20.7 us (8%)
    ppermute x7, waiting for transfers between devices, from_behind(): return lax.ppermute(x, axis, [(i, (i + by) % size) for i in range(size)])  111 us
    dot_general x8, matrix products, attend(): jnp.einsum('qhd,khd->qhk', query, keys_part, preferred_element_type=jnp.f...  18.1 us
    slice x16, local copies, waits for them, and re-layouts, attend(): values_part = keyvals[:, width:].reshape(-1, heads, head_size)  15 us
    ppermute x5, starting transfers between devices, with_halo(): lax.ppermute(tail, axis, [(i, (i + 1) % count) for i in range(ends)])  14.8 us
    dot_general x8, matrix products, attend(): jnp.einsum('qhk,khd->qhd', weights.astype(jnp.bfloat16), values_part, pre...  14.1 us
    ppermute x5, starting transfers between devices, with_halo(): lax.ppermute(head, axis, [((i + 1) % count, i) for i in range(ends)])  11.8 us
    reduce_sum x8, other arithmetic, attend(): summed = summed * factor + jnp.sum(weights, axis=-1)  9.82 us
    slice x8, local copies, waits for them, and re-layouts, attend(): keys_part = keyvals[:, :width].reshape(-1, heads, head_size)  9.59 us
  transfers between devices with their start and end apart: 17, of which 10 were waited for; matrix products, arithmetic and copies ran while one was open for 7% of the time, Pallas kernels for 0%

commit v1 on v0

v1 whole, which is shorter than its diff:
```python
import functools

import jax
import jax.numpy as jnp
import numpy as np
from jax import lax
from jax.experimental import pallas as pl
from jax.experimental.pallas import tpu as pltpu
from jax.sharding import PartitionSpec as P

HEADS = 16
EPSILON = 1e-05
MASKED = -1e30
LANES = 128
GROUP = 256
F32 = jnp.float32
BF16 = jnp.bfloat16
VMEM_LIMIT = 40 * 1024 * 1024


def ring_order(count):
    columns = 1
    while columns * columns * 4 <= count:
        columns *= 2
    rows = count // columns
    order = [z * columns for z in range(rows)]
    for turn, z in enumerate(range(rows - 1, -1, -1)):
        ys = list(range(1, columns))
        if turn % 2:
            ys.reverse()
        order += [z * columns + y for y in ys]
    return order


def shift(x, axis, by):
    size = lax.axis_size(axis)
    return lax.ppermute(x, axis, [(i, (i + by) % size) for i in range(size)])


def spec(memory_space):
    return pl.BlockSpec(memory_space=memory_space)


def conv_taps(ext, weights_ref, level, row, columns):
    total = None
    for a in range(3):
        for b in range(3):
            term = weights_ref[3 * a + b : 3 * a + b + 1, :] * ext[level, row + a, b : b + columns, :]
            total = term if total is None else total + term
    return total


def fill_ext(ext, center_ref, north_ref, south_ref, west_ref, east_ref, inside_ref):
    levels, rows, columns, width = center_ref.shape
    has_north = (inside_ref[0] > 0).astype(F32)
    has_south = (inside_ref[1] > 0).astype(F32)
    for level in range(levels):
        ext[level, 0, 1 : columns + 1, :] = north_ref[level].astype(F32) * has_north
        ext[level, rows + 1, 1 : columns + 1, :] = south_ref[level].astype(F32) * has_south
        for row in range(rows):
            ext[level, row + 1, 1 : columns + 1, :] = center_ref[level, row].astype(F32)
    west = west_ref[...].astype(F32)
    east = east_ref[...].astype(F32)
    for level in range(levels):
        for row in range(rows + 2):
            at = level * (rows + 2) + row
            ext[level, row, 0:1, :] = west[at : at + 1]
            ext[level, row, columns + 1 : columns + 2, :] = east[at : at + 1]


def first_kernel(inside_ref, fields_ref, north_ref, south_ref, west_ref, east_ref, weights_ref, stream_ref, normed_ref, ext, dense):
    levels, rows, columns, width = fields_ref.shape
    fill_ext(ext, fields_ref, north_ref, south_ref, west_ref, east_ref, inside_ref)
    for level in range(levels):
        for row in range(rows):
            total = conv_taps(ext, weights_ref, level, row, columns)
            value = ext[level, row + 1, 1 : columns + 1, :] + total
            at = (level * rows + row) * columns
            dense[at : at + columns, :] = value
    stream = dense[...].astype(BF16)
    stream_ref[...] = stream
    wide = stream.astype(F32)
    mean = jnp.mean(wide * wide, axis=-1, keepdims=True)
    normed_ref[...] = (wide * lax.rsqrt(mean + EPSILON)).astype(BF16)


def second_kernel(inside_ref, after_ref, north_ref, south_ref, west_ref, east_ref, weights_ref, mixed_ref, ext):
    levels, rows, columns, width = after_ref.shape
    fill_ext(ext, after_ref, north_ref, south_ref, west_ref, east_ref, inside_ref)
    for level in range(levels):
        for row in range(rows):
            total = conv_taps(ext, weights_ref, level, row, columns)
            mixed_ref[level, row] = (ext[level, row + 1, 1 : columns + 1, :] + total).astype(BF16)


def pair_attend(query2, keys2, values2, bias, factor):
    half = query2.shape[0] // 2
    scores = lax.dot_general(query2, keys2, (((1,), (1,)), ((), ())), preferred_element_type=F32)
    if bias is not None:
        scores = scores + bias
    highest = jnp.max(scores, axis=-1, keepdims=True)
    weights = jnp.exp2((scores - highest) * factor)
    summed = jnp.sum(weights, axis=-1, keepdims=True)
    result = jnp.dot(weights.astype(BF16), values2, preferred_element_type=F32)
    low = lax.broadcasted_iota(jnp.int32, (half, LANES), 1) < LANES // 2
    merge = lambda x: jnp.where(low, x[:half], x[half:])
    return merge(highest), merge(summed), merge(result)


def key_bias(flags_ref, slots, sizes):
    if all(slot < 0 for slot in slots):
        return None
    lane = lax.broadcasted_iota(jnp.int32, (1, sum(sizes)), 1)
    bias = jnp.zeros((1, sum(sizes)), F32)
    start = 0
    for slot, size in zip(slots, sizes):
        if slot >= 0:
            value = jnp.where(flags_ref[slot] > 0, 0.0, MASKED).astype(F32)
            bias = jnp.where((lane >= start) & (lane < start + size), value, bias)
        start += size
    return bias


def project(blocks, wk_ref, wv_ref):
    x = blocks[0][...] if len(blocks) == 1 else jnp.concatenate([b[...] for b in blocks], axis=0)
    keys = jnp.dot(x, wk_ref[...], preferred_element_type=F32).astype(BF16)
    values = jnp.dot(x, wv_ref[...], preferred_element_type=F32).astype(BF16)
    return keys, values


def own_kernel(factor, x_ref, wq_ref, wk_ref, wv_ref, query_ref, high_ref, sum_ref, acc_ref):
    tokens = x_ref.shape[0]
    query = jnp.dot(x_ref[...], wq_ref[...], preferred_element_type=F32).astype(BF16)
    keys, values = project([x_ref], wk_ref, wv_ref)
    low = lax.broadcasted_iota(jnp.int32, (tokens, LANES), 1) < LANES // 2
    zero = jnp.zeros((tokens, LANES), BF16)
    for pair in range(GROUP // LANES):
        lanes = slice(pair * LANES, (pair + 1) * LANES)
        part = query[:, lanes]
        query2 = jnp.concatenate([jnp.where(low, part, zero), jnp.where(low, zero, part)], axis=0)
        query_ref[pair] = query2
        high, summed, result = pair_attend(query2, keys[:, lanes], values[:, lanes], None, factor)
        high_ref[:, lanes] = high
        sum_ref[:, lanes] = summed
        acc_ref[:, lanes] = result


def combine(state, part, factor):
    high = jnp.maximum(state[0], part[0])
    old = jnp.exp2((state[0] - high) * factor)
    new = jnp.exp2((part[0] - high) * factor)
    return high, state[1] * old + part[1] * new, state[2] * old + part[2] * new


def batch_kernel(factor, slots, sizes, flags_ref, query_ref, wk_ref, wv_ref, high_in, sum_in, acc_in, *refs):
    blocks, (high_ref, sum_ref, acc_ref) = refs[:-3], refs[-3:]
    keys, values = project(blocks, wk_ref, wv_ref)
    bias = key_bias(flags_ref, slots, sizes)
    for pair in range(GROUP // LANES):
        lanes = slice(pair * LANES, (pair + 1) * LANES)
        part = pair_attend(query_ref[pair], keys[:, lanes], values[:, lanes], bias, factor)
        state = combine((high_in[:, lanes], sum_in[:, lanes], acc_in[:, lanes]), part, factor)
        high_ref[:, lanes], sum_ref[:, lanes], acc_ref[:, lanes] = state


def last_kernel(
    factor, slots, sizes, flags_ref, query_ref, wk_ref, wv_ref, high_in, sum_in, acc_in, wo_ref, stream_ref, *refs
):
    count = len(sizes)
    blocks = refs[:count]
    attended_ref, after_ref, north_ref, south_ref, west_ref, east_ref, total, dense = refs[count:]
    group = pl.program_id(0)
    levels, rows, columns, width = after_ref.shape
    keys, values = project(blocks, wk_ref, wv_ref)
    bias = key_bias(flags_ref, slots, sizes)
    for pair in range(GROUP // LANES):
        lanes = slice(pair * LANES, (pair + 1) * LANES)
        part = pair_attend(query_ref[pair], keys[:, lanes], values[:, lanes], bias, factor)
        _, summed, result = combine((high_in[:, lanes], sum_in[:, lanes], acc_in[:, lanes]), part, factor)
        dense[:, lanes] = result / summed
    for level in range(levels):
        for row in range(rows):
            at = (level * rows + row) * columns
            attended_ref[level, row] = dense[at : at + columns, 0:GROUP].astype(BF16)
    product = jnp.dot(dense[:, 0:GROUP].astype(BF16), wo_ref[...], preferred_element_type=F32)

    @pl.when(group == 0)
    def _():
        total[...] = stream_ref[...].astype(F32) + product

    @pl.when(group > 0)
    def _():
        total[...] += product

    @pl.when(group == pl.num_programs(0) - 1)
    def _():
        for level in range(levels):
            for row in range(rows):
                at = (level * rows + row) * columns
                value = total[at : at + columns, :].astype(BF16)
                after_ref[level, row] = value
                if row == 0:
                    north_ref[level] = value
                if row == rows - 1:
                    south_ref[level] = value
        west = [total[i * columns : i * columns + 1, :] for i in range(levels * rows)]
        east = [total[(i + 1) * columns - 1 : (i + 1) * columns, :] for i in range(levels * rows)]
        west_ref[...] = jnp.concatenate(west, axis=0).astype(BF16)
        east_ref[...] = jnp.concatenate(east, axis=0).astype(BF16)


def shape(dims, kind):
    return jax.ShapeDtypeStruct(dims, kind)


def params():
    return pltpu.CompilerParams(vmem_limit_bytes=VMEM_LIMIT)


def cost(flops, size):
    return pl.CostEstimate(flops=int(flops), bytes_accessed=int(size), transcendentals=0)


def exchange(north_edge, south_edge, west_edge, east_edge, inside):
    levels, columns, width = north_edge.shape
    north = shift(south_edge, "lat", 1)
    south = shift(north_edge, "lat", -1)
    keep_north = inside[0] > 0
    keep_south = inside[1] > 0

    def column(middle, at):
        top = jnp.where(keep_north, north[:, at : at + 1], 0)
        bottom = jnp.where(keep_south, south[:, at : at + 1], 0)
        return jnp.concatenate([top, middle, bottom], axis=1).reshape(-1, width)

    west = shift(column(east_edge, columns - 1), "lon", 1)
    east = shift(column(west_edge, 0), "lon", -1)
    return north, south, west, east


def local(fields, conv_first, w_qkv, w_out, conv_second, key_list, key_count):
    levels, rows, columns, width = fields.shape
    tokens = levels * rows * columns
    groups = width // GROUP
    pairs = GROUP // LANES
    head_size = width // HEADS
    factor = float(np.log2(np.e) * head_size ** -0.5)
    lat_here = lax.axis_index("lat")
    lat_total = lax.axis_size("lat")
    lon_here = lax.axis_index("lon")
    lon_total = lax.axis_size("lon")
    order = ring_order(lon_total)
    place = {lon: i for i, lon in enumerate(order)}
    half = lon_total // 2
    sources = np.zeros((lon_total, lon_total), np.int32)
    for lon in range(lon_total):
        row = [lon]
        for step in range(1, half):
            row += [order[(place[lon] - step) % lon_total], order[(place[lon] + step) % lon_total]]
        row.append(order[(place[lon] + half) % lon_total])
        sources[lon] = row
    inside = jnp.stack([lat_here > 0, lat_here < lat_total - 1]).astype(jnp.int32)
    listed = key_list.reshape(lon_total)
    used = jnp.arange(lon_total, dtype=jnp.int32) < key_count.reshape(())
    mine = jnp.arange(lon_total, dtype=jnp.int32) == lon_here
    source = jnp.sum(jnp.where(mine[:, None], sources, 0), axis=0)
    linked = jnp.any((listed[None, :] == source[:, None]) & used[None, :], axis=1).astype(jnp.int32)
    flags = jnp.concatenate([inside, linked])
    slot_of = lambda position: 2 + position

    smem = spec(pltpu.SMEM)
    vmem = spec(pltpu.VMEM)
    ext = pltpu.VMEM((levels, rows + 2, 16, width), F32)

    north, south, west, east = exchange(
        fields[:, 0], fields[:, rows - 1], fields[:, :, 0], fields[:, :, columns - 1], inside
    )
    stream, normed = pl.pallas_call(
        first_kernel,
        out_shape=(shape((tokens, width), BF16), shape((tokens, width), BF16)),
        in_specs=[smem] + [vmem] * 6,
        out_specs=(vmem, vmem),
        scratch_shapes=[ext, pltpu.VMEM((tokens, width), F32)],
        compiler_params=params(),
        name="conv_first",
    )(inside, fields, north, south, west, east, conv_first)

    whole = lambda n: pl.BlockSpec((n, width), lambda g: (0, 0))
    column = lambda offset: pl.BlockSpec((width, GROUP), lambda g, o=offset: (0, o * groups + g))
    state_spec = pl.BlockSpec((tokens, GROUP), lambda g: (0, g))
    state_shape = shape((tokens, width), F32)
    query_spec = pl.BlockSpec((pairs, 2 * tokens, LANES), lambda g: (g, 0, 0))

    forward = [(order[i], order[(i + 1) % lon_total]) for i in range(lon_total)]
    backward = [(b, a) for a, b in forward]

    query, *state = pl.pallas_call(
        functools.partial(own_kernel, factor),
        grid=(groups,),
        out_shape=(shape((groups * pairs, 2 * tokens, LANES), BF16), *[state_shape] * 3),
        in_specs=[whole(tokens), column(0), column(1), column(2)],
        out_specs=(query_spec, *[state_spec] * 3),
        compiler_params=params(),
        cost_estimate=cost(2 * tokens * width * 3 * width, 6 * width * width),
        name="own_block",
    )(normed, w_qkv, w_qkv, w_qkv)

    def batch(state, blocks, slots):
        sizes = [b.shape[0] for b in blocks]
        return pl.pallas_call(
            functools.partial(batch_kernel, factor, slots, sizes),
            grid=(groups,),
            out_shape=(state_shape,) * 3,
            in_specs=[smem, query_spec, column(1), column(2)] + [state_spec] * 3 + [whole(n) for n in sizes],
            out_specs=(state_spec,) * 3,
            compiler_params=params(),
            cost_estimate=cost(2 * sum(sizes) * width * 2 * width, 4 * width * width),
            name="attend_batch",
        )(flags, query, w_qkv, w_qkv, *state, *blocks)

    ahead, behind = normed, normed
    above = shift(normed, "lat", 1)
    below = shift(normed, "lat", -1)
    waiting = [(above, 0), (below, 1)]
    cut = (tokens // 32) * 16
    for step in range(1, half):
        ahead = lax.ppermute(ahead, "lon", forward)
        behind = lax.ppermute(behind, "lon", backward)
        if step > 1:
            state = batch(state, [b for b, _ in waiting], [s for _, s in waiting])
            waiting = []
        waiting += [(ahead, slot_of(2 * step - 1)), (behind, slot_of(2 * step))]
    far_first = lax.ppermute(ahead[:cut], "lon", forward)
    far_second = lax.ppermute(behind[cut:], "lon", backward)
    state = batch(state, [b for b, _ in waiting], [s for _, s in waiting])
    last_slot = slot_of(lon_total - 1)

    grid4 = (levels, rows, columns, width)
    sizes = [cut, tokens - cut]
    fixed = lambda *dims: pl.BlockSpec(dims, lambda g, n=len(dims): (0,) * n)
    attended, after, north_edge, south_edge, west_edge, east_edge = pl.pallas_call(
        functools.partial(last_kernel, factor, [last_slot] * 2, sizes),
        grid=(groups,),
        out_shape=(
            shape(grid4, BF16),
            shape(grid4, BF16),
            shape((levels, columns, width), BF16),
            shape((levels, columns, width), BF16),
            shape((levels * rows, width), BF16),
            shape((levels * rows, width), BF16),
        ),
        in_specs=[smem, query_spec, column(1), column(2)]
        + [state_spec] * 3
        + [pl.BlockSpec((GROUP, width), lambda g: (g, 0)), whole(tokens)]
        + [whole(n) for n in sizes],
        out_specs=(
            pl.BlockSpec((levels, rows, columns, GROUP), lambda g: (0, 0, 0, g)),
            fixed(*grid4),
            fixed(levels, columns, width),
            fixed(levels, columns, width),
            fixed(levels * rows, width),
            fixed(levels * rows, width),
        ),
        scratch_shapes=[pltpu.VMEM((tokens, width), F32), pltpu.VMEM((tokens, GROUP), F32)],
        compiler_params=params(),
        name="attend_last",
    )(flags, query, w_qkv, w_qkv, *state, w_out, stream, far_first, far_second)

    west_edge = west_edge.reshape(levels, rows, width)
    east_edge = east_edge.reshape(levels, rows, width)
    north, south, west, east = exchange(north_edge, south_edge, west_edge, east_edge, inside)
    mixed = pl.pallas_call(
        second_kernel,
        out_shape=shape(grid4, BF16),
        in_specs=[smem] + [vmem] * 6,
        out_specs=vmem,
        scratch_shapes=[ext],
        compiler_params=params(),
        name="conv_second",
    )(inside, after, north, south, west, east, conv_second)
    return attended, mixed


def solution(mesh):
    return jax.shard_map(
        local,
        mesh=mesh,
        in_specs=(
            P(None, "lat", "lon", None),
            P(),
            P(),
            P(),
            P(),
            P("lat", "lon", None),
            P("lat", "lon"),
        ),
        out_specs=(P(None, "lat", "lon", None), P(None, "lat", "lon", None)),
        check_vma=False,
    )
```

time: 268 us -> 94.3 us (0.35)
  waiting for transfers between devices: 117 us -> 20.5 us
  local copies, waits for them, and re-layouts: 60 us -> 9.6 us
  matrix products: 39.6 us -> 0 us
  Pallas kernels: 0 us -> 34.7 us
  other arithmetic: 20.7 us -> 2.14 us
  starting transfers between devices: 26.8 us -> 24 us
    ppermute x17 -> x18, waiting for transfers between devices: 117 us -> 20.5 us  [the longest x10 11.3 us: shift(): return lax.ppermute(x, axis, [(i, (i + by) % size) for i in range(size)])]
    dot_general x19 -> x0, matrix products: 39.6 us -> none  [the longest x8 18.1 us: attend(): jnp.einsum('qhd,khd->qhk', query, keys_part, preferred_element_type=jnp.f...]
    pallas_call x0 -> x7, Pallas kernels: none -> 34.7 us  [the longest x3 20.5 us: batch(): pl.pallas_call(functools.partial(batch_kernel, factor, slots, sizes), gri...]
    slice x29 -> x4, local copies, waits for them, and re-layouts: 28.6 us -> 1.95 us  [the longest x1 1.34 us: local(): fields[:, 0]]
    reduce_sum x9 -> x1, other arithmetic: 14 us -> 0.78 us  [local(): source = jnp.sum(jnp.where(mine[:, None], sources, 0), axis=0)]
    reshape x6, local copies, waits for them, and re-layouts: 8.1 us -> 0.13 us  [the longest x4 0.09 us: column(): return jnp.concatenate([top, middle, bottom], axis=1).reshape(-1, width)]
    while x56 -> x0, local copies, waits for them, and re-layouts: 6.87 us -> none
    dynamic_slice x7 -> x0, local copies, waits for them, and re-layouts: 4.11 us -> none  [turn(): return (buffer, visit(current, buffer, spread(linked[source])))]
  transfers between devices with their start and end apart: 17 -> 18, of which waited for: 10 -> 7; matrix products, arithmetic and copies ran while one was open for 7% -> 6% of each run, Pallas kernels for 0% -> 26%
where the time goes in v1:
time: 94.3 us; the launch traced here: 93.9 us
  Pallas kernels  34.7 us (37%)
  starting transfers between devices  24 us (25%)
  waiting for transfers between devices  20.5 us (22%)
  local copies, waits for them, and re-layouts  9.6 us (10%)
  between operations  2.89 us (3%)
  other arithmetic  2.14 us (2%)
    pallas_call x3, Pallas kernels, batch(): pl.pallas_call(functools.partial(batch_kernel, factor, slots, sizes), gri...  20.5 us
    ppermute x10, starting transfers between devices, shift(): return lax.ppermute(x, axis, [(i, (i + by) % size) for i in range(size)])  15.8 us
    ppermute x10, waiting for transfers between devices, shift(): return lax.ppermute(x, axis, [(i, (i + by) % size) for i in range(size)])  11.3 us
    ppermute x3, waiting for transfers between devices, local(): ahead = lax.ppermute(ahead, 'lon', forward)  9.18 us
    unnamed x15, local copies, waits for them, and re-layouts  6.72 us
    pallas_call x1, Pallas kernels, local(): pl.pallas_call(functools.partial(last_kernel, factor, [last_slot] * 2, si...  5.69 us
    pallas_call x1, Pallas kernels, local(): pl.pallas_call(functools.partial(own_kernel, factor), grid=(groups,), out...  4.27 us
    ppermute x3, starting transfers between devices, local(): ahead = lax.ppermute(ahead, 'lon', forward)  3.33 us
  transfers between devices with their start and end apart: 18, of which 7 were waited for; matrix products, arithmetic and copies ran while one was open for 6% of the time, Pallas kernels for 26%

profile of v1, /device:TPU:0, one launch (start us, length us, event | category | flops | bytes accessed | tf_op | source)
XLA Modules:
  0.0 93.9 jit_solution(15689297358179625759)
XLA Ops:
  0.6 1.3 %fusion = (bf16[4,1,9,1024]{3,1,2,0:T(2,128)(2,1)S(1)}, bf16[4,1,9,1024]{3,1,2,0:T(2,128)(2,1)S(1)}) fusion(bf16[4,4,9,1024]{3,1,2,0:T(4,128)(2,1)} %param.8), kind=kLoop, calls=%fused_computation.22 | loop fusion | bytes 294912 | tf_op jit(solution)/shard_map/slice | solution.py:276
  2.0 0.5 collective-permute-start
  2.6 2.0 %collective-permute-start.1 = (bf16[4,9,1024]{2,1,0:T(8,128)(2,1)S(1)}, bf16[4,9,1024]{2,1,0:T(8,128)(2,1)S(1)}, u32[]{:S(2)}, u32[]{:S(2)}) collective-permute-start(bf16[4,9,1024]{2,1,0:T(8,128)(2,1)S(1)} %bitcast.18), channel_id=1, source_target_pairs={{0,24},{8,0},{16,8},{24,16},{1,25},{9,1},{17,9},{25,17},{2,26},{10... | collective-permute-start | bytes 221192 | tf_op jit(solution)/shard_map/ppermute | solution.py:37
  4.6 0.8 slice_bitcast_fusion
  5.4 0.1 add_convert_fusion.inside_ref
  5.4 0.6 fusion.1
  7.4 0.9 %collective-permute-done.1.south_ref = bf16[4,9,1024]{2,1,0:T(8,128)(2,1)S(1)} collective-permute-done((bf16[4,9,1024]{2,1,0:T(8,128)(2,1)S(1)}, bf16[4,9,1024]{2,1,0:T(8,128)(2,1)S(1)}, u32[]{:S(2)}, u32[]{:S(2)}) %collective-permute-start.1) | collective-permute-done | bytes 73760 | tf_op jit(solution)/shard_map/ppermute | solution.py:37
  8.4 0.1 pad_maximum_fusion
  8.5 1.6 %collective-permute-start.2 = (bf16[24,1024]{1,0:T(8,128)(2,1)S(1)}, bf16[24,1024]{1,0:T(8,128)(2,1)S(1)}, u32[]{:S(2)}, u32[]{:S(2)}) collective-permute-start(bf16[24,1024]{1,0:T(8,128)(2,1)S(1)} %reshape.40), channel_id=1, source_target_pairs={{0,1},{1,2},{2,3},{3,4},{4,5},{5,6},{6,7},{7,0},{8,9},{9,10},{10,1... | collective-permute-start | bytes 147464 | tf_op jit(solution)/shard_map/ppermute | solution.py:37
  10.0 0.1 pad_maximum_fusion.1
  10.1 3.3 %collective-permute-start.3 = (bf16[24,1024]{1,0:T(8,128)(2,1)S(1)}, bf16[24,1024]{1,0:T(8,128)(2,1)S(1)}, u32[]{:S(2)}, u32[]{:S(2)}) collective-permute-start(bf16[24,1024]{1,0:T(8,128)(2,1)S(1)} %reshape.41), channel_id=1, source_target_pairs={{0,7},{1,0},{2,1},{3,2},{4,3},{5,4},{6,5},{7,6},{8,15},{9,8},{10,9... | collective-permute-start | bytes 147464 | tf_op jit(solution)/shard_map/ppermute | solution.py:37
  13.4 1.1 %copy.22.fields_ref = bf16[4,4,9,1024]{3,2,1,0:T(8,128)(2,1)S(1)} copy(bf16[4,4,9,1024]{3,1,2,0:T(4,128)(2,1)} %param.8) | data formatting | bytes 589824 | tf_op args[0]
  14.5 1.0 %collective-permute-done.2.west_ref = bf16[24,1024]{1,0:T(8,128)(2,1)S(1)} collective-permute-done((bf16[24,1024]{1,0:T(8,128)(2,1)S(1)}, bf16[24,1024]{1,0:T(8,128)(2,1)S(1)}, u32[]{:S(2)}, u32[]{:S(2)}) %collective-permute-start.2) | collective-permute-done | bytes 49184 | tf_op jit(solution)/shard_map/ppermute | solution.py:37
  15.5 0.8 copy-done.3
  16.3 2.2 %conv_first.1 = (bf16[144,1024]{1,0:T(8,128)(2,1)S(1)}, bf16[144,1024]{1,0:T(8,128)(2,1)S(1)}) custom-call(s32[2]{0:T(128)S(1)} %add_convert_fusion.inside_ref, bf16[4,4,9,1024]{3,2,1,0:T(8,128)(2,1)S(1)} %copy.22.fields_ref, bf16[4,9,1024]{2,1,0:T(8,128)(2,1)S(1)} %collective-permute-done.north_ref, ...), custom_call_target="tpu_custom_call" | custom-call | tf_op jit(solution)/shard_map/conv_first/pallas_call | solution.py:278
  18.5 1.2 %collective-permute-start.6 = (bf16[144,1024]{1,0:T(8,128)(2,1)S(1)}, bf16[144,1024]{1,0:T(8,128)(2,1)S(1)}, u32[]{:S(2)}, u32[]{:S(2)}) collective-permute-start(bf16[144,1024]{1,0:T(8,128)(2,1)S(1)} %get-tuple-element.23.x_ref), channel_id=1, source_target_pairs={{0,2},{2,4},{4,6},{6,7},{7,5},{5,3},{3,1},{1,0},{8,10},{10,12},{12... | collective-permute-start | bytes 884744 | tf_op jit(solution)/shard_map/ppermute | solution.py:327
  19.7 0.9 collective-permute-start.7
  21.3 0.8 select_reduce_fusion
  22.1 5.6 %collective-permute-done.6.refs_2_ = bf16[144,1024]{1,0:T(8,128)(2,1)S(1)} collective-permute-done((bf16[144,1024]{1,0:T(8,128)(2,1)S(1)}, bf16[144,1024]{1,0:T(8,128)(2,1)S(1)}, u32[]{:S(2)}, u32[]{:S(2)}) %collective-permute-start.6) | collective-permute-done | bytes 294944 | tf_op jit(solution)/shard_map/ppermute | solution.py:327
  27.7 1.1 %collective-permute-start.8 = (bf16[144,1024]{1,0:T(8,128)(2,1)S(1)}, bf16[144,1024]{1,0:T(8,128)(2,1)S(1)}, u32[]{:S(2)}, u32[]{:S(2)}) collective-permute-start(bf16[144,1024]{1,0:T(8,128)(2,1)S(1)} %collective-permute-done.6.refs_2_), channel_id=1, source_target_pairs={{0,2},{2,4},{4,6},{6,7},{7,5},{5,3},{3,1},{1,0},{8,10},{10,12},{12... | collective-permute-start | bytes 884744 | tf_op jit(solution)/shard_map/ppermute | solution.py:327
  28.8 0.9 collective-permute-start.9
  29.7 1.7 %collective-permute-start.5 = (bf16[144,1024]{1,0:T(8,128)(2,1)S(1)}, bf16[144,1024]{1,0:T(8,128)(2,1)S(1)}, u32[]{:S(2)}, u32[]{:S(2)}) collective-permute-start(bf16[144,1024]{1,0:T(8,128)(2,1)S(1)} %get-tuple-element.23.x_ref), channel_id=1, source_target_pairs={{0,24},{8,0},{16,8},{24,16},{1,25},{9,1},{17,9},{25,17},{2,26},{10... | collective-permute-start | bytes 884744 | tf_op jit(solution)/shard_map/ppermute | solution.py:37
  31.5 0.8 and_reduce_fusion
  32.3 0.1 pad_add_fusion.flags_ref
  32.4 3.6 %collective-permute-done.8.refs_0_ = bf16[144,1024]{1,0:T(8,128)(2,1)S(1)} collective-permute-done((bf16[144,1024]{1,0:T(8,128)(2,1)S(1)}, bf16[144,1024]{1,0:T(8,128)(2,1)S(1)}, u32[]{:S(2)}, u32[]{:S(2)}) %collective-permute-start.8) | collective-permute-done | bytes 294944 | tf_op jit(solution)/shard_map/ppermute | solution.py:327
  35.9 1.0 %collective-permute-start.10 = (bf16[144,1024]{1,0:T(8,128)(2,1)S(1)}, bf16[144,1024]{1,0:T(8,128)(2,1)S(1)}, u32[]{:S(2)}, u32[]{:S(2)}) collective-permute-start(bf16[144,1024]{1,0:T(8,128)(2,1)S(1)} %collective-permute-done.8.refs_0_), channel_id=1, source_target_pairs={{0,2},{2,4},{4,6},{6,7},{7,5},{5,3},{3,1},{1,0},{8,10},{10,12},{12... | collective-permute-start | bytes 884744 | tf_op jit(solution)/shard_map/ppermute | solution.py:327
  37.0 1.0 %collective-permute-start.11 = (bf16[144,1024]{1,0:T(8,128)(2,1)S(1)}, bf16[144,1024]{1,0:T(8,128)(2,1)S(1)}, u32[]{:S(2)}, u32[]{:S(2)}) collective-permute-start(bf16[144,1024]{1,0:T(8,128)(2,1)S(1)} %collective-permute-done.9.refs_1_), channel_id=1, source_target_pairs={{2,0},{4,2},{6,4},{7,6},{5,7},{3,5},{1,3},{0,1},{10,8},{12,10},{14... | collective-permute-start | bytes 884744 | tf_op jit(solution)/shard_map/ppermute | solution.py:328
  38.0 2.8 %copy-done = bf16[1024,3072]{1,0:T(8,128)(2,1)S(1)} copy-done((bf16[1024,3072]{1,0:T(8,128)(2,1)S(1)}, bf16[1024,3072]{1,0:T(8,128)(2,1)}, u32[]{:S(2)}) %copy-start) | copy-done | bytes 6291480
  40.8 4.3 %own_block.1 = (bf16[8,288,128]{2,1,0:T(8,128)(2,1)S(1)}, f32[144,1024]{1,0:T(8,128)S(1)}, f32[144,1024]{1,0:T(8,128)S(1)}, f32[144,1024]{1,0:T(8,128)S(1)}) custom-call(bf16[144,1024]{1,0:T(8,128)(2,1)S(1)} %get-tuple-element.23.x_ref, bf16[1024,3072]{1,0:T(8,128)(2,1)S(1)} %copy-done, bf16[1024,3072]{1,0:T(8,128)(2,1)S(1)} %copy-done, ...), custom_call_target="tpu_custom_call" | custom-call | flops 905969664 | bytes 6291456 | tf_op jit(solution)/shard_map/own_block/pallas_call | solution.py:297
  45.1 8.2 %attend_batch.3 = (f32[144,1024]{1,0:T(8,128)S(1)}, f32[144,1024]{1,0:T(8,128)S(1)}, f32[144,1024]{1,0:T(8,128)S(1)}) custom-call(s32[10]{0:T(128)S(1)} %pad_add_fusion.flags_ref, bf16[8,288,128]{2,1,0:T(8,128)(2,1)S(1)} %get-tuple-element.24.query_ref, bf16[1024,3072]{1,0:T(8,128)(2,1)S(1)} %copy-done.1, bf16[1024,3072]{1,0:T(8,128)(2,1)S(1)} %copy-done.1, ...), custom_call_target="tpu_custom_call" | custom-call | flops 2415919104 | bytes 4194304 | tf_op jit(solution)/shard_map/attend_batch/pallas_call | solution.py:310
  53.3 1.6 %collective-permute-start.13 = (bf16[80,1024]{1,0:T(8,128)(2,1)S(1)}, bf16[80,1024]{1,0:T(8,128)(2,1)S(1)}, u32[]{:S(2)}, u32[]{:S(2)}) collective-permute-start(bf16[80,1024]{1,0:T(8,128)(2,1)S(1)} %slice.71), channel_id=1, source_target_pairs={{2,0},{4,2},{6,4},{7,6},{5,7},{3,5},{1,3},{0,1},{10,8},{12,10},{14... | collective-permute-start | bytes 491528 | tf_op jit(solution)/shard_map/ppermute | solution.py:334
  54.9 0.5 collective-permute-start.12
  55.4 6.2 %attend_batch.4 = (f32[144,1024]{1,0:T(8,128)S(1)}, f32[144,1024]{1,0:T(8,128)S(1)}, f32[144,1024]{1,0:T(8,128)S(1)}) custom-call(s32[10]{0:T(128)S(1)} %pad_add_fusion.flags_ref, bf16[8,288,128]{2,1,0:T(8,128)(2,1)S(1)} %get-tuple-element.24.query_ref, bf16[1024,3072]{1,0:T(8,128)(2,1)S(1)} %copy-done.1, bf16[1024,3072]{1,0:T(8,128)(2,1)S(1)} %copy-done.1, ...), custom_call_target="tpu_custom_call" | custom-call | flops 1207959552 | bytes 4194304 | tf_op jit(solution)/shard_map/attend_batch/pallas_call | solution.py:310
  61.6 6.2 %attend_batch.5 = (f32[144,1024]{1,0:T(8,128)S(1)}, f32[144,1024]{1,0:T(8,128)S(1)}, f32[144,1024]{1,0:T(8,128)S(1)}) custom-call(s32[10]{0:T(128)S(1)} %pad_add_fusion.flags_ref, bf16[8,288,128]{2,1,0:T(8,128)(2,1)S(1)} %get-tuple-element.24.query_ref, bf16[1024,3072]{1,0:T(8,128)(2,1)S(1)} %copy-done.1, bf16[1024,3072]{1,0:T(8,128)(2,1)S(1)} %copy-done.1, ...), custom_call_target="tpu_custom_call" | custom-call | flops 1207959552 | bytes 4194304 | tf_op jit(solution)/shard_map/attend_batch/pallas_call | solution.py:310
  67.8 0.0 copy-start.4
  67.8 5.7 %attend_last.1 = (bf16[4,4,9,1024]{3,2,1,0:T(8,128)(2,1)S(1)}, bf16[4,4,9,1024]{3,2,1,0:T(8,128)(2,1)S(1)}, bf16[4,9,1024]{2,1,0:T(8,128)(2,1)S(1)}, bf16[4,9,10...) custom-call(s32[10]{0:T(128)S(1)} %pad_add_fusion.flags_ref, ...), custom_call_target="tpu_custom_call" | custom-call | tf_op jit(solution)/shard_map/attend_last/pallas_call | solution.py:341
  73.5 0.1 collective-permute-start.14
  73.6 1.7 %collective-permute-start.15 = (bf16[4,9,1024]{2,1,0:T(8,128)(2,1)S(1)}, bf16[4,9,1024]{2,1,0:T(8,128)(2,1)S(1)}, u32[]{:S(2)}, u32[]{:S(2)}) collective-permute-start(bf16[4,9,1024]{2,1,0:T(8,128)(2,1)S(1)} %get-tuple-element.41), channel_id=1, source_target_pairs={{0,24},{8,0},{16,8},{24,16},{1,25},{9,1},{17,9},{25,17},{2,26},{10... | collective-permute-start | bytes 221192 | tf_op jit(solution)/shard_map/ppermute | solution.py:37
  75.4 3.5 %collective-permute-done.14.north_ref = bf16[4,9,1024]{2,1,0:T(8,128)(2,1)S(1)} collective-permute-done((bf16[4,9,1024]{2,1,0:T(8,128)(2,1)S(1)}, bf16[4,9,1024]{2,1,0:T(8,128)(2,1)S(1)}, u32[]{:S(2)}, u32[]{:S(2)}) %collective-permute-start.14) | collective-permute-done | bytes 73760 | tf_op jit(solution)/shard_map/ppermute | solution.py:37
  79.0 0.1 pad_maximum_fusion.3
  79.1 4.8 %collective-permute-start.17 = (bf16[24,1024]{1,0:T(8,128)(2,1)S(1)}, bf16[24,1024]{1,0:T(8,128)(2,1)S(1)}, u32[]{:S(2)}, u32[]{:S(2)}) collective-permute-start(bf16[24,1024]{1,0:T(8,128)(2,1)S(1)} %reshape.45), channel_id=1, source_target_pairs={{0,7},{1,0},{2,1},{3,2},{4,3},{5,4},{6,5},{7,6},{8,15},{9,8},{10,9... | collective-permute-start | bytes 147464 | tf_op jit(solution)/shard_map/ppermute | solution.py:37
  83.9 0.1 pad_maximum_fusion.2
  84.0 0.1 collective-permute-start.16
  84.1 1.0 %copy.23 = bf16[4,4,9,1024]{3,1,2,0:T(4,128)(2,1)} copy(bf16[4,4,9,1024]{3,2,1,0:T(8,128)(2,1)S(1)} %get-tuple-element.48) | data formatting | bytes 589824
  85.0 0.6 collective-permute-done.17.east_ref
  85.7 5.2 %collective-permute-done.16.west_ref = bf16[24,1024]{1,0:T(8,128)(2,1)S(1)} collective-permute-done((bf16[24,1024]{1,0:T(8,128)(2,1)S(1)}, bf16[24,1024]{1,0:T(8,128)(2,1)S(1)}, u32[]{:S(2)}, u32[]{:S(2)}) %collective-permute-start.16) | collective-permute-done | bytes 49184 | tf_op jit(solution)/shard_map/ppermute | solution.py:37
  90.9 2.1 %conv_second.1 = bf16[4,4,9,1024]{3,2,1,0:T(8,128)(2,1)S(1)} custom-call(s32[2]{0:T(128)S(1)} %add_convert_fusion.inside_ref, bf16[4,4,9,1024]{3,2,1,0:T(8,128)(2,1)S(1)} %get-tuple-element.39.after_ref, bf16[4,9,1024]{2,1,0:T(8,128)(2,1)S(1)} %collective-permute-done.14.north_ref, bf16[4,9,1024]{2,1,0:T(8,128)(2,1)S(1)} %collective-permute-done.15.south_ref, ...), custom_call_target="tpu_custom_call" | custom-call | tf_op jit(solution)/shard_map/conv_second/pallas_call | solution.py:372
  92.9 1.0 %copy.24 = bf16[4,4,9,1024]{3,1,2,0:T(4,128)(2,1)} copy(bf16[4,4,9,1024]{3,2,1,0:T(8,128)(2,1)S(1)} %conv_second.1) | data formatting | bytes 589824
  (36 shorter events, 0.4 us)
Async XLA Ops:
  2.0 5.3 %collective-permute-start = (bf16[4,9,1024]{2,1,0:T(8,128)(2,1)S(1)}, bf16[4,9,1024]{2,1,0:T(8,128)(2,1)S(1)}, u32[]{:S(2)}, u32[]{:S(2)}) collective-permute-start(bf16[4,9,1024]{2,1,0:T(8,128)(2,1)S(1)} %bitcast.17), channel_id=1, source_target_pairs={{0,8},{8,16},{16,24},{24,0},{1,9},{9,17},{17,25},{25,1},{2,10},{10... | collective-permute-start | bytes 221192 | tf_op jit(solution)/shard_map/ppermute | solution.py:37
  2.6 5.8 %collective-permute-start.1 = (bf16[4,9,1024]{2,1,0:T(8,128)(2,1)S(1)}, bf16[4,9,1024]{2,1,0:T(8,128)(2,1)S(1)}, u32[]{:S(2)}, u32[]{:S(2)}) collective-permute-start(bf16[4,9,1024]{2,1,0:T(8,128)(2,1)S(1)} %bitcast.18), channel_id=1, source_target_pairs={{0,24},{8,0},{16,8},{24,16},{1,25},{9,1},{17,9},{25,17},{2,26},{10... | collective-permute-start | bytes 221192 | tf_op jit(solution)/shard_map/ppermute | solution.py:37
  8.5 7.0 %collective-permute-start.2 = (bf16[24,1024]{1,0:T(8,128)(2,1)S(1)}, bf16[24,1024]{1,0:T(8,128)(2,1)S(1)}, u32[]{:S(2)}, u32[]{:S(2)}) collective-permute-start(bf16[24,1024]{1,0:T(8,128)(2,1)S(1)} %reshape.40), channel_id=1, source_target_pairs={{0,1},{1,2},{2,3},{3,4},{4,5},{5,6},{6,7},{7,0},{8,9},{9,10},{10,1... | collective-permute-start | bytes 147464 | tf_op jit(solution)/shard_map/ppermute | solution.py:37
  10.1 5.4 %collective-permute-start.3 = (bf16[24,1024]{1,0:T(8,128)(2,1)S(1)}, bf16[24,1024]{1,0:T(8,128)(2,1)S(1)}, u32[]{:S(2)}, u32[]{:S(2)}) collective-permute-start(bf16[24,1024]{1,0:T(8,128)(2,1)S(1)} %reshape.41), channel_id=1, source_target_pairs={{0,7},{1,0},{2,1},{3,2},{4,3},{5,4},{6,5},{7,6},{8,15},{9,8},{10,9... | collective-permute-start | bytes 147464 | tf_op jit(solution)/shard_map/ppermute | solution.py:37
  15.5 0.8 copy-start.3
  18.5 9.1 %collective-permute-start.6 = (bf16[144,1024]{1,0:T(8,128)(2,1)S(1)}, bf16[144,1024]{1,0:T(8,128)(2,1)S(1)}, u32[]{:S(2)}, u32[]{:S(2)}) collective-permute-start(bf16[144,1024]{1,0:T(8,128)(2,1)S(1)} %get-tuple-element.23.x_ref), channel_id=1, source_target_pairs={{0,2},{2,4},{4,6},{6,7},{7,5},{5,3},{3,1},{1,0},{8,10},{10,12},{12... | collective-permute-start | bytes 884744 | tf_op jit(solution)/shard_map/ppermute | solution.py:327
  19.7 9.0 %collective-permute-start.7 = (bf16[144,1024]{1,0:T(8,128)(2,1)S(1)}, bf16[144,1024]{1,0:T(8,128)(2,1)S(1)}, u32[]{:S(2)}, u32[]{:S(2)}) collective-permute-start(bf16[144,1024]{1,0:T(8,128)(2,1)S(1)} %get-tuple-element.23.x_ref), channel_id=1, source_target_pairs={{2,0},{4,2},{6,4},{7,6},{5,7},{3,5},{1,3},{0,1},{10,8},{12,10},{14... | collective-permute-start | bytes 884744 | tf_op jit(solution)/shard_map/ppermute | solution.py:328
  27.7 8.3 %collective-permute-start.8 = (bf16[144,1024]{1,0:T(8,128)(2,1)S(1)}, bf16[144,1024]{1,0:T(8,128)(2,1)S(1)}, u32[]{:S(2)}, u32[]{:S(2)}) collective-permute-start(bf16[144,1024]{1,0:T(8,128)(2,1)S(1)} %collective-permute-done.6.refs_2_), channel_id=1, source_target_pairs={{0,2},{2,4},{4,6},{6,7},{7,5},{5,3},{3,1},{1,0},{8,10},{10,12},{12... | collective-permute-start | bytes 884744 | tf_op jit(solution)/shard_map/ppermute | solution.py:327
  28.8 8.2 %collective-permute-start.9 = (bf16[144,1024]{1,0:T(8,128)(2,1)S(1)}, bf16[144,1024]{1,0:T(8,128)(2,1)S(1)}, u32[]{:S(2)}, u32[]{:S(2)}) collective-permute-start(bf16[144,1024]{1,0:T(8,128)(2,1)S(1)} %collective-permute-done.7.refs_3_), channel_id=1, source_target_pairs={{2,0},{4,2},{6,4},{7,6},{5,7},{3,5},{1,3},{0,1},{10,8},{12,10},{14... | collective-permute-start | bytes 884744 | tf_op jit(solution)/shard_map/ppermute | solution.py:328
  29.7 15.3 %collective-permute-start.4 = (bf16[144,1024]{1,0:T(8,128)(2,1)S(1)}, bf16[144,1024]{1,0:T(8,128)(2,1)S(1)}, u32[]{:S(2)}, u32[]{:S(2)}) collective-permute-start(bf16[144,1024]{1,0:T(8,128)(2,1)S(1)} %get-tuple-element.23.x_ref), channel_id=1, source_target_pairs={{0,8},{8,16},{16,24},{24,0},{1,9},{9,17},{17,25},{25,1},{2,10},{10... | collective-permute-start | bytes 884744 | tf_op jit(solution)/shard_map/ppermute | solution.py:37
  29.7 15.3 %collective-permute-start.5 = (bf16[144,1024]{1,0:T(8,128)(2,1)S(1)}, bf16[144,1024]{1,0:T(8,128)(2,1)S(1)}, u32[]{:S(2)}, u32[]{:S(2)}) collective-permute-start(bf16[144,1024]{1,0:T(8,128)(2,1)S(1)} %get-tuple-element.23.x_ref), channel_id=1, source_target_pairs={{0,24},{8,0},{16,8},{24,16},{1,25},{9,1},{17,9},{25,17},{2,26},{10... | collective-permute-start | bytes 884744 | tf_op jit(solution)/shard_map/ppermute | solution.py:37
  35.9 19.0 %collective-permute-start.10 = (bf16[144,1024]{1,0:T(8,128)(2,1)S(1)}, bf16[144,1024]{1,0:T(8,128)(2,1)S(1)}, u32[]{:S(2)}, u32[]{:S(2)}) collective-permute-start(bf16[144,1024]{1,0:T(8,128)(2,1)S(1)} %collective-permute-done.8.refs_0_), channel_id=1, source_target_pairs={{0,2},{2,4},{4,6},{6,7},{7,5},{5,3},{3,1},{1,0},{8,10},{10,12},{12... | collective-permute-start | bytes 884744 | tf_op jit(solution)/shard_map/ppermute | solution.py:327
  37.0 16.3 %collective-permute-start.11 = (bf16[144,1024]{1,0:T(8,128)(2,1)S(1)}, bf16[144,1024]{1,0:T(8,128)(2,1)S(1)}, u32[]{:S(2)}, u32[]{:S(2)}) collective-permute-start(bf16[144,1024]{1,0:T(8,128)(2,1)S(1)} %collective-permute-done.9.refs_1_), channel_id=1, source_target_pairs={{2,0},{4,2},{6,4},{7,6},{5,7},{3,5},{1,3},{0,1},{10,8},{12,10},{14... | collective-permute-start | bytes 884744 | tf_op jit(solution)/shard_map/ppermute | solution.py:328
  38.0 2.8 %copy-start = (bf16[1024,3072]{1,0:T(8,128)(2,1)S(1)}, bf16[1024,3072]{1,0:T(8,128)(2,1)}, u32[]{:S(2)}) copy-start(bf16[1024,3072]{1,0:T(8,128)(2,1)} %wv_ref.9) | copy-start | bytes 18874372
  40.8 4.3 %copy-start.1 = (bf16[1024,3072]{1,0:T(8,128)(2,1)S(1)}, bf16[1024,3072]{1,0:T(8,128)(2,1)}, u32[]{:S(2)}) copy-start(bf16[1024,3072]{1,0:T(8,128)(2,1)} %wv_ref.9) | copy-start | bytes 18874372
  53.3 14.5 %collective-permute-start.13 = (bf16[80,1024]{1,0:T(8,128)(2,1)S(1)}, bf16[80,1024]{1,0:T(8,128)(2,1)S(1)}, u32[]{:S(2)}, u32[]{:S(2)}) collective-permute-start(bf16[80,1024]{1,0:T(8,128)(2,1)S(1)} %slice.71), channel_id=1, source_target_pairs={{2,0},{4,2},{6,4},{7,6},{5,7},{3,5},{1,3},{0,1},{10,8},{12,10},{14... | collective-permute-start | bytes 491528 | tf_op jit(solution)/shard_map/ppermute | solution.py:334
  54.9 12.9 %collective-permute-start.12 = (bf16[64,1024]{1,0:T(8,128)(2,1)S(1)}, bf16[64,1024]{1,0:T(8,128)(2,1)S(1)}, u32[]{:S(2)}, u32[]{:S(2)}) collective-permute-start(bf16[64,1024]{1,0:T(8,128)(2,1)S(1)} %slice.70), channel_id=1, source_target_pairs={{0,2},{2,4},{4,6},{6,7},{7,5},{5,3},{3,1},{1,0},{8,10},{10,12},{12... | collective-permute-start | bytes 393224 | tf_op jit(solution)/shard_map/ppermute | solution.py:333
  61.6 6.2 %copy-start.2 = (bf16[1024,1024]{1,0:T(8,128)(2,1)S(1)}, bf16[1024,1024]{1,0:T(8,128)(2,1)}, u32[]{:S(2)}) copy-start(bf16[1024,1024]{1,0:T(8,128)(2,1)} %wo_ref.1) | copy-start | bytes 6291460
  67.8 23.0 %copy-start.4 = (f32[9,1024]{1,0:T(8,128)S(1)}, f32[9,1024]{1,0:T(8,128)}, u32[]{:S(2)}) copy-start(f32[9,1024]{1,0:T(8,128)} %weights_ref.3) | copy-start | bytes 110596
  73.5 5.4 %collective-permute-start.14 = (bf16[4,9,1024]{2,1,0:T(8,128)(2,1)S(1)}, bf16[4,9,1024]{2,1,0:T(8,128)(2,1)S(1)}, u32[]{:S(2)}, u32[]{:S(2)}) collective-permute-start(bf16[4,9,1024]{2,1,0:T(8,128)(2,1)S(1)} %get-tuple-element.40), channel_id=1, source_target_pairs={{0,8},{8,16},{16,24},{24,0},{1,9},{9,17},{17,25},{25,1},{2,10},{10... | collective-permute-start | bytes 221192 | tf_op jit(solution)/shard_map/ppermute | solution.py:37
  73.6 5.4 %collective-permute-start.15 = (bf16[4,9,1024]{2,1,0:T(8,128)(2,1)S(1)}, bf16[4,9,1024]{2,1,0:T(8,128)(2,1)S(1)}, u32[]{:S(2)}, u32[]{:S(2)}) collective-permute-start(bf16[4,9,1024]{2,1,0:T(8,128)(2,1)S(1)} %get-tuple-element.41), channel_id=1, source_target_pairs={{0,24},{8,0},{16,8},{24,16},{1,25},{9,1},{17,9},{25,17},{2,26},{10... | collective-permute-start | bytes 221192 | tf_op jit(solution)/shard_map/ppermute | solution.py:37
  79.1 6.6 %collective-permute-start.17 = (bf16[24,1024]{1,0:T(8,128)(2,1)S(1)}, bf16[24,1024]{1,0:T(8,128)(2,1)S(1)}, u32[]{:S(2)}, u32[]{:S(2)}) collective-permute-start(bf16[24,1024]{1,0:T(8,128)(2,1)S(1)} %reshape.45), channel_id=1, source_target_pairs={{0,7},{1,0},{2,1},{3,2},{4,3},{5,4},{6,5},{7,6},{8,15},{9,8},{10,9... | collective-permute-start | bytes 147464 | tf_op jit(solution)/shard_map/ppermute | solution.py:37
  84.0 6.8 %collective-permute-start.16 = (bf16[24,1024]{1,0:T(8,128)(2,1)S(1)}, bf16[24,1024]{1,0:T(8,128)(2,1)S(1)}, u32[]{:S(2)}, u32[]{:S(2)}) collective-permute-start(bf16[24,1024]{1,0:T(8,128)(2,1)S(1)} %reshape.43), channel_id=1, source_target_pairs={{0,1},{1,2},{2,3},{3,4},{4,5},{5,6},{6,7},{7,0},{8,9},{9,10},{10,1... | collective-permute-start | bytes 147464 | tf_op jit(solution)/shard_map/ppermute | solution.py:37

commit v2 on v0

v2 whole, which is shorter than its diff:
```python
import functools

import jax
import jax.numpy as jnp
import numpy as np
from jax import lax
from jax.experimental import pallas as pl
from jax.experimental.pallas import tpu as pltpu
from jax.sharding import PartitionSpec as P

HEADS = 16
EPSILON = 1e-05
MASKED = -1e30
LANES = 128
SUBLANES = 8
GROUP = 256
F32 = jnp.float32
BF16 = jnp.bfloat16
VMEM_LIMIT = 32 * 1024 * 1024
ABOVE, BELOW = -1, -2


def ring_order(count):
    columns = 1
    while columns * columns * 4 <= count:
        columns *= 2
    rows = count // columns
    order = [z * columns for z in range(rows)]
    for turn, z in enumerate(range(rows - 1, -1, -1)):
        ys = list(range(1, columns))
        if turn % 2:
            ys.reverse()
        order += [z * columns + y for y in ys]
    return order


def shift(x, axis, by):
    size = lax.axis_size(axis)
    return lax.ppermute(x, axis, [(i, (i + by) % size) for i in range(size)])


def fill_ext(ext, center_ref, north_ref, south_ref, pair_ref, across_ref, here_ref):
    levels, columns, rows, width = center_ref.shape
    has_north = (here_ref[0] > 0).astype(F32)
    has_south = (here_ref[1] > 0).astype(F32)
    even = here_ref[2] > 0
    pair = pair_ref[...].astype(F32)
    across = across_ref[...].astype(F32)
    west = jnp.where(even, across, pair)
    east = jnp.where(even, pair, across)
    for level in range(levels):
        north = north_ref[level].astype(F32) * has_north
        south = south_ref[level].astype(F32) * has_south
        for column in range(columns):
            ext[level, column + 1, 0:1, :] = north[column : column + 1]
            ext[level, column + 1, 1 : rows + 1, :] = center_ref[level, column].astype(F32)
            ext[level, column + 1, rows + 1 : rows + 2, :] = south[column : column + 1]
        ext[level, 0, 0 : rows + 2, :] = west[level]
        ext[level, columns + 1, 0 : rows + 2, :] = east[level]


def each_conv(ext, weights_ref, levels, columns, rows, width, emit):
    def tile(index, carry):
        lanes = pl.ds(pl.multiple_of(index * LANES, LANES), LANES)
        taps = [jnp.broadcast_to(weights_ref[k : k + 1, lanes], (SUBLANES, LANES)) for k in range(9)]
        for level in range(levels):
            strip = [ext[level, column, :, lanes] for column in range(columns + 2)]
            for column in range(columns):
                near = strip[column : column + 3]
                sums = [taps[3 * a] * near[0] + taps[3 * a + 1] * near[1] + taps[3 * a + 2] * near[2] for a in range(3)]
                sums[1] = sums[1] + near[1]
                value = sums[0][0:rows] + sums[1][1 : rows + 1] + sums[2][2 : rows + 2]
                emit(level, column, lanes, value)
        return carry

    lax.fori_loop(0, width // LANES, tile, 0)


def first_kernel(here_ref, fields_ref, north_ref, south_ref, pair_ref, across_ref, weights_ref, stream_ref, normed_ref, ext, dense):
    levels, columns, rows, width = fields_ref.shape
    fill_ext(ext, fields_ref, north_ref, south_ref, pair_ref, across_ref, here_ref)

    def emit(level, column, lanes, value):
        at = (level * columns + column) * rows
        dense[at : at + rows, lanes] = value

    each_conv(ext, weights_ref, levels, columns, rows, width, emit)
    stream = dense[...].astype(BF16)
    stream_ref[...] = stream
    wide = stream.astype(F32)
    mean = jnp.mean(wide * wide, axis=-1, keepdims=True)
    normed_ref[...] = (wide * lax.rsqrt(mean + EPSILON)).astype(BF16)


def second_kernel(here_ref, after_ref, north_ref, south_ref, pair_ref, across_ref, weights_ref, mixed_ref, ext):
    levels, columns, rows, width = after_ref.shape
    fill_ext(ext, after_ref, north_ref, south_ref, pair_ref, across_ref, here_ref)

    def emit(level, column, lanes, value):
        mixed_ref[level, column, :, lanes] = value.astype(BF16)

    each_conv(ext, weights_ref, levels, columns, rows, width, emit)


def pair_attend(query2, keys2, values2, bias, factor):
    half = query2.shape[0] // 2
    scores = lax.dot_general(query2, keys2, (((1,), (1,)), ((), ())), preferred_element_type=F32)
    if bias is not None:
        scores = scores + bias
    highest = jnp.max(scores, axis=-1, keepdims=True)
    weights = jnp.exp2((scores - highest) * factor).astype(BF16)
    beside = jnp.concatenate([values2, jnp.ones_like(values2)], axis=1)
    result = jnp.dot(weights, beside, preferred_element_type=F32)
    low = lax.broadcasted_iota(jnp.int32, (half, LANES), 1) < LANES // 2
    merge = lambda x: jnp.where(low, x[:half], x[half:])
    return merge(highest), merge(result[:, LANES:]), merge(result[:, :LANES])


def key_bias(here_ref, sources_ref, list_ref, count_ref, slots, sizes):
    lane = lax.broadcasted_iota(jnp.int32, (1, sum(sizes)), 1)
    bias = jnp.zeros((1, sum(sizes)), F32)
    count = count_ref[0, 0]
    start = 0
    for slot, size in zip(slots, sizes):
        if slot == ABOVE:
            linked = here_ref[0]
        elif slot == BELOW:
            linked = here_ref[1]
        else:
            source = sources_ref[here_ref[3], slot]
            linked = jnp.int32(0)
            for entry in range(list_ref.shape[-1]):
                hit = (list_ref[0, 0, entry] == source) & (entry < count)
                linked = linked | hit.astype(jnp.int32)
        value = jnp.where(linked > 0, 0.0, MASKED).astype(F32)
        bias = jnp.where((lane >= start) & (lane < start + size), value, bias)
        start += size
    return bias


def project(x, w_ref, group):
    width = w_ref.shape[0]
    columns = lambda part: slice(part * width + group * GROUP, part * width + (group + 1) * GROUP)
    keys = jnp.dot(x, w_ref[:, columns(1)], preferred_element_type=F32).astype(BF16)
    values = jnp.dot(x, w_ref[:, columns(2)], preferred_element_type=F32).astype(BF16)
    return keys, values


def joined(blocks):
    return blocks[0][...] if len(blocks) == 1 else jnp.concatenate([b[...] for b in blocks], axis=0)


def head_pairs(width):
    for group in range(width // GROUP):
        for pair in range(GROUP // LANES):
            start = group * GROUP + pair * LANES
            yield group, pair, slice(pair * LANES, (pair + 1) * LANES), slice(start, start + LANES)


def own_kernel(factor, x_ref, w_ref, query_ref, high_ref, sum_ref, acc_ref):
    tokens, width = x_ref.shape
    x = x_ref[...]
    low = lax.broadcasted_iota(jnp.int32, (tokens, LANES), 1) < LANES // 2
    zero = jnp.zeros((tokens, LANES), BF16)
    for group, pair, inner, lanes in head_pairs(width):
        if pair == 0:
            query = jnp.dot(x, w_ref[:, group * GROUP : (group + 1) * GROUP], preferred_element_type=F32).astype(BF16)
            keys, values = project(x, w_ref, group)
        part = query[:, inner]
        query2 = jnp.concatenate([jnp.where(low, part, zero), jnp.where(low, zero, part)], axis=0)
        query_ref[group * (GROUP // LANES) + pair] = query2
        high, summed, result = pair_attend(query2, keys[:, inner], values[:, inner], None, factor)
        high_ref[:, lanes] = high
        sum_ref[:, lanes] = summed
        acc_ref[:, lanes] = result


def combine(state, part, factor):
    high = jnp.maximum(state[0], part[0])
    old = jnp.exp2((state[0] - high) * factor)
    new = jnp.exp2((part[0] - high) * factor)
    return high, state[1] * old + part[1] * new, state[2] * old + part[2] * new


def batch_kernel(
    factor, slots, sizes, here_ref, sources_ref, list_ref, count_ref, query_ref, w_ref, high_in, sum_in, acc_in, *refs
):
    blocks, (high_ref, sum_ref, acc_ref) = refs[:-3], refs[-3:]
    x = joined(blocks)
    bias = key_bias(here_ref, sources_ref, list_ref, count_ref, slots, sizes)
    for group, pair, inner, lanes in head_pairs(x.shape[1]):
        if pair == 0:
            keys, values = project(x, w_ref, group)
        query2 = query_ref[group * (GROUP // LANES) + pair]
        part = pair_attend(query2, keys[:, inner], values[:, inner], bias, factor)
        state = combine((high_in[:, lanes], sum_in[:, lanes], acc_in[:, lanes]), part, factor)
        high_ref[:, lanes], sum_ref[:, lanes], acc_ref[:, lanes] = state


def last_kernel(
    factor, slots, sizes, here_ref, sources_ref, list_ref, count_ref, query_ref, w_ref, high_in, sum_in, acc_in,
    wo_ref, stream_ref, *refs
):
    blocks = refs[: len(sizes)]
    attended_ref, after_ref, north_ref, south_ref, total, dense = refs[len(sizes) :]
    levels, columns, rows, width = after_ref.shape
    x = joined(blocks)
    bias = key_bias(here_ref, sources_ref, list_ref, count_ref, slots, sizes)
    total[...] = stream_ref[...].astype(F32)
    for group, pair, inner, lanes in head_pairs(width):
        if pair == 0:
            keys, values = project(x, w_ref, group)
        query2 = query_ref[group * (GROUP // LANES) + pair]
        part = pair_attend(query2, keys[:, inner], values[:, inner], bias, factor)
        _, summed, result = combine((high_in[:, lanes], sum_in[:, lanes], acc_in[:, lanes]), part, factor)
        dense[:, lanes] = result / summed
        if pair == GROUP // LANES - 1:
            chunk = slice(group * GROUP, (group + 1) * GROUP)
            total[...] += jnp.dot(dense[:, chunk].astype(BF16), wo_ref[chunk, :], preferred_element_type=F32)
    for level in range(levels):
        for column in range(columns):
            at = (level * columns + column) * rows
            attended_ref[level, column] = dense[at : at + rows, :].astype(BF16)
            after_ref[level, column] = total[at : at + rows, :].astype(BF16)
        for edge_ref, row in ((north_ref, 0), (south_ref, rows - 1)):
            places = [(level * columns + column) * rows + row for column in range(columns)]
            picked = jnp.concatenate([total[at : at + 1, :] for at in places], axis=0)
            edge_ref[level] = picked.astype(BF16)


def shape(dims, kind):
    return jax.ShapeDtypeStruct(dims, kind)


def call(kernel, out_shape, scalars, arrays, scratch, name, microseconds):
    return pl.pallas_call(
        kernel,
        out_shape=out_shape,
        in_specs=[pl.BlockSpec(memory_space=pltpu.SMEM)] * len(scalars) + [pl.BlockSpec(memory_space=pltpu.VMEM)] * len(arrays),
        out_specs=jax.tree.map(lambda _: pl.BlockSpec(memory_space=pltpu.VMEM), out_shape),
        scratch_shapes=scratch,
        compiler_params=pltpu.CompilerParams(vmem_limit_bytes=VMEM_LIMIT),
        cost_estimate=pl.CostEstimate(flops=int(microseconds * 1.1e9), bytes_accessed=0, transcendentals=0),
        name=name,
    )(*scalars, *arrays)


def exchange(block, north_edge, south_edge, here):
    columns = block.shape[1]
    count = lax.axis_size("lon")
    north = shift(south_edge, "lat", 1)
    south = shift(north_edge, "lat", -1)

    def column(at):
        top = jnp.where(here[0] > 0, north[:, at : at + 1], 0)
        bottom = jnp.where(here[1] > 0, south[:, at : at + 1], 0)
        return jnp.concatenate([top, block[:, at], bottom], axis=1)

    west, east = column(0), column(columns - 1)
    even = here[2] > 0
    swap = lambda first: [p for i in range(first, count, 2) for p in ((i, (i + 1) % count), ((i + 1) % count, i))]
    pair = lax.ppermute(jnp.where(even, east, west), "lon", swap(0))
    across = lax.ppermute(jnp.where(even, west, east), "lon", swap(1))
    return north, south, pair, across


def local(fields, conv_first, w_qkv, w_out, conv_second, key_list, key_count):
    fields = fields.transpose(0, 2, 1, 3)
    levels, columns, rows, width = fields.shape
    tokens = levels * rows * columns
    pairs = width // LANES
    factor = float(np.log2(np.e) * (width // HEADS) ** -0.5)
    lat_here = lax.axis_index("lat")
    lon_here = lax.axis_index("lon")
    lon_total = lax.axis_size("lon")
    order = ring_order(lon_total)
    place = {lon: i for i, lon in enumerate(order)}
    half = lon_total // 2
    table = np.zeros((lon_total, lon_total), np.int32)
    for lon in range(lon_total):
        for step in range(1, half + 1):
            table[lon, 2 * step - 2] = order[(place[lon] - step) % lon_total]
            table[lon, 2 * step - 1] = order[(place[lon] + step) % lon_total]
    here = jnp.stack(
        [lat_here > 0, lat_here < lax.axis_size("lat") - 1, lon_here % 2 == 0, lon_here]
    ).astype(jnp.int32)
    links = (here, jnp.asarray(table), key_list, key_count)

    ext = pltpu.VMEM((levels, columns + 2, SUBLANES, width), F32)
    dense = pltpu.VMEM((tokens, width), F32)
    halo = exchange(fields, fields[:, :, 0], fields[:, :, rows - 1], here)
    flat = shape((tokens, width), BF16)
    stream, normed = call(first_kernel, (flat, flat), (here,), (fields, *halo, conv_first), [ext, dense], "conv_first", 2)

    forward = [(order[i], order[(i + 1) % lon_total]) for i in range(lon_total)]
    backward = [(b, a) for a, b in forward]
    state_shape = (shape((tokens, width), F32),) * 3
    query, *state = call(
        functools.partial(own_kernel, factor),
        (shape((pairs, 2 * tokens, LANES), BF16), *state_shape),
        (),
        (normed, w_qkv),
        [],
        "own_block",
        4,
    )

    def batch(state, waiting):
        blocks, slots = zip(*waiting)
        sizes = [b.shape[0] for b in blocks]
        return call(
            functools.partial(batch_kernel, factor, slots, sizes),
            state_shape,
            links,
            (query, w_qkv, *state, *blocks),
            [],
            "attend_batch",
            1 + 1.8 * len(blocks),
        )

    ahead, behind = normed, normed
    waiting = [(shift(normed, "lat", 1), ABOVE), (shift(normed, "lat", -1), BELOW)]
    cut = (tokens // 32) * 16
    for step in range(1, half):
        ahead = lax.ppermute(ahead, "lon", forward)
        behind = lax.ppermute(behind, "lon", backward)
        if step > 1:
            state = batch(state, waiting)
            waiting = []
        waiting += [(ahead, 2 * step - 2), (behind, 2 * step - 1)]
    far_first = lax.ppermute(ahead[:cut], "lon", forward)
    far_second = lax.ppermute(behind[cut:], "lon", backward)
    state = batch(state, waiting)

    grid4 = shape(fields.shape, BF16)
    edge = shape((levels, columns, width), BF16)
    attended, after, north_edge, south_edge = call(
        functools.partial(last_kernel, factor, [lon_total - 2] * 2, [cut, tokens - cut]),
        (grid4, grid4, edge, edge),
        links,
        (query, w_qkv, *state, w_out, stream, far_first, far_second),
        [dense, dense],
        "attend_last",
        5,
    )
    halo = exchange(after, north_edge, south_edge, here)
    mixed = call(second_kernel, grid4, (here,), (after, *halo, conv_second), [ext], "conv_second", 2)
    return attended.transpose(0, 2, 1, 3), mixed.transpose(0, 2, 1, 3)


def solution(mesh):
    return jax.shard_map(
        local,
        mesh=mesh,
        in_specs=(
            P(None, "lat", "lon", None),
            P(),
            P(),
            P(),
            P(),
            P("lat", "lon", None),
            P("lat", "lon"),
        ),
        out_specs=(P(None, "lat", "lon", None), P(None, "lat", "lon", None)),
        check_vma=False,
    )
```

time: 268 us -> 73.8 us (0.28)
  waiting for transfers between devices: 117 us -> 18.2 us
  local copies, waits for them, and re-layouts: 60 us -> 2.43 us
  matrix products: 39.6 us -> 0 us
  Pallas kernels: 0 us -> 26.5 us
  other arithmetic: 20.7 us -> 0.44 us
    ppermute x17 -> x18, waiting for transfers between devices: 117 us -> 18.2 us  [the longest x2 7.09 us: exchange(): across = lax.ppermute(jnp.where(even, west, east), 'lon', swap(1))]
    dot_general x19 -> x0, matrix products: 39.6 us -> none  [the longest x8 18.1 us: attend(): jnp.einsum('qhd,khd->qhk', query, keys_part, preferred_element_type=jnp.f...]
    slice x29 -> x3, local copies, waits for them, and re-layouts: 28.6 us -> 0.1 us  [the longest x1 0.07 us: column(): return jnp.concatenate([top, block[:, at], bottom], axis=1)]
    pallas_call x0 -> x7, Pallas kernels: none -> 26.5 us  [call(): pl.pallas_call(kernel, out_shape=out_shape, in_specs=[pl.BlockSpec(memory...]
    reduce_sum x9 -> x0, other arithmetic: 14 us -> none  [the longest x8 9.82 us: attend(): summed = summed * factor + jnp.sum(weights, axis=-1)]
    reshape x6 -> x0, local copies, waits for them, and re-layouts: 8.1 us -> none  [the longest x2 3.79 us: local(): keyvals.reshape(level_count, row_count, column_count, keyvals.shape[1])]
    while x56 -> x0, local copies, waits for them, and re-layouts: 6.87 us -> none
    dynamic_slice x7 -> x0, local copies, waits for them, and re-layouts: 4.11 us -> none  [turn(): return (buffer, visit(current, buffer, spread(linked[source])))]
  transfers between devices with their start and end apart: 17 -> 18, of which waited for: 10 -> 8; matrix products, arithmetic and copies ran while one was open for 7% -> 1% of each run, Pallas kernels for 0% -> 24%
where the time goes in v2:
time: 73.8 us; the launch traced here: 73.5 us
  Pallas kernels  26.5 us (36%)
  starting transfers between devices  24.5 us (33%)
  waiting for transfers between devices  18.2 us (25%)
  local copies, waits for them, and re-layouts  2.43 us (3%)
  between operations  1.5 us (2%)
    pallas_call x7, Pallas kernels, call(): pl.pallas_call(kernel, out_shape=out_shape, in_specs=[pl.BlockSpec(memory...  26.5 us
    ppermute x2, starting transfers between devices, exchange(): across = lax.ppermute(jnp.where(even, west, east), 'lon', swap(1))  7.11 us
    ppermute x2, waiting for transfers between devices, exchange(): across = lax.ppermute(jnp.where(even, west, east), 'lon', swap(1))  7.09 us
    ppermute x6, waiting for transfers between devices, shift(): return lax.ppermute(x, axis, [(i, (i + by) % size) for i in range(size)])  6.19 us
    ppermute x6, starting transfers between devices, shift(): return lax.ppermute(x, axis, [(i, (i + by) % size) for i in range(size)])  6.04 us
    ppermute x3, starting transfers between devices, local(): behind = lax.ppermute(behind, 'lon', backward)  5.51 us
    ppermute x3, waiting for transfers between devices, local(): ahead = lax.ppermute(ahead, 'lon', forward)  3.56 us
    ppermute x2, starting transfers between devices, exchange(): pair = lax.ppermute(jnp.where(even, east, west), 'lon', swap(0))  3.13 us
  transfers between devices with their start and end apart: 18, of which 8 were waited for; matrix products, arithmetic and copies ran while one was open for 1% of the time, Pallas kernels for 24%

profile of v2, /device:TPU:0, one launch (start us, length us, event | category | flops | bytes accessed | tf_op | source)
XLA Modules:
  0.0 73.5 jit_solution(8116229106461618635)
XLA Ops:
  0.6 1.1 %copy.64 = bf16[4,4,9,1024]{3,2,0,1:T(8,128)(2,1)S(1)} copy(bf16[4,4,9,1024]{3,1,2,0:T(4,128)(2,1)} %param.8) | data formatting | bytes 589824 | tf_op args[0]
  1.7 0.5 collective-permute-start
  2.2 2.0 %collective-permute-start.1 = (bf16[4,9,1024]{2,1,0:T(8,128)(2,1)S(1)}, bf16[4,9,1024]{2,1,0:T(8,128)(2,1)S(1)}, u32[]{:S(2)}, u32[]{:S(2)}) collective-permute-start(bf16[4,9,1024]{2,1,0:T(8,128)(2,1)S(1)} %get-tuple-element.42), channel_id=1, source_target_pairs={{0,24},{8,0},{16,8},{24,16},{1,25},{9,1},{17,9},{25,17},{2,26},{10... | collective-permute-start | bytes 221192 | tf_op jit(solution)/shard_map/ppermute | solution.py:39
  4.2 0.1 fusion
  4.3 0.1 copy_bitcast_fusion.1
  4.4 0.0 copy-start
  4.5 2.4 %collective-permute-done.north_ref = bf16[4,9,1024]{2,1,0:T(8,128)(2,1)S(1)} collective-permute-done((bf16[4,9,1024]{2,1,0:T(8,128)(2,1)S(1)}, bf16[4,9,1024]{2,1,0:T(8,128)(2,1)S(1)}, u32[]{:S(2)}, u32[]{:S(2)}) %collective-permute-start) | collective-permute-done | bytes 73760 | tf_op jit(solution)/shard_map/ppermute | solution.py:39
  6.9 1.2 %collective-permute-done.1.south_ref = bf16[4,9,1024]{2,1,0:T(8,128)(2,1)S(1)} collective-permute-done((bf16[4,9,1024]{2,1,0:T(8,128)(2,1)S(1)}, bf16[4,9,1024]{2,1,0:T(8,128)(2,1)S(1)}, u32[]{:S(2)}, u32[]{:S(2)}) %collective-permute-start.1) | collective-permute-done | bytes 73760 | tf_op jit(solution)/shard_map/ppermute | solution.py:39
  8.1 0.1 broadcast_select_fusion.2
  8.2 1.6 %collective-permute-start.2 = (bf16[4,6,1024]{2,1,0:T(8,128)(2,1)S(1)}, bf16[4,6,1024]{2,1,0:T(8,128)(2,1)S(1)}, u32[]{:S(2)}, u32[]{:S(2)}) collective-permute-start(bf16[4,6,1024]{2,1,0:T(8,128)(2,1)S(1)} %get-tuple-element.53), channel_id=1, source_target_pairs={{0,1},{1,0},{2,3},{3,2},{4,5},{5,4},{6,7},{7,6},{8,9},{9,8},{10,11... | collective-permute-start | bytes 147464 | tf_op jit(solution)/shard_map/ppermute | solution.py:262
  9.8 3.5 %collective-permute-start.3 = (bf16[4,6,1024]{2,1,0:T(8,128)(2,1)S(1)}, bf16[4,6,1024]{2,1,0:T(8,128)(2,1)S(1)}, u32[]{:S(2)}, u32[]{:S(2)}) collective-permute-start(bf16[4,6,1024]{2,1,0:T(8,128)(2,1)S(1)} %get-tuple-element.52), channel_id=1, source_target_pairs={{1,2},{2,1},{3,4},{4,3},{5,6},{6,5},{7,0},{0,7},{9,10},{10,9},{11,... | collective-permute-start | bytes 147464 | tf_op jit(solution)/shard_map/ppermute | solution.py:263
  13.3 0.1 pad_add_fusion.here_ref
  13.4 0.2 copy.56.fields_ref
  14.3 0.0 collective-permute-done.2.pair_ref
  14.3 3.1 %collective-permute-done.3.across_ref = bf16[4,6,1024]{2,1,0:T(8,128)(2,1)S(1)} collective-permute-done((bf16[4,6,1024]{2,1,0:T(8,128)(2,1)S(1)}, bf16[4,6,1024]{2,1,0:T(8,128)(2,1)S(1)}, u32[]{:S(2)}, u32[]{:S(2)}) %collective-permute-start.3) | collective-permute-done | bytes 49184 | tf_op jit(solution)/shard_map/ppermute | solution.py:263
  17.4 0.8 %copy-done.2 = f32[9,1024]{1,0:T(8,128)S(1)} copy-done((f32[9,1024]{1,0:T(8,128)S(1)}, f32[9,1024]{1,0:T(8,128)}, u32[]{:S(2)}) %copy-start.2) | copy-done | bytes 36888
  18.2 1.7 %conv_first.1 = (bf16[144,1024]{1,0:T(8,128)(2,1)S(1)}, bf16[144,1024]{1,0:T(8,128)(2,1)S(1)}) custom-call(s32[4]{0:T(128)S(1)} %pad_add_fusion.here_ref, bf16[4,9,4,1024]{3,2,1,0:T(4,128)(2,1)S(1)} %copy.56.fields_ref, bf16[4,9,1024]{2,1,0:T(8,128)(2,1)S(1)} %collective-permute-done.north_ref, bf16[4,9,1024]{2,1,0:T(8,128)(2,1)S(1)} %collective-permute-done.1.south_ref, ...), custom_call_target="tpu_custom_call" | custom-call | flops 2200000000 | tf_op jit(solution)/shard_map/conv_first/pallas_call | solution.py:236
  20.0 0.0 copy-start.4
  20.0 0.0 copy-start.5
  20.0 0.1 collective-permute-start.4
  20.1 1.7 %collective-permute-start.5 = (bf16[144,1024]{1,0:T(8,128)(2,1)S(1)}, bf16[144,1024]{1,0:T(8,128)(2,1)S(1)}, u32[]{:S(2)}, u32[]{:S(2)}) collective-permute-start(bf16[144,1024]{1,0:T(8,128)(2,1)S(1)} %get-tuple-element.21.x_ref), channel_id=1, source_target_pairs={{0,24},{8,0},{16,8},{24,16},{1,25},{9,1},{17,9},{25,17},{2,26},{10... | collective-permute-start | bytes 884744 | tf_op jit(solution)/shard_map/ppermute | solution.py:39
  21.8 0.0 collective-permute-start.6
  21.8 2.0 %collective-permute-start.7 = (bf16[144,1024]{1,0:T(8,128)(2,1)S(1)}, bf16[144,1024]{1,0:T(8,128)(2,1)S(1)}, u32[]{:S(2)}, u32[]{:S(2)}) collective-permute-start(bf16[144,1024]{1,0:T(8,128)(2,1)S(1)} %get-tuple-element.21.x_ref), channel_id=1, source_target_pairs={{2,0},{4,2},{6,4},{7,6},{5,7},{3,5},{1,3},{0,1},{10,8},{12,10},{14... | collective-permute-start | bytes 884744 | tf_op jit(solution)/shard_map/ppermute | solution.py:326
  23.9 2.8 %own_block.1 = (bf16[8,288,128]{2,1,0:T(8,128)(2,1)S(1)}, f32[144,1024]{1,0:T(8,128)S(1)}, f32[144,1024]{1,0:T(8,128)S(1)}, f32[144,1024]{1,0:T(8,128)S(1)}) custom-call(bf16[144,1024]{1,0:T(8,128)(2,1)S(1)} %get-tuple-element.21.x_ref, bf16[1024,3072]{1,0:T(8,128)(2,1)S(1)} %copy-done), custom_call_target="tpu_custom_call" | custom-call | flops 4400000000 | tf_op jit(solution)/shard_map/own_block/pallas_call | solution.py:236
  26.7 3.6 %collective-permute-done.6.refs_2_ = bf16[144,1024]{1,0:T(8,128)(2,1)S(1)} collective-permute-done((bf16[144,1024]{1,0:T(8,128)(2,1)S(1)}, bf16[144,1024]{1,0:T(8,128)(2,1)S(1)}, u32[]{:S(2)}, u32[]{:S(2)}) %collective-permute-start.6) | collective-permute-done | bytes 294944 | tf_op jit(solution)/shard_map/ppermute | solution.py:325
  30.2 0.3 collective-permute-start.8
  30.5 1.7 %collective-permute-start.9 = (bf16[144,1024]{1,0:T(8,128)(2,1)S(1)}, bf16[144,1024]{1,0:T(8,128)(2,1)S(1)}, u32[]{:S(2)}, u32[]{:S(2)}) collective-permute-start(bf16[144,1024]{1,0:T(8,128)(2,1)S(1)} %collective-permute-done.7.refs_3_), channel_id=1, source_target_pairs={{2,0},{4,2},{6,4},{7,6},{5,7},{3,5},{1,3},{0,1},{10,8},{12,10},{14... | collective-permute-start | bytes 884744 | tf_op jit(solution)/shard_map/ppermute | solution.py:326
  32.3 6.1 %attend_batch.3 = (f32[144,1024]{1,0:T(8,128)S(1)}, f32[144,1024]{1,0:T(8,128)S(1)}, f32[144,1024]{1,0:T(8,128)S(1)}) custom-call(s32[4]{0:T(128)S(1)} %pad_add_fusion.here_ref, s32[8,8]{1,0:T(8,128)S(1)} %copy-done.5, s32[1,1,8]{2,1,0:T(1,128)S(1)} %copy-done.4, s32[1,1]{1,0:T(1,128)S(6)} %copy.65.count_ref, ...), custom_call_target="tpu_custom_call" | custom-call | flops 9020000256 | tf_op jit(solution)/shard_map/attend_batch/pallas_call | solution.py:236
  38.4 0.0 collective-permute-done.8.refs_0_
  38.4 0.3 collective-permute-start.10
  38.8 0.0 collective-permute-done.9.refs_1_
  38.8 1.7 %collective-permute-start.11 = (bf16[144,1024]{1,0:T(8,128)(2,1)S(1)}, bf16[144,1024]{1,0:T(8,128)(2,1)S(1)}, u32[]{:S(2)}, u32[]{:S(2)}) collective-permute-start(bf16[144,1024]{1,0:T(8,128)(2,1)S(1)} %collective-permute-done.9.refs_1_), channel_id=1, source_target_pairs={{2,0},{4,2},{6,4},{7,6},{5,7},{3,5},{1,3},{0,1},{10,8},{12,10},{14... | collective-permute-start | bytes 884744 | tf_op jit(solution)/shard_map/ppermute | solution.py:326
  40.5 4.4 %attend_batch.4 = (f32[144,1024]{1,0:T(8,128)S(1)}, f32[144,1024]{1,0:T(8,128)S(1)}, f32[144,1024]{1,0:T(8,128)S(1)}) custom-call(s32[4]{0:T(128)S(1)} %pad_add_fusion.here_ref, s32[8,8]{1,0:T(8,128)S(1)} %copy-done.5, s32[1,1,8]{2,1,0:T(1,128)S(1)} %copy-done.4, s32[1,1]{1,0:T(1,128)S(6)} %copy.65.count_ref, ...), custom_call_target="tpu_custom_call" | custom-call | flops 5059999744 | tf_op jit(solution)/shard_map/attend_batch/pallas_call | solution.py:236
  44.9 1.0 %collective-permute-done.11.refs_1_ = bf16[144,1024]{1,0:T(8,128)(2,1)S(1)} collective-permute-done((bf16[144,1024]{1,0:T(8,128)(2,1)S(1)}, bf16[144,1024]{1,0:T(8,128)(2,1)S(1)}, u32[]{:S(2)}, u32[]{:S(2)}) %collective-permute-start.11) | collective-permute-done | bytes 294944 | tf_op jit(solution)/shard_map/ppermute | solution.py:326
  45.9 1.8 %collective-permute-start.13 = (bf16[80,1024]{1,0:T(8,128)(2,1)S(1)}, bf16[80,1024]{1,0:T(8,128)(2,1)S(1)}, u32[]{:S(2)}, u32[]{:S(2)}) collective-permute-start(bf16[80,1024]{1,0:T(8,128)(2,1)S(1)} %slice.73), channel_id=1, source_target_pairs={{2,0},{4,2},{6,4},{7,6},{5,7},{3,5},{1,3},{0,1},{10,8},{12,10},{14... | collective-permute-start | bytes 491528 | tf_op jit(solution)/shard_map/ppermute | solution.py:332
  47.7 0.3 collective-permute-start.12
  48.0 4.4 %attend_batch.5 = (f32[144,1024]{1,0:T(8,128)S(1)}, f32[144,1024]{1,0:T(8,128)S(1)}, f32[144,1024]{1,0:T(8,128)S(1)}) custom-call(s32[4]{0:T(128)S(1)} %pad_add_fusion.here_ref, s32[8,8]{1,0:T(8,128)S(1)} %copy-done.5, s32[1,1,8]{2,1,0:T(1,128)S(1)} %copy-done.4, s32[1,1]{1,0:T(1,128)S(6)} %copy.65.count_ref, ...), custom_call_target="tpu_custom_call" | custom-call | flops 5059999744 | tf_op jit(solution)/shard_map/attend_batch/pallas_call | solution.py:236
  52.4 0.3 collective-permute-done.12.refs_0_
  52.7 0.0 collective-permute-done.13.refs_1_
  52.8 4.7 %attend_last.1 = (bf16[4,9,4,1024]{3,2,1,0:T(4,128)(2,1)}, bf16[4,9,4,1024]{3,2,1,0:T(4,128)(2,1)S(1)}, bf16[4,9,1024]{2,1,0:T(8,128)(2,1)S(1)}, bf16[4,9,1024]{2,1,0:T(8,128)(2,1)S(1)}) custom-call(s32[4]{0:T(128)S(1)} %pad_add_fusion.here_ref, s32[8,8]{1,0:T(8,128)S(1)} %copy-done.5, s32[1,1,8]{2,1,0:T(1,128)S(1)} %copy-done.4, ...), custom_call_target="tpu_custom_call" | custom-call | flops 5500000256 | tf_op jit(solution)/shard_map/attend_last/pallas_call | solution.py:236
  57.5 0.0 collective-permute-start.14
  57.5 1.7 %collective-permute-start.15 = (bf16[4,9,1024]{2,1,0:T(8,128)(2,1)S(1)}, bf16[4,9,1024]{2,1,0:T(8,128)(2,1)S(1)}, u32[]{:S(2)}, u32[]{:S(2)}) collective-permute-start(bf16[4,9,1024]{2,1,0:T(8,128)(2,1)S(1)} %get-tuple-element.39), channel_id=1, source_target_pairs={{0,24},{8,0},{16,8},{24,16},{1,25},{9,1},{17,9},{25,17},{2,26},{10... | collective-permute-start | bytes 221192 | tf_op jit(solution)/shard_map/ppermute | solution.py:39
  59.3 2.6 %collective-permute-done.14.north_ref = bf16[4,9,1024]{2,1,0:T(8,128)(2,1)S(1)} collective-permute-done((bf16[4,9,1024]{2,1,0:T(8,128)(2,1)S(1)}, bf16[4,9,1024]{2,1,0:T(8,128)(2,1)S(1)}, u32[]{:S(2)}, u32[]{:S(2)}) %collective-permute-start.14) | collective-permute-done | bytes 73760 | tf_op jit(solution)/shard_map/ppermute | solution.py:39
  62.0 0.1 broadcast_select_fusion
  62.1 1.5 %collective-permute-start.16 = (bf16[4,6,1024]{2,1,0:T(8,128)(2,1)S(1)}, bf16[4,6,1024]{2,1,0:T(8,128)(2,1)S(1)}, u32[]{:S(2)}, u32[]{:S(2)}) collective-permute-start(bf16[4,6,1024]{2,1,0:T(8,128)(2,1)S(1)} %get-tuple-element.47), channel_id=1, source_target_pairs={{0,1},{1,0},{2,3},{3,2},{4,5},{5,4},{6,7},{7,6},{8,9},{9,8},{10,11... | collective-permute-start | bytes 147464 | tf_op jit(solution)/shard_map/ppermute | solution.py:262
  63.6 3.6 %collective-permute-start.17 = (bf16[4,6,1024]{2,1,0:T(8,128)(2,1)S(1)}, bf16[4,6,1024]{2,1,0:T(8,128)(2,1)S(1)}, u32[]{:S(2)}, u32[]{:S(2)}) collective-permute-start(bf16[4,6,1024]{2,1,0:T(8,128)(2,1)S(1)} %get-tuple-element.46), channel_id=1, source_target_pairs={{1,2},{2,1},{3,4},{4,3},{5,6},{6,5},{7,0},{0,7},{9,10},{10,9},{11,... | collective-permute-start | bytes 147464 | tf_op jit(solution)/shard_map/ppermute | solution.py:263
  67.2 4.0 %collective-permute-done.17.across_ref = bf16[4,6,1024]{2,1,0:T(8,128)(2,1)S(1)} collective-permute-done((bf16[4,6,1024]{2,1,0:T(8,128)(2,1)S(1)}, bf16[4,6,1024]{2,1,0:T(8,128)(2,1)S(1)}, u32[]{:S(2)}, u32[]{:S(2)}) %collective-permute-start.17) | collective-permute-done | bytes 49184 | tf_op jit(solution)/shard_map/ppermute | solution.py:263
  71.2 2.3 %conv_second.1 = bf16[4,9,4,1024]{3,2,1,0:T(4,128)(2,1)} custom-call(s32[4]{0:T(128)S(1)} %pad_add_fusion.here_ref, bf16[4,9,4,1024]{3,2,1,0:T(4,128)(2,1)S(1)} %get-tuple-element.37.after_ref, bf16[4,9,1024]{2,1,0:T(8,128)(2,1)S(1)} %collective-permute-done.14.north_ref, bf16[4,9,1024]{2,1,0:T(8,128)(2,1)S(1)} %collective-permute-done.15.south_ref, ...), custom_call_target="tpu_custom_call" | custom-call | flops 2200000000 | tf_op jit(solution)/shard_map/conv_second/pallas_call | solution.py:236
  (22 shorter events, 0.2 us)
Async XLA Ops:
  1.7 5.1 %collective-permute-start = (bf16[4,9,1024]{2,1,0:T(8,128)(2,1)S(1)}, bf16[4,9,1024]{2,1,0:T(8,128)(2,1)S(1)}, u32[]{:S(2)}, u32[]{:S(2)}) collective-permute-start(bf16[4,9,1024]{2,1,0:T(8,128)(2,1)S(1)} %get-tuple-element.43), channel_id=1, source_target_pairs={{0,8},{8,16},{16,24},{24,0},{1,9},{9,17},{17,25},{25,1},{2,10},{10... | collective-permute-start | bytes 221192 | tf_op jit(solution)/shard_map/ppermute | solution.py:39
  2.2 5.8 %collective-permute-start.1 = (bf16[4,9,1024]{2,1,0:T(8,128)(2,1)S(1)}, bf16[4,9,1024]{2,1,0:T(8,128)(2,1)S(1)}, u32[]{:S(2)}, u32[]{:S(2)}) collective-permute-start(bf16[4,9,1024]{2,1,0:T(8,128)(2,1)S(1)} %get-tuple-element.42), channel_id=1, source_target_pairs={{0,24},{8,0},{16,8},{24,16},{1,25},{9,1},{17,9},{25,17},{2,26},{10... | collective-permute-start | bytes 221192 | tf_op jit(solution)/shard_map/ppermute | solution.py:39
  4.4 19.4 %copy-start = (bf16[1024,3072]{1,0:T(8,128)(2,1)S(1)}, bf16[1024,3072]{1,0:T(8,128)(2,1)}, u32[]{:S(2)}) copy-start(bf16[1024,3072]{1,0:T(8,128)(2,1)} %w_ref.9) | copy-start | bytes 18874372
  8.2 6.1 %collective-permute-start.2 = (bf16[4,6,1024]{2,1,0:T(8,128)(2,1)S(1)}, bf16[4,6,1024]{2,1,0:T(8,128)(2,1)S(1)}, u32[]{:S(2)}, u32[]{:S(2)}) collective-permute-start(bf16[4,6,1024]{2,1,0:T(8,128)(2,1)S(1)} %get-tuple-element.53), channel_id=1, source_target_pairs={{0,1},{1,0},{2,3},{3,2},{4,5},{5,4},{6,7},{7,6},{8,9},{9,8},{10,11... | collective-permute-start | bytes 147464 | tf_op jit(solution)/shard_map/ppermute | solution.py:262
  9.8 7.6 %collective-permute-start.3 = (bf16[4,6,1024]{2,1,0:T(8,128)(2,1)S(1)}, bf16[4,6,1024]{2,1,0:T(8,128)(2,1)S(1)}, u32[]{:S(2)}, u32[]{:S(2)}) collective-permute-start(bf16[4,6,1024]{2,1,0:T(8,128)(2,1)S(1)} %get-tuple-element.52), channel_id=1, source_target_pairs={{1,2},{2,1},{3,4},{4,3},{5,6},{6,5},{7,0},{0,7},{9,10},{10,9},{11,... | collective-permute-start | bytes 147464 | tf_op jit(solution)/shard_map/ppermute | solution.py:263
  17.4 0.8 %copy-start.2 = (f32[9,1024]{1,0:T(8,128)S(1)}, f32[9,1024]{1,0:T(8,128)}, u32[]{:S(2)}) copy-start(f32[9,1024]{1,0:T(8,128)} %weights_ref.2) | copy-start | bytes 110596
  20.0 12.3 %copy-start.4 = (s32[1,1,8]{2,1,0:T(1,128)S(1)}, s32[1,1,8]{2,1,0:T(1,128)}, u32[]{:S(2)}) copy-start(s32[1,1,8]{2,1,0:T(1,128)} %list_ref.7) | copy-start | bytes 100
  20.0 12.2 %copy-start.5 = (s32[8,8]{1,0:T(8,128)S(1)}, s32[8,8]{1,0:T(8,128)}, u32[]{:S(2)}) copy-start(s32[8,8]{1,0:T(8,128)} %constant.28.clone.sources_ref) | copy-start | bytes 772
  20.0 12.2 %collective-permute-start.4 = (bf16[144,1024]{1,0:T(8,128)(2,1)S(1)}, bf16[144,1024]{1,0:T(8,128)(2,1)S(1)}, u32[]{:S(2)}, u32[]{:S(2)}) collective-permute-start(bf16[144,1024]{1,0:T(8,128)(2,1)S(1)} %get-tuple-element.21.x_ref), channel_id=1, source_target_pairs={{0,8},{8,16},{16,24},{24,0},{1,9},{9,17},{17,25},{25,1},{2,10},{10... | collective-permute-start | bytes 884744 | tf_op jit(solution)/shard_map/ppermute | solution.py:39
  20.1 12.1 %collective-permute-start.5 = (bf16[144,1024]{1,0:T(8,128)(2,1)S(1)}, bf16[144,1024]{1,0:T(8,128)(2,1)S(1)}, u32[]{:S(2)}, u32[]{:S(2)}) collective-permute-start(bf16[144,1024]{1,0:T(8,128)(2,1)S(1)} %get-tuple-element.21.x_ref), channel_id=1, source_target_pairs={{0,24},{8,0},{16,8},{24,16},{1,25},{9,1},{17,9},{25,17},{2,26},{10... | collective-permute-start | bytes 884744 | tf_op jit(solution)/shard_map/ppermute | solution.py:39
  21.8 8.4 %collective-permute-start.6 = (bf16[144,1024]{1,0:T(8,128)(2,1)S(1)}, bf16[144,1024]{1,0:T(8,128)(2,1)S(1)}, u32[]{:S(2)}, u32[]{:S(2)}) collective-permute-start(bf16[144,1024]{1,0:T(8,128)(2,1)S(1)} %get-tuple-element.21.x_ref), channel_id=1, source_target_pairs={{0,2},{2,4},{4,6},{6,7},{7,5},{5,3},{3,1},{1,0},{8,10},{10,12},{12... | collective-permute-start | bytes 884744 | tf_op jit(solution)/shard_map/ppermute | solution.py:325
  21.8 8.7 %collective-permute-start.7 = (bf16[144,1024]{1,0:T(8,128)(2,1)S(1)}, bf16[144,1024]{1,0:T(8,128)(2,1)S(1)}, u32[]{:S(2)}, u32[]{:S(2)}) collective-permute-start(bf16[144,1024]{1,0:T(8,128)(2,1)S(1)} %get-tuple-element.21.x_ref), channel_id=1, source_target_pairs={{2,0},{4,2},{6,4},{7,6},{5,7},{3,5},{1,3},{0,1},{10,8},{12,10},{14... | collective-permute-start | bytes 884744 | tf_op jit(solution)/shard_map/ppermute | solution.py:326
  30.2 8.2 %collective-permute-start.8 = (bf16[144,1024]{1,0:T(8,128)(2,1)S(1)}, bf16[144,1024]{1,0:T(8,128)(2,1)S(1)}, u32[]{:S(2)}, u32[]{:S(2)}) collective-permute-start(bf16[144,1024]{1,0:T(8,128)(2,1)S(1)} %collective-permute-done.6.refs_2_), channel_id=1, source_target_pairs={{0,2},{2,4},{4,6},{6,7},{7,5},{5,3},{3,1},{1,0},{8,10},{10,12},{12... | collective-permute-start | bytes 884744 | tf_op jit(solution)/shard_map/ppermute | solution.py:325
  30.5 8.3 %collective-permute-start.9 = (bf16[144,1024]{1,0:T(8,128)(2,1)S(1)}, bf16[144,1024]{1,0:T(8,128)(2,1)S(1)}, u32[]{:S(2)}, u32[]{:S(2)}) collective-permute-start(bf16[144,1024]{1,0:T(8,128)(2,1)S(1)} %collective-permute-done.7.refs_3_), channel_id=1, source_target_pairs={{2,0},{4,2},{6,4},{7,6},{5,7},{3,5},{1,3},{0,1},{10,8},{12,10},{14... | collective-permute-start | bytes 884744 | tf_op jit(solution)/shard_map/ppermute | solution.py:326
  38.4 9.3 %collective-permute-start.10 = (bf16[144,1024]{1,0:T(8,128)(2,1)S(1)}, bf16[144,1024]{1,0:T(8,128)(2,1)S(1)}, u32[]{:S(2)}, u32[]{:S(2)}) collective-permute-start(bf16[144,1024]{1,0:T(8,128)(2,1)S(1)} %collective-permute-done.8.refs_0_), channel_id=1, source_target_pairs={{0,2},{2,4},{4,6},{6,7},{7,5},{5,3},{3,1},{1,0},{8,10},{10,12},{12... | collective-permute-start | bytes 884744 | tf_op jit(solution)/shard_map/ppermute | solution.py:325
  38.8 7.1 %collective-permute-start.11 = (bf16[144,1024]{1,0:T(8,128)(2,1)S(1)}, bf16[144,1024]{1,0:T(8,128)(2,1)S(1)}, u32[]{:S(2)}, u32[]{:S(2)}) collective-permute-start(bf16[144,1024]{1,0:T(8,128)(2,1)S(1)} %collective-permute-done.9.refs_1_), channel_id=1, source_target_pairs={{2,0},{4,2},{6,4},{7,6},{5,7},{3,5},{1,3},{0,1},{10,8},{12,10},{14... | collective-permute-start | bytes 884744 | tf_op jit(solution)/shard_map/ppermute | solution.py:326
  45.9 6.9 %collective-permute-start.13 = (bf16[80,1024]{1,0:T(8,128)(2,1)S(1)}, bf16[80,1024]{1,0:T(8,128)(2,1)S(1)}, u32[]{:S(2)}, u32[]{:S(2)}) collective-permute-start(bf16[80,1024]{1,0:T(8,128)(2,1)S(1)} %slice.73), channel_id=1, source_target_pairs={{2,0},{4,2},{6,4},{7,6},{5,7},{3,5},{1,3},{0,1},{10,8},{12,10},{14... | collective-permute-start | bytes 491528 | tf_op jit(solution)/shard_map/ppermute | solution.py:332
  47.7 5.0 %collective-permute-start.12 = (bf16[64,1024]{1,0:T(8,128)(2,1)S(1)}, bf16[64,1024]{1,0:T(8,128)(2,1)S(1)}, u32[]{:S(2)}, u32[]{:S(2)}) collective-permute-start(bf16[64,1024]{1,0:T(8,128)(2,1)S(1)} %slice.72), channel_id=1, source_target_pairs={{0,2},{2,4},{4,6},{6,7},{7,5},{5,3},{3,1},{1,0},{8,10},{10,12},{12... | collective-permute-start | bytes 393224 | tf_op jit(solution)/shard_map/ppermute | solution.py:331
  48.0 4.7 %copy-start.1 = (bf16[1024,1024]{1,0:T(8,128)(2,1)S(1)}, bf16[1024,1024]{1,0:T(8,128)(2,1)}, u32[]{:S(2)}) copy-start(bf16[1024,1024]{1,0:T(8,128)(2,1)} %wo_ref.1) | copy-start | bytes 6291460
  52.7 18.5 %copy-start.3 = (f32[9,1024]{1,0:T(8,128)S(1)}, f32[9,1024]{1,0:T(8,128)}, u32[]{:S(2)}) copy-start(f32[9,1024]{1,0:T(8,128)} %weights_ref.3) | copy-start | bytes 110596
  57.5 4.4 %collective-permute-start.14 = (bf16[4,9,1024]{2,1,0:T(8,128)(2,1)S(1)}, bf16[4,9,1024]{2,1,0:T(8,128)(2,1)S(1)}, u32[]{:S(2)}, u32[]{:S(2)}) collective-permute-start(bf16[4,9,1024]{2,1,0:T(8,128)(2,1)S(1)} %get-tuple-element.38), channel_id=1, source_target_pairs={{0,8},{8,16},{16,24},{24,0},{1,9},{9,17},{17,25},{25,1},{2,10},{10... | collective-permute-start | bytes 221192 | tf_op jit(solution)/shard_map/ppermute | solution.py:39
  57.5 4.4 %collective-permute-start.15 = (bf16[4,9,1024]{2,1,0:T(8,128)(2,1)S(1)}, bf16[4,9,1024]{2,1,0:T(8,128)(2,1)S(1)}, u32[]{:S(2)}, u32[]{:S(2)}) collective-permute-start(bf16[4,9,1024]{2,1,0:T(8,128)(2,1)S(1)} %get-tuple-element.39), channel_id=1, source_target_pairs={{0,24},{8,0},{16,8},{24,16},{1,25},{9,1},{17,9},{25,17},{2,26},{10... | collective-permute-start | bytes 221192 | tf_op jit(solution)/shard_map/ppermute | solution.py:39
  62.1 5.1 %collective-permute-start.16 = (bf16[4,6,1024]{2,1,0:T(8,128)(2,1)S(1)}, bf16[4,6,1024]{2,1,0:T(8,128)(2,1)S(1)}, u32[]{:S(2)}, u32[]{:S(2)}) collective-permute-start(bf16[4,6,1024]{2,1,0:T(8,128)(2,1)S(1)} %get-tuple-element.47), channel_id=1, source_target_pairs={{0,1},{1,0},{2,3},{3,2},{4,5},{5,4},{6,7},{7,6},{8,9},{9,8},{10,11... | collective-permute-start | bytes 147464 | tf_op jit(solution)/shard_map/ppermute | solution.py:262
  63.6 7.6 %collective-permute-start.17 = (bf16[4,6,1024]{2,1,0:T(8,128)(2,1)S(1)}, bf16[4,6,1024]{2,1,0:T(8,128)(2,1)S(1)}, u32[]{:S(2)}, u32[]{:S(2)}) collective-permute-start(bf16[4,6,1024]{2,1,0:T(8,128)(2,1)S(1)} %get-tuple-element.46), channel_id=1, source_target_pairs={{1,2},{2,1},{3,4},{4,3},{5,6},{6,5},{7,0},{0,7},{9,10},{10,9},{11,... | collective-permute-start | bytes 147464 | tf_op jit(solution)/shard_map/ppermute | solution.py:263

commit v3 on v2

--- a/solution.py
+++ b/solution.py
@@ -39,67 +39,112 @@
     return lax.ppermute(x, axis, [(i, (i + by) % size) for i in range(size)])
 
 
-def fill_ext(ext, center_ref, north_ref, south_ref, pair_ref, across_ref, here_ref):
-    levels, columns, rows, width = center_ref.shape
-    has_north = (here_ref[0] > 0).astype(F32)
-    has_south = (here_ref[1] > 0).astype(F32)
-    even = here_ref[2] > 0
-    pair = pair_ref[...].astype(F32)
-    across = across_ref[...].astype(F32)
-    west = jnp.where(even, across, pair)
-    east = jnp.where(even, pair, across)
-    for level in range(levels):
-        north = north_ref[level].astype(F32) * has_north
-        south = south_ref[level].astype(F32) * has_south
-        for column in range(columns):
-            ext[level, column + 1, 0:1, :] = north[column : column + 1]
-            ext[level, column + 1, 1 : rows + 1, :] = center_ref[level, column].astype(F32)
-            ext[level, column + 1, rows + 1 : rows + 2, :] = south[column : column + 1]
-        ext[level, 0, 0 : rows + 2, :] = west[level]
-        ext[level, columns + 1, 0 : rows + 2, :] = east[level]
-
-
-def each_conv(ext, weights_ref, levels, columns, rows, width, emit):
+def conv_part(load, dims, weights_ref, part_ref, taps_ref):
+    levels, columns, rows = dims
+    above = lax.broadcasted_iota(jnp.int32, (SUBLANES, LANES), 0) > 0
+    blank = jnp.zeros((SUBLANES - rows, LANES), F32)
+    nothing = jnp.zeros((SUBLANES, LANES), F32)
+
     def tile(index, carry):
         lanes = pl.ds(pl.multiple_of(index * LANES, LANES), LANES)
+        taps_ref[index] = weights_ref[:, lanes]
         taps = [jnp.broadcast_to(weights_ref[k : k + 1, lanes], (SUBLANES, LANES)) for k in range(9)]
         for level in range(levels):
-            strip = [ext[level, column, :, lanes] for column in range(columns + 2)]
+            strip = [jnp.concatenate([load(level, column, index, lanes), blank], axis=0) for column in range(columns)]
+            strip = [nothing, *strip, nothing]
             for column in range(columns):
                 near = strip[column : column + 3]
                 sums = [taps[3 * a] * near[0] + taps[3 * a + 1] * near[1] + taps[3 * a + 2] * near[2] for a in range(3)]
-                sums[1] = sums[1] + near[1]
-                value = sums[0][0:rows] + sums[1][1 : rows + 1] + sums[2][2 : rows + 2]
-                emit(level, column, lanes, value)
+                value = near[1] + sums[1]
+                value += jnp.where(above, pltpu.roll(sums[0], 1, 0), 0.0)
+                value += pltpu.roll(sums[2], SUBLANES - 1, 0)
+                at = (level * columns + column) * rows
+                part_ref[index, at : at + rows, :] = value[0:rows]
         return carry
 
-    lax.fori_loop(0, width // LANES, tile, 0)
-
-
-def first_kernel(here_ref, fields_ref, north_ref, south_ref, pair_ref, across_ref, weights_ref, stream_ref, normed_ref, ext, dense):
-    levels, columns, rows, width = fields_ref.shape
-    fill_ext(ext, fields_ref, north_ref, south_ref, pair_ref, across_ref, here_ref)
-
-    def emit(level, column, lanes, value):
+    lax.fori_loop(0, part_ref.shape[0], tile, 0)
+
+
+def first_part_kernel(field_ref, weights_ref, after_ref, part_ref, taps_ref):
+    levels, columns, rows, _ = field_ref.shape
+    load = lambda level, column, index, lanes: field_ref[level, column, :, lanes].astype(F32)
+    conv_part(load, (levels, columns, rows), weights_ref, part_ref, taps_ref)
+
+
+def weights_kernel(after_ref, far_ref, near_ref, arrived):
+    copy = pltpu.make_async_copy(far_ref, near_ref, arrived)
+    copy.start()
+    copy.wait()
+
+
+def second_part_kernel(dims, field_ref, weights_ref, dense_ref, part_ref, taps_ref, attended_ref):
+    levels, columns, rows = dims
+
+    def load(level, column, index, lanes):
         at = (level * columns + column) * rows
-        dense[at : at + rows, lanes] = value
-
-    each_conv(ext, weights_ref, levels, columns, rows, width, emit)
-    stream = dense[...].astype(BF16)
-    stream_ref[...] = stream
-    wide = stream.astype(F32)
-    mean = jnp.mean(wide * wide, axis=-1, keepdims=True)
-    normed_ref[...] = (wide * lax.rsqrt(mean + EPSILON)).astype(BF16)
-
-
-def second_kernel(here_ref, after_ref, north_ref, south_ref, pair_ref, across_ref, weights_ref, mixed_ref, ext):
-    levels, columns, rows, width = after_ref.shape
-    fill_ext(ext, after_ref, north_ref, south_ref, pair_ref, across_ref, here_ref)
-
-    def emit(level, column, lanes, value):
-        mixed_ref[level, column, :, lanes] = value.astype(BF16)
-
-    each_conv(ext, weights_ref, levels, columns, rows, width, emit)
+        return field_ref[index, at : at + rows, :]
+
+    conv_part(load, dims, weights_ref, part_ref, taps_ref)
+    for level in range(levels):
+        for column in range(columns):
+            at = (level * columns + column) * rows
+            attended_ref[level, column] = dense_ref[at : at + rows, :].astype(BF16)
+
+
+def add_halo(index, dims, here_ref, north_ref, south_ref, across_ref, pair_ref, part_ref, taps_ref, full):
+    levels, columns, rows = dims
+    lanes = pl.ds(pl.multiple_of(index * LANES, LANES), LANES)
+    even = here_ref[2] > 0
+    full[index] = part_ref[index]
+    blank = jnp.zeros((1, LANES), F32)
+    for level in range(levels):
+        start = level * columns * rows
+        for ref, flag, a, row in ((north_ref, 0, 0, 0), (south_ref, 1, 2, rows - 1)):
+            line = ref[level, :, lanes].astype(F32)
+            left = jnp.concatenate([blank, line[:-1]], axis=0)
+            right = jnp.concatenate([line[1:], blank], axis=0)
+            tap = [taps_ref[index, 3 * a + b : 3 * a + b + 1, :] for b in range(3)]
+            more = tap[0] * left + tap[1] * line + tap[2] * right
+            more = jnp.where(here_ref[flag] > 0, more, 0.0)
+            full[index, pl.ds(start + row, columns, stride=rows), :] += more
+        pair = pair_ref[level, :, lanes].astype(F32)
+        across = across_ref[level, :, lanes].astype(F32)
+        west = jnp.where(even, across, pair)
+        east = jnp.where(even, pair, across)
+        for side, b, column in ((west, 0, 0), (east, 2, columns - 1)):
+            more = None
+            for a in range(3):
+                term = taps_ref[index, 3 * a + b : 3 * a + b + 1, :] * side[a : a + rows]
+                more = term if more is None else more + term
+            full[index, start + column * rows : start + (column + 1) * rows, :] += more
+
+
+def first_kernel(dims, here_ref, part_ref, taps_ref, north_ref, south_ref, across_ref, pair_ref, stream_ref, normed_ref, full):
+    tiles, tokens, _ = part_ref.shape
+    squares = jnp.zeros((tokens, LANES), F32)
+    for index in range(tiles):
+        lanes = slice(index * LANES, (index + 1) * LANES)
+        add_halo(index, dims, here_ref, north_ref, south_ref, across_ref, pair_ref, part_ref, taps_ref, full)
+        stream = full[index].astype(BF16)
+        stream_ref[:, lanes] = stream
+        wide = stream.astype(F32)
+        squares += wide * wide
+    mean = jnp.sum(squares, axis=-1, keepdims=True) * (1.0 / (tiles * LANES))
+    scale = jnp.broadcast_to(lax.rsqrt(mean + EPSILON), (tokens, LANES))
+    for index in range(tiles):
+        lanes = slice(index * LANES, (index + 1) * LANES)
+        normed_ref[:, lanes] = (stream_ref[:, lanes].astype(F32) * scale).astype(BF16)
+
+
+def second_kernel(dims, here_ref, part_ref, taps_ref, north_ref, south_ref, across_ref, pair_ref, mixed_ref, full):
+    levels, columns, rows = dims
+    for index in range(part_ref.shape[0]):
+        lanes = slice(index * LANES, (index + 1) * LANES)
+        add_halo(index, dims, here_ref, north_ref, south_ref, across_ref, pair_ref, part_ref, taps_ref, full)
+        for level in range(levels):
+            for column in range(columns):
+                at = (level * columns + column) * rows
+                mixed_ref[level, column, :, lanes] = full[index, at : at + rows, :].astype(BF16)
 
 
 def pair_attend(query2, keys2, values2, bias, factor):
@@ -157,9 +202,10 @@
             yield group, pair, slice(pair * LANES, (pair + 1) * LANES), slice(start, start + LANES)
 
 
-def own_kernel(factor, x_ref, w_ref, query_ref, high_ref, sum_ref, acc_ref):
+def own_kernel(factor, x_ref, w_ref, handed_ref, query_ref, high_ref, sum_ref, acc_ref):
     tokens, width = x_ref.shape
     x = x_ref[...]
+    handed_ref[...] = x
     low = lax.broadcasted_iota(jnp.int32, (tokens, LANES), 1) < LANES // 2
     zero = jnp.zeros((tokens, LANES), BF16)
     for group, pair, inner, lanes in head_pairs(width):
@@ -198,13 +244,14 @@
 
 
 def last_kernel(
-    factor, slots, sizes, here_ref, sources_ref, list_ref, count_ref, query_ref, w_ref, high_in, sum_in, acc_in,
+    factor, dims, slots, sizes, here_ref, sources_ref, list_ref, count_ref, query_ref, w_ref, high_in, sum_in, acc_in,
     wo_ref, stream_ref, *refs
 ):
     blocks = refs[: len(sizes)]
-    attended_ref, after_ref, north_ref, south_ref, total, dense = refs[len(sizes) :]
-    levels, columns, rows, width = after_ref.shape
+    dense, after_ref, north_ref, south_ref, west_ref, east_ref, total = refs[len(sizes) :]
+    levels, columns, rows = dims
     x = joined(blocks)
+    width = x.shape[1]
     bias = key_bias(here_ref, sources_ref, list_ref, count_ref, slots, sizes)
     total[...] = stream_ref[...].astype(F32)
     for group, pair, inner, lanes in head_pairs(width):
@@ -217,15 +264,16 @@
         if pair == GROUP // LANES - 1:
             chunk = slice(group * GROUP, (group + 1) * GROUP)
             total[...] += jnp.dot(dense[:, chunk].astype(BF16), wo_ref[chunk, :], preferred_element_type=F32)
-    for level in range(levels):
-        for column in range(columns):
-            at = (level * columns + column) * rows
-            attended_ref[level, column] = dense[at : at + rows, :].astype(BF16)
-            after_ref[level, column] = total[at : at + rows, :].astype(BF16)
-        for edge_ref, row in ((north_ref, 0), (south_ref, rows - 1)):
-            places = [(level * columns + column) * rows + row for column in range(columns)]
-            picked = jnp.concatenate([total[at : at + 1, :] for at in places], axis=0)
-            edge_ref[level] = picked.astype(BF16)
+    for index in range(width // LANES):
+        lanes = slice(index * LANES, (index + 1) * LANES)
+        after_ref[index] = total[:, lanes].astype(BF16).astype(F32)
+        for level in range(levels):
+            start = level * columns * rows
+            stop = start + columns * rows
+            north_ref[level, :, lanes] = after_ref[index, pl.ds(start, columns, stride=rows), :].astype(BF16)
+            south_ref[level, :, lanes] = after_ref[index, pl.ds(start + rows - 1, columns, stride=rows), :].astype(BF16)
+            west_ref[level, :, lanes] = after_ref[index, start : start + rows, :].astype(BF16)
+            east_ref[level, :, lanes] = after_ref[index, stop - rows : stop, :].astype(BF16)
 
 
 def shape(dims, kind):
@@ -245,23 +293,23 @@
     )(*scalars, *arrays)
 
 
-def exchange(block, north_edge, south_edge, here):
-    columns = block.shape[1]
+def exchange(north_edge, south_edge, west_edge, east_edge, here):
+    columns = north_edge.shape[1]
     count = lax.axis_size("lon")
     north = shift(south_edge, "lat", 1)
     south = shift(north_edge, "lat", -1)
 
-    def column(at):
+    def column(edge, at):
         top = jnp.where(here[0] > 0, north[:, at : at + 1], 0)
         bottom = jnp.where(here[1] > 0, south[:, at : at + 1], 0)
-        return jnp.concatenate([top, block[:, at], bottom], axis=1)
-
-    west, east = column(0), column(columns - 1)
+        return jnp.concatenate([top, edge, bottom], axis=1)
+
+    west, east = column(west_edge, 0), column(east_edge, columns - 1)
     even = here[2] > 0
     swap = lambda first: [p for i in range(first, count, 2) for p in ((i, (i + 1) % count), ((i + 1) % count, i))]
+    across = lax.ppermute(jnp.where(even, west, east), "lon", swap(1))
     pair = lax.ppermute(jnp.where(even, east, west), "lon", swap(0))
-    across = lax.ppermute(jnp.where(even, west, east), "lon", swap(1))
-    return north, south, pair, across
+    return north, south, across, pair
 
 
 def local(fields, conv_first, w_qkv, w_out, conv_second, key_list, key_count):
@@ -286,18 +334,43 @@
     ).astype(jnp.int32)
     links = (here, jnp.asarray(table), key_list, key_count)
 
-    ext = pltpu.VMEM((levels, columns + 2, SUBLANES, width), F32)
-    dense = pltpu.VMEM((tokens, width), F32)
-    halo = exchange(fields, fields[:, :, 0], fields[:, :, rows - 1], here)
+    dims = (levels, columns, rows)
+    tiles = width // LANES
+    full = pltpu.VMEM((tiles, tokens, LANES), F32)
+    part_shape = (shape((tiles, tokens, LANES), F32), shape((tiles, 9, LANES), F32))
+    halo = exchange(fields[:, :, 0], fields[:, :, rows - 1], fields[:, 0], fields[:, columns - 1], here)
+    vmem = pl.BlockSpec(memory_space=pltpu.VMEM)
+    anywhere = pl.BlockSpec(memory_space=pl.ANY)
+    part = pl.pallas_call(
+        first_part_kernel,
+        out_shape=part_shape,
+        in_specs=[vmem, vmem, anywhere],
+        out_specs=(vmem,) * 2,
+        compiler_params=pltpu.CompilerParams(vmem_limit_bytes=VMEM_LIMIT),
+        cost_estimate=pl.CostEstimate(flops=int(2e9), bytes_accessed=0, transcendentals=0),
+        name="conv_part",
+    )(fields, conv_first, halo[0])
+    w_qkv = pl.pallas_call(
+        weights_kernel,
+        out_shape=shape(w_qkv.shape, BF16),
+        in_specs=[anywhere, anywhere],
+        out_specs=vmem,
+        scratch_shapes=[pltpu.SemaphoreType.DMA],
+        compiler_params=pltpu.CompilerParams(vmem_limit_bytes=VMEM_LIMIT),
+        cost_estimate=pl.CostEstimate(flops=int(2e9), bytes_accessed=0, transcendentals=0),
+        name="weights_near",
+    )(halo[0], w_qkv)
     flat = shape((tokens, width), BF16)
-    stream, normed = call(first_kernel, (flat, flat), (here,), (fields, *halo, conv_first), [ext, dense], "conv_first", 2)
+    stream, normed = call(
+        functools.partial(first_kernel, dims), (flat, flat), (here,), (*part, *halo), [full], "conv_first", 2
+    )
 
     forward = [(order[i], order[(i + 1) % lon_total]) for i in range(lon_total)]
     backward = [(b, a) for a, b in forward]
     state_shape = (shape((tokens, width), F32),) * 3
-    query, *state = call(
+    handed, query, *state = call(
         functools.partial(own_kernel, factor),
-        (shape((pairs, 2 * tokens, LANES), BF16), *state_shape),
+        (flat, shape((pairs, 2 * tokens, LANES), BF16), *state_shape),
         (),
         (normed, w_qkv),
         [],
@@ -319,32 +392,42 @@
         )
 
     ahead, behind = normed, normed
-    waiting = [(shift(normed, "lat", 1), ABOVE), (shift(normed, "lat", -1), BELOW)]
+    waiting = []
     cut = (tokens // 32) * 16
     for step in range(1, half):
         ahead = lax.ppermute(ahead, "lon", forward)
         behind = lax.ppermute(behind, "lon", backward)
         if step > 1:
             state = batch(state, waiting)
-            waiting = []
-        waiting += [(ahead, 2 * step - 2), (behind, 2 * step - 1)]
+        waiting = [(ahead, 2 * step - 2), (behind, 2 * step - 1)]
+        if step == 2:
+            waiting += [(shift(handed, "lat", 1), ABOVE), (shift(handed, "lat", -1), BELOW)]
     far_first = lax.ppermute(ahead[:cut], "lon", forward)
     far_second = lax.ppermute(behind[cut:], "lon", backward)
     state = batch(state, waiting)
 
-    grid4 = shape(fields.shape, BF16)
-    edge = shape((levels, columns, width), BF16)
-    attended, after, north_edge, south_edge = call(
-        functools.partial(last_kernel, factor, [lon_total - 2] * 2, [cut, tokens - cut]),
-        (grid4, grid4, edge, edge),
+    row_edge, column_edge = shape((levels, columns, width), BF16), shape((levels, rows, width), BF16)
+    dense, after, *edges = call(
+        functools.partial(last_kernel, factor, dims, [lon_total - 2] * 2, [cut, tokens - cut]),
+        (shape((tokens, width), F32), part_shape[0], row_edge, row_edge, column_edge, column_edge),
         links,
         (query, w_qkv, *state, w_out, stream, far_first, far_second),
-        [dense, dense],
+        [pltpu.VMEM((tokens, width), F32)],
         "attend_last",
         5,
     )
-    halo = exchange(after, north_edge, south_edge, here)
-    mixed = call(second_kernel, grid4, (here,), (after, *halo, conv_second), [ext], "conv_second", 2)
+    halo = exchange(*edges, here)
+    grid4 = shape(fields.shape, BF16)
+    *part, attended = call(
+        functools.partial(second_part_kernel, dims),
+        (*part_shape, grid4),
+        (),
+        (after, conv_second, dense),
+        [],
+        "conv_part",
+        2,
+    )
+    mixed = call(functools.partial(second_kernel, dims), grid4, (here,), (*part, *halo), [full], "conv_second", 2)
     return attended.transpose(0, 2, 1, 3), mixed.transpose(0, 2, 1, 3)
 
 

time: 73.8 us -> 71.1 us (0.963)
  starting transfers between devices: 24.5 us -> 20.9 us
  waiting for transfers between devices: 18.2 us -> 15.5 us
  local copies, waits for them, and re-layouts: 2.43 us -> 4.74 us
  Pallas kernels: 26.5 us -> 27.8 us
    ppermute x2, waiting for transfers between devices: 7.09 us -> 3.93 us  [exchange(): across = lax.ppermute(jnp.where(even, west, east), 'lon', swap(1))]
    ppermute x2, starting transfers between devices: 3.13 us -> 0.01 us  [exchange(): pair = lax.ppermute(jnp.where(even, east, west), 'lon', swap(0))]
    unnamed x13, local copies, waits for them, and re-layouts: 1.95 us -> 4.29 us
    ppermute x3, waiting for transfers between devices: 3.56 us -> 5.07 us  [local(): ahead = lax.ppermute(ahead, 'lon', forward)]
    pallas_call x0 -> x2, Pallas kernels: none -> 1.34 us  [the longest x1 0.92 us: local(): pl.pallas_call(first_part_kernel, out_shape=part_shape, in_specs=[vmem, v...]
    ppermute x3, waiting for transfers between devices: 1 us -> 0.07 us  [local(): behind = lax.ppermute(behind, 'lon', backward)]
    pallas_call x7 -> x8, Pallas kernels: 26.5 us -> 26.4 us  [call(): pl.pallas_call(kernel, out_shape=out_shape, in_specs=[pl.BlockSpec(memory...]
  transfers between devices with their start and end apart: 18 -> 18, of which waited for: 8 -> 10; matrix products, arithmetic and copies ran while one was open for 1% -> 1% of each run, Pallas kernels for 24% -> 29%
where the time goes in v3:
time: 71.1 us; the launch traced here: 70.8 us
  Pallas kernels  27.8 us (39%)
  starting transfers between devices  20.9 us (29%)
  waiting for transfers between devices  15.5 us (22%)
  local copies, waits for them, and re-layouts  4.74 us (7%)
  between operations  1.51 us (2%)
    pallas_call x8, Pallas kernels, call(): pl.pallas_call(kernel, out_shape=out_shape, in_specs=[pl.BlockSpec(memory...  26.4 us
    ppermute x2, starting transfers between devices, exchange(): across = lax.ppermute(jnp.where(even, west, east), 'lon', swap(1))  6.55 us
    ppermute x6, starting transfers between devices, shift(): return lax.ppermute(x, axis, [(i, (i + by) % size) for i in range(size)])  6.08 us
    ppermute x6, waiting for transfers between devices, shift(): return lax.ppermute(x, axis, [(i, (i + by) % size) for i in range(size)])  5.78 us
    ppermute x3, starting transfers between devices, local(): behind = lax.ppermute(behind, 'lon', backward)  5.33 us
    ppermute x3, waiting for transfers between devices, local(): ahead = lax.ppermute(ahead, 'lon', forward)  5.07 us
    unnamed x13, local copies, waits for them, and re-layouts  4.29 us
    ppermute x2, waiting for transfers between devices, exchange(): across = lax.ppermute(jnp.where(even, west, east), 'lon', swap(1))  3.93 us
  transfers between devices with their start and end apart: 18, of which 10 were waited for; matrix products, arithmetic and copies ran while one was open for 1% of the time, Pallas kernels for 29%

profile of v3, /device:TPU:0, one launch (start us, length us, event | category | flops | bytes accessed | tf_op | source)
XLA Modules:
  0.0 70.8 jit_solution(7876197665826213426)
XLA Ops:
  0.6 1.1 %copy.56 = bf16[4,4,9,1024]{3,2,0,1:T(8,128)(2,1)S(1)} copy(bf16[4,4,9,1024]{3,1,2,0:T(4,128)(2,1)} %param.8) | data formatting | bytes 589824 | tf_op args[0]
  1.7 0.5 collective-permute-start
  2.2 2.0 %collective-permute-start.1 = (bf16[4,9,1024]{2,1,0:T(8,128)(2,1)S(1)}, bf16[4,9,1024]{2,1,0:T(8,128)(2,1)S(1)}, u32[]{:S(2)}, u32[]{:S(2)}) collective-permute-start(bf16[4,9,1024]{2,1,0:T(8,128)(2,1)S(1)} %get-tuple-element.58), channel_id=1, source_target_pairs={{0,24},{8,0},{16,8},{24,16},{1,25},{9,1},{17,9},{25,17},{2,26},{10... | collective-permute-start | bytes 221192 | tf_op jit(solution)/shard_map/ppermute | solution.py:39
  4.2 0.1 fusion
  4.3 0.2 copy.50.field_ref
  5.3 0.1 copy_bitcast_fusion.1
  5.3 0.1 pad_add_fusion.here_ref
  5.4 1.4 %collective-permute-done.after_ref.north_ref = bf16[4,9,1024]{2,1,0:T(8,128)(2,1)S(1)} collective-permute-done((bf16[4,9,1024]{2,1,0:T(8,128)(2,1)S(1)}, bf16[4,9,1024]{2,1,0:T(8,128)(2,1)S(1)}, u32[]{:S(2)}, u32[]{:S(2)}) %collective-permute-start) | collective-permute-done | bytes 73760 | tf_op jit(solution)/shard_map/ppermute | solution.py:39
  6.9 1.2 %collective-permute-done.1.south_ref = bf16[4,9,1024]{2,1,0:T(8,128)(2,1)S(1)} collective-permute-done((bf16[4,9,1024]{2,1,0:T(8,128)(2,1)S(1)}, bf16[4,9,1024]{2,1,0:T(8,128)(2,1)S(1)}, u32[]{:S(2)}, u32[]{:S(2)}) %collective-permute-start.1) | collective-permute-done | bytes 73760 | tf_op jit(solution)/shard_map/ppermute | solution.py:39
  8.1 0.1 broadcast_select_fusion.2
  8.2 4.6 %collective-permute-start.2 = (bf16[4,6,1024]{2,1,0:T(8,128)(2,1)S(1)}, bf16[4,6,1024]{2,1,0:T(8,128)(2,1)S(1)}, u32[]{:S(2)}, u32[]{:S(2)}) collective-permute-start(bf16[4,6,1024]{2,1,0:T(8,128)(2,1)S(1)} %get-tuple-element.67), channel_id=1, source_target_pairs={{1,2},{2,1},{3,4},{4,3},{5,6},{6,5},{7,0},{0,7},{9,10},{10,9},{11,... | collective-permute-start | bytes 147464 | tf_op jit(solution)/shard_map/ppermute | solution.py:310
  12.8 2.8 %copy-done = bf16[1024,3072]{1,0:T(8,128)(2,1)S(1)} copy-done((bf16[1024,3072]{1,0:T(8,128)(2,1)S(1)}, bf16[1024,3072]{1,0:T(8,128)(2,1)}, u32[]{:S(2)}) %copy-start) | copy-done | bytes 6291480
  15.6 0.4 weights_near.1.w_ref
  16.1 0.4 copy-done.2
  16.5 0.9 %conv_part.2 = (f32[8,144,128]{2,1,0:T(8,128)S(1)}, f32[8,9,128]{2,1,0:T(8,128)S(1)}) custom-call(bf16[4,9,4,1024]{3,2,1,0:T(4,128)(2,1)S(1)} %copy.50.field_ref, f32[9,1024]{1,0:T(8,128)S(1)} %copy-done.2, bf16[4,9,1024]{2,1,0:T(8,128)(2,1)S(1)} %collective-permute-done.after_ref.north_ref), custom_call_target="tpu_custom_call" | custom-call | flops 2000000000 | tf_op jit(solution)/shard_map/conv_part/pallas_call | solution.py:344
  17.4 0.3 collective-permute-done.3.pair_ref
  17.7 1.1 %conv_first.1 = (bf16[144,1024]{1,0:T(8,128)(2,1)S(1)}, bf16[144,1024]{1,0:T(8,128)(2,1)S(1)}) custom-call(s32[4]{0:T(128)S(1)} %pad_add_fusion.here_ref, f32[8,144,128]{2,1,0:T(8,128)S(1)} %get-tuple-element.29.part_ref, f32[8,9,128]{2,1,0:T(8,128)S(1)} %get-tuple-element.30.taps_ref, bf16[4,9,1024]{2,1,0:T(8,128)(2,1)S(1)} %collective-permute-done.after_ref.north_ref, ...), custom_call_target="tpu_custom_call" | custom-call | flops 2200000000 | tf_op jit(solution)/shard_map/conv_first/pallas_call | solution.py:284
  18.9 0.0 copy-start.4
  18.9 0.0 copy-start.5
  18.9 0.1 collective-permute-start.4
  19.0 2.0 %collective-permute-start.5 = (bf16[144,1024]{1,0:T(8,128)(2,1)S(1)}, bf16[144,1024]{1,0:T(8,128)(2,1)S(1)}, u32[]{:S(2)}, u32[]{:S(2)}) collective-permute-start(bf16[144,1024]{1,0:T(8,128)(2,1)S(1)} %get-tuple-element.31.x_ref), channel_id=1, source_target_pairs={{2,0},{4,2},{6,4},{7,6},{5,7},{3,5},{1,3},{0,1},{10,8},{12,10},{14... | collective-permute-start | bytes 884744 | tf_op jit(solution)/shard_map/ppermute | solution.py:399
  21.0 2.8 %own_block.1 = (bf16[144,1024]{1,0:T(8,128)(2,1)S(1)}, bf16[8,288,128]{2,1,0:T(8,128)(2,1)S(1)}, f32[144,1024]{1,0:T(8,128)S(1)}, f32[144,1024]{1,0:T(8,128)S(1)}, f32[144,1024]{1,0:T(8,128)S(1)}) custom-call(bf16[144,1024]{1,0:T(8,128)(2,1)S(1)} %get-tuple-element.31.x_ref, bf16[1024,3072]{1,0:T(8,128)(2,1)S(1)} %weights_near.1.w_ref), custom_call_target="tpu_custom_call" | custom-call | flops 4400000000 | tf_op jit(solution)/shard_map/own_block/pallas_call | solution.py:284
  23.8 0.1 collective-permute-start.8
  24.0 1.7 %collective-permute-start.9 = (bf16[144,1024]{1,0:T(8,128)(2,1)S(1)}, bf16[144,1024]{1,0:T(8,128)(2,1)S(1)}, u32[]{:S(2)}, u32[]{:S(2)}) collective-permute-start(bf16[144,1024]{1,0:T(8,128)(2,1)S(1)} %get-tuple-element.39), channel_id=1, source_target_pairs={{0,24},{8,0},{16,8},{24,16},{1,25},{9,1},{17,9},{25,17},{2,26},{10... | collective-permute-start | bytes 884744 | tf_op jit(solution)/shard_map/ppermute | solution.py:39
  25.6 2.8 %collective-permute-done.4.refs_0_ = bf16[144,1024]{1,0:T(8,128)(2,1)S(1)} collective-permute-done((bf16[144,1024]{1,0:T(8,128)(2,1)S(1)}, bf16[144,1024]{1,0:T(8,128)(2,1)S(1)}, u32[]{:S(2)}, u32[]{:S(2)}) %collective-permute-start.4) | collective-permute-done | bytes 294944 | tf_op jit(solution)/shard_map/ppermute | solution.py:398
  28.4 0.3 collective-permute-start.6
  28.7 0.0 collective-permute-done.5.refs_1_
  28.7 1.7 %collective-permute-start.7 = (bf16[144,1024]{1,0:T(8,128)(2,1)S(1)}, bf16[144,1024]{1,0:T(8,128)(2,1)S(1)}, u32[]{:S(2)}, u32[]{:S(2)}) collective-permute-start(bf16[144,1024]{1,0:T(8,128)(2,1)S(1)} %collective-permute-done.5.refs_1_), channel_id=1, source_target_pairs={{2,0},{4,2},{6,4},{7,6},{5,7},{3,5},{1,3},{0,1},{10,8},{12,10},{14... | collective-permute-start | bytes 884744 | tf_op jit(solution)/shard_map/ppermute | solution.py:399
  30.5 4.4 %attend_batch.3 = (f32[144,1024]{1,0:T(8,128)S(1)}, f32[144,1024]{1,0:T(8,128)S(1)}, f32[144,1024]{1,0:T(8,128)S(1)}) custom-call(s32[4]{0:T(128)S(1)} %pad_add_fusion.here_ref, s32[8,8]{1,0:T(8,128)S(1)} %copy-done.5, s32[1,1,8]{2,1,0:T(1,128)S(1)} %copy-done.4, s32[1,1]{1,0:T(1,128)S(6)} %copy.57.count_ref, ...), custom_call_target="tpu_custom_call" | custom-call | flops 5059999744 | tf_op jit(solution)/shard_map/attend_batch/pallas_call | solution.py:284
  34.9 2.3 %collective-permute-done.6.refs_0_ = bf16[144,1024]{1,0:T(8,128)(2,1)S(1)} collective-permute-done((bf16[144,1024]{1,0:T(8,128)(2,1)S(1)}, bf16[144,1024]{1,0:T(8,128)(2,1)S(1)}, u32[]{:S(2)}, u32[]{:S(2)}) %collective-permute-start.6) | collective-permute-done | bytes 294944 | tf_op jit(solution)/shard_map/ppermute | solution.py:398
  37.2 0.5 collective-permute-start.10
  37.6 1.6 %collective-permute-start.11 = (bf16[144,1024]{1,0:T(8,128)(2,1)S(1)}, bf16[144,1024]{1,0:T(8,128)(2,1)S(1)}, u32[]{:S(2)}, u32[]{:S(2)}) collective-permute-start(bf16[144,1024]{1,0:T(8,128)(2,1)S(1)} %collective-permute-done.7.refs_1_), channel_id=1, source_target_pairs={{2,0},{4,2},{6,4},{7,6},{5,7},{3,5},{1,3},{0,1},{10,8},{12,10},{14... | collective-permute-start | bytes 884744 | tf_op jit(solution)/shard_map/ppermute | solution.py:399
  39.2 6.1 %attend_batch.4 = (f32[144,1024]{1,0:T(8,128)S(1)}, f32[144,1024]{1,0:T(8,128)S(1)}, f32[144,1024]{1,0:T(8,128)S(1)}) custom-call(s32[4]{0:T(128)S(1)} %pad_add_fusion.here_ref, s32[8,8]{1,0:T(8,128)S(1)} %copy-done.5, s32[1,1,8]{2,1,0:T(1,128)S(1)} %copy-done.4, s32[1,1]{1,0:T(1,128)S(6)} %copy.57.count_ref, ...), custom_call_target="tpu_custom_call" | custom-call | flops 9020000256 | tf_op jit(solution)/shard_map/attend_batch/pallas_call | solution.py:284
  45.4 0.1 collective-permute-done.11.refs_1_
  45.4 1.7 %collective-permute-start.13 = (bf16[80,1024]{1,0:T(8,128)(2,1)S(1)}, bf16[80,1024]{1,0:T(8,128)(2,1)S(1)}, u32[]{:S(2)}, u32[]{:S(2)}) collective-permute-start(bf16[80,1024]{1,0:T(8,128)(2,1)S(1)} %slice.65), channel_id=1, source_target_pairs={{2,0},{4,2},{6,4},{7,6},{5,7},{3,5},{1,3},{0,1},{10,8},{12,10},{14... | collective-permute-start | bytes 491528 | tf_op jit(solution)/shard_map/ppermute | solution.py:406
  47.2 0.4 collective-permute-start.12
  47.6 4.4 %attend_batch.5 = (f32[144,1024]{1,0:T(8,128)S(1)}, f32[144,1024]{1,0:T(8,128)S(1)}, f32[144,1024]{1,0:T(8,128)S(1)}) custom-call(s32[4]{0:T(128)S(1)} %pad_add_fusion.here_ref, s32[8,8]{1,0:T(8,128)S(1)} %copy-done.5, s32[1,1,8]{2,1,0:T(1,128)S(1)} %copy-done.4, s32[1,1]{1,0:T(1,128)S(6)} %copy.57.count_ref, ...), custom_call_target="tpu_custom_call" | custom-call | flops 5059999744 | tf_op jit(solution)/shard_map/attend_batch/pallas_call | solution.py:284
  52.0 0.2 collective-permute-done.12.refs_0_
  52.2 4.2 %attend_last.1 = (f32[144,1024]{1,0:T(8,128)S(1)}, f32[8,144,128]{2,1,0:T(8,128)S(1)}, bf16[4,9,1024]{2,1,0:T(8,128)(2,1)S(1)}, bf16[4,9,1024]{2,1,0:T(8,128)(2,...) custom-call(s32[4]{0:T(128)S(1)} %pad_add_fusion.here_ref, s32[8,8]{1,0:T(8,128)S(1)} %copy-done.5, ...), custom_call_target="tpu_custom_call" | custom-call | flops 5500000256 | tf_op jit(solution)/shard_map/attend_last/pallas_call | solution.py:284
  56.4 0.1 collective-permute-start.14
  56.5 1.7 %collective-permute-start.15 = (bf16[4,9,1024]{2,1,0:T(8,128)(2,1)S(1)}, bf16[4,9,1024]{2,1,0:T(8,128)(2,1)S(1)}, u32[]{:S(2)}, u32[]{:S(2)}) collective-permute-start(bf16[4,9,1024]{2,1,0:T(8,128)(2,1)S(1)} %get-tuple-element.53), channel_id=1, source_target_pairs={{0,24},{8,0},{16,8},{24,16},{1,25},{9,1},{17,9},{25,17},{2,26},{10... | collective-permute-start | bytes 221192 | tf_op jit(solution)/shard_map/ppermute | solution.py:39
  58.2 3.2 %collective-permute-done.14.north_ref = bf16[4,9,1024]{2,1,0:T(8,128)(2,1)S(1)} collective-permute-done((bf16[4,9,1024]{2,1,0:T(8,128)(2,1)S(1)}, bf16[4,9,1024]{2,1,0:T(8,128)(2,1)S(1)}, u32[]{:S(2)}, u32[]{:S(2)}) %collective-permute-start.14) | collective-permute-done | bytes 73760 | tf_op jit(solution)/shard_map/ppermute | solution.py:39
  61.5 0.1 broadcast_select_fusion
  61.6 1.9 %collective-permute-start.16 = (bf16[4,6,1024]{2,1,0:T(8,128)(2,1)S(1)}, bf16[4,6,1024]{2,1,0:T(8,128)(2,1)S(1)}, u32[]{:S(2)}, u32[]{:S(2)}) collective-permute-start(bf16[4,6,1024]{2,1,0:T(8,128)(2,1)S(1)} %get-tuple-element.61), channel_id=1, source_target_pairs={{1,2},{2,1},{3,4},{4,3},{5,6},{6,5},{7,0},{0,7},{9,10},{10,9},{11,... | collective-permute-start | bytes 147464 | tf_op jit(solution)/shard_map/ppermute | solution.py:310
  63.5 1.7 %conv_part.3 = (f32[8,144,128]{2,1,0:T(8,128)S(1)}, f32[8,9,128]{2,1,0:T(8,128)S(1)}, bf16[4,9,4,1024]{3,2,1,0:T(4,128)(2,1)}) custom-call(f32[8,144,128]{2,1,0:T(8,128)S(1)} %get-tuple-element.47.field_ref, f32[9,1024]{1,0:T(8,128)S(1)} %copy-done.3, f32[144,1024]{1,0:T(8,128)S(1)} %get-tuple-element.48.dense_ref), custom_call_target="tpu_custom_call" | custom-call | flops 2200000000 | tf_op jit(solution)/shard_map/conv_part/pallas_call | solution.py:284
  65.2 3.9 %collective-permute-done.16.across_ref = bf16[4,6,1024]{2,1,0:T(8,128)(2,1)S(1)} collective-permute-done((bf16[4,6,1024]{2,1,0:T(8,128)(2,1)S(1)}, bf16[4,6,1024]{2,1,0:T(8,128)(2,1)S(1)}, u32[]{:S(2)}, u32[]{:S(2)}) %collective-permute-start.16) | collective-permute-done | bytes 49184 | tf_op jit(solution)/shard_map/ppermute | solution.py:310
  69.1 0.1 collective-permute-done.17.pair_ref
  69.2 1.7 %conv_second.1 = bf16[4,9,4,1024]{3,2,1,0:T(4,128)(2,1)} custom-call(s32[4]{0:T(128)S(1)} %pad_add_fusion.here_ref, f32[8,144,128]{2,1,0:T(8,128)S(1)} %get-tuple-element.50.part_ref, f32[8,9,128]{2,1,0:T(8,128)S(1)} %get-tuple-element.51.taps_ref, bf16[4,9,1024]{2,1,0:T(8,128)(2,1)S(1)} %collective-permute-done.14.north_ref, ...), custom_call_target="tpu_custom_call" | custom-call | flops 2200000000 | tf_op jit(solution)/shard_map/conv_second/pallas_call | solution.py:284
  (24 shorter events, 0.2 us)
Async XLA Ops:
  1.7 5.1 %collective-permute-start = (bf16[4,9,1024]{2,1,0:T(8,128)(2,1)S(1)}, bf16[4,9,1024]{2,1,0:T(8,128)(2,1)S(1)}, u32[]{:S(2)}, u32[]{:S(2)}) collective-permute-start(bf16[4,9,1024]{2,1,0:T(8,128)(2,1)S(1)} %get-tuple-element.59), channel_id=1, source_target_pairs={{0,8},{8,16},{16,24},{24,0},{1,9},{9,17},{17,25},{25,1},{2,10},{10... | collective-permute-start | bytes 221192 | tf_op jit(solution)/shard_map/ppermute | solution.py:39
  2.2 5.8 %collective-permute-start.1 = (bf16[4,9,1024]{2,1,0:T(8,128)(2,1)S(1)}, bf16[4,9,1024]{2,1,0:T(8,128)(2,1)S(1)}, u32[]{:S(2)}, u32[]{:S(2)}) collective-permute-start(bf16[4,9,1024]{2,1,0:T(8,128)(2,1)S(1)} %get-tuple-element.58), channel_id=1, source_target_pairs={{0,24},{8,0},{16,8},{24,16},{1,25},{9,1},{17,9},{25,17},{2,26},{10... | collective-permute-start | bytes 221192 | tf_op jit(solution)/shard_map/ppermute | solution.py:39
  8.2 9.2 %collective-permute-start.2 = (bf16[4,6,1024]{2,1,0:T(8,128)(2,1)S(1)}, bf16[4,6,1024]{2,1,0:T(8,128)(2,1)S(1)}, u32[]{:S(2)}, u32[]{:S(2)}) collective-permute-start(bf16[4,6,1024]{2,1,0:T(8,128)(2,1)S(1)} %get-tuple-element.67), channel_id=1, source_target_pairs={{1,2},{2,1},{3,4},{4,3},{5,6},{6,5},{7,0},{0,7},{9,10},{10,9},{11,... | collective-permute-start | bytes 147464 | tf_op jit(solution)/shard_map/ppermute | solution.py:310
  12.8 4.9 %collective-permute-start.3 = (bf16[4,6,1024]{2,1,0:T(8,128)(2,1)S(1)}, bf16[4,6,1024]{2,1,0:T(8,128)(2,1)S(1)}, u32[]{:S(2)}, u32[]{:S(2)}) collective-permute-start(bf16[4,6,1024]{2,1,0:T(8,128)(2,1)S(1)} %get-tuple-element.66), channel_id=1, source_target_pairs={{0,1},{1,0},{2,3},{3,2},{4,5},{5,4},{6,7},{7,6},{8,9},{9,8},{10,11... | collective-permute-start | bytes 147464 | tf_op jit(solution)/shard_map/ppermute | solution.py:311
  12.8 2.8 %copy-start = (bf16[1024,3072]{1,0:T(8,128)(2,1)S(1)}, bf16[1024,3072]{1,0:T(8,128)(2,1)}, u32[]{:S(2)}) copy-start(bf16[1024,3072]{1,0:T(8,128)(2,1)} %far_ref.1) | copy-start | bytes 18874372
  15.6 0.8 %copy-start.2 = (f32[9,1024]{1,0:T(8,128)S(1)}, f32[9,1024]{1,0:T(8,128)}, u32[]{:S(2)}) copy-start(f32[9,1024]{1,0:T(8,128)} %weights_ref.2) | copy-start | bytes 110596
  18.9 11.6 %copy-start.4 = (s32[1,1,8]{2,1,0:T(1,128)S(1)}, s32[1,1,8]{2,1,0:T(1,128)}, u32[]{:S(2)}) copy-start(s32[1,1,8]{2,1,0:T(1,128)} %list_ref.7) | copy-start | bytes 100
  18.9 11.6 %copy-start.5 = (s32[8,8]{1,0:T(8,128)S(1)}, s32[8,8]{1,0:T(8,128)}, u32[]{:S(2)}) copy-start(s32[8,8]{1,0:T(8,128)} %constant.28.clone.sources_ref) | copy-start | bytes 772
  18.9 9.5 %collective-permute-start.4 = (bf16[144,1024]{1,0:T(8,128)(2,1)S(1)}, bf16[144,1024]{1,0:T(8,128)(2,1)S(1)}, u32[]{:S(2)}, u32[]{:S(2)}) collective-permute-start(bf16[144,1024]{1,0:T(8,128)(2,1)S(1)} %get-tuple-element.31.x_ref), channel_id=1, source_target_pairs={{0,2},{2,4},{4,6},{6,7},{7,5},{5,3},{3,1},{1,0},{8,10},{10,12},{12... | collective-permute-start | bytes 884744 | tf_op jit(solution)/shard_map/ppermute | solution.py:398
  19.0 9.8 %collective-permute-start.5 = (bf16[144,1024]{1,0:T(8,128)(2,1)S(1)}, bf16[144,1024]{1,0:T(8,128)(2,1)S(1)}, u32[]{:S(2)}, u32[]{:S(2)}) collective-permute-start(bf16[144,1024]{1,0:T(8,128)(2,1)S(1)} %get-tuple-element.31.x_ref), channel_id=1, source_target_pairs={{2,0},{4,2},{6,4},{7,6},{5,7},{3,5},{1,3},{0,1},{10,8},{12,10},{14... | collective-permute-start | bytes 884744 | tf_op jit(solution)/shard_map/ppermute | solution.py:399
  23.8 15.4 %collective-permute-start.8 = (bf16[144,1024]{1,0:T(8,128)(2,1)S(1)}, bf16[144,1024]{1,0:T(8,128)(2,1)S(1)}, u32[]{:S(2)}, u32[]{:S(2)}) collective-permute-start(bf16[144,1024]{1,0:T(8,128)(2,1)S(1)} %get-tuple-element.39), channel_id=1, source_target_pairs={{0,8},{8,16},{16,24},{24,0},{1,9},{9,17},{17,25},{25,1},{2,10},{10... | collective-permute-start | bytes 884744 | tf_op jit(solution)/shard_map/ppermute | solution.py:39
  24.0 15.2 %collective-permute-start.9 = (bf16[144,1024]{1,0:T(8,128)(2,1)S(1)}, bf16[144,1024]{1,0:T(8,128)(2,1)S(1)}, u32[]{:S(2)}, u32[]{:S(2)}) collective-permute-start(bf16[144,1024]{1,0:T(8,128)(2,1)S(1)} %get-tuple-element.39), channel_id=1, source_target_pairs={{0,24},{8,0},{16,8},{24,16},{1,25},{9,1},{17,9},{25,17},{2,26},{10... | collective-permute-start | bytes 884744 | tf_op jit(solution)/shard_map/ppermute | solution.py:39
  28.4 8.7 %collective-permute-start.6 = (bf16[144,1024]{1,0:T(8,128)(2,1)S(1)}, bf16[144,1024]{1,0:T(8,128)(2,1)S(1)}, u32[]{:S(2)}, u32[]{:S(2)}) collective-permute-start(bf16[144,1024]{1,0:T(8,128)(2,1)S(1)} %collective-permute-done.4.refs_0_), channel_id=1, source_target_pairs={{0,2},{2,4},{4,6},{6,7},{7,5},{5,3},{3,1},{1,0},{8,10},{10,12},{12... | collective-permute-start | bytes 884744 | tf_op jit(solution)/shard_map/ppermute | solution.py:398
  28.7 8.9 %collective-permute-start.7 = (bf16[144,1024]{1,0:T(8,128)(2,1)S(1)}, bf16[144,1024]{1,0:T(8,128)(2,1)S(1)}, u32[]{:S(2)}, u32[]{:S(2)}) collective-permute-start(bf16[144,1024]{1,0:T(8,128)(2,1)S(1)} %collective-permute-done.5.refs_1_), channel_id=1, source_target_pairs={{2,0},{4,2},{6,4},{7,6},{5,7},{3,5},{1,3},{0,1},{10,8},{12,10},{14... | collective-permute-start | bytes 884744 | tf_op jit(solution)/shard_map/ppermute | solution.py:399
  37.2 10.0 %collective-permute-start.10 = (bf16[144,1024]{1,0:T(8,128)(2,1)S(1)}, bf16[144,1024]{1,0:T(8,128)(2,1)S(1)}, u32[]{:S(2)}, u32[]{:S(2)}) collective-permute-start(bf16[144,1024]{1,0:T(8,128)(2,1)S(1)} %collective-permute-done.6.refs_0_), channel_id=1, source_target_pairs={{0,2},{2,4},{4,6},{6,7},{7,5},{5,3},{3,1},{1,0},{8,10},{10,12},{12... | collective-permute-start | bytes 884744 | tf_op jit(solution)/shard_map/ppermute | solution.py:398
  37.6 7.8 %collective-permute-start.11 = (bf16[144,1024]{1,0:T(8,128)(2,1)S(1)}, bf16[144,1024]{1,0:T(8,128)(2,1)S(1)}, u32[]{:S(2)}, u32[]{:S(2)}) collective-permute-start(bf16[144,1024]{1,0:T(8,128)(2,1)S(1)} %collective-permute-done.7.refs_1_), channel_id=1, source_target_pairs={{2,0},{4,2},{6,4},{7,6},{5,7},{3,5},{1,3},{0,1},{10,8},{12,10},{14... | collective-permute-start | bytes 884744 | tf_op jit(solution)/shard_map/ppermute | solution.py:399
  45.4 6.8 %collective-permute-start.13 = (bf16[80,1024]{1,0:T(8,128)(2,1)S(1)}, bf16[80,1024]{1,0:T(8,128)(2,1)S(1)}, u32[]{:S(2)}, u32[]{:S(2)}) collective-permute-start(bf16[80,1024]{1,0:T(8,128)(2,1)S(1)} %slice.65), channel_id=1, source_target_pairs={{2,0},{4,2},{6,4},{7,6},{5,7},{3,5},{1,3},{0,1},{10,8},{12,10},{14... | collective-permute-start | bytes 491528 | tf_op jit(solution)/shard_map/ppermute | solution.py:406
  47.2 5.0 %collective-permute-start.12 = (bf16[64,1024]{1,0:T(8,128)(2,1)S(1)}, bf16[64,1024]{1,0:T(8,128)(2,1)S(1)}, u32[]{:S(2)}, u32[]{:S(2)}) collective-permute-start(bf16[64,1024]{1,0:T(8,128)(2,1)S(1)} %slice.64), channel_id=1, source_target_pairs={{0,2},{2,4},{4,6},{6,7},{7,5},{5,3},{3,1},{1,0},{8,10},{10,12},{12... | collective-permute-start | bytes 393224 | tf_op jit(solution)/shard_map/ppermute | solution.py:405
  47.6 4.6 %copy-start.1 = (bf16[1024,1024]{1,0:T(8,128)(2,1)S(1)}, bf16[1024,1024]{1,0:T(8,128)(2,1)}, u32[]{:S(2)}) copy-start(bf16[1024,1024]{1,0:T(8,128)(2,1)} %wo_ref.1) | copy-start | bytes 6291460
  52.2 11.3 %copy-start.3 = (f32[9,1024]{1,0:T(8,128)S(1)}, f32[9,1024]{1,0:T(8,128)}, u32[]{:S(2)}) copy-start(f32[9,1024]{1,0:T(8,128)} %weights_ref.3) | copy-start | bytes 110596
  56.4 5.0 %collective-permute-start.14 = (bf16[4,9,1024]{2,1,0:T(8,128)(2,1)S(1)}, bf16[4,9,1024]{2,1,0:T(8,128)(2,1)S(1)}, u32[]{:S(2)}, u32[]{:S(2)}) collective-permute-start(bf16[4,9,1024]{2,1,0:T(8,128)(2,1)S(1)} %get-tuple-element.52), channel_id=1, source_target_pairs={{0,8},{8,16},{16,24},{24,0},{1,9},{9,17},{17,25},{25,1},{2,10},{10... | collective-permute-start | bytes 221192 | tf_op jit(solution)/shard_map/ppermute | solution.py:39
  56.5 4.9 %collective-permute-start.15 = (bf16[4,9,1024]{2,1,0:T(8,128)(2,1)S(1)}, bf16[4,9,1024]{2,1,0:T(8,128)(2,1)S(1)}, u32[]{:S(2)}, u32[]{:S(2)}) collective-permute-start(bf16[4,9,1024]{2,1,0:T(8,128)(2,1)S(1)} %get-tuple-element.53), channel_id=1, source_target_pairs={{0,24},{8,0},{16,8},{24,16},{1,25},{9,1},{17,9},{25,17},{2,26},{10... | collective-permute-start | bytes 221192 | tf_op jit(solution)/shard_map/ppermute | solution.py:39
  61.6 7.5 %collective-permute-start.16 = (bf16[4,6,1024]{2,1,0:T(8,128)(2,1)S(1)}, bf16[4,6,1024]{2,1,0:T(8,128)(2,1)S(1)}, u32[]{:S(2)}, u32[]{:S(2)}) collective-permute-start(bf16[4,6,1024]{2,1,0:T(8,128)(2,1)S(1)} %get-tuple-element.61), channel_id=1, source_target_pairs={{1,2},{2,1},{3,4},{4,3},{5,6},{6,5},{7,0},{0,7},{9,10},{10,9},{11,... | collective-permute-start | bytes 147464 | tf_op jit(solution)/shard_map/ppermute | solution.py:310
  63.5 5.7 %collective-permute-start.17 = (bf16[4,6,1024]{2,1,0:T(8,128)(2,1)S(1)}, bf16[4,6,1024]{2,1,0:T(8,128)(2,1)S(1)}, u32[]{:S(2)}, u32[]{:S(2)}) collective-permute-start(bf16[4,6,1024]{2,1,0:T(8,128)(2,1)S(1)} %get-tuple-element.60), channel_id=1, source_target_pairs={{0,1},{1,0},{2,3},{3,2},{4,5},{5,4},{6,7},{7,6},{8,9},{9,8},{10,11... | collective-permute-start | bytes 147464 | tf_op jit(solution)/shard_map/ppermute | solution.py:311

commit v4 on v3

--- a/solution.py
+++ b/solution.py
@@ -147,18 +147,57 @@
                 mixed_ref[level, column, :, lanes] = full[index, at : at + rows, :].astype(BF16)
 
 
-def pair_attend(query2, keys2, values2, bias, factor):
-    half = query2.shape[0] // 2
+def scores_of(query2, keys2, bias):
     scores = lax.dot_general(query2, keys2, (((1,), (1,)), ((), ())), preferred_element_type=F32)
-    if bias is not None:
-        scores = scores + bias
-    highest = jnp.max(scores, axis=-1, keepdims=True)
-    weights = jnp.exp2((scores - highest) * factor).astype(BF16)
-    beside = jnp.concatenate([values2, jnp.ones_like(values2)], axis=1)
-    result = jnp.dot(weights, beside, preferred_element_type=F32)
+    return scores if bias is None else scores + bias
+
+
+def merge(both):
+    half = both.shape[0] // 2
     low = lax.broadcasted_iota(jnp.int32, (half, LANES), 1) < LANES // 2
-    merge = lambda x: jnp.where(low, x[:half], x[half:])
-    return merge(highest), merge(result[:, LANES:]), merge(result[:, :LANES])
+    return jnp.where(low, both[:half], both[half:])
+
+
+def attend_pairs(factor, x, w_ref, bias, query_of, finish):
+    width = x.shape[1]
+    pairs = width // LANES
+    inside = GROUP // LANES
+    groups, scores = {}, {}
+
+    def project(group):
+        if group * GROUP < width and group not in groups:
+            columns = lambda part: slice(part * width + group * GROUP, part * width + (group + 1) * GROUP)
+            groups[group] = [
+                jnp.dot(x, w_ref[:, columns(part)], preferred_element_type=F32).astype(BF16) for part in (1, 2)
+            ]
+
+    def lanes_of(pair):
+        return slice(pair % inside * LANES, (pair % inside + 1) * LANES)
+
+    def score(pair):
+        if pair < pairs:
+            project(pair // inside)
+            scores[pair] = scores_of(query_of(pair), groups[pair // inside][0][:, lanes_of(pair)], bias)
+
+    def weigh(pair, highest, weights):
+        values2 = groups[pair // inside][1][:, lanes_of(pair)]
+        beside = jnp.concatenate([values2, jnp.ones_like(values2)], axis=1)
+        result = jnp.dot(weights, beside, preferred_element_type=F32)
+        finish(pair, (merge(highest), merge(result[:, LANES:]), merge(result[:, :LANES])))
+
+    score(0)
+    waiting = None
+    for pair in range(pairs):
+        if (pair + 1) % inside == 1:
+            project((pair + 1) // inside + 1)
+        score(pair + 1)
+        current = scores.pop(pair)
+        highest = jnp.max(current, axis=-1, keepdims=True)
+        weights = jnp.exp2((current - highest) * factor).astype(BF16)
+        if waiting is not None:
+            weigh(*waiting)
+        waiting = (pair, highest, weights)
+    weigh(*waiting)
 
 
 def key_bias(here_ref, sources_ref, list_ref, count_ref, slots, sizes):
@@ -183,23 +222,8 @@
     return bias
 
 
-def project(x, w_ref, group):
-    width = w_ref.shape[0]
-    columns = lambda part: slice(part * width + group * GROUP, part * width + (group + 1) * GROUP)
-    keys = jnp.dot(x, w_ref[:, columns(1)], preferred_element_type=F32).astype(BF16)
-    values = jnp.dot(x, w_ref[:, columns(2)], preferred_element_type=F32).astype(BF16)
-    return keys, values
-
-
 def joined(blocks):
     return blocks[0][...] if len(blocks) == 1 else jnp.concatenate([b[...] for b in blocks], axis=0)
-
-
-def head_pairs(width):
-    for group in range(width // GROUP):
-        for pair in range(GROUP // LANES):
-            start = group * GROUP + pair * LANES
-            yield group, pair, slice(pair * LANES, (pair + 1) * LANES), slice(start, start + LANES)
 
 
 def own_kernel(factor, x_ref, w_ref, handed_ref, query_ref, high_ref, sum_ref, acc_ref):
@@ -208,17 +232,24 @@
     handed_ref[...] = x
     low = lax.broadcasted_iota(jnp.int32, (tokens, LANES), 1) < LANES // 2
     zero = jnp.zeros((tokens, LANES), BF16)
-    for group, pair, inner, lanes in head_pairs(width):
-        if pair == 0:
-            query = jnp.dot(x, w_ref[:, group * GROUP : (group + 1) * GROUP], preferred_element_type=F32).astype(BF16)
-            keys, values = project(x, w_ref, group)
-        part = query[:, inner]
+    inside = GROUP // LANES
+    queries = {}
+
+    def query_of(pair):
+        group = pair // inside
+        if group not in queries:
+            columns = slice(group * GROUP, (group + 1) * GROUP)
+            queries[group] = jnp.dot(x, w_ref[:, columns], preferred_element_type=F32).astype(BF16)
+        part = queries[group][:, pair % inside * LANES : (pair % inside + 1) * LANES]
         query2 = jnp.concatenate([jnp.where(low, part, zero), jnp.where(low, zero, part)], axis=0)
-        query_ref[group * (GROUP // LANES) + pair] = query2
-        high, summed, result = pair_attend(query2, keys[:, inner], values[:, inner], None, factor)
-        high_ref[:, lanes] = high
-        sum_ref[:, lanes] = summed
-        acc_ref[:, lanes] = result
+        query_ref[pair] = query2
+        return query2
+
+    def finish(pair, part):
+        lanes = slice(pair * LANES, (pair + 1) * LANES)
+        high_ref[:, lanes], sum_ref[:, lanes], acc_ref[:, lanes] = part
+
+    attend_pairs(factor, x, w_ref, None, query_of, finish)
 
 
 def combine(state, part, factor):
@@ -232,15 +263,14 @@
     factor, slots, sizes, here_ref, sources_ref, list_ref, count_ref, query_ref, w_ref, high_in, sum_in, acc_in, *refs
 ):
     blocks, (high_ref, sum_ref, acc_ref) = refs[:-3], refs[-3:]
-    x = joined(blocks)
     bias = key_bias(here_ref, sources_ref, list_ref, count_ref, slots, sizes)
-    for group, pair, inner, lanes in head_pairs(x.shape[1]):
-        if pair == 0:
-            keys, values = project(x, w_ref, group)
-        query2 = query_ref[group * (GROUP // LANES) + pair]
-        part = pair_attend(query2, keys[:, inner], values[:, inner], bias, factor)
+
+    def finish(pair, part):
+        lanes = slice(pair * LANES, (pair + 1) * LANES)
         state = combine((high_in[:, lanes], sum_in[:, lanes], acc_in[:, lanes]), part, factor)
         high_ref[:, lanes], sum_ref[:, lanes], acc_ref[:, lanes] = state
+
+    attend_pairs(factor, joined(blocks), w_ref, bias, lambda pair: query_ref[pair], finish)
 
 
 def last_kernel(
@@ -254,16 +284,16 @@
     width = x.shape[1]
     bias = key_bias(here_ref, sources_ref, list_ref, count_ref, slots, sizes)
     total[...] = stream_ref[...].astype(F32)
-    for group, pair, inner, lanes in head_pairs(width):
-        if pair == 0:
-            keys, values = project(x, w_ref, group)
-        query2 = query_ref[group * (GROUP // LANES) + pair]
-        part = pair_attend(query2, keys[:, inner], values[:, inner], bias, factor)
+
+    def finish(pair, part):
+        lanes = slice(pair * LANES, (pair + 1) * LANES)
         _, summed, result = combine((high_in[:, lanes], sum_in[:, lanes], acc_in[:, lanes]), part, factor)
         dense[:, lanes] = result / summed
-        if pair == GROUP // LANES - 1:
-            chunk = slice(group * GROUP, (group + 1) * GROUP)
+        if (pair + 1) * LANES % GROUP == 0:
+            chunk = slice((pair + 1) * LANES - GROUP, (pair + 1) * LANES)
             total[...] += jnp.dot(dense[:, chunk].astype(BF16), wo_ref[chunk, :], preferred_element_type=F32)
+
+    attend_pairs(factor, x, w_ref, bias, lambda pair: query_ref[pair], finish)
     for index in range(width // LANES):
         lanes = slice(index * LANES, (index + 1) * LANES)
         after_ref[index] = total[:, lanes].astype(BF16).astype(F32)
@@ -392,6 +422,7 @@
         )
 
     ahead, behind = normed, normed
+    near = [(shift(handed, "lat", 1), ABOVE), (shift(handed, "lat", -1), BELOW)]
     waiting = []
     cut = (tokens // 32) * 16
     for step in range(1, half):
@@ -399,9 +430,7 @@
         behind = lax.ppermute(behind, "lon", backward)
         if step > 1:
             state = batch(state, waiting)
-        waiting = [(ahead, 2 * step - 2), (behind, 2 * step - 1)]
-        if step == 2:
-            waiting += [(shift(handed, "lat", 1), ABOVE), (shift(handed, "lat", -1), BELOW)]
+        waiting = [(ahead, 2 * step - 2), (behind, 2 * step - 1), *near[step - 1 : step]]
     far_first = lax.ppermute(ahead[:cut], "lon", forward)
     far_second = lax.ppermute(behind[cut:], "lon", backward)
     state = batch(state, waiting)

time: 71.1 us -> 69.7 us (0.980)
  Pallas kernels: 27.8 us -> 23.3 us
  waiting for transfers between devices: 15.5 us -> 18.1 us
    pallas_call x8, Pallas kernels: 26.4 us -> 21.9 us  [call(): pl.pallas_call(kernel, out_shape=out_shape, in_specs=[pl.BlockSpec(memory...]
    ppermute x3, waiting for transfers between devices: 0.07 us -> 1.87 us  [local(): behind = lax.ppermute(behind, 'lon', backward)]
    ppermute x2, starting transfers between devices: 0.01 us -> 1.15 us  [exchange(): pair = lax.ppermute(jnp.where(even, east, west), 'lon', swap(0))]
    ppermute x2, starting transfers between devices: 6.55 us -> 5.67 us  [exchange(): across = lax.ppermute(jnp.where(even, west, east), 'lon', swap(1))]
    ppermute x6, waiting for transfers between devices: 5.78 us -> 6.62 us  [shift(): return lax.ppermute(x, axis, [(i, (i + by) % size) for i in range(size)])]
  transfers between devices with their start and end apart: 18 -> 18, of which waited for: 10 -> 9; matrix products, arithmetic and copies ran while one was open for 1% -> 1% of each run, Pallas kernels for 29% -> 25%
where the time goes in v4:
time: 69.7 us; the launch traced here: 69.5 us
  Pallas kernels  23.3 us (33%)
  starting transfers between devices  21.4 us (31%)
  waiting for transfers between devices  18.1 us (26%)
  local copies, waits for them, and re-layouts  4.74 us (7%)
  between operations  1.52 us (2%)
    pallas_call x8, Pallas kernels, call(): pl.pallas_call(kernel, out_shape=out_shape, in_specs=[pl.BlockSpec(memory...  21.9 us
    ppermute x6, waiting for transfers between devices, shift(): return lax.ppermute(x, axis, [(i, (i + by) % size) for i in range(size)])  6.62 us
    ppermute x6, starting transfers between devices, shift(): return lax.ppermute(x, axis, [(i, (i + by) % size) for i in range(size)])  6.13 us
    ppermute x2, starting transfers between devices, exchange(): across = lax.ppermute(jnp.where(even, west, east), 'lon', swap(1))  5.67 us
    ppermute x3, starting transfers between devices, local(): behind = lax.ppermute(behind, 'lon', backward)  5.33 us
    ppermute x3, waiting for transfers between devices, local(): ahead = lax.ppermute(ahead, 'lon', forward)  5.24 us
    unnamed x13, local copies, waits for them, and re-layouts  4.29 us
    ppermute x2, waiting for transfers between devices, exchange(): across = lax.ppermute(jnp.where(even, west, east), 'lon', swap(1))  3.36 us
  transfers between devices with their start and end apart: 18, of which 9 were waited for; matrix products, arithmetic and copies ran while one was open for 1% of the time, Pallas kernels for 25%

profile of v4, /device:TPU:0, one launch (start us, length us, event | category | flops | bytes accessed | tf_op | source)
XLA Modules:
  0.0 69.5 jit_solution(6660219124857636220)
XLA Ops:
  0.6 1.1 %copy.56 = bf16[4,4,9,1024]{3,2,0,1:T(8,128)(2,1)S(1)} copy(bf16[4,4,9,1024]{3,1,2,0:T(4,128)(2,1)} %param.8) | data formatting | bytes 589824 | tf_op args[0]
  1.7 0.5 collective-permute-start
  2.2 2.0 %collective-permute-start.1 = (bf16[4,9,1024]{2,1,0:T(8,128)(2,1)S(1)}, bf16[4,9,1024]{2,1,0:T(8,128)(2,1)S(1)}, u32[]{:S(2)}, u32[]{:S(2)}) collective-permute-start(bf16[4,9,1024]{2,1,0:T(8,128)(2,1)S(1)} %get-tuple-element.58), channel_id=1, source_target_pairs={{0,24},{8,0},{16,8},{24,16},{1,25},{9,1},{17,9},{25,17},{2,26},{10... | collective-permute-start | bytes 221192 | tf_op jit(solution)/shard_map/ppermute | solution.py:39
  4.2 0.1 fusion
  4.3 0.2 copy.50.field_ref
  4.6 0.1 copy_bitcast_fusion.1
  4.7 0.1 pad_add_fusion.here_ref
  4.8 2.0 %collective-permute-done.after_ref.north_ref = bf16[4,9,1024]{2,1,0:T(8,128)(2,1)S(1)} collective-permute-done((bf16[4,9,1024]{2,1,0:T(8,128)(2,1)S(1)}, bf16[4,9,1024]{2,1,0:T(8,128)(2,1)S(1)}, u32[]{:S(2)}, u32[]{:S(2)}) %collective-permute-start) | collective-permute-done | bytes 73760 | tf_op jit(solution)/shard_map/ppermute | solution.py:39
  6.9 1.2 %collective-permute-done.1.south_ref = bf16[4,9,1024]{2,1,0:T(8,128)(2,1)S(1)} collective-permute-done((bf16[4,9,1024]{2,1,0:T(8,128)(2,1)S(1)}, bf16[4,9,1024]{2,1,0:T(8,128)(2,1)S(1)}, u32[]{:S(2)}, u32[]{:S(2)}) %collective-permute-start.1) | collective-permute-done | bytes 73760 | tf_op jit(solution)/shard_map/ppermute | solution.py:39
  8.1 0.1 broadcast_select_fusion.2
  8.2 4.6 %collective-permute-start.2 = (bf16[4,6,1024]{2,1,0:T(8,128)(2,1)S(1)}, bf16[4,6,1024]{2,1,0:T(8,128)(2,1)S(1)}, u32[]{:S(2)}, u32[]{:S(2)}) collective-permute-start(bf16[4,6,1024]{2,1,0:T(8,128)(2,1)S(1)} %get-tuple-element.67), channel_id=1, source_target_pairs={{1,2},{2,1},{3,4},{4,3},{5,6},{6,5},{7,0},{0,7},{9,10},{10,9},{11,... | collective-permute-start | bytes 147464 | tf_op jit(solution)/shard_map/ppermute | solution.py:340
  12.8 0.0 collective-permute-start.3
  12.8 2.8 %copy-done = bf16[1024,3072]{1,0:T(8,128)(2,1)S(1)} copy-done((bf16[1024,3072]{1,0:T(8,128)(2,1)S(1)}, bf16[1024,3072]{1,0:T(8,128)(2,1)}, u32[]{:S(2)}) %copy-start) | copy-done | bytes 6291480
  15.6 0.4 weights_near.1.w_ref
  16.1 0.4 copy-done.2
  16.5 0.9 %conv_part.2 = (f32[8,144,128]{2,1,0:T(8,128)S(1)}, f32[8,9,128]{2,1,0:T(8,128)S(1)}) custom-call(bf16[4,9,4,1024]{3,2,1,0:T(4,128)(2,1)S(1)} %copy.50.field_ref, f32[9,1024]{1,0:T(8,128)S(1)} %copy-done.2, bf16[4,9,1024]{2,1,0:T(8,128)(2,1)S(1)} %collective-permute-done.after_ref.north_ref), custom_call_target="tpu_custom_call" | custom-call | flops 2000000000 | tf_op jit(solution)/shard_map/conv_part/pallas_call | solution.py:374
  17.4 0.3 collective-permute-done.3.pair_ref
  17.7 1.1 %conv_first.1 = (bf16[144,1024]{1,0:T(8,128)(2,1)S(1)}, bf16[144,1024]{1,0:T(8,128)(2,1)S(1)}) custom-call(s32[4]{0:T(128)S(1)} %pad_add_fusion.here_ref, f32[8,144,128]{2,1,0:T(8,128)S(1)} %get-tuple-element.29.part_ref, f32[8,9,128]{2,1,0:T(8,128)S(1)} %get-tuple-element.30.taps_ref, bf16[4,9,1024]{2,1,0:T(8,128)(2,1)S(1)} %collective-permute-done.after_ref.north_ref, ...), custom_call_target="tpu_custom_call" | custom-call | flops 2200000000 | tf_op jit(solution)/shard_map/conv_first/pallas_call | solution.py:314
  18.9 0.0 copy-start.4
  18.9 0.0 copy-start.5
  18.9 0.1 collective-permute-start.4
  19.0 2.0 %collective-permute-start.5 = (bf16[144,1024]{1,0:T(8,128)(2,1)S(1)}, bf16[144,1024]{1,0:T(8,128)(2,1)S(1)}, u32[]{:S(2)}, u32[]{:S(2)}) collective-permute-start(bf16[144,1024]{1,0:T(8,128)(2,1)S(1)} %get-tuple-element.31.x_ref), channel_id=1, source_target_pairs={{2,0},{4,2},{6,4},{7,6},{5,7},{3,5},{1,3},{0,1},{10,8},{12,10},{14... | collective-permute-start | bytes 884744 | tf_op jit(solution)/shard_map/ppermute | solution.py:430
  21.0 2.1 %own_block.1 = (bf16[144,1024]{1,0:T(8,128)(2,1)S(1)}, bf16[8,288,128]{2,1,0:T(8,128)(2,1)S(1)}, f32[144,1024]{1,0:T(8,128)S(1)}, f32[144,1024]{1,0:T(8,128)S(1)}, f32[144,1024]{1,0:T(8,128)S(1)}) custom-call(bf16[144,1024]{1,0:T(8,128)(2,1)S(1)} %get-tuple-element.31.x_ref, bf16[1024,3072]{1,0:T(8,128)(2,1)S(1)} %weights_near.1.w_ref), custom_call_target="tpu_custom_call" | custom-call | flops 4400000000 | tf_op jit(solution)/shard_map/own_block/pallas_call | solution.py:314
  23.1 0.1 collective-permute-start.6
  23.8 1.7 %collective-permute-start.9 = (bf16[144,1024]{1,0:T(8,128)(2,1)S(1)}, bf16[144,1024]{1,0:T(8,128)(2,1)S(1)}, u32[]{:S(2)}, u32[]{:S(2)}) collective-permute-start(bf16[144,1024]{1,0:T(8,128)(2,1)S(1)} %get-tuple-element.36), channel_id=1, source_target_pairs={{0,24},{8,0},{16,8},{24,16},{1,25},{9,1},{17,9},{25,17},{2,26},{10... | collective-permute-start | bytes 884744 | tf_op jit(solution)/shard_map/ppermute | solution.py:39
  25.6 2.9 %collective-permute-done.4.refs_0_ = bf16[144,1024]{1,0:T(8,128)(2,1)S(1)} collective-permute-done((bf16[144,1024]{1,0:T(8,128)(2,1)S(1)}, bf16[144,1024]{1,0:T(8,128)(2,1)S(1)}, u32[]{:S(2)}, u32[]{:S(2)}) %collective-permute-start.4) | collective-permute-done | bytes 294944 | tf_op jit(solution)/shard_map/ppermute | solution.py:429
  28.4 0.3 collective-permute-start.7
  28.7 1.7 %collective-permute-start.8 = (bf16[144,1024]{1,0:T(8,128)(2,1)S(1)}, bf16[144,1024]{1,0:T(8,128)(2,1)S(1)}, u32[]{:S(2)}, u32[]{:S(2)}) collective-permute-start(bf16[144,1024]{1,0:T(8,128)(2,1)S(1)} %collective-permute-done.5.refs_1_), channel_id=1, source_target_pairs={{2,0},{4,2},{6,4},{7,6},{5,7},{3,5},{1,3},{0,1},{10,8},{12,10},{14... | collective-permute-start | bytes 884744 | tf_op jit(solution)/shard_map/ppermute | solution.py:430
  30.5 4.3 %attend_batch.3 = (f32[144,1024]{1,0:T(8,128)S(1)}, f32[144,1024]{1,0:T(8,128)S(1)}, f32[144,1024]{1,0:T(8,128)S(1)}) custom-call(s32[4]{0:T(128)S(1)} %pad_add_fusion.here_ref, s32[8,8]{1,0:T(8,128)S(1)} %copy-done.5, s32[1,1,8]{2,1,0:T(1,128)S(1)} %copy-done.4, s32[1,1]{1,0:T(1,128)S(6)} %copy.57.count_ref, ...), custom_call_target="tpu_custom_call" | custom-call | flops 7040000000 | tf_op jit(solution)/shard_map/attend_batch/pallas_call | solution.py:314
  34.8 2.4 %collective-permute-done.7.refs_0_ = bf16[144,1024]{1,0:T(8,128)(2,1)S(1)} collective-permute-done((bf16[144,1024]{1,0:T(8,128)(2,1)S(1)}, bf16[144,1024]{1,0:T(8,128)(2,1)S(1)}, u32[]{:S(2)}, u32[]{:S(2)}) %collective-permute-start.7) | collective-permute-done | bytes 294944 | tf_op jit(solution)/shard_map/ppermute | solution.py:429
  37.2 0.5 collective-permute-start.10
  37.6 1.6 %collective-permute-start.11 = (bf16[144,1024]{1,0:T(8,128)(2,1)S(1)}, bf16[144,1024]{1,0:T(8,128)(2,1)S(1)}, u32[]{:S(2)}, u32[]{:S(2)}) collective-permute-start(bf16[144,1024]{1,0:T(8,128)(2,1)S(1)} %collective-permute-done.8.refs_1_), channel_id=1, source_target_pairs={{2,0},{4,2},{6,4},{7,6},{5,7},{3,5},{1,3},{0,1},{10,8},{12,10},{14... | collective-permute-start | bytes 884744 | tf_op jit(solution)/shard_map/ppermute | solution.py:430
  39.2 4.3 %attend_batch.4 = (f32[144,1024]{1,0:T(8,128)S(1)}, f32[144,1024]{1,0:T(8,128)S(1)}, f32[144,1024]{1,0:T(8,128)S(1)}) custom-call(s32[4]{0:T(128)S(1)} %pad_add_fusion.here_ref, s32[8,8]{1,0:T(8,128)S(1)} %copy-done.5, s32[1,1,8]{2,1,0:T(1,128)S(1)} %copy-done.4, s32[1,1]{1,0:T(1,128)S(6)} %copy.57.count_ref, ...), custom_call_target="tpu_custom_call" | custom-call | flops 7040000000 | tf_op jit(solution)/shard_map/attend_batch/pallas_call | solution.py:314
  43.5 1.9 %collective-permute-done.11.refs_1_ = bf16[144,1024]{1,0:T(8,128)(2,1)S(1)} collective-permute-done((bf16[144,1024]{1,0:T(8,128)(2,1)S(1)}, bf16[144,1024]{1,0:T(8,128)(2,1)S(1)}, u32[]{:S(2)}, u32[]{:S(2)}) %collective-permute-start.11) | collective-permute-done | bytes 294944 | tf_op jit(solution)/shard_map/ppermute | solution.py:430
  45.4 1.4 %collective-permute-start.13 = (bf16[80,1024]{1,0:T(8,128)(2,1)S(1)}, bf16[80,1024]{1,0:T(8,128)(2,1)S(1)}, u32[]{:S(2)}, u32[]{:S(2)}) collective-permute-start(bf16[80,1024]{1,0:T(8,128)(2,1)S(1)} %slice.65), channel_id=1, source_target_pairs={{2,0},{4,2},{6,4},{7,6},{5,7},{3,5},{1,3},{0,1},{10,8},{12,10},{14... | collective-permute-start | bytes 491528 | tf_op jit(solution)/shard_map/ppermute | solution.py:435
  46.8 0.9 %collective-permute-start.12 = (bf16[64,1024]{1,0:T(8,128)(2,1)S(1)}, bf16[64,1024]{1,0:T(8,128)(2,1)S(1)}, u32[]{:S(2)}, u32[]{:S(2)}) collective-permute-start(bf16[64,1024]{1,0:T(8,128)(2,1)S(1)} %slice.64), channel_id=1, source_target_pairs={{0,2},{2,4},{4,6},{6,7},{7,5},{5,3},{3,1},{1,0},{8,10},{10,12},{12... | collective-permute-start | bytes 393224 | tf_op jit(solution)/shard_map/ppermute | solution.py:434
  47.8 3.7 %attend_batch.5 = (f32[144,1024]{1,0:T(8,128)S(1)}, f32[144,1024]{1,0:T(8,128)S(1)}, f32[144,1024]{1,0:T(8,128)S(1)}) custom-call(s32[4]{0:T(128)S(1)} %pad_add_fusion.here_ref, s32[8,8]{1,0:T(8,128)S(1)} %copy-done.5, s32[1,1,8]{2,1,0:T(1,128)S(1)} %copy-done.4, s32[1,1]{1,0:T(1,128)S(6)} %copy.57.count_ref, ...), custom_call_target="tpu_custom_call" | custom-call | flops 5059999744 | tf_op jit(solution)/shard_map/attend_batch/pallas_call | solution.py:314
  51.4 0.6 collective-permute-done.12.refs_0_
  52.1 3.1 %attend_last.1 = (f32[144,1024]{1,0:T(8,128)S(1)}, f32[8,144,128]{2,1,0:T(8,128)S(1)}, bf16[4,9,1024]{2,1,0:T(8,128)(2,1)S(1)}, bf16[4,9,1024]{2,1,0:T(8,128)(2,...) custom-call(s32[4]{0:T(128)S(1)} %pad_add_fusion.here_ref, s32[8,8]{1,0:T(8,128)S(1)} %copy-done.5, ...), custom_call_target="tpu_custom_call" | custom-call | flops 5500000256 | tf_op jit(solution)/shard_map/attend_last/pallas_call | solution.py:314
  55.2 0.1 collective-permute-start.14
  55.3 1.7 %collective-permute-start.15 = (bf16[4,9,1024]{2,1,0:T(8,128)(2,1)S(1)}, bf16[4,9,1024]{2,1,0:T(8,128)(2,1)S(1)}, u32[]{:S(2)}, u32[]{:S(2)}) collective-permute-start(bf16[4,9,1024]{2,1,0:T(8,128)(2,1)S(1)} %get-tuple-element.53), channel_id=1, source_target_pairs={{0,24},{8,0},{16,8},{24,16},{1,25},{9,1},{17,9},{25,17},{2,26},{10... | collective-permute-start | bytes 221192 | tf_op jit(solution)/shard_map/ppermute | solution.py:39
  57.0 3.4 %collective-permute-done.14.north_ref = bf16[4,9,1024]{2,1,0:T(8,128)(2,1)S(1)} collective-permute-done((bf16[4,9,1024]{2,1,0:T(8,128)(2,1)S(1)}, bf16[4,9,1024]{2,1,0:T(8,128)(2,1)S(1)}, u32[]{:S(2)}, u32[]{:S(2)}) %collective-permute-start.14) | collective-permute-done | bytes 73760 | tf_op jit(solution)/shard_map/ppermute | solution.py:39
  60.5 0.1 broadcast_select_fusion
  60.6 1.0 %collective-permute-start.16 = (bf16[4,6,1024]{2,1,0:T(8,128)(2,1)S(1)}, bf16[4,6,1024]{2,1,0:T(8,128)(2,1)S(1)}, u32[]{:S(2)}, u32[]{:S(2)}) collective-permute-start(bf16[4,6,1024]{2,1,0:T(8,128)(2,1)S(1)} %get-tuple-element.61), channel_id=1, source_target_pairs={{1,2},{2,1},{3,4},{4,3},{5,6},{6,5},{7,0},{0,7},{9,10},{10,9},{11,... | collective-permute-start | bytes 147464 | tf_op jit(solution)/shard_map/ppermute | solution.py:340
  61.6 1.2 %collective-permute-start.17 = (bf16[4,6,1024]{2,1,0:T(8,128)(2,1)S(1)}, bf16[4,6,1024]{2,1,0:T(8,128)(2,1)S(1)}, u32[]{:S(2)}, u32[]{:S(2)}) collective-permute-start(bf16[4,6,1024]{2,1,0:T(8,128)(2,1)S(1)} %get-tuple-element.60), channel_id=1, source_target_pairs={{0,1},{1,0},{2,3},{3,2},{4,5},{5,4},{6,7},{7,6},{8,9},{9,8},{10,11... | collective-permute-start | bytes 147464 | tf_op jit(solution)/shard_map/ppermute | solution.py:341
  62.8 1.7 %conv_part.3 = (f32[8,144,128]{2,1,0:T(8,128)S(1)}, f32[8,9,128]{2,1,0:T(8,128)S(1)}, bf16[4,9,4,1024]{3,2,1,0:T(4,128)(2,1)}) custom-call(f32[8,144,128]{2,1,0:T(8,128)S(1)} %get-tuple-element.47.field_ref, f32[9,1024]{1,0:T(8,128)S(1)} %copy-done.3, f32[144,1024]{1,0:T(8,128)S(1)} %get-tuple-element.48.dense_ref), custom_call_target="tpu_custom_call" | custom-call | flops 2200000000 | tf_op jit(solution)/shard_map/conv_part/pallas_call | solution.py:314
  64.4 3.4 %collective-permute-done.16.across_ref = bf16[4,6,1024]{2,1,0:T(8,128)(2,1)S(1)} collective-permute-done((bf16[4,6,1024]{2,1,0:T(8,128)(2,1)S(1)}, bf16[4,6,1024]{2,1,0:T(8,128)(2,1)S(1)}, u32[]{:S(2)}, u32[]{:S(2)}) %collective-permute-start.16) | collective-permute-done | bytes 49184 | tf_op jit(solution)/shard_map/ppermute | solution.py:340
  67.8 1.7 %conv_second.1 = bf16[4,9,4,1024]{3,2,1,0:T(4,128)(2,1)} custom-call(s32[4]{0:T(128)S(1)} %pad_add_fusion.here_ref, f32[8,144,128]{2,1,0:T(8,128)S(1)} %get-tuple-element.50.part_ref, f32[8,9,128]{2,1,0:T(8,128)S(1)} %get-tuple-element.51.taps_ref, bf16[4,9,1024]{2,1,0:T(8,128)(2,1)S(1)} %collective-permute-done.14.north_ref, ...), custom_call_target="tpu_custom_call" | custom-call | flops 2200000000 | tf_op jit(solution)/shard_map/conv_second/pallas_call | solution.py:314
  (24 shorter events, 0.2 us)
Async XLA Ops:
  1.7 5.1 %collective-permute-start = (bf16[4,9,1024]{2,1,0:T(8,128)(2,1)S(1)}, bf16[4,9,1024]{2,1,0:T(8,128)(2,1)S(1)}, u32[]{:S(2)}, u32[]{:S(2)}) collective-permute-start(bf16[4,9,1024]{2,1,0:T(8,128)(2,1)S(1)} %get-tuple-element.59), channel_id=1, source_target_pairs={{0,8},{8,16},{16,24},{24,0},{1,9},{9,17},{17,25},{25,1},{2,10},{10... | collective-permute-start | bytes 221192 | tf_op jit(solution)/shard_map/ppermute | solution.py:39
  2.2 5.8 %collective-permute-start.1 = (bf16[4,9,1024]{2,1,0:T(8,128)(2,1)S(1)}, bf16[4,9,1024]{2,1,0:T(8,128)(2,1)S(1)}, u32[]{:S(2)}, u32[]{:S(2)}) collective-permute-start(bf16[4,9,1024]{2,1,0:T(8,128)(2,1)S(1)} %get-tuple-element.58), channel_id=1, source_target_pairs={{0,24},{8,0},{16,8},{24,16},{1,25},{9,1},{17,9},{25,17},{2,26},{10... | collective-permute-start | bytes 221192 | tf_op jit(solution)/shard_map/ppermute | solution.py:39
  8.2 9.2 %collective-permute-start.2 = (bf16[4,6,1024]{2,1,0:T(8,128)(2,1)S(1)}, bf16[4,6,1024]{2,1,0:T(8,128)(2,1)S(1)}, u32[]{:S(2)}, u32[]{:S(2)}) collective-permute-start(bf16[4,6,1024]{2,1,0:T(8,128)(2,1)S(1)} %get-tuple-element.67), channel_id=1, source_target_pairs={{1,2},{2,1},{3,4},{4,3},{5,6},{6,5},{7,0},{0,7},{9,10},{10,9},{11,... | collective-permute-start | bytes 147464 | tf_op jit(solution)/shard_map/ppermute | solution.py:340
  12.8 4.9 %collective-permute-start.3 = (bf16[4,6,1024]{2,1,0:T(8,128)(2,1)S(1)}, bf16[4,6,1024]{2,1,0:T(8,128)(2,1)S(1)}, u32[]{:S(2)}, u32[]{:S(2)}) collective-permute-start(bf16[4,6,1024]{2,1,0:T(8,128)(2,1)S(1)} %get-tuple-element.66), channel_id=1, source_target_pairs={{0,1},{1,0},{2,3},{3,2},{4,5},{5,4},{6,7},{7,6},{8,9},{9,8},{10,11... | collective-permute-start | bytes 147464 | tf_op jit(solution)/shard_map/ppermute | solution.py:341
  12.8 2.8 %copy-start = (bf16[1024,3072]{1,0:T(8,128)(2,1)S(1)}, bf16[1024,3072]{1,0:T(8,128)(2,1)}, u32[]{:S(2)}) copy-start(bf16[1024,3072]{1,0:T(8,128)(2,1)} %far_ref.1) | copy-start | bytes 18874372
  15.6 0.8 %copy-start.2 = (f32[9,1024]{1,0:T(8,128)S(1)}, f32[9,1024]{1,0:T(8,128)}, u32[]{:S(2)}) copy-start(f32[9,1024]{1,0:T(8,128)} %weights_ref.2) | copy-start | bytes 110596
  18.9 11.6 %copy-start.4 = (s32[1,1,8]{2,1,0:T(1,128)S(1)}, s32[1,1,8]{2,1,0:T(1,128)}, u32[]{:S(2)}) copy-start(s32[1,1,8]{2,1,0:T(1,128)} %list_ref.7) | copy-start | bytes 100
  18.9 11.6 %copy-start.5 = (s32[8,8]{1,0:T(8,128)S(1)}, s32[8,8]{1,0:T(8,128)}, u32[]{:S(2)}) copy-start(s32[8,8]{1,0:T(8,128)} %constant.28.clone.sources_ref) | copy-start | bytes 772
  18.9 9.5 %collective-permute-start.4 = (bf16[144,1024]{1,0:T(8,128)(2,1)S(1)}, bf16[144,1024]{1,0:T(8,128)(2,1)S(1)}, u32[]{:S(2)}, u32[]{:S(2)}) collective-permute-start(bf16[144,1024]{1,0:T(8,128)(2,1)S(1)} %get-tuple-element.31.x_ref), channel_id=1, source_target_pairs={{0,2},{2,4},{4,6},{6,7},{7,5},{5,3},{3,1},{1,0},{8,10},{10,12},{12... | collective-permute-start | bytes 884744 | tf_op jit(solution)/shard_map/ppermute | solution.py:429
  19.0 9.8 %collective-permute-start.5 = (bf16[144,1024]{1,0:T(8,128)(2,1)S(1)}, bf16[144,1024]{1,0:T(8,128)(2,1)S(1)}, u32[]{:S(2)}, u32[]{:S(2)}) collective-permute-start(bf16[144,1024]{1,0:T(8,128)(2,1)S(1)} %get-tuple-element.31.x_ref), channel_id=1, source_target_pairs={{2,0},{4,2},{6,4},{7,6},{5,7},{3,5},{1,3},{0,1},{10,8},{12,10},{14... | collective-permute-start | bytes 884744 | tf_op jit(solution)/shard_map/ppermute | solution.py:430
  23.1 7.4 %collective-permute-start.6 = (bf16[144,1024]{1,0:T(8,128)(2,1)S(1)}, bf16[144,1024]{1,0:T(8,128)(2,1)S(1)}, u32[]{:S(2)}, u32[]{:S(2)}) collective-permute-start(bf16[144,1024]{1,0:T(8,128)(2,1)S(1)} %get-tuple-element.36), channel_id=1, source_target_pairs={{0,8},{8,16},{16,24},{24,0},{1,9},{9,17},{17,25},{25,1},{2,10},{10... | collective-permute-start | bytes 884744 | tf_op jit(solution)/shard_map/ppermute | solution.py:39
  23.8 15.4 %collective-permute-start.9 = (bf16[144,1024]{1,0:T(8,128)(2,1)S(1)}, bf16[144,1024]{1,0:T(8,128)(2,1)S(1)}, u32[]{:S(2)}, u32[]{:S(2)}) collective-permute-start(bf16[144,1024]{1,0:T(8,128)(2,1)S(1)} %get-tuple-element.36), channel_id=1, source_target_pairs={{0,24},{8,0},{16,8},{24,16},{1,25},{9,1},{17,9},{25,17},{2,26},{10... | collective-permute-start | bytes 884744 | tf_op jit(solution)/shard_map/ppermute | solution.py:39
  28.4 8.7 %collective-permute-start.7 = (bf16[144,1024]{1,0:T(8,128)(2,1)S(1)}, bf16[144,1024]{1,0:T(8,128)(2,1)S(1)}, u32[]{:S(2)}, u32[]{:S(2)}) collective-permute-start(bf16[144,1024]{1,0:T(8,128)(2,1)S(1)} %collective-permute-done.4.refs_0_), channel_id=1, source_target_pairs={{0,2},{2,4},{4,6},{6,7},{7,5},{5,3},{3,1},{1,0},{8,10},{10,12},{12... | collective-permute-start | bytes 884744 | tf_op jit(solution)/shard_map/ppermute | solution.py:429
  28.7 8.9 %collective-permute-start.8 = (bf16[144,1024]{1,0:T(8,128)(2,1)S(1)}, bf16[144,1024]{1,0:T(8,128)(2,1)S(1)}, u32[]{:S(2)}, u32[]{:S(2)}) collective-permute-start(bf16[144,1024]{1,0:T(8,128)(2,1)S(1)} %collective-permute-done.5.refs_1_), channel_id=1, source_target_pairs={{2,0},{4,2},{6,4},{7,6},{5,7},{3,5},{1,3},{0,1},{10,8},{12,10},{14... | collective-permute-start | bytes 884744 | tf_op jit(solution)/shard_map/ppermute | solution.py:430
  37.2 9.7 %collective-permute-start.10 = (bf16[144,1024]{1,0:T(8,128)(2,1)S(1)}, bf16[144,1024]{1,0:T(8,128)(2,1)S(1)}, u32[]{:S(2)}, u32[]{:S(2)}) collective-permute-start(bf16[144,1024]{1,0:T(8,128)(2,1)S(1)} %collective-permute-done.7.refs_0_), channel_id=1, source_target_pairs={{0,2},{2,4},{4,6},{6,7},{7,5},{5,3},{3,1},{1,0},{8,10},{10,12},{12... | collective-permute-start | bytes 884744 | tf_op jit(solution)/shard_map/ppermute | solution.py:429
  37.6 7.8 %collective-permute-start.11 = (bf16[144,1024]{1,0:T(8,128)(2,1)S(1)}, bf16[144,1024]{1,0:T(8,128)(2,1)S(1)}, u32[]{:S(2)}, u32[]{:S(2)}) collective-permute-start(bf16[144,1024]{1,0:T(8,128)(2,1)S(1)} %collective-permute-done.8.refs_1_), channel_id=1, source_target_pairs={{2,0},{4,2},{6,4},{7,6},{5,7},{3,5},{1,3},{0,1},{10,8},{12,10},{14... | collective-permute-start | bytes 884744 | tf_op jit(solution)/shard_map/ppermute | solution.py:430
  45.4 6.6 %collective-permute-start.13 = (bf16[80,1024]{1,0:T(8,128)(2,1)S(1)}, bf16[80,1024]{1,0:T(8,128)(2,1)S(1)}, u32[]{:S(2)}, u32[]{:S(2)}) collective-permute-start(bf16[80,1024]{1,0:T(8,128)(2,1)S(1)} %slice.65), channel_id=1, source_target_pairs={{2,0},{4,2},{6,4},{7,6},{5,7},{3,5},{1,3},{0,1},{10,8},{12,10},{14... | collective-permute-start | bytes 491528 | tf_op jit(solution)/shard_map/ppermute | solution.py:435
  46.8 5.2 %collective-permute-start.12 = (bf16[64,1024]{1,0:T(8,128)(2,1)S(1)}, bf16[64,1024]{1,0:T(8,128)(2,1)S(1)}, u32[]{:S(2)}, u32[]{:S(2)}) collective-permute-start(bf16[64,1024]{1,0:T(8,128)(2,1)S(1)} %slice.64), channel_id=1, source_target_pairs={{0,2},{2,4},{4,6},{6,7},{7,5},{5,3},{3,1},{1,0},{8,10},{10,12},{12... | collective-permute-start | bytes 393224 | tf_op jit(solution)/shard_map/ppermute | solution.py:434
  47.8 4.3 %copy-start.1 = (bf16[1024,1024]{1,0:T(8,128)(2,1)S(1)}, bf16[1024,1024]{1,0:T(8,128)(2,1)}, u32[]{:S(2)}) copy-start(bf16[1024,1024]{1,0:T(8,128)(2,1)} %wo_ref.1) | copy-start | bytes 6291460
  52.1 10.7 %copy-start.3 = (f32[9,1024]{1,0:T(8,128)S(1)}, f32[9,1024]{1,0:T(8,128)}, u32[]{:S(2)}) copy-start(f32[9,1024]{1,0:T(8,128)} %weights_ref.3) | copy-start | bytes 110596
  55.2 5.2 %collective-permute-start.14 = (bf16[4,9,1024]{2,1,0:T(8,128)(2,1)S(1)}, bf16[4,9,1024]{2,1,0:T(8,128)(2,1)S(1)}, u32[]{:S(2)}, u32[]{:S(2)}) collective-permute-start(bf16[4,9,1024]{2,1,0:T(8,128)(2,1)S(1)} %get-tuple-element.52), channel_id=1, source_target_pairs={{0,8},{8,16},{16,24},{24,0},{1,9},{9,17},{17,25},{25,1},{2,10},{10... | collective-permute-start | bytes 221192 | tf_op jit(solution)/shard_map/ppermute | solution.py:39
  55.3 5.1 %collective-permute-start.15 = (bf16[4,9,1024]{2,1,0:T(8,128)(2,1)S(1)}, bf16[4,9,1024]{2,1,0:T(8,128)(2,1)S(1)}, u32[]{:S(2)}, u32[]{:S(2)}) collective-permute-start(bf16[4,9,1024]{2,1,0:T(8,128)(2,1)S(1)} %get-tuple-element.53), channel_id=1, source_target_pairs={{0,24},{8,0},{16,8},{24,16},{1,25},{9,1},{17,9},{25,17},{2,26},{10... | collective-permute-start | bytes 221192 | tf_op jit(solution)/shard_map/ppermute | solution.py:39
  60.6 7.2 %collective-permute-start.16 = (bf16[4,6,1024]{2,1,0:T(8,128)(2,1)S(1)}, bf16[4,6,1024]{2,1,0:T(8,128)(2,1)S(1)}, u32[]{:S(2)}, u32[]{:S(2)}) collective-permute-start(bf16[4,6,1024]{2,1,0:T(8,128)(2,1)S(1)} %get-tuple-element.61), channel_id=1, source_target_pairs={{1,2},{2,1},{3,4},{4,3},{5,6},{6,5},{7,0},{0,7},{9,10},{10,9},{11,... | collective-permute-start | bytes 147464 | tf_op jit(solution)/shard_map/ppermute | solution.py:340
  61.6 6.2 %collective-permute-start.17 = (bf16[4,6,1024]{2,1,0:T(8,128)(2,1)S(1)}, bf16[4,6,1024]{2,1,0:T(8,128)(2,1)S(1)}, u32[]{:S(2)}, u32[]{:S(2)}) collective-permute-start(bf16[4,6,1024]{2,1,0:T(8,128)(2,1)S(1)} %get-tuple-element.60), channel_id=1, source_target_pairs={{0,1},{1,0},{2,3},{3,2},{4,5},{5,4},{6,7},{7,6},{8,9},{9,8},{10,11... | collective-permute-start | bytes 147464 | tf_op jit(solution)/shard_map/ppermute | solution.py:341

commit v5 on v4

--- a/solution.py
+++ b/solution.py
@@ -16,8 +16,8 @@
 GROUP = 256
 F32 = jnp.float32
 BF16 = jnp.bfloat16
-VMEM_LIMIT = 32 * 1024 * 1024
-ABOVE, BELOW = -1, -2
+VMEM_LIMIT = 16 * 1024 * 1024
+ABOVE, BELOW, OWN = -1, -2, -3
 
 
 def ring_order(count):
@@ -37,6 +37,14 @@
 def shift(x, axis, by):
     size = lax.axis_size(axis)
     return lax.ppermute(x, axis, [(i, (i + by) % size) for i in range(size)])
+
+
+def place(dims, level, column):
+    levels, columns, rows = dims
+    inner = columns - 2
+    if 0 < column <= inner:
+        return (level * inner + column - 1) * rows
+    return (levels * inner + level * 2 + (column > 0)) * rows
 
 
 def conv_part(load, dims, weights_ref, part_ref, taps_ref):
@@ -58,22 +66,23 @@
                 value = near[1] + sums[1]
                 value += jnp.where(above, pltpu.roll(sums[0], 1, 0), 0.0)
                 value += pltpu.roll(sums[2], SUBLANES - 1, 0)
-                at = (level * columns + column) * rows
+                at = place(dims, level, column)
                 part_ref[index, at : at + rows, :] = value[0:rows]
         return carry
 
     lax.fori_loop(0, part_ref.shape[0], tile, 0)
 
 
-def first_part_kernel(field_ref, weights_ref, after_ref, part_ref, taps_ref):
+def first_part_kernel(field_ref, weights_ref, part_ref, taps_ref):
     levels, columns, rows, _ = field_ref.shape
     load = lambda level, column, index, lanes: field_ref[level, column, :, lanes].astype(F32)
     conv_part(load, (levels, columns, rows), weights_ref, part_ref, taps_ref)
 
 
-def weights_kernel(after_ref, far_ref, near_ref, arrived):
+def weights_kernel(inner_ref, far_ref, passed_ref, near_ref, arrived):
     copy = pltpu.make_async_copy(far_ref, near_ref, arrived)
     copy.start()
+    passed_ref[...] = inner_ref[...]
     copy.wait()
 
 
@@ -81,69 +90,134 @@
     levels, columns, rows = dims
 
     def load(level, column, index, lanes):
-        at = (level * columns + column) * rows
+        at = place(dims, level, column)
         return field_ref[index, at : at + rows, :]
 
     conv_part(load, dims, weights_ref, part_ref, taps_ref)
     for level in range(levels):
         for column in range(columns):
-            at = (level * columns + column) * rows
+            at = place(dims, level, column)
             attended_ref[level, column] = dense_ref[at : at + rows, :].astype(BF16)
 
 
-def add_halo(index, dims, here_ref, north_ref, south_ref, across_ref, pair_ref, part_ref, taps_ref, full):
-    levels, columns, rows = dims
-    lanes = pl.ds(pl.multiple_of(index * LANES, LANES), LANES)
-    even = here_ref[2] > 0
-    full[index] = part_ref[index]
+def add_rows(index, dims, here_ref, north_ref, south_ref, taps_ref, full, inner_at, edge_at):
+    levels, columns, rows = dims
+    inner = columns - 2
+    lanes = slice(index * LANES, (index + 1) * LANES)
     blank = jnp.zeros((1, LANES), F32)
     for level in range(levels):
-        start = level * columns * rows
         for ref, flag, a, row in ((north_ref, 0, 0, 0), (south_ref, 1, 2, rows - 1)):
             line = ref[level, :, lanes].astype(F32)
-            left = jnp.concatenate([blank, line[:-1]], axis=0)
-            right = jnp.concatenate([line[1:], blank], axis=0)
+            if line.shape[0] == columns:
+                line = jnp.concatenate([blank, line, blank], axis=0)
+            left, line, right = (line[b : b + columns] for b in range(3))
             tap = [taps_ref[index, 3 * a + b : 3 * a + b + 1, :] for b in range(3)]
             more = tap[0] * left + tap[1] * line + tap[2] * right
             more = jnp.where(here_ref[flag] > 0, more, 0.0)
-            full[index, pl.ds(start + row, columns, stride=rows), :] += more
+            if inner_at is not None:
+                full[index, pl.ds(inner_at + level * inner * rows + row, inner, stride=rows), :] += more[1 : columns - 1]
+            if edge_at is not None:
+                ends = jnp.concatenate([more[:1], more[columns - 1 :]], axis=0)
+                full[index, pl.ds(edge_at + level * 2 * rows + row, 2, stride=rows), :] += ends
+
+
+def add_sides(index, dims, here_ref, across_ref, pair_ref, taps_ref, full, edge_at):
+    levels, columns, rows = dims
+    lanes = slice(index * LANES, (index + 1) * LANES)
+    even = here_ref[2] > 0
+    blank = jnp.zeros((1, LANES), F32)
+    for level in range(levels):
         pair = pair_ref[level, :, lanes].astype(F32)
         across = across_ref[level, :, lanes].astype(F32)
         west = jnp.where(even, across, pair)
         east = jnp.where(even, pair, across)
-        for side, b, column in ((west, 0, 0), (east, 2, columns - 1)):
+        for side, b, order in ((west, 0, 0), (east, 2, 1)):
+            if side.shape[0] == rows:
+                side = jnp.concatenate([blank, side, blank], axis=0)
             more = None
             for a in range(3):
                 term = taps_ref[index, 3 * a + b : 3 * a + b + 1, :] * side[a : a + rows]
                 more = term if more is None else more + term
-            full[index, start + column * rows : start + (column + 1) * rows, :] += more
-
-
-def first_kernel(dims, here_ref, part_ref, taps_ref, north_ref, south_ref, across_ref, pair_ref, stream_ref, normed_ref, full):
-    tiles, tokens, _ = part_ref.shape
+            at = edge_at + (level * 2 + order) * rows
+            full[index, at : at + rows, :] += more
+
+
+def normalise(full, stream_ref, put):
+    tiles, tokens, _ = full.shape
     squares = jnp.zeros((tokens, LANES), F32)
     for index in range(tiles):
-        lanes = slice(index * LANES, (index + 1) * LANES)
-        add_halo(index, dims, here_ref, north_ref, south_ref, across_ref, pair_ref, part_ref, taps_ref, full)
         stream = full[index].astype(BF16)
-        stream_ref[:, lanes] = stream
+        stream_ref[:, index * LANES : (index + 1) * LANES] = stream
         wide = stream.astype(F32)
         squares += wide * wide
     mean = jnp.sum(squares, axis=-1, keepdims=True) * (1.0 / (tiles * LANES))
     scale = jnp.broadcast_to(lax.rsqrt(mean + EPSILON), (tokens, LANES))
     for index in range(tiles):
         lanes = slice(index * LANES, (index + 1) * LANES)
-        normed_ref[:, lanes] = (stream_ref[:, lanes].astype(F32) * scale).astype(BF16)
+        put(lanes, (stream_ref[:, lanes].astype(F32) * scale).astype(BF16))
+
+
+def inner_kernel(
+    dims, here_ref, part_ref, taps_ref, north_ref, south_ref, west_ref, east_ref,
+    stream_ref, normed_ref, across_ref, pair_ref, full,
+):
+    levels, columns, rows = dims
+    tiles, tokens, _ = full.shape
+    for index in range(tiles):
+        full[index] = part_ref[index, 0:tokens, :]
+        add_rows(index, dims, here_ref, north_ref, south_ref, taps_ref, full, 0, None)
+
+    def put(lanes, value):
+        normed_ref[:, lanes] = value
+
+    normalise(full, stream_ref, put)
+    has_north = (here_ref[0] > 0).astype(F32)
+    has_south = (here_ref[1] > 0).astype(F32)
+    even = here_ref[2] > 0
+    for level in range(levels):
+        north = north_ref[level].astype(F32) * has_north
+        south = south_ref[level].astype(F32) * has_south
+        tall = []
+        for edge_ref, at in ((west_ref, 0), (east_ref, columns - 1)):
+            middle = edge_ref[level].astype(F32)
+            tall.append(jnp.concatenate([north[at : at + 1], middle, south[at : at + 1]], axis=0))
+        across_ref[level] = jnp.where(even, tall[0], tall[1]).astype(BF16)
+        pair_ref[level] = jnp.where(even, tall[1], tall[0]).astype(BF16)
+
+
+def edge_kernel(
+    dims, here_ref, part_ref, taps_ref, north_ref, south_ref, across_ref, pair_ref, inner_ref, ahead_ref, behind_ref,
+    stream_ref, edge_ref, normed_ref, ahead_joined, behind_joined, full,
+):
+    tiles, tokens, _ = full.shape
+    start = part_ref.shape[1] - tokens
+    normed_ref[0:start, :] = inner_ref[...]
+    ahead_joined[0:start, :] = ahead_ref[...]
+    behind_joined[0:start, :] = behind_ref[...]
+    for index in range(tiles):
+        full[index] = part_ref[index, start : start + tokens, :]
+        add_rows(index, dims, here_ref, north_ref, south_ref, taps_ref, full, None, 0)
+        add_sides(index, dims, here_ref, across_ref, pair_ref, taps_ref, full, 0)
+
+    def put(lanes, value):
+        edge_ref[:, lanes] = value
+        for ref in (normed_ref, ahead_joined, behind_joined):
+            ref[start : start + tokens, lanes] = value
+
+    normalise(full, stream_ref, put)
 
 
 def second_kernel(dims, here_ref, part_ref, taps_ref, north_ref, south_ref, across_ref, pair_ref, mixed_ref, full):
     levels, columns, rows = dims
+    edge_at = levels * (columns - 2) * rows
     for index in range(part_ref.shape[0]):
         lanes = slice(index * LANES, (index + 1) * LANES)
-        add_halo(index, dims, here_ref, north_ref, south_ref, across_ref, pair_ref, part_ref, taps_ref, full)
+        full[index] = part_ref[index]
+        add_rows(index, dims, here_ref, north_ref, south_ref, taps_ref, full, 0, edge_at)
+        add_sides(index, dims, here_ref, across_ref, pair_ref, taps_ref, full, edge_at)
         for level in range(levels):
             for column in range(columns):
-                at = (level * columns + column) * rows
+                at = place(dims, level, column)
                 mixed_ref[level, column, :, lanes] = full[index, at : at + rows, :].astype(BF16)
 
 
@@ -206,6 +280,9 @@
     count = count_ref[0, 0]
     start = 0
     for slot, size in zip(slots, sizes):
+        if slot == OWN:
+            start += size
+            continue
         if slot == ABOVE:
             linked = here_ref[0]
         elif slot == BELOW:
@@ -226,10 +303,14 @@
     return blocks[0][...] if len(blocks) == 1 else jnp.concatenate([b[...] for b in blocks], axis=0)
 
 
-def own_kernel(factor, x_ref, w_ref, handed_ref, query_ref, high_ref, sum_ref, acc_ref):
+def own_kernel(
+    factor, slots, sizes, here_ref, sources_ref, list_ref, count_ref, x_ref, ahead_ref, behind_ref, w_ref,
+    handed_ref, query_ref, high_ref, sum_ref, acc_ref,
+):
     tokens, width = x_ref.shape
     x = x_ref[...]
-    handed_ref[...] = x
+    handed_ref[...] = x_ref[tokens - handed_ref.shape[0] :, :]
+    bias = key_bias(here_ref, sources_ref, list_ref, count_ref, slots, sizes)
     low = lax.broadcasted_iota(jnp.int32, (tokens, LANES), 1) < LANES // 2
     zero = jnp.zeros((tokens, LANES), BF16)
     inside = GROUP // LANES
@@ -249,7 +330,7 @@
         lanes = slice(pair * LANES, (pair + 1) * LANES)
         high_ref[:, lanes], sum_ref[:, lanes], acc_ref[:, lanes] = part
 
-    attend_pairs(factor, x, w_ref, None, query_of, finish)
+    attend_pairs(factor, joined([x_ref, ahead_ref, behind_ref]), w_ref, bias, query_of, finish)
 
 
 def combine(state, part, factor):
@@ -260,9 +341,10 @@
 
 
 def batch_kernel(
-    factor, slots, sizes, here_ref, sources_ref, list_ref, count_ref, query_ref, w_ref, high_in, sum_in, acc_in, *refs
+    factor, slots, sizes, here_ref, sources_ref, list_ref, count_ref, query_ref, w_ref, high_in, sum_in, acc_in, edge_ref, *refs
 ):
-    blocks, (high_ref, sum_ref, acc_ref) = refs[:-3], refs[-3:]
+    blocks, (high_ref, sum_ref, acc_ref, handed_ref) = refs[:-4], refs[-4:]
+    handed_ref[...] = edge_ref[...]
     bias = key_bias(here_ref, sources_ref, list_ref, count_ref, slots, sizes)
 
     def finish(pair, part):
@@ -275,15 +357,16 @@
 
 def last_kernel(
     factor, dims, slots, sizes, here_ref, sources_ref, list_ref, count_ref, query_ref, w_ref, high_in, sum_in, acc_in,
-    wo_ref, stream_ref, *refs
+    wo_ref, inner_ref, edge_ref, *refs
 ):
-    blocks = refs[: len(sizes)]
-    dense, after_ref, north_ref, south_ref, west_ref, east_ref, total = refs[len(sizes) :]
+    blocks, (dense, after_ref, north_ref, south_ref, west_ref, east_ref, total) = refs[:-7], refs[-7:]
     levels, columns, rows = dims
     x = joined(blocks)
     width = x.shape[1]
     bias = key_bias(here_ref, sources_ref, list_ref, count_ref, slots, sizes)
-    total[...] = stream_ref[...].astype(F32)
+    edge_at = inner_ref.shape[0]
+    total[0:edge_at, :] = inner_ref[...].astype(F32)
+    total[edge_at:, :] = edge_ref[...].astype(F32)
 
     def finish(pair, part):
         lanes = slice(pair * LANES, (pair + 1) * LANES)
@@ -298,47 +381,53 @@
         lanes = slice(index * LANES, (index + 1) * LANES)
         after_ref[index] = total[:, lanes].astype(BF16).astype(F32)
         for level in range(levels):
-            start = level * columns * rows
-            stop = start + columns * rows
-            north_ref[level, :, lanes] = after_ref[index, pl.ds(start, columns, stride=rows), :].astype(BF16)
-            south_ref[level, :, lanes] = after_ref[index, pl.ds(start + rows - 1, columns, stride=rows), :].astype(BF16)
-            west_ref[level, :, lanes] = after_ref[index, start : start + rows, :].astype(BF16)
-            east_ref[level, :, lanes] = after_ref[index, stop - rows : stop, :].astype(BF16)
+            west_at = edge_at + level * 2 * rows
+            east_at = west_at + rows
+            for out_ref, row in ((north_ref, 0), (south_ref, rows - 1)):
+                inner = after_ref[index, pl.ds(level * (columns - 2) * rows + row, columns - 2, stride=rows), :]
+                west = after_ref[index, west_at + row : west_at + row + 1, :]
+                east = after_ref[index, east_at + row : east_at + row + 1, :]
+                out_ref[level, :, lanes] = jnp.concatenate([west, inner, east], axis=0).astype(BF16)
+            west_ref[level, :, lanes] = after_ref[index, west_at : west_at + rows, :].astype(BF16)
+            east_ref[level, :, lanes] = after_ref[index, east_at : east_at + rows, :].astype(BF16)
 
 
 def shape(dims, kind):
     return jax.ShapeDtypeStruct(dims, kind)
 
 
-def call(kernel, out_shape, scalars, arrays, scratch, name, microseconds):
+def call(kernel, out_shape, scalars, arrays, scratch, name, microseconds, outside=()):
     return pl.pallas_call(
         kernel,
         out_shape=out_shape,
-        in_specs=[pl.BlockSpec(memory_space=pltpu.SMEM)] * len(scalars) + [pl.BlockSpec(memory_space=pltpu.VMEM)] * len(arrays),
+        in_specs=[pl.BlockSpec(memory_space=pltpu.SMEM)] * len(scalars) + [pl.BlockSpec(memory_space=pltpu.VMEM)] * len(arrays)
+        + [pl.BlockSpec(memory_space=pl.ANY)] * len(outside),
         out_specs=jax.tree.map(lambda _: pl.BlockSpec(memory_space=pltpu.VMEM), out_shape),
         scratch_shapes=scratch,
         compiler_params=pltpu.CompilerParams(vmem_limit_bytes=VMEM_LIMIT),
         cost_estimate=pl.CostEstimate(flops=int(microseconds * 1.1e9), bytes_accessed=0, transcendentals=0),
         name=name,
-    )(*scalars, *arrays)
+    )(*scalars, *arrays, *outside)
+
+
+def swap(value, first):
+    count = lax.axis_size("lon")
+    pairs = [p for i in range(first, count, 2) for p in ((i, (i + 1) % count), ((i + 1) % count, i))]
+    return lax.ppermute(value, "lon", pairs)
 
 
 def exchange(north_edge, south_edge, west_edge, east_edge, here):
-    columns = north_edge.shape[1]
-    count = lax.axis_size("lon")
-    north = shift(south_edge, "lat", 1)
-    south = shift(north_edge, "lat", -1)
-
-    def column(edge, at):
-        top = jnp.where(here[0] > 0, north[:, at : at + 1], 0)
-        bottom = jnp.where(here[1] > 0, south[:, at : at + 1], 0)
-        return jnp.concatenate([top, edge, bottom], axis=1)
-
-    west, east = column(west_edge, 0), column(east_edge, columns - 1)
+    rows = west_edge.shape[1]
     even = here[2] > 0
-    swap = lambda first: [p for i in range(first, count, 2) for p in ((i, (i + 1) % count), ((i + 1) % count, i))]
-    across = lax.ppermute(jnp.where(even, west, east), "lon", swap(1))
-    pair = lax.ppermute(jnp.where(even, east, west), "lon", swap(0))
+    across = swap(jnp.where(even, west_edge, east_edge), 1)
+    pair = swap(jnp.where(even, east_edge, west_edge), 0)
+    west, east = jnp.where(even, across, pair), jnp.where(even, pair, across)
+
+    def row(edge, at):
+        return jnp.concatenate([west[:, at : at + 1], edge, east[:, at : at + 1]], axis=1)
+
+    north = shift(row(south_edge, rows - 1), "lat", 1)
+    south = shift(row(north_edge, 0), "lat", -1)
     return north, south, across, pair
 
 
@@ -366,81 +455,110 @@
 
     dims = (levels, columns, rows)
     tiles = width // LANES
-    full = pltpu.VMEM((tiles, tokens, LANES), F32)
+    edge_tokens = levels * 2 * rows
+    inner_tokens = tokens - edge_tokens
+    full = lambda count: pltpu.VMEM((tiles, count, LANES), F32)
+    flat = lambda count: shape((count, width), BF16)
     part_shape = (shape((tiles, tokens, LANES), F32), shape((tiles, 9, LANES), F32))
-    halo = exchange(fields[:, :, 0], fields[:, :, rows - 1], fields[:, 0], fields[:, columns - 1], here)
+    tall = shape((levels, rows + 2, width), BF16)
+    forward = [(order[i], order[(i + 1) % lon_total]) for i in range(lon_total)]
+    backward = [(b, a) for a, b in forward]
+
+    north = shift(fields[:, :, rows - 1], "lat", 1)
+    south = shift(fields[:, :, 0], "lat", -1)
+    part = call(first_part_kernel, part_shape, (), (fields, conv_first), [], "conv_part", 1)
+    stream_inner, normed_inner, across, pair = call(
+        functools.partial(inner_kernel, dims),
+        (flat(inner_tokens), flat(inner_tokens), tall, tall),
+        (here,),
+        (*part, north, south, fields[:, 0], fields[:, columns - 1]),
+        [full(inner_tokens)],
+        "conv_inner",
+        1,
+    )
+    ahead = lax.ppermute(normed_inner, "lon", forward)
+    behind = lax.ppermute(normed_inner, "lon", backward)
+    across, pair = swap(across, 1), swap(pair, 0)
+    anywhere = pl.BlockSpec(memory_space=pl.ANY)
     vmem = pl.BlockSpec(memory_space=pltpu.VMEM)
-    anywhere = pl.BlockSpec(memory_space=pl.ANY)
-    part = pl.pallas_call(
-        first_part_kernel,
-        out_shape=part_shape,
-        in_specs=[vmem, vmem, anywhere],
-        out_specs=(vmem,) * 2,
-        compiler_params=pltpu.CompilerParams(vmem_limit_bytes=VMEM_LIMIT),
-        cost_estimate=pl.CostEstimate(flops=int(2e9), bytes_accessed=0, transcendentals=0),
-        name="conv_part",
-    )(fields, conv_first, halo[0])
-    w_qkv = pl.pallas_call(
+    normed_passed, w_qkv = pl.pallas_call(
         weights_kernel,
-        out_shape=shape(w_qkv.shape, BF16),
-        in_specs=[anywhere, anywhere],
-        out_specs=vmem,
+        out_shape=(flat(inner_tokens), shape(w_qkv.shape, BF16)),
+        in_specs=[vmem, anywhere],
+        out_specs=(vmem, vmem),
         scratch_shapes=[pltpu.SemaphoreType.DMA],
         compiler_params=pltpu.CompilerParams(vmem_limit_bytes=VMEM_LIMIT),
         cost_estimate=pl.CostEstimate(flops=int(2e9), bytes_accessed=0, transcendentals=0),
         name="weights_near",
-    )(halo[0], w_qkv)
-    flat = shape((tokens, width), BF16)
-    stream, normed = call(
-        functools.partial(first_kernel, dims), (flat, flat), (here,), (*part, *halo), [full], "conv_first", 2
+    )(normed_inner, w_qkv)
+    stream_edge, normed_edge, normed, *both = call(
+        functools.partial(edge_kernel, dims),
+        (flat(edge_tokens), flat(edge_tokens), flat(tokens), flat(tokens), flat(tokens)),
+        (here,),
+        (*part, north, south, across, pair, normed_inner, ahead, behind),
+        [full(edge_tokens)],
+        "conv_edge",
+        1,
     )
 
-    forward = [(order[i], order[(i + 1) % lon_total]) for i in range(lon_total)]
-    backward = [(b, a) for a, b in forward]
     state_shape = (shape((tokens, width), F32),) * 3
-    handed, query, *state = call(
-        functools.partial(own_kernel, factor),
-        (flat, shape((pairs, 2 * tokens, LANES), BF16), *state_shape),
-        (),
-        (normed, w_qkv),
+    edge_passed, query, *state = call(
+        functools.partial(own_kernel, factor, [OWN, 0, 1], [tokens, inner_tokens, inner_tokens]),
+        (flat(edge_tokens), shape((pairs, 2 * tokens, LANES), BF16), *state_shape),
+        links,
+        (normed, ahead, behind, w_qkv),
         [],
         "own_block",
         4,
     )
 
     def batch(state, waiting):
-        blocks, slots = zip(*waiting)
-        sizes = [b.shape[0] for b in blocks]
-        return call(
+        blocks = [block for block, _ in waiting]
+        slots, sizes = zip(*[piece for _, pieces in waiting for piece in pieces])
+        *state, handed = call(
             functools.partial(batch_kernel, factor, slots, sizes),
-            state_shape,
+            (*state_shape, flat(edge_tokens)),
             links,
-            (query, w_qkv, *state, *blocks),
+            (query, w_qkv, *state, normed_edge, *blocks),
             [],
             "attend_batch",
-            1 + 1.8 * len(blocks),
+            1 + 1.2 * len(blocks),
         )
-
-    ahead, behind = normed, normed
-    near = [(shift(handed, "lat", 1), ABOVE), (shift(handed, "lat", -1), BELOW)]
-    waiting = []
-    cut = (tokens // 32) * 16
-    for step in range(1, half):
+        return state, handed
+
+    sides = ((ABOVE, 1), (BELOW, -1))
+    near = {
+        2: [(shift(normed_passed, "lat", by), [(slot, inner_tokens)]) for slot, by in sides],
+        3: [(shift(edge_passed, "lat", by), [(slot, edge_tokens)]) for slot, by in sides],
+    }
+    ahead, behind = both
+    handed = None
+    for step in range(2, half):
         ahead = lax.ppermute(ahead, "lon", forward)
         behind = lax.ppermute(behind, "lon", backward)
-        if step > 1:
-            state = batch(state, waiting)
-        waiting = [(ahead, 2 * step - 2), (behind, 2 * step - 1), *near[step - 1 : step]]
-    far_first = lax.ppermute(ahead[:cut], "lon", forward)
+        if step > 2:
+            state, hand = batch(state, waiting)
+            handed = hand if handed is None else handed
+        waiting = [
+            *near.get(step, ()),
+            (ahead, [(2 * step - 2, inner_tokens), (2 * step - 4, edge_tokens)]),
+            (behind, [(2 * step - 1, inner_tokens), (2 * step - 3, edge_tokens)]),
+        ]
+    last = lon_total - 2
+    cut = (inner_tokens + 31) // 32 * 16
+    far_first = lax.ppermute(jnp.concatenate([ahead[:cut], ahead[inner_tokens:]]), "lon", forward)
     far_second = lax.ppermute(behind[cut:], "lon", backward)
-    state = batch(state, waiting)
+    state, _ = batch(state, waiting)
+    far_edge = lax.ppermute(handed, "lon", [(order[i], order[(i + half) % lon_total]) for i in range(lon_total)])
+    slots = [last, last - 2, last, last - 1, last]
+    sizes = [cut, edge_tokens, inner_tokens - cut, edge_tokens, edge_tokens]
 
     row_edge, column_edge = shape((levels, columns, width), BF16), shape((levels, rows, width), BF16)
     dense, after, *edges = call(
-        functools.partial(last_kernel, factor, dims, [lon_total - 2] * 2, [cut, tokens - cut]),
+        functools.partial(last_kernel, factor, dims, slots, sizes),
         (shape((tokens, width), F32), part_shape[0], row_edge, row_edge, column_edge, column_edge),
         links,
-        (query, w_qkv, *state, w_out, stream, far_first, far_second),
+        (query, w_qkv, *state, w_out, stream_inner, stream_edge, far_first, far_second, far_edge),
         [pltpu.VMEM((tokens, width), F32)],
         "attend_last",
         5,
@@ -456,7 +574,7 @@
         "conv_part",
         2,
     )
-    mixed = call(functools.partial(second_kernel, dims), grid4, (here,), (*part, *halo), [full], "conv_second", 2)
+    mixed = call(functools.partial(second_kernel, dims), grid4, (here,), (*part, *halo), [full(tokens)], "conv_second", 2)
     return attended.transpose(0, 2, 1, 3), mixed.transpose(0, 2, 1, 3)
 
 

time: 69.7 us -> 66.5 us (0.954)
  waiting for transfers between devices: 18.1 us -> 11.3 us
  starting transfers between devices: 21.4 us -> 24.3 us
    ppermute x3 -> x2, waiting for transfers between devices: 5.24 us -> 0.19 us  [local(): ahead = lax.ppermute(ahead, 'lon', forward)]
    ppermute x5 -> x8, starting transfers between devices: 7.74 us -> 11.7 us  [the longest x4 6.66 us: swap(): return lax.ppermute(value, 'lon', pairs)]
    ppermute x5 -> x8, waiting for transfers between devices: 4.33 us -> 6.45 us  [the longest x4 6.44 us: swap(): return lax.ppermute(value, 'lon', pairs)]
    ppermute x6 -> x8, waiting for transfers between devices: 6.62 us -> 4.64 us  [shift(): return lax.ppermute(x, axis, [(i, (i + by) % size) for i in range(size)])]
    ppermute x3 -> x2, waiting for transfers between devices: 1.87 us -> 0.01 us  [local(): behind = lax.ppermute(behind, 'lon', backward)]
    ppermute x3 -> x2, starting transfers between devices: 5.33 us -> 3.75 us  [local(): behind = lax.ppermute(behind, 'lon', backward)]
    pallas_call x8 -> x9, Pallas kernels: 21.9 us -> 23.2 us  [call(): pl.pallas_call(kernel, out_shape=out_shape, in_specs=[pl.BlockSpec(memory...]
    pallas_call x2 -> x1, Pallas kernels: 1.34 us -> 0.44 us  [local(): pl.pallas_call(weights_kernel, out_shape=(flat(inner_tokens), shape(w_qkv...]
  transfers between devices with their start and end apart: 18 -> 21, of which waited for: 9 -> 7; matrix products, arithmetic and copies ran while one was open for 1% -> 1% of each run, Pallas kernels for 25% -> 27%
where the time goes in v5:
time: 66.5 us; the launch traced here: 66.3 us
  starting transfers between devices  24.3 us (37%)
  Pallas kernels  23.7 us (36%)
  waiting for transfers between devices  11.3 us (17%)
  local copies, waits for them, and re-layouts  5.25 us (8%)
  between operations  1.57 us (2%)
    pallas_call x9, Pallas kernels, call(): pl.pallas_call(kernel, out_shape=out_shape, in_specs=[pl.BlockSpec(memory...  23.2 us
    ppermute x4, starting transfers between devices, swap(): return lax.ppermute(value, 'lon', pairs)  6.66 us
    ppermute x4, waiting for transfers between devices, swap(): return lax.ppermute(value, 'lon', pairs)  6.44 us
    ppermute x8, starting transfers between devices, shift(): return lax.ppermute(x, axis, [(i, (i + by) % size) for i in range(size)])  6.2 us
    unnamed x13, local copies, waits for them, and re-layouts  4.73 us
    ppermute x8, waiting for transfers between devices, shift(): return lax.ppermute(x, axis, [(i, (i + by) % size) for i in range(size)])  4.64 us
    ppermute x2, starting transfers between devices, local(): behind = lax.ppermute(behind, 'lon', backward)  3.75 us
    ppermute x1, starting transfers between devices, local(): lax.ppermute(handed, 'lon', [(order[i], order[(i + half) % lon_total]) fo...  2.94 us
  transfers between devices with their start and end apart: 21, of which 7 were waited for; matrix products, arithmetic and copies ran while one was open for 1% of the time, Pallas kernels for 27%

profile of v5, /device:TPU:0, one launch (start us, length us, event | category | flops | bytes accessed | tf_op | source)
XLA Modules:
  0.0 66.3 jit_solution(5032305625644830236)
XLA Ops:
  0.6 1.1 %copy.21 = bf16[4,4,9,1024]{3,2,0,1:T(8,128)(2,1)S(1)} copy(bf16[4,4,9,1024]{3,1,2,0:T(4,128)(2,1)} %param.8) | data formatting | bytes 589824 | tf_op args[0]
  1.7 0.5 collective-permute-start
  2.2 2.0 %collective-permute-start.1 = (bf16[4,9,1024]{2,1,0:T(8,128)(2,1)S(1)}, bf16[4,9,1024]{2,1,0:T(8,128)(2,1)S(1)}, u32[]{:S(2)}, u32[]{:S(2)}) collective-permute-start(bf16[4,9,1024]{2,1,0:T(8,128)(2,1)S(1)} %get-tuple-element.72), channel_id=1, source_target_pairs={{0,24},{8,0},{16,8},{24,16},{1,25},{9,1},{17,9},{25,17},{2,26},{10... | collective-permute-start | bytes 221192 | tf_op jit(solution)/shard_map/ppermute | solution.py:39
  4.2 0.1 fusion
  4.3 0.2 copy.15.field_ref
  4.6 0.1 copy_bitcast_fusion.1
  4.7 0.1 pad_add_fusion.here_ref
  4.8 0.8 %copy-done.2 = f32[9,1024]{1,0:T(8,128)S(1)} copy-done((f32[9,1024]{1,0:T(8,128)S(1)}, f32[9,1024]{1,0:T(8,128)}, u32[]{:S(2)}) %copy-start.2) | copy-done | bytes 36888
  5.6 0.9 %conv_part.2 = (f32[8,144,128]{2,1,0:T(8,128)S(1)}, f32[8,9,128]{2,1,0:T(8,128)S(1)}) custom-call(bf16[4,9,4,1024]{3,2,1,0:T(4,128)(2,1)S(1)} %copy.15.field_ref, f32[9,1024]{1,0:T(8,128)S(1)} %copy-done.2), custom_call_target="tpu_custom_call" | custom-call | flops 1100000000 | tf_op jit(solution)/shard_map/conv_part/pallas_call | solution.py:400
  6.5 0.3 collective-permute-done.north_ref
  6.8 1.2 %collective-permute-done.1.south_ref = bf16[4,9,1024]{2,1,0:T(8,128)(2,1)S(1)} collective-permute-done((bf16[4,9,1024]{2,1,0:T(8,128)(2,1)S(1)}, bf16[4,9,1024]{2,1,0:T(8,128)(2,1)S(1)}, u32[]{:S(2)}, u32[]{:S(2)}) %collective-permute-start.1) | collective-permute-done | bytes 73760 | tf_op jit(solution)/shard_map/ppermute | solution.py:39
  8.1 1.0 %conv_inner.1 = (bf16[112,1024]{1,0:T(8,128)(2,1)S(1)}, bf16[112,1024]{1,0:T(8,128)(2,1)S(1)}, bf16[4,6,1024]{2,1,0:T(8,128)(2,1)S(1)}, bf16[4,6,1024]{2,1,0:T(8,128)(2,1)S(1)}) custom-call(s32[4]{0:T(128)S(1)} %pad_add_fusion.here_ref, f32[8,144,128]{2,1,0:T(8,128)S(1)} %get-tuple-element.36.part_ref, f32[8,9,128]{2,1,0:T(8,128)S(1)} %get-tuple-element.37.taps_ref, ...), custom_call_target="tpu_custom_call" | custom-call | flops 1100000000 | tf_op jit(solution)/shard_map/conv_inner/pallas_call | solution.py:400
  9.1 0.0 copy-start.5
  9.1 1.6 %collective-permute-start.4 = (bf16[112,1024]{1,0:T(8,128)(2,1)S(1)}, bf16[112,1024]{1,0:T(8,128)(2,1)S(1)}, u32[]{:S(2)}, u32[]{:S(2)}) collective-permute-start(bf16[112,1024]{1,0:T(8,128)(2,1)S(1)} %get-tuple-element.40.inner_ref), channel_id=1, source_target_pairs={{0,2},{2,4},{4,6},{6,7},{7,5},{5,3},{3,1},{1,0},{8,10},{10,12},{12... | collective-permute-start | bytes 688136 | tf_op jit(solution)/shard_map/ppermute | solution.py:479
  10.7 0.4 collective-permute-start.5
  11.8 4.6 %collective-permute-start.2 = (bf16[4,6,1024]{2,1,0:T(8,128)(2,1)S(1)}, bf16[4,6,1024]{2,1,0:T(8,128)(2,1)S(1)}, u32[]{:S(2)}, u32[]{:S(2)}) collective-permute-start(bf16[4,6,1024]{2,1,0:T(8,128)(2,1)S(1)} %get-tuple-element.38), channel_id=1, source_target_pairs={{1,2},{2,1},{3,4},{4,3},{5,6},{6,5},{7,0},{0,7},{9,10},{10,9},{11,... | collective-permute-start | bytes 147464 | tf_op jit(solution)/shard_map/ppermute | solution.py:416
  16.4 2.8 %copy-done = bf16[1024,3072]{1,0:T(8,128)(2,1)S(1)} copy-done((bf16[1024,3072]{1,0:T(8,128)(2,1)S(1)}, bf16[1024,3072]{1,0:T(8,128)(2,1)}, u32[]{:S(2)}) %copy-start) | copy-done | bytes 6291480
  19.2 0.4 weights_near.1
  19.7 0.4 collective-permute-start.6
  20.1 1.8 %collective-permute-done.2.across_ref = bf16[4,6,1024]{2,1,0:T(8,128)(2,1)S(1)} collective-permute-done((bf16[4,6,1024]{2,1,0:T(8,128)(2,1)S(1)}, bf16[4,6,1024]{2,1,0:T(8,128)(2,1)S(1)}, u32[]{:S(2)}, u32[]{:S(2)}) %collective-permute-start.2) | collective-permute-done | bytes 49184 | tf_op jit(solution)/shard_map/ppermute | solution.py:416
  21.9 0.9 %collective-permute-start.7 = (bf16[112,1024]{1,0:T(8,128)(2,1)S(1)}, bf16[112,1024]{1,0:T(8,128)(2,1)S(1)}, u32[]{:S(2)}, u32[]{:S(2)}) collective-permute-start(bf16[112,1024]{1,0:T(8,128)(2,1)S(1)} %get-tuple-element.48), channel_id=1, source_target_pairs={{0,24},{8,0},{16,8},{24,16},{1,25},{9,1},{17,9},{25,17},{2,26},{10... | collective-permute-start | bytes 688136 | tf_op jit(solution)/shard_map/ppermute | solution.py:39
  22.8 1.1 %conv_edge.1 = (bf16[32,1024]{1,0:T(8,128)(2,1)S(1)}, bf16[32,1024]{1,0:T(8,128)(2,1)S(1)}, bf16[144,1024]{1,0:T(8,128)(2,1)S(1)}, bf16[144,1024]{1,0:T(8,128)(2,1)S(1)}, bf16[144,1024]{1,0:T(8,128)(2,1)S(1)}) custom-call(s32[4]{0:T(128)S(1)} %pad_add_fusion.here_ref, f32[8,144,128]{2,1,0:T(8,128)S(1)} %get-tuple-element.36.part_ref, ...), custom_call_target="tpu_custom_call" | custom-call | flops 1100000000 | tf_op jit(solution)/shard_map/conv_edge/pallas_call | solution.py:400
  23.9 0.1 collective-permute-start.8
  24.0 2.0 %collective-permute-start.9 = (bf16[144,1024]{1,0:T(8,128)(2,1)S(1)}, bf16[144,1024]{1,0:T(8,128)(2,1)S(1)}, u32[]{:S(2)}, u32[]{:S(2)}) collective-permute-start(bf16[144,1024]{1,0:T(8,128)(2,1)S(1)} %get-tuple-element.50), channel_id=1, source_target_pairs={{2,0},{4,2},{6,4},{7,6},{5,7},{3,5},{1,3},{0,1},{10,8},{12,10},{14... | collective-permute-start | bytes 884744 | tf_op jit(solution)/shard_map/ppermute | solution.py:538
  26.0 4.5 %own_block.1 = (bf16[32,1024]{1,0:T(8,128)(2,1)S(1)}, bf16[8,288,128]{2,1,0:T(8,128)(2,1)S(1)}, f32[144,1024]{1,0:T(8,128)S(1)}, f32[144,1024]{1,0:T(8,128)S(1)}, f32[144,1024]{1,0:T(8,128)S(1)}) custom-call(s32[4]{0:T(128)S(1)} %pad_add_fusion.here_ref, s32[8,8]{1,0:T(8,128)S(1)} %copy-done.5, s32[1,1,8]{2,1,0:T(1,128)S(1)} %copy-done.4, ...), custom_call_target="tpu_custom_call" | custom-call | flops 4400000000 | tf_op jit(solution)/shard_map/own_block/pallas_call | solution.py:400
  30.5 0.1 collective-permute-start.10
  30.5 1.7 %collective-permute-start.11 = (bf16[32,1024]{1,0:T(8,128)(2,1)S(1)}, bf16[32,1024]{1,0:T(8,128)(2,1)S(1)}, u32[]{:S(2)}, u32[]{:S(2)}) collective-permute-start(bf16[32,1024]{1,0:T(8,128)(2,1)S(1)} %get-tuple-element.54), channel_id=1, source_target_pairs={{0,24},{8,0},{16,8},{24,16},{1,25},{9,1},{17,9},{25,17},{2,26},{10... | collective-permute-start | bytes 196616 | tf_op jit(solution)/shard_map/ppermute | solution.py:39
  32.3 0.2 collective-permute-done.8.refs_2_
  32.4 0.3 collective-permute-start.12
  32.7 1.7 %collective-permute-start.13 = (bf16[144,1024]{1,0:T(8,128)(2,1)S(1)}, bf16[144,1024]{1,0:T(8,128)(2,1)S(1)}, u32[]{:S(2)}, u32[]{:S(2)}) collective-permute-start(bf16[144,1024]{1,0:T(8,128)(2,1)S(1)} %collective-permute-done.9.refs_3_), channel_id=1, source_target_pairs={{2,0},{4,2},{6,4},{7,6},{5,7},{3,5},{1,3},{0,1},{10,8},{12,10},{14... | collective-permute-start | bytes 884744 | tf_op jit(solution)/shard_map/ppermute | solution.py:538
  34.5 4.6 %attend_batch.2 = (f32[144,1024]{1,0:T(8,128)S(1)}, f32[144,1024]{1,0:T(8,128)S(1)}, f32[144,1024]{1,0:T(8,128)S(1)}, bf16[32,1024]{1,0:T(8,128)(2,1)S(1)}) custom-call(s32[4]{0:T(128)S(1)} %pad_add_fusion.here_ref, s32[8,8]{1,0:T(8,128)S(1)} %copy-done.5, s32[1,1,8]{2,1,0:T(1,128)S(1)} %copy-done.4, s32[1,1]{1,0:T(1,128)S(6)} %copy.22.count_ref, ...), custom_call_target="tpu_custom_call" | custom-call | flops 6380000256 | tf_op jit(solution)/shard_map/attend_batch/pallas_call | solution.py:400
  39.1 2.9 %collective-permute-start.16 = (bf16[32,1024]{1,0:T(8,128)(2,1)S(1)}, bf16[32,1024]{1,0:T(8,128)(2,1)S(1)}, u32[]{:S(2)}, u32[]{:S(2)}) collective-permute-start(bf16[32,1024]{1,0:T(8,128)(2,1)S(1)} %get-tuple-element.60), channel_id=1, source_target_pairs={{0,7},{2,5},{4,3},{6,1},{7,0},{5,2},{3,4},{1,6},{8,15},{10,13},{12... | collective-permute-start | bytes 196616 | tf_op jit(solution)/shard_map/ppermute | solution.py:552
  42.1 0.1 collective-permute-start.14
  42.2 2.2 %collective-permute-start.15 = (bf16[80,1024]{1,0:T(8,128)(2,1)S(1)}, bf16[80,1024]{1,0:T(8,128)(2,1)S(1)}, u32[]{:S(2)}, u32[]{:S(2)}) collective-permute-start(bf16[80,1024]{1,0:T(8,128)(2,1)S(1)} %slice.50), channel_id=1, source_target_pairs={{2,0},{4,2},{6,4},{7,6},{5,7},{3,5},{1,3},{0,1},{10,8},{12,10},{14... | collective-permute-start | bytes 491528 | tf_op jit(solution)/shard_map/ppermute | solution.py:550
  44.4 4.4 %attend_batch.3 = (f32[144,1024]{1,0:T(8,128)S(1)}, f32[144,1024]{1,0:T(8,128)S(1)}, f32[144,1024]{1,0:T(8,128)S(1)}, bf16[32,1024]{1,0:T(8,128)(2,1)}) custom-call(s32[4]{0:T(128)S(1)} %pad_add_fusion.here_ref, s32[8,8]{1,0:T(8,128)S(1)} %copy-done.5, s32[1,1,8]{2,1,0:T(1,128)S(1)} %copy-done.4, s32[1,1]{1,0:T(1,128)S(6)} %copy.22.count_ref, ...), custom_call_target="tpu_custom_call" | custom-call | flops 6380000256 | tf_op jit(solution)/shard_map/attend_batch/pallas_call | solution.py:400
  48.9 0.0 copy-start.3
  48.9 3.4 %attend_last.1 = (f32[144,1024]{1,0:T(8,128)S(1)}, f32[8,144,128]{2,1,0:T(8,128)S(1)}, bf16[4,9,1024]{2,1,0:T(8,128)(2,1)S(1)}, bf16[4,9,1024]{2,1,0:T(8,128)(2,...) custom-call(s32[4]{0:T(128)S(1)} %pad_add_fusion.here_ref, s32[8,8]{1,0:T(8,128)S(1)} %copy-done.5, ...), custom_call_target="tpu_custom_call" | custom-call | flops 5500000256 | tf_op jit(solution)/shard_map/attend_last/pallas_call | solution.py:400
  52.3 2.0 %collective-permute-start.17 = (bf16[4,4,1024]{2,1,0:T(4,128)(2,1)S(1)}, bf16[4,4,1024]{2,1,0:T(4,128)(2,1)S(1)}, u32[]{:S(2)}, u32[]{:S(2)}) collective-permute-start(bf16[4,4,1024]{2,1,0:T(4,128)(2,1)S(1)} %bitcast.35), channel_id=1, source_target_pairs={{1,2},{2,1},{3,4},{4,3},{5,6},{6,5},{7,0},{0,7},{9,10},{10,9},{11,... | collective-permute-start | bytes 98312 | tf_op jit(solution)/shard_map/ppermute | solution.py:416
  54.3 0.1 collective-permute-start.18
  54.3 4.6 %collective-permute-done.17.across_ref = bf16[4,4,1024]{2,1,0:T(4,128)(2,1)S(1)} collective-permute-done((bf16[4,4,1024]{2,1,0:T(4,128)(2,1)S(1)}, bf16[4,4,1024]{2,1,0:T(4,128)(2,1)S(1)}, u32[]{:S(2)}, u32[]{:S(2)}) %collective-permute-start.17) | collective-permute-done | bytes 32800 | tf_op jit(solution)/shard_map/ppermute | solution.py:416
  59.1 0.1 pad_maximum_fusion.2
  59.1 0.1 collective-permute-start.20
  59.2 0.1 pad_maximum_fusion.1
  59.3 0.5 collective-permute-start.19
  59.8 1.7 %conv_part.3 = (f32[8,144,128]{2,1,0:T(8,128)S(1)}, f32[8,9,128]{2,1,0:T(8,128)S(1)}, bf16[4,9,4,1024]{3,2,1,0:T(4,128)(2,1)}) custom-call(f32[8,144,128]{2,1,0:T(8,128)S(1)} %get-tuple-element.61.field_ref, f32[9,1024]{1,0:T(8,128)S(1)} %copy-done.3, f32[144,1024]{1,0:T(8,128)S(1)} %get-tuple-element.62.dense_ref), custom_call_target="tpu_custom_call" | custom-call | flops 2200000000 | tf_op jit(solution)/shard_map/conv_part/pallas_call | solution.py:400
  61.5 1.0 %collective-permute-done.20.south_ref = bf16[4,11,1024]{2,1,0:T(8,128)(2,1)S(1)} collective-permute-done((bf16[4,11,1024]{2,1,0:T(8,128)(2,1)S(1)}, bf16[4,11,1024]{2,1,0:T(8,128)(2,1)S(1)}, u32[]{:S(2)}, u32[]{:S(2)}) %collective-permute-start.20) | collective-permute-done | bytes 90144 | tf_op jit(solution)/shard_map/ppermute | solution.py:39
  62.5 2.1 %collective-permute-done.19.north_ref = bf16[4,11,1024]{2,1,0:T(8,128)(2,1)S(1)} collective-permute-done((bf16[4,11,1024]{2,1,0:T(8,128)(2,1)S(1)}, bf16[4,11,1024]{2,1,0:T(8,128)(2,1)S(1)}, u32[]{:S(2)}, u32[]{:S(2)}) %collective-permute-start.19) | collective-permute-done | bytes 90144 | tf_op jit(solution)/shard_map/ppermute | solution.py:39
  64.6 1.7 %conv_second.1 = bf16[4,9,4,1024]{3,2,1,0:T(4,128)(2,1)} custom-call(s32[4]{0:T(128)S(1)} %pad_add_fusion.here_ref, f32[8,144,128]{2,1,0:T(8,128)S(1)} %get-tuple-element.64.part_ref, f32[8,9,128]{2,1,0:T(8,128)S(1)} %get-tuple-element.65.taps_ref, bf16[4,11,1024]{2,1,0:T(8,128)(2,1)S(1)} %collective-permute-done.19.north_ref, ...), custom_call_target="tpu_custom_call" | custom-call | flops 2200000000 | tf_op jit(solution)/shard_map/conv_second/pallas_call | solution.py:400
  (32 shorter events, 0.2 us)
Async XLA Ops:
  1.7 5.1 %collective-permute-start = (bf16[4,9,1024]{2,1,0:T(8,128)(2,1)S(1)}, bf16[4,9,1024]{2,1,0:T(8,128)(2,1)S(1)}, u32[]{:S(2)}, u32[]{:S(2)}) collective-permute-start(bf16[4,9,1024]{2,1,0:T(8,128)(2,1)S(1)} %get-tuple-element.73), channel_id=1, source_target_pairs={{0,8},{8,16},{16,24},{24,0},{1,9},{9,17},{17,25},{25,1},{2,10},{10... | collective-permute-start | bytes 221192 | tf_op jit(solution)/shard_map/ppermute | solution.py:39
  2.2 5.8 %collective-permute-start.1 = (bf16[4,9,1024]{2,1,0:T(8,128)(2,1)S(1)}, bf16[4,9,1024]{2,1,0:T(8,128)(2,1)S(1)}, u32[]{:S(2)}, u32[]{:S(2)}) collective-permute-start(bf16[4,9,1024]{2,1,0:T(8,128)(2,1)S(1)} %get-tuple-element.72), channel_id=1, source_target_pairs={{0,24},{8,0},{16,8},{24,16},{1,25},{9,1},{17,9},{25,17},{2,26},{10... | collective-permute-start | bytes 221192 | tf_op jit(solution)/shard_map/ppermute | solution.py:39
  4.8 0.8 %copy-start.2 = (f32[9,1024]{1,0:T(8,128)S(1)}, f32[9,1024]{1,0:T(8,128)}, u32[]{:S(2)}) copy-start(f32[9,1024]{1,0:T(8,128)} %weights_ref.2) | copy-start | bytes 110596
  9.1 16.9 %copy-start.4 = (s32[1,1,8]{2,1,0:T(1,128)S(1)}, s32[1,1,8]{2,1,0:T(1,128)}, u32[]{:S(2)}) copy-start(s32[1,1,8]{2,1,0:T(1,128)} %list_ref.7) | copy-start | bytes 100
  9.1 16.9 %copy-start.5 = (s32[8,8]{1,0:T(8,128)S(1)}, s32[8,8]{1,0:T(8,128)}, u32[]{:S(2)}) copy-start(s32[8,8]{1,0:T(8,128)} %constant.26.clone.sources_ref) | copy-start | bytes 772
  9.1 13.7 %collective-permute-start.4 = (bf16[112,1024]{1,0:T(8,128)(2,1)S(1)}, bf16[112,1024]{1,0:T(8,128)(2,1)S(1)}, u32[]{:S(2)}, u32[]{:S(2)}) collective-permute-start(bf16[112,1024]{1,0:T(8,128)(2,1)S(1)} %get-tuple-element.40.inner_ref), channel_id=1, source_target_pairs={{0,2},{2,4},{4,6},{6,7},{7,5},{5,3},{3,1},{1,0},{8,10},{10,12},{12... | collective-permute-start | bytes 688136 | tf_op jit(solution)/shard_map/ppermute | solution.py:479
  10.7 12.1 %collective-permute-start.5 = (bf16[112,1024]{1,0:T(8,128)(2,1)S(1)}, bf16[112,1024]{1,0:T(8,128)(2,1)S(1)}, u32[]{:S(2)}, u32[]{:S(2)}) collective-permute-start(bf16[112,1024]{1,0:T(8,128)(2,1)S(1)} %get-tuple-element.40.inner_ref), channel_id=1, source_target_pairs={{2,0},{4,2},{6,4},{7,6},{5,7},{3,5},{1,3},{0,1},{10,8},{12,10},{14... | collective-permute-start | bytes 688136 | tf_op jit(solution)/shard_map/ppermute | solution.py:480
  11.8 10.1 %collective-permute-start.2 = (bf16[4,6,1024]{2,1,0:T(8,128)(2,1)S(1)}, bf16[4,6,1024]{2,1,0:T(8,128)(2,1)S(1)}, u32[]{:S(2)}, u32[]{:S(2)}) collective-permute-start(bf16[4,6,1024]{2,1,0:T(8,128)(2,1)S(1)} %get-tuple-element.38), channel_id=1, source_target_pairs={{1,2},{2,1},{3,4},{4,3},{5,6},{6,5},{7,0},{0,7},{9,10},{10,9},{11,... | collective-permute-start | bytes 147464 | tf_op jit(solution)/shard_map/ppermute | solution.py:416
  16.4 6.4 %collective-permute-start.3 = (bf16[4,6,1024]{2,1,0:T(8,128)(2,1)S(1)}, bf16[4,6,1024]{2,1,0:T(8,128)(2,1)S(1)}, u32[]{:S(2)}, u32[]{:S(2)}) collective-permute-start(bf16[4,6,1024]{2,1,0:T(8,128)(2,1)S(1)} %get-tuple-element.39), channel_id=1, source_target_pairs={{0,1},{1,0},{2,3},{3,2},{4,5},{5,4},{6,7},{7,6},{8,9},{9,8},{10,11... | collective-permute-start | bytes 147464 | tf_op jit(solution)/shard_map/ppermute | solution.py:416
  16.4 2.8 %copy-start = (bf16[1024,3072]{1,0:T(8,128)(2,1)S(1)}, bf16[1024,3072]{1,0:T(8,128)(2,1)}, u32[]{:S(2)}) copy-start(bf16[1024,3072]{1,0:T(8,128)(2,1)} %far_ref.1) | copy-start | bytes 18874372
  19.7 10.8 %collective-permute-start.6 = (bf16[112,1024]{1,0:T(8,128)(2,1)S(1)}, bf16[112,1024]{1,0:T(8,128)(2,1)S(1)}, u32[]{:S(2)}, u32[]{:S(2)}) collective-permute-start(bf16[112,1024]{1,0:T(8,128)(2,1)S(1)} %get-tuple-element.48), channel_id=1, source_target_pairs={{0,8},{8,16},{16,24},{24,0},{1,9},{9,17},{17,25},{25,1},{2,10},{10... | collective-permute-start | bytes 688136 | tf_op jit(solution)/shard_map/ppermute | solution.py:39
  21.9 12.6 %collective-permute-start.7 = (bf16[112,1024]{1,0:T(8,128)(2,1)S(1)}, bf16[112,1024]{1,0:T(8,128)(2,1)S(1)}, u32[]{:S(2)}, u32[]{:S(2)}) collective-permute-start(bf16[112,1024]{1,0:T(8,128)(2,1)S(1)} %get-tuple-element.48), channel_id=1, source_target_pairs={{0,24},{8,0},{16,8},{24,16},{1,25},{9,1},{17,9},{25,17},{2,26},{10... | collective-permute-start | bytes 688136 | tf_op jit(solution)/shard_map/ppermute | solution.py:39
  23.9 8.6 %collective-permute-start.8 = (bf16[144,1024]{1,0:T(8,128)(2,1)S(1)}, bf16[144,1024]{1,0:T(8,128)(2,1)S(1)}, u32[]{:S(2)}, u32[]{:S(2)}) collective-permute-start(bf16[144,1024]{1,0:T(8,128)(2,1)S(1)} %get-tuple-element.49), channel_id=1, source_target_pairs={{0,2},{2,4},{4,6},{6,7},{7,5},{5,3},{3,1},{1,0},{8,10},{10,12},{12... | collective-permute-start | bytes 884744 | tf_op jit(solution)/shard_map/ppermute | solution.py:537
  24.0 8.8 %collective-permute-start.9 = (bf16[144,1024]{1,0:T(8,128)(2,1)S(1)}, bf16[144,1024]{1,0:T(8,128)(2,1)S(1)}, u32[]{:S(2)}, u32[]{:S(2)}) collective-permute-start(bf16[144,1024]{1,0:T(8,128)(2,1)S(1)} %get-tuple-element.50), channel_id=1, source_target_pairs={{2,0},{4,2},{6,4},{7,6},{5,7},{3,5},{1,3},{0,1},{10,8},{12,10},{14... | collective-permute-start | bytes 884744 | tf_op jit(solution)/shard_map/ppermute | solution.py:538
  30.5 14.0 %collective-permute-start.10 = (bf16[32,1024]{1,0:T(8,128)(2,1)S(1)}, bf16[32,1024]{1,0:T(8,128)(2,1)S(1)}, u32[]{:S(2)}, u32[]{:S(2)}) collective-permute-start(bf16[32,1024]{1,0:T(8,128)(2,1)S(1)} %get-tuple-element.54), channel_id=1, source_target_pairs={{0,8},{8,16},{16,24},{24,0},{1,9},{9,17},{17,25},{25,1},{2,10},{10... | collective-permute-start | bytes 196616 | tf_op jit(solution)/shard_map/ppermute | solution.py:39
  30.5 13.9 %collective-permute-start.11 = (bf16[32,1024]{1,0:T(8,128)(2,1)S(1)}, bf16[32,1024]{1,0:T(8,128)(2,1)S(1)}, u32[]{:S(2)}, u32[]{:S(2)}) collective-permute-start(bf16[32,1024]{1,0:T(8,128)(2,1)S(1)} %get-tuple-element.54), channel_id=1, source_target_pairs={{0,24},{8,0},{16,8},{24,16},{1,25},{9,1},{17,9},{25,17},{2,26},{10... | collective-permute-start | bytes 196616 | tf_op jit(solution)/shard_map/ppermute | solution.py:39
  32.4 9.6 %collective-permute-start.12 = (bf16[144,1024]{1,0:T(8,128)(2,1)S(1)}, bf16[144,1024]{1,0:T(8,128)(2,1)S(1)}, u32[]{:S(2)}, u32[]{:S(2)}) collective-permute-start(bf16[144,1024]{1,0:T(8,128)(2,1)S(1)} %collective-permute-done.8.refs_2_), channel_id=1, source_target_pairs={{0,2},{2,4},{4,6},{6,7},{7,5},{5,3},{3,1},{1,0},{8,10},{10,12},{12... | collective-permute-start | bytes 884744 | tf_op jit(solution)/shard_map/ppermute | solution.py:537
  32.7 9.4 %collective-permute-start.13 = (bf16[144,1024]{1,0:T(8,128)(2,1)S(1)}, bf16[144,1024]{1,0:T(8,128)(2,1)S(1)}, u32[]{:S(2)}, u32[]{:S(2)}) collective-permute-start(bf16[144,1024]{1,0:T(8,128)(2,1)S(1)} %collective-permute-done.9.refs_3_), channel_id=1, source_target_pairs={{2,0},{4,2},{6,4},{7,6},{5,7},{3,5},{1,3},{0,1},{10,8},{12,10},{14... | collective-permute-start | bytes 884744 | tf_op jit(solution)/shard_map/ppermute | solution.py:538
  39.1 9.8 %collective-permute-start.16 = (bf16[32,1024]{1,0:T(8,128)(2,1)S(1)}, bf16[32,1024]{1,0:T(8,128)(2,1)S(1)}, u32[]{:S(2)}, u32[]{:S(2)}) collective-permute-start(bf16[32,1024]{1,0:T(8,128)(2,1)S(1)} %get-tuple-element.60), channel_id=1, source_target_pairs={{0,7},{2,5},{4,3},{6,1},{7,0},{5,2},{3,4},{1,6},{8,15},{10,13},{12... | collective-permute-start | bytes 196616 | tf_op jit(solution)/shard_map/ppermute | solution.py:552
  42.1 6.8 %collective-permute-start.14 = (bf16[96,1024]{1,0:T(8,128)(2,1)S(1)}, bf16[96,1024]{1,0:T(8,128)(2,1)S(1)}, u32[]{:S(2)}, u32[]{:S(2)}) collective-permute-start(bf16[96,1024]{1,0:T(8,128)(2,1)S(1)} %pad_maximum_fusion), channel_id=1, source_target_pairs={{0,2},{2,4},{4,6},{6,7},{7,5},{5,3},{3,1},{1,0},{8,10},{10,12},{12... | collective-permute-start | bytes 589832 | tf_op jit(solution)/shard_map/ppermute | solution.py:549
  42.2 6.7 %collective-permute-start.15 = (bf16[80,1024]{1,0:T(8,128)(2,1)S(1)}, bf16[80,1024]{1,0:T(8,128)(2,1)S(1)}, u32[]{:S(2)}, u32[]{:S(2)}) collective-permute-start(bf16[80,1024]{1,0:T(8,128)(2,1)S(1)} %slice.50), channel_id=1, source_target_pairs={{2,0},{4,2},{6,4},{7,6},{5,7},{3,5},{1,3},{0,1},{10,8},{12,10},{14... | collective-permute-start | bytes 491528 | tf_op jit(solution)/shard_map/ppermute | solution.py:550
  44.4 4.4 %copy-start.1 = (bf16[1024,1024]{1,0:T(8,128)(2,1)S(1)}, bf16[1024,1024]{1,0:T(8,128)(2,1)}, u32[]{:S(2)}) copy-start(bf16[1024,1024]{1,0:T(8,128)(2,1)} %wo_ref.1) | copy-start | bytes 6291460
  48.9 10.9 %copy-start.3 = (f32[9,1024]{1,0:T(8,128)S(1)}, f32[9,1024]{1,0:T(8,128)}, u32[]{:S(2)}) copy-start(f32[9,1024]{1,0:T(8,128)} %weights_ref.3) | copy-start | bytes 110596
  52.3 6.7 %collective-permute-start.17 = (bf16[4,4,1024]{2,1,0:T(4,128)(2,1)S(1)}, bf16[4,4,1024]{2,1,0:T(4,128)(2,1)S(1)}, u32[]{:S(2)}, u32[]{:S(2)}) collective-permute-start(bf16[4,4,1024]{2,1,0:T(4,128)(2,1)S(1)} %bitcast.35), channel_id=1, source_target_pairs={{1,2},{2,1},{3,4},{4,3},{5,6},{6,5},{7,0},{0,7},{9,10},{10,9},{11,... | collective-permute-start | bytes 98312 | tf_op jit(solution)/shard_map/ppermute | solution.py:416
  54.3 4.7 %collective-permute-start.18 = (bf16[4,4,1024]{2,1,0:T(4,128)(2,1)S(1)}, bf16[4,4,1024]{2,1,0:T(4,128)(2,1)S(1)}, u32[]{:S(2)}, u32[]{:S(2)}) collective-permute-start(bf16[4,4,1024]{2,1,0:T(4,128)(2,1)S(1)} %bitcast.34), channel_id=1, source_target_pairs={{0,1},{1,0},{2,3},{3,2},{4,5},{5,4},{6,7},{7,6},{8,9},{9,8},{10,11... | collective-permute-start | bytes 98312 | tf_op jit(solution)/shard_map/ppermute | solution.py:416
  59.1 3.4 %collective-permute-start.20 = (bf16[4,11,1024]{2,1,0:T(8,128)(2,1)S(1)}, bf16[4,11,1024]{2,1,0:T(8,128)(2,1)S(1)}, u32[]{:S(2)}, u32[]{:S(2)}) collective-permute-start(bf16[4,11,1024]{2,1,0:T(8,128)(2,1)S(1)} %pad_maximum_fusion.2), channel_id=1, source_target_pairs={{0,24},{8,0},{16,8},{24,16},{1,25},{9,1},{17,9},{25,17},{2,26},{10... | collective-permute-start | bytes 270344 | tf_op jit(solution)/shard_map/ppermute | solution.py:39
  59.3 5.3 %collective-permute-start.19 = (bf16[4,11,1024]{2,1,0:T(8,128)(2,1)S(1)}, bf16[4,11,1024]{2,1,0:T(8,128)(2,1)S(1)}, u32[]{:S(2)}, u32[]{:S(2)}) collective-permute-start(bf16[4,11,1024]{2,1,0:T(8,128)(2,1)S(1)} %pad_maximum_fusion.1), channel_id=1, source_target_pairs={{0,8},{8,16},{16,24},{24,0},{1,9},{9,17},{17,25},{25,1},{2,10},{10... | collective-permute-start | bytes 270344 | tf_op jit(solution)/shard_map/ppermute | solution.py:39

commit v6 on v5

--- a/solution.py
+++ b/solution.py
@@ -105,11 +105,14 @@
     inner = columns - 2
     lanes = slice(index * LANES, (index + 1) * LANES)
     blank = jnp.zeros((1, LANES), F32)
-    for level in range(levels):
-        for ref, flag, a, row in ((north_ref, 0, 0, 0), (south_ref, 1, 2, rows - 1)):
-            line = ref[level, :, lanes].astype(F32)
-            if line.shape[0] == columns:
-                line = jnp.concatenate([blank, line, blank], axis=0)
+    count = levels * columns
+    for ref, flag, a, row in ((north_ref, 0, 0, 0), (south_ref, 1, 2, rows - 1)):
+        lines = ref[:, lanes].astype(F32)
+        for level in range(levels):
+            ends = [blank, blank]
+            if lines.shape[0] > count:
+                ends = [lines[at : at + 1] for at in (count + level, count + levels + level)]
+            line = jnp.concatenate([ends[0], lines[level * columns : (level + 1) * columns], ends[1]], axis=0)
             left, line, right = (line[b : b + columns] for b in range(3))
             tap = [taps_ref[index, 3 * a + b : 3 * a + b + 1, :] for b in range(3)]
             more = tap[0] * left + tap[1] * line + tap[2] * right
@@ -159,7 +162,7 @@
 
 def inner_kernel(
     dims, here_ref, part_ref, taps_ref, north_ref, south_ref, west_ref, east_ref,
-    stream_ref, normed_ref, across_ref, pair_ref, full,
+    stream_ref, normed_ref, across_ref, pair_ref, even_ref, full,
 ):
     levels, columns, rows = dims
     tiles, tokens, _ = full.shape
@@ -171,15 +174,17 @@
         normed_ref[:, lanes] = value
 
     normalise(full, stream_ref, put)
+    even_ref[...] = jnp.full(even_ref.shape, here_ref[2], jnp.int32)
     has_north = (here_ref[0] > 0).astype(F32)
     has_south = (here_ref[1] > 0).astype(F32)
     even = here_ref[2] > 0
+    north = north_ref[...].astype(F32) * has_north
+    south = south_ref[...].astype(F32) * has_south
     for level in range(levels):
-        north = north_ref[level].astype(F32) * has_north
-        south = south_ref[level].astype(F32) * has_south
         tall = []
-        for edge_ref, at in ((west_ref, 0), (east_ref, columns - 1)):
+        for edge_ref, column in ((west_ref, 0), (east_ref, columns - 1)):
             middle = edge_ref[level].astype(F32)
+            at = level * columns + column
             tall.append(jnp.concatenate([north[at : at + 1], middle, south[at : at + 1]], axis=0))
         across_ref[level] = jnp.where(even, tall[0], tall[1]).astype(BF16)
         pair_ref[level] = jnp.where(even, tall[1], tall[0]).astype(BF16)
@@ -330,7 +335,8 @@
         lanes = slice(pair * LANES, (pair + 1) * LANES)
         high_ref[:, lanes], sum_ref[:, lanes], acc_ref[:, lanes] = part
 
-    attend_pairs(factor, joined([x_ref, ahead_ref, behind_ref]), w_ref, bias, query_of, finish)
+    seen = joined([x_ref, ahead_ref, behind_ref])
+    attend_pairs(factor, seen, w_ref, bias, query_of, finish)
 
 
 def combine(state, part, factor):
@@ -359,7 +365,7 @@
     factor, dims, slots, sizes, here_ref, sources_ref, list_ref, count_ref, query_ref, w_ref, high_in, sum_in, acc_in,
     wo_ref, inner_ref, edge_ref, *refs
 ):
-    blocks, (dense, after_ref, north_ref, south_ref, west_ref, east_ref, total) = refs[:-7], refs[-7:]
+    blocks, (dense, after_ref, north_ref, south_ref, across_ref, pair_ref, total) = refs[:-7], refs[-7:]
     levels, columns, rows = dims
     x = joined(blocks)
     width = x.shape[1]
@@ -380,16 +386,21 @@
     for index in range(width // LANES):
         lanes = slice(index * LANES, (index + 1) * LANES)
         after_ref[index] = total[:, lanes].astype(BF16).astype(F32)
+        for out_ref, row in ((north_ref, 0), (south_ref, rows - 1)):
+            pieces = []
+            for level in range(levels):
+                west_at = edge_at + level * 2 * rows + row
+                inner = after_ref[index, pl.ds(level * (columns - 2) * rows + row, columns - 2, stride=rows), :]
+                pieces += [after_ref[index, west_at : west_at + 1, :], inner]
+                pieces += [after_ref[index, west_at + rows : west_at + rows + 1, :]]
+            out_ref[:, lanes] = jnp.concatenate(pieces, axis=0).astype(BF16)
         for level in range(levels):
             west_at = edge_at + level * 2 * rows
             east_at = west_at + rows
-            for out_ref, row in ((north_ref, 0), (south_ref, rows - 1)):
-                inner = after_ref[index, pl.ds(level * (columns - 2) * rows + row, columns - 2, stride=rows), :]
-                west = after_ref[index, west_at + row : west_at + row + 1, :]
-                east = after_ref[index, east_at + row : east_at + row + 1, :]
-                out_ref[level, :, lanes] = jnp.concatenate([west, inner, east], axis=0).astype(BF16)
-            west_ref[level, :, lanes] = after_ref[index, west_at : west_at + rows, :].astype(BF16)
-            east_ref[level, :, lanes] = after_ref[index, east_at : east_at + rows, :].astype(BF16)
+            west = after_ref[index, west_at : west_at + rows, :]
+            east = after_ref[index, east_at : east_at + rows, :]
+            across_ref[level, :, lanes] = jnp.where(here_ref[2] > 0, west, east).astype(BF16)
+            pair_ref[level, :, lanes] = jnp.where(here_ref[2] > 0, east, west).astype(BF16)
 
 
 def shape(dims, kind):
@@ -416,15 +427,14 @@
     return lax.ppermute(value, "lon", pairs)
 
 
-def exchange(north_edge, south_edge, west_edge, east_edge, here):
-    rows = west_edge.shape[1]
-    even = here[2] > 0
-    across = swap(jnp.where(even, west_edge, east_edge), 1)
-    pair = swap(jnp.where(even, east_edge, west_edge), 0)
+def exchange(north_edge, south_edge, across, pair, even):
+    rows = across.shape[1]
+    across, pair = swap(across, 1), swap(pair, 0)
+    even = even[None] > 0
     west, east = jnp.where(even, across, pair), jnp.where(even, pair, across)
 
     def row(edge, at):
-        return jnp.concatenate([west[:, at : at + 1], edge, east[:, at : at + 1]], axis=1)
+        return jnp.concatenate([edge, west[:, at], east[:, at]], axis=0)
 
     north = shift(row(south_edge, rows - 1), "lat", 1)
     south = shift(row(north_edge, 0), "lat", -1)
@@ -464,12 +474,12 @@
     forward = [(order[i], order[(i + 1) % lon_total]) for i in range(lon_total)]
     backward = [(b, a) for a, b in forward]
 
-    north = shift(fields[:, :, rows - 1], "lat", 1)
-    south = shift(fields[:, :, 0], "lat", -1)
+    north = shift(fields[:, :, rows - 1].reshape(levels * columns, width), "lat", 1)
+    south = shift(fields[:, :, 0].reshape(levels * columns, width), "lat", -1)
     part = call(first_part_kernel, part_shape, (), (fields, conv_first), [], "conv_part", 1)
-    stream_inner, normed_inner, across, pair = call(
+    stream_inner, normed_inner, across, pair, even = call(
         functools.partial(inner_kernel, dims),
-        (flat(inner_tokens), flat(inner_tokens), tall, tall),
+        (flat(inner_tokens), flat(inner_tokens), tall, tall, shape((1, width), jnp.int32)),
         (here,),
         (*part, north, south, fields[:, 0], fields[:, columns - 1]),
         [full(inner_tokens)],
@@ -481,7 +491,7 @@
     across, pair = swap(across, 1), swap(pair, 0)
     anywhere = pl.BlockSpec(memory_space=pl.ANY)
     vmem = pl.BlockSpec(memory_space=pltpu.VMEM)
-    normed_passed, w_qkv = pl.pallas_call(
+    inner_passed, w_qkv = pl.pallas_call(
         weights_kernel,
         out_shape=(flat(inner_tokens), shape(w_qkv.shape, BF16)),
         in_specs=[vmem, anywhere],
@@ -528,32 +538,32 @@
 
     sides = ((ABOVE, 1), (BELOW, -1))
     near = {
-        2: [(shift(normed_passed, "lat", by), [(slot, inner_tokens)]) for slot, by in sides],
+        2: [(shift(inner_passed, "lat", by), [(slot, inner_tokens)]) for slot, by in sides],
         3: [(shift(edge_passed, "lat", by), [(slot, edge_tokens)]) for slot, by in sides],
     }
     ahead, behind = both
-    handed = None
     for step in range(2, half):
         ahead = lax.ppermute(ahead, "lon", forward)
         behind = lax.ppermute(behind, "lon", backward)
         if step > 2:
-            state, hand = batch(state, waiting)
-            handed = hand if handed is None else handed
+            state, handed = batch(state, waiting)
+            if step == 3:
+                opposite = [(order[i], order[(i + half) % lon_total]) for i in range(lon_total)]
+                far_edge = lax.ppermute(handed, "lon", opposite)
         waiting = [
-            *near.get(step, ()),
             (ahead, [(2 * step - 2, inner_tokens), (2 * step - 4, edge_tokens)]),
             (behind, [(2 * step - 1, inner_tokens), (2 * step - 3, edge_tokens)]),
+            *near.get(step, ()),
         ]
     last = lon_total - 2
     cut = (inner_tokens + 31) // 32 * 16
     far_first = lax.ppermute(jnp.concatenate([ahead[:cut], ahead[inner_tokens:]]), "lon", forward)
     far_second = lax.ppermute(behind[cut:], "lon", backward)
     state, _ = batch(state, waiting)
-    far_edge = lax.ppermute(handed, "lon", [(order[i], order[(i + half) % lon_total]) for i in range(lon_total)])
     slots = [last, last - 2, last, last - 1, last]
     sizes = [cut, edge_tokens, inner_tokens - cut, edge_tokens, edge_tokens]
 
-    row_edge, column_edge = shape((levels, columns, width), BF16), shape((levels, rows, width), BF16)
+    row_edge, column_edge = flat(levels * columns), shape((levels, rows, width), BF16)
     dense, after, *edges = call(
         functools.partial(last_kernel, factor, dims, slots, sizes),
         (shape((tokens, width), F32), part_shape[0], row_edge, row_edge, column_edge, column_edge),
@@ -563,7 +573,7 @@
         "attend_last",
         5,
     )
-    halo = exchange(*edges, here)
+    halo = exchange(*edges, even)
     grid4 = shape(fields.shape, BF16)
     *part, attended = call(
         functools.partial(second_part_kernel, dims),

time: 66.5 us -> 65.4 us (0.983)
  local copies, waits for them, and re-layouts: 5.25 us -> 3.5 us
  waiting for transfers between devices: 11.3 us -> 12.3 us
    ppermute x4, waiting for transfers between devices: 6.44 us -> 9.38 us  [swap(): return lax.ppermute(value, 'lon', pairs)]
    ppermute x8, waiting for transfers between devices: 4.64 us -> 1.92 us  [shift(): return lax.ppermute(x, axis, [(i, (i + by) % size) for i in range(size)])]
    unnamed x13 -> x19, local copies, waits for them, and re-layouts: 4.73 us -> 2.93 us
    ppermute x8, starting transfers between devices: 6.2 us -> 4.93 us  [shift(): return lax.ppermute(x, axis, [(i, (i + by) % size) for i in range(size)])]
    ppermute x4, starting transfers between devices: 6.66 us -> 7.72 us  [swap(): return lax.ppermute(value, 'lon', pairs)]
    ppermute x2, waiting for transfers between devices: 0.19 us -> 0.99 us  [local(): ahead = lax.ppermute(ahead, 'lon', forward)]
    ppermute x1, starting transfers between devices: 1.63 us -> 2.42 us  [local(): ahead = lax.ppermute(normed_inner, 'lon', forward)]
where the time goes in v6:
time: 65.4 us; the launch traced here: 65.1 us
  starting transfers between devices  23.9 us (37%)
  Pallas kernels  23.6 us (36%)
  waiting for transfers between devices  12.3 us (19%)
  local copies, waits for them, and re-layouts  3.5 us (5%)
  between operations  1.61 us (2%)
    pallas_call x9, Pallas kernels, call(): pl.pallas_call(kernel, out_shape=out_shape, in_specs=[pl.BlockSpec(memory...  23.1 us
    ppermute x4, waiting for transfers between devices, swap(): return lax.ppermute(value, 'lon', pairs)  9.38 us
    ppermute x4, starting transfers between devices, swap(): return lax.ppermute(value, 'lon', pairs)  7.72 us
    ppermute x8, starting transfers between devices, shift(): return lax.ppermute(x, axis, [(i, (i + by) % size) for i in range(size)])  4.93 us
    ppermute x2, starting transfers between devices, local(): behind = lax.ppermute(behind, 'lon', backward)  3.78 us
    unnamed x19, local copies, waits for them, and re-layouts  2.93 us
    ppermute x1, starting transfers between devices, local(): ahead = lax.ppermute(normed_inner, 'lon', forward)  2.42 us
    ppermute x1, starting transfers between devices, local(): far_edge = lax.ppermute(handed, 'lon', opposite)  2.41 us
  transfers between devices with their start and end apart: 21, of which 7 were waited for; matrix products, arithmetic and copies ran while one was open for 1% of the time, Pallas kernels for 27%

profile of v6, /device:TPU:0, one launch (start us, length us, event | category | flops | bytes accessed | tf_op | source)
XLA Modules:
  0.0 65.1 jit_solution(17802466948775104494)
XLA Ops:
  0.6 1.1 %copy.28 = bf16[4,4,9,1024]{3,1,0,2:T(4,128)(2,1)S(1)} copy(bf16[4,4,9,1024]{3,1,2,0:T(4,128)(2,1)} %param.8) | data formatting | bytes 589824 | tf_op args[0]
  1.7 0.2 fusion
  1.9 0.1 copy.16
  2.1 0.5 collective-permute-start
  2.6 0.1 copy.17
  2.7 2.0 %collective-permute-start.1 = (bf16[36,1024]{1,0:T(8,128)(2,1)S(1)}, bf16[36,1024]{1,0:T(8,128)(2,1)S(1)}, u32[]{:S(2)}, u32[]{:S(2)}) collective-permute-start(bf16[36,1024]{1,0:T(8,128)(2,1)S(1)} %reshape_squeeze.7), channel_id=1, source_target_pairs={{0,24},{8,0},{16,8},{24,16},{1,25},{9,1},{17,9},{25,17},{2,26},{10... | collective-permute-start | bytes 221192 | tf_op jit(solution)/shard_map/ppermute | solution.py:39
  4.8 0.1 pad_add_fusion.here_ref
  4.8 1.0 %copy-done = bf16[4,4,9,1024]{3,1,2,0:T(4,128)(2,1)S(1)} copy-done((bf16[4,4,9,1024]{3,1,2,0:T(4,128)(2,1)S(1)}, bf16[4,4,9,1024]{3,1,2,0:T(4,128)(2,1)}, u32[]{:S(2)}) %copy-start) | copy-done | bytes 294936
  5.8 0.8 %copy-done.3 = f32[9,1024]{1,0:T(8,128)S(1)} copy-done((f32[9,1024]{1,0:T(8,128)S(1)}, f32[9,1024]{1,0:T(8,128)}, u32[]{:S(2)}) %copy-start.3) | copy-done | bytes 36888
  6.6 0.9 %conv_part.2 = (f32[8,144,128]{2,1,0:T(8,128)S(1)}, f32[8,9,128]{2,1,0:T(8,128)S(1)}) custom-call(bf16[4,9,4,1024]{3,2,1,0:T(4,128)(2,1)S(1)} %bitcast.30, f32[9,1024]{1,0:T(8,128)S(1)} %copy-done.3), custom_call_target="tpu_custom_call" | custom-call | flops 1100000000 | tf_op jit(solution)/shard_map/conv_part/pallas_call | solution.py:411
  7.6 0.0 collective-permute-done.north_ref
  7.6 1.0 %conv_inner.1 = (bf16[112,1024]{1,0:T(8,128)(2,1)S(1)}, bf16[112,1024]{1,0:T(8,128)(2,1)S(1)}, bf16[4,6,1024]{2,1,0:T(8,128)(2,1)S(1)}, bf16[4,6,1024]{2,1,0:T(8,128)(2,1)S(1)}, s32[1,1024]{1,0:T(1,128)S(1)}) custom-call(s32[4]{0:T(128)S(1)} %pad_add_fusion.here_ref, f32[8,144,128]{2,1,0:T(8,128)S(1)} %get-tuple-element.37.part_ref, ...), custom_call_target="tpu_custom_call" | custom-call | flops 1100000000 | tf_op jit(solution)/shard_map/conv_inner/pallas_call | solution.py:411
  8.6 0.0 copy-start.5
  8.6 0.0 copy-start.6
  8.6 2.4 %collective-permute-start.4 = (bf16[112,1024]{1,0:T(8,128)(2,1)S(1)}, bf16[112,1024]{1,0:T(8,128)(2,1)S(1)}, u32[]{:S(2)}, u32[]{:S(2)}) collective-permute-start(bf16[112,1024]{1,0:T(8,128)(2,1)S(1)} %get-tuple-element.41.inner_ref), channel_id=1, source_target_pairs={{0,2},{2,4},{4,6},{6,7},{7,5},{5,3},{3,1},{1,0},{8,10},{10,12},{12... | collective-permute-start | bytes 688136 | tf_op jit(solution)/shard_map/ppermute | solution.py:489
  11.0 0.0 collective-permute-start.5
  11.7 5.1 %collective-permute-start.2 = (bf16[4,6,1024]{2,1,0:T(8,128)(2,1)S(1)}, bf16[4,6,1024]{2,1,0:T(8,128)(2,1)S(1)}, u32[]{:S(2)}, u32[]{:S(2)}) collective-permute-start(bf16[4,6,1024]{2,1,0:T(8,128)(2,1)S(1)} %get-tuple-element.39), channel_id=1, source_target_pairs={{1,2},{2,1},{3,4},{4,3},{5,6},{6,5},{7,0},{0,7},{9,10},{10,9},{11,... | collective-permute-start | bytes 147464 | tf_op jit(solution)/shard_map/ppermute | solution.py:427
  16.8 0.0 collective-permute-start.3
  16.8 0.4 weights_near.1
  17.2 0.1 collective-permute-start.8
  17.3 5.0 %collective-permute-done.2.across_ref = bf16[4,6,1024]{2,1,0:T(8,128)(2,1)S(1)} collective-permute-done((bf16[4,6,1024]{2,1,0:T(8,128)(2,1)S(1)}, bf16[4,6,1024]{2,1,0:T(8,128)(2,1)S(1)}, u32[]{:S(2)}, u32[]{:S(2)}) %collective-permute-start.2) | collective-permute-done | bytes 49184 | tf_op jit(solution)/shard_map/ppermute | solution.py:427
  22.3 0.1 collective-permute-done.3.pair_ref
  22.4 1.1 %conv_edge.1 = (bf16[32,1024]{1,0:T(8,128)(2,1)S(1)}, bf16[32,1024]{1,0:T(8,128)(2,1)S(1)}, bf16[144,1024]{1,0:T(8,128)(2,1)S(1)}, bf16[144,1024]{1,0:T(8,128)(2,1)S(1)}, bf16[144,1024]{1,0:T(8,128)(2,1)S(1)}) custom-call(s32[4]{0:T(128)S(1)} %pad_add_fusion.here_ref, f32[8,144,128]{2,1,0:T(8,128)S(1)} %get-tuple-element.37.part_ref, ...), custom_call_target="tpu_custom_call" | custom-call | flops 1100000000 | tf_op jit(solution)/shard_map/conv_edge/pallas_call | solution.py:411
  23.5 0.1 collective-permute-start.6
  23.6 2.0 %collective-permute-start.7 = (bf16[144,1024]{1,0:T(8,128)(2,1)S(1)}, bf16[144,1024]{1,0:T(8,128)(2,1)S(1)}, u32[]{:S(2)}, u32[]{:S(2)}) collective-permute-start(bf16[144,1024]{1,0:T(8,128)(2,1)S(1)} %get-tuple-element.50), channel_id=1, source_target_pairs={{2,0},{4,2},{6,4},{7,6},{5,7},{3,5},{1,3},{0,1},{10,8},{12,10},{14... | collective-permute-start | bytes 884744 | tf_op jit(solution)/shard_map/ppermute | solution.py:547
  25.6 4.4 %own_block.1 = (bf16[32,1024]{1,0:T(8,128)(2,1)S(1)}, bf16[8,288,128]{2,1,0:T(8,128)(2,1)S(1)}, f32[144,1024]{1,0:T(8,128)S(1)}, f32[144,1024]{1,0:T(8,128)S(1)}, f32[144,1024]{1,0:T(8,128)S(1)}) custom-call(s32[4]{0:T(128)S(1)} %pad_add_fusion.here_ref, s32[8,8]{1,0:T(8,128)S(1)} %copy-done.6, s32[1,1,8]{2,1,0:T(1,128)S(1)} %copy-done.5, ...), custom_call_target="tpu_custom_call" | custom-call | flops 4400000000 | tf_op jit(solution)/shard_map/own_block/pallas_call | solution.py:411
  30.1 0.1 collective-permute-start.12
  30.2 1.7 %collective-permute-start.13 = (bf16[32,1024]{1,0:T(8,128)(2,1)S(1)}, bf16[32,1024]{1,0:T(8,128)(2,1)S(1)}, u32[]{:S(2)}, u32[]{:S(2)}) collective-permute-start(bf16[32,1024]{1,0:T(8,128)(2,1)S(1)} %get-tuple-element.55), channel_id=1, source_target_pairs={{0,24},{8,0},{16,8},{24,16},{1,25},{9,1},{17,9},{25,17},{2,26},{10... | collective-permute-start | bytes 196616 | tf_op jit(solution)/shard_map/ppermute | solution.py:39
  31.9 1.0 %collective-permute-done.6.refs_0_ = bf16[144,1024]{1,0:T(8,128)(2,1)S(1)} collective-permute-done((bf16[144,1024]{1,0:T(8,128)(2,1)S(1)}, bf16[144,1024]{1,0:T(8,128)(2,1)S(1)}, u32[]{:S(2)}, u32[]{:S(2)}) %collective-permute-start.6) | collective-permute-done | bytes 294944 | tf_op jit(solution)/shard_map/ppermute | solution.py:546
  32.9 0.3 collective-permute-start.10
  33.2 1.7 %collective-permute-start.11 = (bf16[144,1024]{1,0:T(8,128)(2,1)S(1)}, bf16[144,1024]{1,0:T(8,128)(2,1)S(1)}, u32[]{:S(2)}, u32[]{:S(2)}) collective-permute-start(bf16[144,1024]{1,0:T(8,128)(2,1)S(1)} %collective-permute-done.7.refs_1_), channel_id=1, source_target_pairs={{2,0},{4,2},{6,4},{7,6},{5,7},{3,5},{1,3},{0,1},{10,8},{12,10},{14... | collective-permute-start | bytes 884744 | tf_op jit(solution)/shard_map/ppermute | solution.py:547
  34.9 4.6 %attend_batch.2 = (f32[144,1024]{1,0:T(8,128)S(1)}, f32[144,1024]{1,0:T(8,128)S(1)}, f32[144,1024]{1,0:T(8,128)S(1)}, bf16[32,1024]{1,0:T(8,128)(2,1)S(1)}) custom-call(s32[4]{0:T(128)S(1)} %pad_add_fusion.here_ref, s32[8,8]{1,0:T(8,128)S(1)} %copy-done.6, s32[1,1,8]{2,1,0:T(1,128)S(1)} %copy-done.5, s32[1,1]{1,0:T(1,128)S(6)} %copy.33.count_ref, ...), custom_call_target="tpu_custom_call" | custom-call | flops 6380000256 | tf_op jit(solution)/shard_map/attend_batch/pallas_call | solution.py:411
  39.5 2.4 %collective-permute-start.16 = (bf16[32,1024]{1,0:T(8,128)(2,1)S(1)}, bf16[32,1024]{1,0:T(8,128)(2,1)S(1)}, u32[]{:S(2)}, u32[]{:S(2)}) collective-permute-start(bf16[32,1024]{1,0:T(8,128)(2,1)S(1)} %get-tuple-element.61), channel_id=1, source_target_pairs={{0,7},{2,5},{4,3},{6,1},{7,0},{5,2},{3,4},{1,6},{8,15},{10,13},{12... | collective-permute-start | bytes 196616 | tf_op jit(solution)/shard_map/ppermute | solution.py:552
  42.0 0.1 collective-permute-start.14
  42.1 2.2 %collective-permute-start.15 = (bf16[80,1024]{1,0:T(8,128)(2,1)S(1)}, bf16[80,1024]{1,0:T(8,128)(2,1)S(1)}, u32[]{:S(2)}, u32[]{:S(2)}) collective-permute-start(bf16[80,1024]{1,0:T(8,128)(2,1)S(1)} %slice.50), channel_id=1, source_target_pairs={{2,0},{4,2},{6,4},{7,6},{5,7},{3,5},{1,3},{0,1},{10,8},{12,10},{14... | collective-permute-start | bytes 491528 | tf_op jit(solution)/shard_map/ppermute | solution.py:561
  44.3 4.4 %attend_batch.3 = (f32[144,1024]{1,0:T(8,128)S(1)}, f32[144,1024]{1,0:T(8,128)S(1)}, f32[144,1024]{1,0:T(8,128)S(1)}, bf16[32,1024]{1,0:T(8,128)(2,1)}) custom-call(s32[4]{0:T(128)S(1)} %pad_add_fusion.here_ref, s32[8,8]{1,0:T(8,128)S(1)} %copy-done.6, s32[1,1,8]{2,1,0:T(1,128)S(1)} %copy-done.5, s32[1,1]{1,0:T(1,128)S(6)} %copy.33.count_ref, ...), custom_call_target="tpu_custom_call" | custom-call | flops 6380000256 | tf_op jit(solution)/shard_map/attend_batch/pallas_call | solution.py:411
  48.7 0.0 copy-start.4
  48.7 3.4 %attend_last.1 = (f32[144,1024]{1,0:T(8,128)S(1)}, f32[8,144,128]{2,1,0:T(8,128)S(1)}, bf16[36,1024]{1,0:T(8,128)(2,1)S(1)}, bf16[36,1024]{1,0:T(8,128)(2,1)S(1)...) custom-call(s32[4]{0:T(128)S(1)} %pad_add_fusion.here_ref, s32[8,8]{1,0:T(8,128)S(1)} %copy-done.6, ...), custom_call_target="tpu_custom_call" | custom-call | flops 5500000256 | tf_op jit(solution)/shard_map/attend_last/pallas_call | solution.py:411
  52.1 2.6 %collective-permute-start.17 = (bf16[4,4,1024]{2,1,0:T(4,128)(2,1)S(1)}, bf16[4,4,1024]{2,1,0:T(4,128)(2,1)S(1)}, u32[]{:S(2)}, u32[]{:S(2)}) collective-permute-start(bf16[4,4,1024]{2,1,0:T(4,128)(2,1)S(1)} %get-tuple-element.69), channel_id=1, source_target_pairs={{1,2},{2,1},{3,4},{4,3},{5,6},{6,5},{7,0},{0,7},{9,10},{10,9},{11,... | collective-permute-start | bytes 98312 | tf_op jit(solution)/shard_map/ppermute | solution.py:427
  54.8 4.1 %collective-permute-done.17.across_ref = bf16[4,4,1024]{2,1,0:T(4,128)(2,1)S(1)} collective-permute-done((bf16[4,4,1024]{2,1,0:T(4,128)(2,1)S(1)}, bf16[4,4,1024]{2,1,0:T(4,128)(2,1)S(1)}, u32[]{:S(2)}, u32[]{:S(2)}) %collective-permute-start.17) | collective-permute-done | bytes 32800 | tf_op jit(solution)/shard_map/ppermute | solution.py:427
  58.9 0.1 collective-permute-done.18.pair_ref
  59.0 0.1 fusion.1
  59.2 0.1 collective-permute-start.20
  59.3 0.5 collective-permute-start.19
  59.8 1.7 %conv_part.3 = (f32[8,144,128]{2,1,0:T(8,128)S(1)}, f32[8,9,128]{2,1,0:T(8,128)S(1)}, bf16[4,9,4,1024]{3,2,1,0:T(4,128)(2,1)}) custom-call(f32[8,144,128]{2,1,0:T(8,128)S(1)} %get-tuple-element.62.field_ref, f32[9,1024]{1,0:T(8,128)S(1)} %copy-done.4, f32[144,1024]{1,0:T(8,128)S(1)} %get-tuple-element.63.dense_ref), custom_call_target="tpu_custom_call" | custom-call | flops 2200000000 | tf_op jit(solution)/shard_map/conv_part/pallas_call | solution.py:411
  61.5 0.9 %collective-permute-done.20.south_ref = bf16[44,1024]{1,0:T(8,128)(2,1)S(1)} collective-permute-done((bf16[44,1024]{1,0:T(8,128)(2,1)S(1)}, bf16[44,1024]{1,0:T(8,128)(2,1)S(1)}, u32[]{:S(2)}, u32[]{:S(2)}) %collective-permute-start.20) | collective-permute-done | bytes 90144 | tf_op jit(solution)/shard_map/ppermute | solution.py:39
  62.4 1.0 %collective-permute-done.19.north_ref = bf16[44,1024]{1,0:T(8,128)(2,1)S(1)} collective-permute-done((bf16[44,1024]{1,0:T(8,128)(2,1)S(1)}, bf16[44,1024]{1,0:T(8,128)(2,1)S(1)}, u32[]{:S(2)}, u32[]{:S(2)}) %collective-permute-start.19) | collective-permute-done | bytes 90144 | tf_op jit(solution)/shard_map/ppermute | solution.py:39
  63.4 1.7 %conv_second.1 = bf16[4,9,4,1024]{3,2,1,0:T(4,128)(2,1)} custom-call(s32[4]{0:T(128)S(1)} %pad_add_fusion.here_ref, f32[8,144,128]{2,1,0:T(8,128)S(1)} %get-tuple-element.65.part_ref, f32[8,9,128]{2,1,0:T(8,128)S(1)} %get-tuple-element.66.taps_ref, bf16[44,1024]{1,0:T(8,128)(2,1)S(1)} %collective-permute-done.19.north_ref, ...), custom_call_target="tpu_custom_call" | custom-call | flops 2200000000 | tf_op jit(solution)/shard_map/conv_second/pallas_call | solution.py:411
  (39 shorter events, 0.3 us)
Async XLA Ops:
  2.1 5.5 %collective-permute-start = (bf16[36,1024]{1,0:T(8,128)(2,1)S(1)}, bf16[36,1024]{1,0:T(8,128)(2,1)S(1)}, u32[]{:S(2)}, u32[]{:S(2)}) collective-permute-start(bf16[36,1024]{1,0:T(8,128)(2,1)S(1)} %reshape_squeeze.6), channel_id=1, source_target_pairs={{0,8},{8,16},{16,24},{24,0},{1,9},{9,17},{17,25},{25,1},{2,10},{10... | collective-permute-start | bytes 221192 | tf_op jit(solution)/shard_map/ppermute | solution.py:39
  2.7 4.9 %collective-permute-start.1 = (bf16[36,1024]{1,0:T(8,128)(2,1)S(1)}, bf16[36,1024]{1,0:T(8,128)(2,1)S(1)}, u32[]{:S(2)}, u32[]{:S(2)}) collective-permute-start(bf16[36,1024]{1,0:T(8,128)(2,1)S(1)} %reshape_squeeze.7), channel_id=1, source_target_pairs={{0,24},{8,0},{16,8},{24,16},{1,25},{9,1},{17,9},{25,17},{2,26},{10... | collective-permute-start | bytes 221192 | tf_op jit(solution)/shard_map/ppermute | solution.py:39
  4.8 1.0 %copy-start = (bf16[4,4,9,1024]{3,1,2,0:T(4,128)(2,1)S(1)}, bf16[4,4,9,1024]{3,1,2,0:T(4,128)(2,1)}, u32[]{:S(2)}) copy-start(bf16[4,4,9,1024]{3,1,2,0:T(4,128)(2,1)} %param.8) | copy-start | bytes 884740
  5.8 0.8 %copy-start.3 = (f32[9,1024]{1,0:T(8,128)S(1)}, f32[9,1024]{1,0:T(8,128)}, u32[]{:S(2)}) copy-start(f32[9,1024]{1,0:T(8,128)} %weights_ref.2) | copy-start | bytes 110596
  6.6 10.1 %copy-start.1 = (bf16[1024,3072]{1,0:T(8,128)(2,1)S(1)}, bf16[1024,3072]{1,0:T(8,128)(2,1)}, u32[]{:S(2)}) copy-start(bf16[1024,3072]{1,0:T(8,128)(2,1)} %far_ref.1) | copy-start | bytes 18874372
  8.6 17.0 %copy-start.5 = (s32[1,1,8]{2,1,0:T(1,128)S(1)}, s32[1,1,8]{2,1,0:T(1,128)}, u32[]{:S(2)}) copy-start(s32[1,1,8]{2,1,0:T(1,128)} %list_ref.7) | copy-start | bytes 100
  8.6 17.0 %copy-start.6 = (s32[8,8]{1,0:T(8,128)S(1)}, s32[8,8]{1,0:T(8,128)}, u32[]{:S(2)}) copy-start(s32[8,8]{1,0:T(8,128)} %constant.27.clone.sources_ref) | copy-start | bytes 772
  8.6 13.8 %collective-permute-start.4 = (bf16[112,1024]{1,0:T(8,128)(2,1)S(1)}, bf16[112,1024]{1,0:T(8,128)(2,1)S(1)}, u32[]{:S(2)}, u32[]{:S(2)}) collective-permute-start(bf16[112,1024]{1,0:T(8,128)(2,1)S(1)} %get-tuple-element.41.inner_ref), channel_id=1, source_target_pairs={{0,2},{2,4},{4,6},{6,7},{7,5},{5,3},{3,1},{1,0},{8,10},{10,12},{12... | collective-permute-start | bytes 688136 | tf_op jit(solution)/shard_map/ppermute | solution.py:489
  11.0 11.4 %collective-permute-start.5 = (bf16[112,1024]{1,0:T(8,128)(2,1)S(1)}, bf16[112,1024]{1,0:T(8,128)(2,1)S(1)}, u32[]{:S(2)}, u32[]{:S(2)}) collective-permute-start(bf16[112,1024]{1,0:T(8,128)(2,1)S(1)} %get-tuple-element.41.inner_ref), channel_id=1, source_target_pairs={{2,0},{4,2},{6,4},{7,6},{5,7},{3,5},{1,3},{0,1},{10,8},{12,10},{14... | collective-permute-start | bytes 688136 | tf_op jit(solution)/shard_map/ppermute | solution.py:490
  11.7 10.6 %collective-permute-start.2 = (bf16[4,6,1024]{2,1,0:T(8,128)(2,1)S(1)}, bf16[4,6,1024]{2,1,0:T(8,128)(2,1)S(1)}, u32[]{:S(2)}, u32[]{:S(2)}) collective-permute-start(bf16[4,6,1024]{2,1,0:T(8,128)(2,1)S(1)} %get-tuple-element.39), channel_id=1, source_target_pairs={{1,2},{2,1},{3,4},{4,3},{5,6},{6,5},{7,0},{0,7},{9,10},{10,9},{11,... | collective-permute-start | bytes 147464 | tf_op jit(solution)/shard_map/ppermute | solution.py:427
  16.8 5.7 %collective-permute-start.3 = (bf16[4,6,1024]{2,1,0:T(8,128)(2,1)S(1)}, bf16[4,6,1024]{2,1,0:T(8,128)(2,1)S(1)}, u32[]{:S(2)}, u32[]{:S(2)}) collective-permute-start(bf16[4,6,1024]{2,1,0:T(8,128)(2,1)S(1)} %get-tuple-element.40), channel_id=1, source_target_pairs={{0,1},{1,0},{2,3},{3,2},{4,5},{5,4},{6,7},{7,6},{8,9},{9,8},{10,11... | collective-permute-start | bytes 147464 | tf_op jit(solution)/shard_map/ppermute | solution.py:427
  17.2 12.9 %collective-permute-start.8 = (bf16[112,1024]{1,0:T(8,128)(2,1)S(1)}, bf16[112,1024]{1,0:T(8,128)(2,1)S(1)}, u32[]{:S(2)}, u32[]{:S(2)}) collective-permute-start(bf16[112,1024]{1,0:T(8,128)(2,1)S(1)} %get-tuple-element.51), channel_id=1, source_target_pairs={{0,8},{8,16},{16,24},{24,0},{1,9},{9,17},{17,25},{25,1},{2,10},{10... | collective-permute-start | bytes 688136 | tf_op jit(solution)/shard_map/ppermute | solution.py:39
  22.3 12.6 %collective-permute-start.9 = (bf16[112,1024]{1,0:T(8,128)(2,1)S(1)}, bf16[112,1024]{1,0:T(8,128)(2,1)S(1)}, u32[]{:S(2)}, u32[]{:S(2)}) collective-permute-start(bf16[112,1024]{1,0:T(8,128)(2,1)S(1)} %get-tuple-element.51), channel_id=1, source_target_pairs={{0,24},{8,0},{16,8},{24,16},{1,25},{9,1},{17,9},{25,17},{2,26},{10... | collective-permute-start | bytes 688136 | tf_op jit(solution)/shard_map/ppermute | solution.py:39
  23.5 9.4 %collective-permute-start.6 = (bf16[144,1024]{1,0:T(8,128)(2,1)S(1)}, bf16[144,1024]{1,0:T(8,128)(2,1)S(1)}, u32[]{:S(2)}, u32[]{:S(2)}) collective-permute-start(bf16[144,1024]{1,0:T(8,128)(2,1)S(1)} %get-tuple-element.49), channel_id=1, source_target_pairs={{0,2},{2,4},{4,6},{6,7},{7,5},{5,3},{3,1},{1,0},{8,10},{10,12},{12... | collective-permute-start | bytes 884744 | tf_op jit(solution)/shard_map/ppermute | solution.py:546
  23.6 9.6 %collective-permute-start.7 = (bf16[144,1024]{1,0:T(8,128)(2,1)S(1)}, bf16[144,1024]{1,0:T(8,128)(2,1)S(1)}, u32[]{:S(2)}, u32[]{:S(2)}) collective-permute-start(bf16[144,1024]{1,0:T(8,128)(2,1)S(1)} %get-tuple-element.50), channel_id=1, source_target_pairs={{2,0},{4,2},{6,4},{7,6},{5,7},{3,5},{1,3},{0,1},{10,8},{12,10},{14... | collective-permute-start | bytes 884744 | tf_op jit(solution)/shard_map/ppermute | solution.py:547
  30.1 14.2 %collective-permute-start.12 = (bf16[32,1024]{1,0:T(8,128)(2,1)S(1)}, bf16[32,1024]{1,0:T(8,128)(2,1)S(1)}, u32[]{:S(2)}, u32[]{:S(2)}) collective-permute-start(bf16[32,1024]{1,0:T(8,128)(2,1)S(1)} %get-tuple-element.55), channel_id=1, source_target_pairs={{0,8},{8,16},{16,24},{24,0},{1,9},{9,17},{17,25},{25,1},{2,10},{10... | collective-permute-start | bytes 196616 | tf_op jit(solution)/shard_map/ppermute | solution.py:39
  30.2 14.2 %collective-permute-start.13 = (bf16[32,1024]{1,0:T(8,128)(2,1)S(1)}, bf16[32,1024]{1,0:T(8,128)(2,1)S(1)}, u32[]{:S(2)}, u32[]{:S(2)}) collective-permute-start(bf16[32,1024]{1,0:T(8,128)(2,1)S(1)} %get-tuple-element.55), channel_id=1, source_target_pairs={{0,24},{8,0},{16,8},{24,16},{1,25},{9,1},{17,9},{25,17},{2,26},{10... | collective-permute-start | bytes 196616 | tf_op jit(solution)/shard_map/ppermute | solution.py:39
  32.9 9.0 %collective-permute-start.10 = (bf16[144,1024]{1,0:T(8,128)(2,1)S(1)}, bf16[144,1024]{1,0:T(8,128)(2,1)S(1)}, u32[]{:S(2)}, u32[]{:S(2)}) collective-permute-start(bf16[144,1024]{1,0:T(8,128)(2,1)S(1)} %collective-permute-done.6.refs_0_), channel_id=1, source_target_pairs={{0,2},{2,4},{4,6},{6,7},{7,5},{5,3},{3,1},{1,0},{8,10},{10,12},{12... | collective-permute-start | bytes 884744 | tf_op jit(solution)/shard_map/ppermute | solution.py:546
  33.2 8.9 %collective-permute-start.11 = (bf16[144,1024]{1,0:T(8,128)(2,1)S(1)}, bf16[144,1024]{1,0:T(8,128)(2,1)S(1)}, u32[]{:S(2)}, u32[]{:S(2)}) collective-permute-start(bf16[144,1024]{1,0:T(8,128)(2,1)S(1)} %collective-permute-done.7.refs_1_), channel_id=1, source_target_pairs={{2,0},{4,2},{6,4},{7,6},{5,7},{3,5},{1,3},{0,1},{10,8},{12,10},{14... | collective-permute-start | bytes 884744 | tf_op jit(solution)/shard_map/ppermute | solution.py:547
  39.5 9.2 %collective-permute-start.16 = (bf16[32,1024]{1,0:T(8,128)(2,1)S(1)}, bf16[32,1024]{1,0:T(8,128)(2,1)S(1)}, u32[]{:S(2)}, u32[]{:S(2)}) collective-permute-start(bf16[32,1024]{1,0:T(8,128)(2,1)S(1)} %get-tuple-element.61), channel_id=1, source_target_pairs={{0,7},{2,5},{4,3},{6,1},{7,0},{5,2},{3,4},{1,6},{8,15},{10,13},{12... | collective-permute-start | bytes 196616 | tf_op jit(solution)/shard_map/ppermute | solution.py:552
  42.0 6.7 %collective-permute-start.14 = (bf16[96,1024]{1,0:T(8,128)(2,1)S(1)}, bf16[96,1024]{1,0:T(8,128)(2,1)S(1)}, u32[]{:S(2)}, u32[]{:S(2)}) collective-permute-start(bf16[96,1024]{1,0:T(8,128)(2,1)S(1)} %pad_maximum_fusion), channel_id=1, source_target_pairs={{0,2},{2,4},{4,6},{6,7},{7,5},{5,3},{3,1},{1,0},{8,10},{10,12},{12... | collective-permute-start | bytes 589832 | tf_op jit(solution)/shard_map/ppermute | solution.py:560
  42.1 6.6 %collective-permute-start.15 = (bf16[80,1024]{1,0:T(8,128)(2,1)S(1)}, bf16[80,1024]{1,0:T(8,128)(2,1)S(1)}, u32[]{:S(2)}, u32[]{:S(2)}) collective-permute-start(bf16[80,1024]{1,0:T(8,128)(2,1)S(1)} %slice.50), channel_id=1, source_target_pairs={{2,0},{4,2},{6,4},{7,6},{5,7},{3,5},{1,3},{0,1},{10,8},{12,10},{14... | collective-permute-start | bytes 491528 | tf_op jit(solution)/shard_map/ppermute | solution.py:561
  44.3 4.4 %copy-start.2 = (bf16[1024,1024]{1,0:T(8,128)(2,1)S(1)}, bf16[1024,1024]{1,0:T(8,128)(2,1)}, u32[]{:S(2)}) copy-start(bf16[1024,1024]{1,0:T(8,128)(2,1)} %wo_ref.1) | copy-start | bytes 6291460
  48.7 11.1 %copy-start.4 = (f32[9,1024]{1,0:T(8,128)S(1)}, f32[9,1024]{1,0:T(8,128)}, u32[]{:S(2)}) copy-start(f32[9,1024]{1,0:T(8,128)} %weights_ref.3) | copy-start | bytes 110596
  52.1 6.8 %collective-permute-start.17 = (bf16[4,4,1024]{2,1,0:T(4,128)(2,1)S(1)}, bf16[4,4,1024]{2,1,0:T(4,128)(2,1)S(1)}, u32[]{:S(2)}, u32[]{:S(2)}) collective-permute-start(bf16[4,4,1024]{2,1,0:T(4,128)(2,1)S(1)} %get-tuple-element.69), channel_id=1, source_target_pairs={{1,2},{2,1},{3,4},{4,3},{5,6},{6,5},{7,0},{0,7},{9,10},{10,9},{11,... | collective-permute-start | bytes 98312 | tf_op jit(solution)/shard_map/ppermute | solution.py:427
  54.7 4.3 %collective-permute-start.18 = (bf16[4,4,1024]{2,1,0:T(4,128)(2,1)S(1)}, bf16[4,4,1024]{2,1,0:T(4,128)(2,1)S(1)}, u32[]{:S(2)}, u32[]{:S(2)}) collective-permute-start(bf16[4,4,1024]{2,1,0:T(4,128)(2,1)S(1)} %get-tuple-element.70), channel_id=1, source_target_pairs={{0,1},{1,0},{2,3},{3,2},{4,5},{5,4},{6,7},{7,6},{8,9},{9,8},{10,11... | collective-permute-start | bytes 98312 | tf_op jit(solution)/shard_map/ppermute | solution.py:427
  59.2 3.2 %collective-permute-start.20 = (bf16[44,1024]{1,0:T(8,128)(2,1)S(1)}, bf16[44,1024]{1,0:T(8,128)(2,1)S(1)}, u32[]{:S(2)}, u32[]{:S(2)}) collective-permute-start(bf16[44,1024]{1,0:T(8,128)(2,1)S(1)} %pad_maximum_fusion.2), channel_id=1, source_target_pairs={{0,24},{8,0},{16,8},{24,16},{1,25},{9,1},{17,9},{25,17},{2,26},{10... | collective-permute-start | bytes 270344 | tf_op jit(solution)/shard_map/ppermute | solution.py:39
  59.3 4.1 %collective-permute-start.19 = (bf16[44,1024]{1,0:T(8,128)(2,1)S(1)}, bf16[44,1024]{1,0:T(8,128)(2,1)S(1)}, u32[]{:S(2)}, u32[]{:S(2)}) collective-permute-start(bf16[44,1024]{1,0:T(8,128)(2,1)S(1)} %pad_maximum_fusion.1), channel_id=1, source_target_pairs={{0,8},{8,16},{16,24},{24,0},{1,9},{9,17},{17,25},{25,1},{2,10},{10... | collective-permute-start | bytes 270344 | tf_op jit(solution)/shard_map/ppermute | solution.py:39

commit v7 on v6

--- a/solution.py
+++ b/solution.py
@@ -73,6 +73,20 @@
     lax.fori_loop(0, part_ref.shape[0], tile, 0)
 
 
+def rows_kernel(field_ref, north_ref, south_ref, near_ref, flat_ref):
+    near_ref[...] = field_ref[...]
+    levels, columns, rows, width = field_ref.shape
+    count = levels * columns
+    for index in range(width // LANES):
+        lanes = slice(index * LANES, (index + 1) * LANES)
+        for level in range(levels):
+            for column in range(columns):
+                at = (level * columns + column) * rows
+                flat_ref[index, at : at + rows, :] = field_ref[level, column, :, lanes].astype(F32)
+        north_ref[:, lanes] = flat_ref[index, pl.ds(0, count, stride=rows), :].astype(BF16)
+        south_ref[:, lanes] = flat_ref[index, pl.ds(rows - 1, count, stride=rows), :].astype(BF16)
+
+
 def first_part_kernel(field_ref, weights_ref, part_ref, taps_ref):
     levels, columns, rows, _ = field_ref.shape
     load = lambda level, column, index, lanes: field_ref[level, column, :, lanes].astype(F32)
@@ -86,7 +100,9 @@
     copy.wait()
 
 
-def second_part_kernel(dims, field_ref, weights_ref, dense_ref, part_ref, taps_ref, attended_ref):
+def second_part_kernel(
+    dims, here_ref, field_ref, weights_ref, dense_ref, across_ref, pair_ref, part_ref, taps_ref, attended_ref
+):
     levels, columns, rows = dims
 
     def load(level, column, index, lanes):
@@ -94,6 +110,8 @@
         return field_ref[index, at : at + rows, :]
 
     conv_part(load, dims, weights_ref, part_ref, taps_ref)
+    for index in range(part_ref.shape[0]):
+        add_sides(index, dims, here_ref, across_ref, pair_ref, taps_ref, part_ref, levels * (columns - 2) * rows)
     for level in range(levels):
         for column in range(columns):
             at = place(dims, level, column)
@@ -129,11 +147,12 @@
     lanes = slice(index * LANES, (index + 1) * LANES)
     even = here_ref[2] > 0
     blank = jnp.zeros((1, LANES), F32)
+    pair = pair_ref[:, lanes].astype(F32)
+    across = across_ref[:, lanes].astype(F32)
+    both = jnp.where(even, across, pair), jnp.where(even, pair, across)
+    tall = pair.shape[0] // levels
     for level in range(levels):
-        pair = pair_ref[level, :, lanes].astype(F32)
-        across = across_ref[level, :, lanes].astype(F32)
-        west = jnp.where(even, across, pair)
-        east = jnp.where(even, pair, across)
+        west, east = (side[level * tall : (level + 1) * tall] for side in both)
         for side, b, order in ((west, 0, 0), (east, 2, 1)):
             if side.shape[0] == rows:
                 side = jnp.concatenate([blank, side, blank], axis=0)
@@ -161,7 +180,7 @@
 
 
 def inner_kernel(
-    dims, here_ref, part_ref, taps_ref, north_ref, south_ref, west_ref, east_ref,
+    dims, here_ref, part_ref, taps_ref, north_ref, south_ref, field_ref,
     stream_ref, normed_ref, across_ref, pair_ref, even_ref, full,
 ):
     levels, columns, rows = dims
@@ -180,14 +199,15 @@
     even = here_ref[2] > 0
     north = north_ref[...].astype(F32) * has_north
     south = south_ref[...].astype(F32) * has_south
-    for level in range(levels):
-        tall = []
-        for edge_ref, column in ((west_ref, 0), (east_ref, columns - 1)):
-            middle = edge_ref[level].astype(F32)
+    tall = []
+    for column in (0, columns - 1):
+        pieces = []
+        for level in range(levels):
             at = level * columns + column
-            tall.append(jnp.concatenate([north[at : at + 1], middle, south[at : at + 1]], axis=0))
-        across_ref[level] = jnp.where(even, tall[0], tall[1]).astype(BF16)
-        pair_ref[level] = jnp.where(even, tall[1], tall[0]).astype(BF16)
+            pieces += [north[at : at + 1], field_ref[level, column].astype(F32), south[at : at + 1]]
+        tall.append(jnp.concatenate(pieces, axis=0))
+    across_ref[...] = jnp.where(even, tall[0], tall[1]).astype(BF16)
+    pair_ref[...] = jnp.where(even, tall[1], tall[0]).astype(BF16)
 
 
 def edge_kernel(
@@ -212,14 +232,13 @@
     normalise(full, stream_ref, put)
 
 
-def second_kernel(dims, here_ref, part_ref, taps_ref, north_ref, south_ref, across_ref, pair_ref, mixed_ref, full):
+def second_kernel(dims, here_ref, part_ref, taps_ref, north_ref, south_ref, mixed_ref, full):
     levels, columns, rows = dims
     edge_at = levels * (columns - 2) * rows
     for index in range(part_ref.shape[0]):
         lanes = slice(index * LANES, (index + 1) * LANES)
         full[index] = part_ref[index]
         add_rows(index, dims, here_ref, north_ref, south_ref, taps_ref, full, 0, edge_at)
-        add_sides(index, dims, here_ref, across_ref, pair_ref, taps_ref, full, edge_at)
         for level in range(levels):
             for column in range(columns):
                 at = place(dims, level, column)
@@ -394,13 +413,12 @@
                 pieces += [after_ref[index, west_at : west_at + 1, :], inner]
                 pieces += [after_ref[index, west_at + rows : west_at + rows + 1, :]]
             out_ref[:, lanes] = jnp.concatenate(pieces, axis=0).astype(BF16)
-        for level in range(levels):
-            west_at = edge_at + level * 2 * rows
-            east_at = west_at + rows
-            west = after_ref[index, west_at : west_at + rows, :]
-            east = after_ref[index, east_at : east_at + rows, :]
-            across_ref[level, :, lanes] = jnp.where(here_ref[2] > 0, west, east).astype(BF16)
-            pair_ref[level, :, lanes] = jnp.where(here_ref[2] > 0, east, west).astype(BF16)
+        sides = []
+        for side in range(2):
+            places = [edge_at + (level * 2 + side) * rows for level in range(levels)]
+            sides.append(jnp.concatenate([after_ref[index, at : at + rows, :] for at in places], axis=0))
+        across_ref[:, lanes] = jnp.where(here_ref[2] > 0, sides[0], sides[1]).astype(BF16)
+        pair_ref[:, lanes] = jnp.where(here_ref[2] > 0, sides[1], sides[0]).astype(BF16)
 
 
 def shape(dims, kind):
@@ -427,14 +445,13 @@
     return lax.ppermute(value, "lon", pairs)
 
 
-def exchange(north_edge, south_edge, across, pair, even):
-    rows = across.shape[1]
+def exchange(north_edge, south_edge, across, pair, even, rows):
     across, pair = swap(across, 1), swap(pair, 0)
-    even = even[None] > 0
+    even = even > 0
     west, east = jnp.where(even, across, pair), jnp.where(even, pair, across)
 
     def row(edge, at):
-        return jnp.concatenate([edge, west[:, at], east[:, at]], axis=0)
+        return jnp.concatenate([edge, west[at::rows], east[at::rows]], axis=0)
 
     north = shift(row(south_edge, rows - 1), "lat", 1)
     south = shift(row(north_edge, 0), "lat", -1)
@@ -470,18 +487,23 @@
     full = lambda count: pltpu.VMEM((tiles, count, LANES), F32)
     flat = lambda count: shape((count, width), BF16)
     part_shape = (shape((tiles, tokens, LANES), F32), shape((tiles, 9, LANES), F32))
-    tall = shape((levels, rows + 2, width), BF16)
+    tall = flat(levels * (rows + 2))
     forward = [(order[i], order[(i + 1) % lon_total]) for i in range(lon_total)]
     backward = [(b, a) for a, b in forward]
 
-    north = shift(fields[:, :, rows - 1].reshape(levels * columns, width), "lat", 1)
-    south = shift(fields[:, :, 0].reshape(levels * columns, width), "lat", -1)
+    edge_rows = flat(levels * columns)
+    near = shape(fields.shape, BF16)
+    north_edge, south_edge, fields = call(
+        rows_kernel, (edge_rows, edge_rows, near), (), (fields,), [full(tokens)], "edge_rows", 1
+    )
+    north = shift(south_edge, "lat", 1)
+    south = shift(north_edge, "lat", -1)
     part = call(first_part_kernel, part_shape, (), (fields, conv_first), [], "conv_part", 1)
     stream_inner, normed_inner, across, pair, even = call(
         functools.partial(inner_kernel, dims),
         (flat(inner_tokens), flat(inner_tokens), tall, tall, shape((1, width), jnp.int32)),
         (here,),
-        (*part, north, south, fields[:, 0], fields[:, columns - 1]),
+        (*part, north, south, fields),
         [full(inner_tokens)],
         "conv_inner",
         1,
@@ -563,7 +585,7 @@
     slots = [last, last - 2, last, last - 1, last]
     sizes = [cut, edge_tokens, inner_tokens - cut, edge_tokens, edge_tokens]
 
-    row_edge, column_edge = flat(levels * columns), shape((levels, rows, width), BF16)
+    row_edge, column_edge = flat(levels * columns), flat(levels * rows)
     dense, after, *edges = call(
         functools.partial(last_kernel, factor, dims, slots, sizes),
         (shape((tokens, width), F32), part_shape[0], row_edge, row_edge, column_edge, column_edge),
@@ -573,18 +595,18 @@
         "attend_last",
         5,
     )
-    halo = exchange(*edges, even)
+    north, south, across, pair = exchange(*edges, even, rows)
     grid4 = shape(fields.shape, BF16)
     *part, attended = call(
         functools.partial(second_part_kernel, dims),
         (*part_shape, grid4),
-        (),
-        (after, conv_second, dense),
+        (here,),
+        (after, conv_second, dense, across, pair),
         [],
         "conv_part",
         2,
     )
-    mixed = call(functools.partial(second_kernel, dims), grid4, (here,), (*part, *halo), [full(tokens)], "conv_second", 2)
+    mixed = call(functools.partial(second_kernel, dims), grid4, (here,), (*part, north, south), [full(tokens)], "conv_second", 2)
     return attended.transpose(0, 2, 1, 3), mixed.transpose(0, 2, 1, 3)
 
 

time: 65.4 us -> 64.2 us (0.982)
  waiting for transfers between devices: 12.3 us -> 10.8 us
  local copies, waits for them, and re-layouts: 3.5 us -> 2.11 us
  starting transfers between devices: 23.9 us -> 25.2 us
  Pallas kernels: 23.6 us -> 24.3 us
    ppermute x8, starting transfers between devices: 4.93 us -> 6.95 us  [shift(): return lax.ppermute(x, axis, [(i, (i + by) % size) for i in range(size)])]
    ppermute x4, waiting for transfers between devices: 9.38 us -> 7.76 us  [swap(): return lax.ppermute(value, 'lon', pairs)]
    ppermute x2, waiting for transfers between devices: 0.99 us -> 0.01 us  [local(): ahead = lax.ppermute(ahead, 'lon', forward)]
    unnamed x19 -> x14, local copies, waits for them, and re-layouts: 2.93 us -> 1.97 us
    ppermute x8, waiting for transfers between devices: 1.92 us -> 2.75 us  [shift(): return lax.ppermute(x, axis, [(i, (i + by) % size) for i in range(size)])]
    pallas_call x9 -> x10, Pallas kernels: 23.1 us -> 23.9 us  [call(): pl.pallas_call(kernel, out_shape=out_shape, in_specs=[pl.BlockSpec(memory...]
    ppermute x4, starting transfers between devices: 7.72 us -> 7 us  [swap(): return lax.ppermute(value, 'lon', pairs)]
    ppermute x1, starting transfers between devices: 2.42 us -> 1.75 us  [local(): ahead = lax.ppermute(normed_inner, 'lon', forward)]
  transfers between devices with their start and end apart: 21 -> 21, of which waited for: 7 -> 6; matrix products, arithmetic and copies ran while one was open for 1% -> 0% of each run, Pallas kernels for 27% -> 28%
where the time goes in v7:
time: 64.2 us; the launch traced here: 64 us
  starting transfers between devices  25.2 us (39%)
  Pallas kernels  24.3 us (38%)
  waiting for transfers between devices  10.8 us (17%)
  local copies, waits for them, and re-layouts  2.11 us (3%)
  between operations  1.46 us (2%)
    pallas_call x10, Pallas kernels, call(): pl.pallas_call(kernel, out_shape=out_shape, in_specs=[pl.BlockSpec(memory...  23.9 us
    ppermute x4, waiting for transfers between devices, swap(): return lax.ppermute(value, 'lon', pairs)  7.76 us
    ppermute x4, starting transfers between devices, swap(): return lax.ppermute(value, 'lon', pairs)  7 us
    ppermute x8, starting transfers between devices, shift(): return lax.ppermute(x, axis, [(i, (i + by) % size) for i in range(size)])  6.95 us
    ppermute x2, starting transfers between devices, local(): behind = lax.ppermute(behind, 'lon', backward)  3.9 us
    ppermute x8, waiting for transfers between devices, shift(): return lax.ppermute(x, axis, [(i, (i + by) % size) for i in range(size)])  2.75 us
    ppermute x1, starting transfers between devices, local(): far_edge = lax.ppermute(handed, 'lon', opposite)  2.72 us
    ppermute x1, starting transfers between devices, local(): far_second = lax.ppermute(behind[cut:], 'lon', backward)  2.12 us
  transfers between devices with their start and end apart: 21, of which 6 were waited for; matrix products, arithmetic and copies ran while one was open for 0% of the time, Pallas kernels for 28%

profile of v7, /device:TPU:0, one launch (start us, length us, event | category | flops | bytes accessed | tf_op | source)
XLA Modules:
  0.0 64.0 jit_solution(12957405268855481784)
XLA Ops:
  0.6 1.0 %copy-done.2 = bf16[4,4,9,1024]{3,1,2,0:T(4,128)(2,1)S(1)} copy-done((bf16[4,4,9,1024]{3,1,2,0:T(4,128)(2,1)S(1)}, bf16[4,4,9,1024]{3,1,2,0:T(4,128)(2,1)}, u32[]{:S(2)}) %copy-start.2) | copy-done | bytes 294936
  1.6 0.1 edge_rows.1
  1.7 0.5 collective-permute-start
  2.2 2.0 %collective-permute-start.1 = (bf16[36,1024]{1,0:T(8,128)(2,1)S(1)}, bf16[36,1024]{1,0:T(8,128)(2,1)S(1)}, u32[]{:S(2)}, u32[]{:S(2)}) collective-permute-start(bf16[36,1024]{1,0:T(8,128)(2,1)S(1)} %get-tuple-element.44), channel_id=1, source_target_pairs={{0,24},{8,0},{16,8},{24,16},{1,25},{9,1},{17,9},{25,17},{2,26},{10... | collective-permute-start | bytes 221192 | tf_op jit(solution)/shard_map/ppermute | solution.py:39
  4.2 0.1 pad_add_fusion.here_ref
  4.3 1.0 %copy-done.3 = f32[9,1024]{1,0:T(8,128)S(1)} copy-done((f32[9,1024]{1,0:T(8,128)S(1)}, f32[9,1024]{1,0:T(8,128)}, u32[]{:S(2)}) %copy-start.3) | copy-done | bytes 36888
  5.3 0.9 %conv_part.2 = (f32[8,144,128]{2,1,0:T(8,128)S(1)}, f32[8,9,128]{2,1,0:T(8,128)S(1)}) custom-call(bf16[4,9,4,1024]{3,2,1,0:T(4,128)(2,1)S(1)} %get-tuple-element.40.field_ref, f32[9,1024]{1,0:T(8,128)S(1)} %copy-done.3), custom_call_target="tpu_custom_call" | custom-call | flops 1100000000 | tf_op jit(solution)/shard_map/conv_part/pallas_call | solution.py:429
  6.2 0.1 collective-permute-done.north_ref
  6.3 0.7 %collective-permute-done.1.south_ref = bf16[36,1024]{1,0:T(8,128)(2,1)S(1)} collective-permute-done((bf16[36,1024]{1,0:T(8,128)(2,1)S(1)}, bf16[36,1024]{1,0:T(8,128)(2,1)S(1)}, u32[]{:S(2)}, u32[]{:S(2)}) %collective-permute-start.1) | collective-permute-done | bytes 73760 | tf_op jit(solution)/shard_map/ppermute | solution.py:39
  7.0 1.0 %conv_inner.1 = (bf16[112,1024]{1,0:T(8,128)(2,1)S(1)}, bf16[112,1024]{1,0:T(8,128)(2,1)S(1)}, bf16[24,1024]{1,0:T(8,128)(2,1)S(1)}, bf16[24,1024]{1,0:T(8,128)(2,1)S(1)}, s32[1,1024]{1,0:T(1,128)S(1)}) custom-call(s32[4]{0:T(128)S(1)} %pad_add_fusion.here_ref, f32[8,144,128]{2,1,0:T(8,128)S(1)} %get-tuple-element.41.part_ref, ...), custom_call_target="tpu_custom_call" | custom-call | flops 1100000000 | tf_op jit(solution)/shard_map/conv_inner/pallas_call | solution.py:429
  8.0 0.0 copy-start.5
  8.0 0.0 copy-start.6
  8.0 1.7 %collective-permute-start.4 = (bf16[112,1024]{1,0:T(8,128)(2,1)S(1)}, bf16[112,1024]{1,0:T(8,128)(2,1)S(1)}, u32[]{:S(2)}, u32[]{:S(2)}) collective-permute-start(bf16[112,1024]{1,0:T(8,128)(2,1)S(1)} %get-tuple-element.47.inner_ref), channel_id=1, source_target_pairs={{0,2},{2,4},{4,6},{6,7},{7,5},{5,3},{3,1},{1,0},{8,10},{10,12},{12... | collective-permute-start | bytes 688136 | tf_op jit(solution)/shard_map/ppermute | solution.py:511
  9.8 0.3 collective-permute-start.5
  10.7 4.7 %collective-permute-start.2 = (bf16[24,1024]{1,0:T(8,128)(2,1)S(1)}, bf16[24,1024]{1,0:T(8,128)(2,1)S(1)}, u32[]{:S(2)}, u32[]{:S(2)}) collective-permute-start(bf16[24,1024]{1,0:T(8,128)(2,1)S(1)} %get-tuple-element.45), channel_id=1, source_target_pairs={{1,2},{2,1},{3,4},{4,3},{5,6},{6,5},{7,0},{0,7},{9,10},{10,9},{11,... | collective-permute-start | bytes 147464 | tf_op jit(solution)/shard_map/ppermute | solution.py:445
  15.5 0.0 collective-permute-start.3
  15.5 0.4 weights_near.1
  15.9 0.8 %collective-permute-start.8 = (bf16[112,1024]{1,0:T(8,128)(2,1)S(1)}, bf16[112,1024]{1,0:T(8,128)(2,1)S(1)}, u32[]{:S(2)}, u32[]{:S(2)}) collective-permute-start(bf16[112,1024]{1,0:T(8,128)(2,1)S(1)} %get-tuple-element.57), channel_id=1, source_target_pairs={{0,8},{8,16},{16,24},{24,0},{1,9},{9,17},{17,25},{25,1},{2,10},{10... | collective-permute-start | bytes 688136 | tf_op jit(solution)/shard_map/ppermute | solution.py:39
  16.8 3.4 %collective-permute-done.2.across_ref = bf16[24,1024]{1,0:T(8,128)(2,1)S(1)} collective-permute-done((bf16[24,1024]{1,0:T(8,128)(2,1)S(1)}, bf16[24,1024]{1,0:T(8,128)(2,1)S(1)}, u32[]{:S(2)}, u32[]{:S(2)}) %collective-permute-start.2) | collective-permute-done | bytes 49184 | tf_op jit(solution)/shard_map/ppermute | solution.py:445
  20.1 1.3 %collective-permute-start.9 = (bf16[112,1024]{1,0:T(8,128)(2,1)S(1)}, bf16[112,1024]{1,0:T(8,128)(2,1)S(1)}, u32[]{:S(2)}, u32[]{:S(2)}) collective-permute-start(bf16[112,1024]{1,0:T(8,128)(2,1)S(1)} %get-tuple-element.57), channel_id=1, source_target_pairs={{0,24},{8,0},{16,8},{24,16},{1,25},{9,1},{17,9},{25,17},{2,26},{10... | collective-permute-start | bytes 688136 | tf_op jit(solution)/shard_map/ppermute | solution.py:39
  21.4 0.0 collective-permute-done.3.pair_ref
  21.4 0.0 collective-permute-done.4.ahead_ref
  21.4 1.1 %conv_edge.1 = (bf16[32,1024]{1,0:T(8,128)(2,1)S(1)}, bf16[32,1024]{1,0:T(8,128)(2,1)S(1)}, bf16[144,1024]{1,0:T(8,128)(2,1)S(1)}, bf16[144,1024]{1,0:T(8,128)(2,1)S(1)}, bf16[144,1024]{1,0:T(8,128)(2,1)S(1)}) custom-call(s32[4]{0:T(128)S(1)} %pad_add_fusion.here_ref, f32[8,144,128]{2,1,0:T(8,128)S(1)} %get-tuple-element.41.part_ref, ...), custom_call_target="tpu_custom_call" | custom-call | flops 1100000000 | tf_op jit(solution)/shard_map/conv_edge/pallas_call | solution.py:429
  22.5 0.1 collective-permute-start.6
  22.5 2.0 %collective-permute-start.7 = (bf16[144,1024]{1,0:T(8,128)(2,1)S(1)}, bf16[144,1024]{1,0:T(8,128)(2,1)S(1)}, u32[]{:S(2)}, u32[]{:S(2)}) collective-permute-start(bf16[144,1024]{1,0:T(8,128)(2,1)S(1)} %get-tuple-element.56), channel_id=1, source_target_pairs={{2,0},{4,2},{6,4},{7,6},{5,7},{3,5},{1,3},{0,1},{10,8},{12,10},{14... | collective-permute-start | bytes 884744 | tf_op jit(solution)/shard_map/ppermute | solution.py:569
  24.5 4.5 %own_block.1 = (bf16[32,1024]{1,0:T(8,128)(2,1)S(1)}, bf16[8,288,128]{2,1,0:T(8,128)(2,1)S(1)}, f32[144,1024]{1,0:T(8,128)S(1)}, f32[144,1024]{1,0:T(8,128)S(1)}, f32[144,1024]{1,0:T(8,128)S(1)}) custom-call(s32[4]{0:T(128)S(1)} %pad_add_fusion.here_ref, s32[8,8]{1,0:T(8,128)S(1)} %copy-done.6, s32[1,1,8]{2,1,0:T(1,128)S(1)} %copy-done.5, ...), custom_call_target="tpu_custom_call" | custom-call | flops 4400000000 | tf_op jit(solution)/shard_map/own_block/pallas_call | solution.py:429
  29.1 0.1 collective-permute-start.12
  29.1 0.0 collective-permute-done.8.refs_2_
  29.1 1.7 %collective-permute-start.13 = (bf16[32,1024]{1,0:T(8,128)(2,1)S(1)}, bf16[32,1024]{1,0:T(8,128)(2,1)S(1)}, u32[]{:S(2)}, u32[]{:S(2)}) collective-permute-start(bf16[32,1024]{1,0:T(8,128)(2,1)S(1)} %get-tuple-element.61), channel_id=1, source_target_pairs={{0,24},{8,0},{16,8},{24,16},{1,25},{9,1},{17,9},{25,17},{2,26},{10... | collective-permute-start | bytes 196616 | tf_op jit(solution)/shard_map/ppermute | solution.py:39
  30.9 0.0 collective-permute-done.6.refs_0_
  30.9 0.1 collective-permute-start.10
  31.0 1.9 %collective-permute-start.11 = (bf16[144,1024]{1,0:T(8,128)(2,1)S(1)}, bf16[144,1024]{1,0:T(8,128)(2,1)S(1)}, u32[]{:S(2)}, u32[]{:S(2)}) collective-permute-start(bf16[144,1024]{1,0:T(8,128)(2,1)S(1)} %collective-permute-done.7.refs_1_), channel_id=1, source_target_pairs={{2,0},{4,2},{6,4},{7,6},{5,7},{3,5},{1,3},{0,1},{10,8},{12,10},{14... | collective-permute-start | bytes 884744 | tf_op jit(solution)/shard_map/ppermute | solution.py:569
  32.9 4.6 %attend_batch.2 = (f32[144,1024]{1,0:T(8,128)S(1)}, f32[144,1024]{1,0:T(8,128)S(1)}, f32[144,1024]{1,0:T(8,128)S(1)}, bf16[32,1024]{1,0:T(8,128)(2,1)S(1)}) custom-call(s32[4]{0:T(128)S(1)} %pad_add_fusion.here_ref, s32[8,8]{1,0:T(8,128)S(1)} %copy-done.6, s32[1,1,8]{2,1,0:T(1,128)S(1)} %copy-done.5, s32[1,1]{1,0:T(1,128)S(6)} %copy.10.count_ref, ...), custom_call_target="tpu_custom_call" | custom-call | flops 6380000256 | tf_op jit(solution)/shard_map/attend_batch/pallas_call | solution.py:429
  37.5 2.7 %collective-permute-start.16 = (bf16[32,1024]{1,0:T(8,128)(2,1)S(1)}, bf16[32,1024]{1,0:T(8,128)(2,1)S(1)}, u32[]{:S(2)}, u32[]{:S(2)}) collective-permute-start(bf16[32,1024]{1,0:T(8,128)(2,1)S(1)} %get-tuple-element.67), channel_id=1, source_target_pairs={{0,7},{2,5},{4,3},{6,1},{7,0},{5,2},{3,4},{1,6},{8,15},{10,13},{12... | collective-permute-start | bytes 196616 | tf_op jit(solution)/shard_map/ppermute | solution.py:574
  40.3 0.2 collective-permute-start.14
  40.5 2.1 %collective-permute-start.15 = (bf16[80,1024]{1,0:T(8,128)(2,1)S(1)}, bf16[80,1024]{1,0:T(8,128)(2,1)S(1)}, u32[]{:S(2)}, u32[]{:S(2)}) collective-permute-start(bf16[80,1024]{1,0:T(8,128)(2,1)S(1)} %slice.30), channel_id=1, source_target_pairs={{2,0},{4,2},{6,4},{7,6},{5,7},{3,5},{1,3},{0,1},{10,8},{12,10},{14... | collective-permute-start | bytes 491528 | tf_op jit(solution)/shard_map/ppermute | solution.py:583
  42.6 0.0 collective-permute-done.13.refs_3_
  42.7 4.4 %attend_batch.3 = (f32[144,1024]{1,0:T(8,128)S(1)}, f32[144,1024]{1,0:T(8,128)S(1)}, f32[144,1024]{1,0:T(8,128)S(1)}, bf16[32,1024]{1,0:T(8,128)(2,1)}) custom-call(s32[4]{0:T(128)S(1)} %pad_add_fusion.here_ref, s32[8,8]{1,0:T(8,128)S(1)} %copy-done.6, s32[1,1,8]{2,1,0:T(1,128)S(1)} %copy-done.5, s32[1,1]{1,0:T(1,128)S(6)} %copy.10.count_ref, ...), custom_call_target="tpu_custom_call" | custom-call | flops 6380000256 | tf_op jit(solution)/shard_map/attend_batch/pallas_call | solution.py:429
  47.1 0.0 collective-permute-done.16.refs_2_
  47.1 0.2 collective-permute-done.14.refs_0_
  47.3 3.4 %attend_last.1 = (f32[144,1024]{1,0:T(8,128)S(1)}, f32[8,144,128]{2,1,0:T(8,128)S(1)}, bf16[36,1024]{1,0:T(8,128)(2,1)S(1)}, bf16[36,1024]{1,0:T(8,128)(2,1)S(1)...) custom-call(s32[4]{0:T(128)S(1)} %pad_add_fusion.here_ref, s32[8,8]{1,0:T(8,128)S(1)} %copy-done.6, ...), custom_call_target="tpu_custom_call" | custom-call | flops 5500000256 | tf_op jit(solution)/shard_map/attend_last/pallas_call | solution.py:429
  50.7 2.3 %collective-permute-start.17 = (bf16[16,1024]{1,0:T(8,128)(2,1)S(1)}, bf16[16,1024]{1,0:T(8,128)(2,1)S(1)}, u32[]{:S(2)}, u32[]{:S(2)}) collective-permute-start(bf16[16,1024]{1,0:T(8,128)(2,1)S(1)} %get-tuple-element.70), channel_id=1, source_target_pairs={{1,2},{2,1},{3,4},{4,3},{5,6},{6,5},{7,0},{0,7},{9,10},{10,9},{11,... | collective-permute-start | bytes 98312 | tf_op jit(solution)/shard_map/ppermute | solution.py:445
  53.0 4.4 %collective-permute-done.17.across_ref = bf16[16,1024]{1,0:T(8,128)(2,1)S(1)} collective-permute-done((bf16[16,1024]{1,0:T(8,128)(2,1)S(1)}, bf16[16,1024]{1,0:T(8,128)(2,1)S(1)}, u32[]{:S(2)}, u32[]{:S(2)}) %collective-permute-start.17) | collective-permute-done | bytes 32800 | tf_op jit(solution)/shard_map/ppermute | solution.py:445
  57.5 0.1 collective-permute-start.20
  57.6 0.5 collective-permute-start.19
  58.2 2.2 %conv_part.3 = (f32[8,144,128]{2,1,0:T(8,128)S(1)}, f32[8,9,128]{2,1,0:T(8,128)S(1)}, bf16[4,9,4,1024]{3,2,1,0:T(4,128)(2,1)}) custom-call(s32[4]{0:T(128)S(1)} %pad_add_fusion.here_ref, f32[8,144,128]{2,1,0:T(8,128)S(1)} %get-tuple-element.68.field_ref, f32[9,1024]{1,0:T(8,128)S(1)} %copy-done.4, f32[144,1024]{1,0:T(8,128)S(1)} %get-tuple-element.69.dense_ref, ...), custom_call_target="tpu_custom_call" | custom-call | flops 2200000000 | tf_op jit(solution)/shard_map/conv_part/pallas_call | solution.py:429
  60.4 2.0 %collective-permute-done.19.north_ref = bf16[44,1024]{1,0:T(8,128)(2,1)S(1)} collective-permute-done((bf16[44,1024]{1,0:T(8,128)(2,1)S(1)}, bf16[44,1024]{1,0:T(8,128)(2,1)S(1)}, u32[]{:S(2)}, u32[]{:S(2)}) %collective-permute-start.19) | collective-permute-done | bytes 90144 | tf_op jit(solution)/shard_map/ppermute | solution.py:39
  62.3 1.6 %conv_second.1 = bf16[4,9,4,1024]{3,2,1,0:T(4,128)(2,1)} custom-call(s32[4]{0:T(128)S(1)} %pad_add_fusion.here_ref, f32[8,144,128]{2,1,0:T(8,128)S(1)} %get-tuple-element.73.part_ref, f32[8,9,128]{2,1,0:T(8,128)S(1)} %get-tuple-element.74.taps_ref, bf16[44,1024]{1,0:T(8,128)(2,1)S(1)} %collective-permute-done.19.north_ref, ...), custom_call_target="tpu_custom_call" | custom-call | flops 2200000000 | tf_op jit(solution)/shard_map/conv_second/pallas_call | solution.py:429
  (32 shorter events, 0.3 us)
Async XLA Ops:
  0.6 1.0 %copy-start.2 = (bf16[4,4,9,1024]{3,1,2,0:T(4,128)(2,1)S(1)}, bf16[4,4,9,1024]{3,1,2,0:T(4,128)(2,1)}, u32[]{:S(2)}) copy-start(bf16[4,4,9,1024]{3,1,2,0:T(4,128)(2,1)} %param.8) | copy-start | bytes 884740
  1.7 4.6 %collective-permute-start = (bf16[36,1024]{1,0:T(8,128)(2,1)S(1)}, bf16[36,1024]{1,0:T(8,128)(2,1)S(1)}, u32[]{:S(2)}, u32[]{:S(2)}) collective-permute-start(bf16[36,1024]{1,0:T(8,128)(2,1)S(1)} %get-tuple-element.43), channel_id=1, source_target_pairs={{0,8},{8,16},{16,24},{24,0},{1,9},{9,17},{17,25},{25,1},{2,10},{10... | collective-permute-start | bytes 221192 | tf_op jit(solution)/shard_map/ppermute | solution.py:39
  2.2 4.7 %collective-permute-start.1 = (bf16[36,1024]{1,0:T(8,128)(2,1)S(1)}, bf16[36,1024]{1,0:T(8,128)(2,1)S(1)}, u32[]{:S(2)}, u32[]{:S(2)}) collective-permute-start(bf16[36,1024]{1,0:T(8,128)(2,1)S(1)} %get-tuple-element.44), channel_id=1, source_target_pairs={{0,24},{8,0},{16,8},{24,16},{1,25},{9,1},{17,9},{25,17},{2,26},{10... | collective-permute-start | bytes 221192 | tf_op jit(solution)/shard_map/ppermute | solution.py:39
  4.2 11.3 %copy-start = (bf16[1024,3072]{1,0:T(8,128)(2,1)S(1)}, bf16[1024,3072]{1,0:T(8,128)(2,1)}, u32[]{:S(2)}) copy-start(bf16[1024,3072]{1,0:T(8,128)(2,1)} %far_ref.1) | copy-start | bytes 18874372
  4.3 1.0 %copy-start.3 = (f32[9,1024]{1,0:T(8,128)S(1)}, f32[9,1024]{1,0:T(8,128)}, u32[]{:S(2)}) copy-start(f32[9,1024]{1,0:T(8,128)} %weights_ref.2) | copy-start | bytes 110596
  8.0 16.6 %copy-start.5 = (s32[1,1,8]{2,1,0:T(1,128)S(1)}, s32[1,1,8]{2,1,0:T(1,128)}, u32[]{:S(2)}) copy-start(s32[1,1,8]{2,1,0:T(1,128)} %list_ref.7) | copy-start | bytes 100
  8.0 16.6 %copy-start.6 = (s32[8,8]{1,0:T(8,128)S(1)}, s32[8,8]{1,0:T(8,128)}, u32[]{:S(2)}) copy-start(s32[8,8]{1,0:T(8,128)} %constant.27.clone.sources_ref) | copy-start | bytes 772
  8.0 13.4 %collective-permute-start.4 = (bf16[112,1024]{1,0:T(8,128)(2,1)S(1)}, bf16[112,1024]{1,0:T(8,128)(2,1)S(1)}, u32[]{:S(2)}, u32[]{:S(2)}) collective-permute-start(bf16[112,1024]{1,0:T(8,128)(2,1)S(1)} %get-tuple-element.47.inner_ref), channel_id=1, source_target_pairs={{0,2},{2,4},{4,6},{6,7},{7,5},{5,3},{3,1},{1,0},{8,10},{10,12},{12... | collective-permute-start | bytes 688136 | tf_op jit(solution)/shard_map/ppermute | solution.py:511
  9.8 11.6 %collective-permute-start.5 = (bf16[112,1024]{1,0:T(8,128)(2,1)S(1)}, bf16[112,1024]{1,0:T(8,128)(2,1)S(1)}, u32[]{:S(2)}, u32[]{:S(2)}) collective-permute-start(bf16[112,1024]{1,0:T(8,128)(2,1)S(1)} %get-tuple-element.47.inner_ref), channel_id=1, source_target_pairs={{2,0},{4,2},{6,4},{7,6},{5,7},{3,5},{1,3},{0,1},{10,8},{12,10},{14... | collective-permute-start | bytes 688136 | tf_op jit(solution)/shard_map/ppermute | solution.py:512
  10.7 9.4 %collective-permute-start.2 = (bf16[24,1024]{1,0:T(8,128)(2,1)S(1)}, bf16[24,1024]{1,0:T(8,128)(2,1)S(1)}, u32[]{:S(2)}, u32[]{:S(2)}) collective-permute-start(bf16[24,1024]{1,0:T(8,128)(2,1)S(1)} %get-tuple-element.45), channel_id=1, source_target_pairs={{1,2},{2,1},{3,4},{4,3},{5,6},{6,5},{7,0},{0,7},{9,10},{10,9},{11,... | collective-permute-start | bytes 147464 | tf_op jit(solution)/shard_map/ppermute | solution.py:445
  15.5 5.9 %collective-permute-start.3 = (bf16[24,1024]{1,0:T(8,128)(2,1)S(1)}, bf16[24,1024]{1,0:T(8,128)(2,1)S(1)}, u32[]{:S(2)}, u32[]{:S(2)}) collective-permute-start(bf16[24,1024]{1,0:T(8,128)(2,1)S(1)} %get-tuple-element.46), channel_id=1, source_target_pairs={{0,1},{1,0},{2,3},{3,2},{4,5},{5,4},{6,7},{7,6},{8,9},{9,8},{10,11... | collective-permute-start | bytes 147464 | tf_op jit(solution)/shard_map/ppermute | solution.py:445
  15.9 13.2 %collective-permute-start.8 = (bf16[112,1024]{1,0:T(8,128)(2,1)S(1)}, bf16[112,1024]{1,0:T(8,128)(2,1)S(1)}, u32[]{:S(2)}, u32[]{:S(2)}) collective-permute-start(bf16[112,1024]{1,0:T(8,128)(2,1)S(1)} %get-tuple-element.57), channel_id=1, source_target_pairs={{0,8},{8,16},{16,24},{24,0},{1,9},{9,17},{17,25},{25,1},{2,10},{10... | collective-permute-start | bytes 688136 | tf_op jit(solution)/shard_map/ppermute | solution.py:39
  20.1 12.8 %collective-permute-start.9 = (bf16[112,1024]{1,0:T(8,128)(2,1)S(1)}, bf16[112,1024]{1,0:T(8,128)(2,1)S(1)}, u32[]{:S(2)}, u32[]{:S(2)}) collective-permute-start(bf16[112,1024]{1,0:T(8,128)(2,1)S(1)} %get-tuple-element.57), channel_id=1, source_target_pairs={{0,24},{8,0},{16,8},{24,16},{1,25},{9,1},{17,9},{25,17},{2,26},{10... | collective-permute-start | bytes 688136 | tf_op jit(solution)/shard_map/ppermute | solution.py:39
  22.5 8.4 %collective-permute-start.6 = (bf16[144,1024]{1,0:T(8,128)(2,1)S(1)}, bf16[144,1024]{1,0:T(8,128)(2,1)S(1)}, u32[]{:S(2)}, u32[]{:S(2)}) collective-permute-start(bf16[144,1024]{1,0:T(8,128)(2,1)S(1)} %get-tuple-element.55), channel_id=1, source_target_pairs={{0,2},{2,4},{4,6},{6,7},{7,5},{5,3},{3,1},{1,0},{8,10},{10,12},{12... | collective-permute-start | bytes 884744 | tf_op jit(solution)/shard_map/ppermute | solution.py:568
  22.5 8.5 %collective-permute-start.7 = (bf16[144,1024]{1,0:T(8,128)(2,1)S(1)}, bf16[144,1024]{1,0:T(8,128)(2,1)S(1)}, u32[]{:S(2)}, u32[]{:S(2)}) collective-permute-start(bf16[144,1024]{1,0:T(8,128)(2,1)S(1)} %get-tuple-element.56), channel_id=1, source_target_pairs={{2,0},{4,2},{6,4},{7,6},{5,7},{3,5},{1,3},{0,1},{10,8},{12,10},{14... | collective-permute-start | bytes 884744 | tf_op jit(solution)/shard_map/ppermute | solution.py:569
  29.1 13.6 %collective-permute-start.12 = (bf16[32,1024]{1,0:T(8,128)(2,1)S(1)}, bf16[32,1024]{1,0:T(8,128)(2,1)S(1)}, u32[]{:S(2)}, u32[]{:S(2)}) collective-permute-start(bf16[32,1024]{1,0:T(8,128)(2,1)S(1)} %get-tuple-element.61), channel_id=1, source_target_pairs={{0,8},{8,16},{16,24},{24,0},{1,9},{9,17},{17,25},{25,1},{2,10},{10... | collective-permute-start | bytes 196616 | tf_op jit(solution)/shard_map/ppermute | solution.py:39
  29.1 13.5 %collective-permute-start.13 = (bf16[32,1024]{1,0:T(8,128)(2,1)S(1)}, bf16[32,1024]{1,0:T(8,128)(2,1)S(1)}, u32[]{:S(2)}, u32[]{:S(2)}) collective-permute-start(bf16[32,1024]{1,0:T(8,128)(2,1)S(1)} %get-tuple-element.61), channel_id=1, source_target_pairs={{0,24},{8,0},{16,8},{24,16},{1,25},{9,1},{17,9},{25,17},{2,26},{10... | collective-permute-start | bytes 196616 | tf_op jit(solution)/shard_map/ppermute | solution.py:39
  30.9 9.4 %collective-permute-start.10 = (bf16[144,1024]{1,0:T(8,128)(2,1)S(1)}, bf16[144,1024]{1,0:T(8,128)(2,1)S(1)}, u32[]{:S(2)}, u32[]{:S(2)}) collective-permute-start(bf16[144,1024]{1,0:T(8,128)(2,1)S(1)} %collective-permute-done.6.refs_0_), channel_id=1, source_target_pairs={{0,2},{2,4},{4,6},{6,7},{7,5},{5,3},{3,1},{1,0},{8,10},{10,12},{12... | collective-permute-start | bytes 884744 | tf_op jit(solution)/shard_map/ppermute | solution.py:568
  31.0 9.5 %collective-permute-start.11 = (bf16[144,1024]{1,0:T(8,128)(2,1)S(1)}, bf16[144,1024]{1,0:T(8,128)(2,1)S(1)}, u32[]{:S(2)}, u32[]{:S(2)}) collective-permute-start(bf16[144,1024]{1,0:T(8,128)(2,1)S(1)} %collective-permute-done.7.refs_1_), channel_id=1, source_target_pairs={{2,0},{4,2},{6,4},{7,6},{5,7},{3,5},{1,3},{0,1},{10,8},{12,10},{14... | collective-permute-start | bytes 884744 | tf_op jit(solution)/shard_map/ppermute | solution.py:569
  37.5 9.6 %collective-permute-start.16 = (bf16[32,1024]{1,0:T(8,128)(2,1)S(1)}, bf16[32,1024]{1,0:T(8,128)(2,1)S(1)}, u32[]{:S(2)}, u32[]{:S(2)}) collective-permute-start(bf16[32,1024]{1,0:T(8,128)(2,1)S(1)} %get-tuple-element.67), channel_id=1, source_target_pairs={{0,7},{2,5},{4,3},{6,1},{7,0},{5,2},{3,4},{1,6},{8,15},{10,13},{12... | collective-permute-start | bytes 196616 | tf_op jit(solution)/shard_map/ppermute | solution.py:574
  40.3 7.0 %collective-permute-start.14 = (bf16[96,1024]{1,0:T(8,128)(2,1)S(1)}, bf16[96,1024]{1,0:T(8,128)(2,1)S(1)}, u32[]{:S(2)}, u32[]{:S(2)}) collective-permute-start(bf16[96,1024]{1,0:T(8,128)(2,1)S(1)} %pad_maximum_fusion), channel_id=1, source_target_pairs={{0,2},{2,4},{4,6},{6,7},{7,5},{5,3},{3,1},{1,0},{8,10},{10,12},{12... | collective-permute-start | bytes 589832 | tf_op jit(solution)/shard_map/ppermute | solution.py:582
  40.5 6.6 %collective-permute-start.15 = (bf16[80,1024]{1,0:T(8,128)(2,1)S(1)}, bf16[80,1024]{1,0:T(8,128)(2,1)S(1)}, u32[]{:S(2)}, u32[]{:S(2)}) collective-permute-start(bf16[80,1024]{1,0:T(8,128)(2,1)S(1)} %slice.30), channel_id=1, source_target_pairs={{2,0},{4,2},{6,4},{7,6},{5,7},{3,5},{1,3},{0,1},{10,8},{12,10},{14... | collective-permute-start | bytes 491528 | tf_op jit(solution)/shard_map/ppermute | solution.py:583
  42.6 4.7 %copy-start.1 = (bf16[1024,1024]{1,0:T(8,128)(2,1)S(1)}, bf16[1024,1024]{1,0:T(8,128)(2,1)}, u32[]{:S(2)}) copy-start(bf16[1024,1024]{1,0:T(8,128)(2,1)} %wo_ref.1) | copy-start | bytes 6291460
  47.3 10.8 %copy-start.4 = (f32[9,1024]{1,0:T(8,128)S(1)}, f32[9,1024]{1,0:T(8,128)}, u32[]{:S(2)}) copy-start(f32[9,1024]{1,0:T(8,128)} %weights_ref.3) | copy-start | bytes 110596
  50.7 6.7 %collective-permute-start.17 = (bf16[16,1024]{1,0:T(8,128)(2,1)S(1)}, bf16[16,1024]{1,0:T(8,128)(2,1)S(1)}, u32[]{:S(2)}, u32[]{:S(2)}) collective-permute-start(bf16[16,1024]{1,0:T(8,128)(2,1)S(1)} %get-tuple-element.70), channel_id=1, source_target_pairs={{1,2},{2,1},{3,4},{4,3},{5,6},{6,5},{7,0},{0,7},{9,10},{10,9},{11,... | collective-permute-start | bytes 98312 | tf_op jit(solution)/shard_map/ppermute | solution.py:445
  53.0 4.4 %collective-permute-start.18 = (bf16[16,1024]{1,0:T(8,128)(2,1)S(1)}, bf16[16,1024]{1,0:T(8,128)(2,1)S(1)}, u32[]{:S(2)}, u32[]{:S(2)}) collective-permute-start(bf16[16,1024]{1,0:T(8,128)(2,1)S(1)} %get-tuple-element.71), channel_id=1, source_target_pairs={{0,1},{1,0},{2,3},{3,2},{4,5},{5,4},{6,7},{7,6},{8,9},{9,8},{10,11... | collective-permute-start | bytes 98312 | tf_op jit(solution)/shard_map/ppermute | solution.py:445
  57.5 2.8 %collective-permute-start.20 = (bf16[44,1024]{1,0:T(8,128)(2,1)S(1)}, bf16[44,1024]{1,0:T(8,128)(2,1)S(1)}, u32[]{:S(2)}, u32[]{:S(2)}) collective-permute-start(bf16[44,1024]{1,0:T(8,128)(2,1)S(1)} %pad_maximum_fusion.2), channel_id=1, source_target_pairs={{0,24},{8,0},{16,8},{24,16},{1,25},{9,1},{17,9},{25,17},{2,26},{10... | collective-permute-start | bytes 270344 | tf_op jit(solution)/shard_map/ppermute | solution.py:39
  57.6 4.7 %collective-permute-start.19 = (bf16[44,1024]{1,0:T(8,128)(2,1)S(1)}, bf16[44,1024]{1,0:T(8,128)(2,1)S(1)}, u32[]{:S(2)}, u32[]{:S(2)}) collective-permute-start(bf16[44,1024]{1,0:T(8,128)(2,1)S(1)} %pad_maximum_fusion.1), channel_id=1, source_target_pairs={{0,8},{8,16},{16,24},{24,0},{1,9},{9,17},{17,25},{25,1},{2,10},{10... | collective-permute-start | bytes 270344 | tf_op jit(solution)/shard_map/ppermute | solution.py:39

commit v8 on v7

--- a/solution.py
+++ b/solution.py
@@ -232,17 +232,24 @@
     normalise(full, stream_ref, put)
 
 
-def second_kernel(dims, here_ref, part_ref, taps_ref, north_ref, south_ref, mixed_ref, full):
+def second_kernel(dims, here_ref, part_ref, taps_ref, north_ref, south_ref, mixed_ref, full, near_ref, sent):
     levels, columns, rows = dims
     edge_at = levels * (columns - 2) * rows
-    for index in range(part_ref.shape[0]):
-        lanes = slice(index * LANES, (index + 1) * LANES)
+    tiles = part_ref.shape[0]
+    for index in range(tiles):
         full[index] = part_ref[index]
         add_rows(index, dims, here_ref, north_ref, south_ref, taps_ref, full, 0, edge_at)
-        for level in range(levels):
+    copies = []
+    for level in range(levels):
+        for index in range(tiles):
+            lanes = slice(index * LANES, (index + 1) * LANES)
             for column in range(columns):
                 at = place(dims, level, column)
-                mixed_ref[level, column, :, lanes] = full[index, at : at + rows, :].astype(BF16)
+                near_ref[level, column, :, lanes] = full[index, at : at + rows, :].astype(BF16)
+        copies.append(pltpu.make_async_copy(near_ref.at[level], mixed_ref.at[level], sent.at[level]))
+        copies[-1].start()
+    for copy in copies:
+        copy.wait()
 
 
 def scores_of(query2, keys2, bias):
@@ -606,7 +613,17 @@
         "conv_part",
         2,
     )
-    mixed = call(functools.partial(second_kernel, dims), grid4, (here,), (*part, north, south), [full(tokens)], "conv_second", 2)
+    vmem = pl.BlockSpec(memory_space=pltpu.VMEM)
+    mixed = pl.pallas_call(
+        functools.partial(second_kernel, dims),
+        out_shape=grid4,
+        in_specs=[pl.BlockSpec(memory_space=pltpu.SMEM)] + [vmem] * 4,
+        out_specs=pl.BlockSpec(memory_space=pl.ANY),
+        scratch_shapes=[full(tokens), pltpu.VMEM(grid4.shape, BF16), pltpu.SemaphoreType.DMA((levels,))],
+        compiler_params=pltpu.CompilerParams(vmem_limit_bytes=VMEM_LIMIT),
+        cost_estimate=pl.CostEstimate(flops=int(2e9), bytes_accessed=0, transcendentals=0),
+        name="conv_second",
+    )(here, *part, north, south)
     return attended.transpose(0, 2, 1, 3), mixed.transpose(0, 2, 1, 3)
 
 

time: 64.2 us -> 64.3 us (level)
    pallas_call x10 -> x9, Pallas kernels: 23.9 us -> 22.3 us  [call(): pl.pallas_call(kernel, out_shape=out_shape, in_specs=[pl.BlockSpec(memory...]
    pallas_call x0 -> x1, Pallas kernels: none -> 1.59 us  [local(): pl.pallas_call(functools.partial(second_kernel, dims), out_shape=grid4, i...]
where the time goes in v8:
time: 64.3 us; the launch traced here: 64.1 us
  starting transfers between devices  25.2 us (39%)
  Pallas kernels  24.3 us (38%)
  waiting for transfers between devices  10.8 us (17%)
  local copies, waits for them, and re-layouts  2.11 us (3%)
  between operations  1.62 us (3%)
    pallas_call x9, Pallas kernels, call(): pl.pallas_call(kernel, out_shape=out_shape, in_specs=[pl.BlockSpec(memory...  22.3 us
    ppermute x4, waiting for transfers between devices, swap(): return lax.ppermute(value, 'lon', pairs)  7.76 us
    ppermute x4, starting transfers between devices, swap(): return lax.ppermute(value, 'lon', pairs)  7 us
    ppermute x8, starting transfers between devices, shift(): return lax.ppermute(x, axis, [(i, (i + by) % size) for i in range(size)])  6.95 us
    ppermute x2, starting transfers between devices, local(): behind = lax.ppermute(behind, 'lon', backward)  3.9 us
    ppermute x8, waiting for transfers between devices, shift(): return lax.ppermute(x, axis, [(i, (i + by) % size) for i in range(size)])  2.75 us
    ppermute x1, starting transfers between devices, local(): far_edge = lax.ppermute(handed, 'lon', opposite)  2.72 us
    ppermute x1, starting transfers between devices, local(): far_second = lax.ppermute(behind[cut:], 'lon', backward)  2.12 us
  transfers between devices with their start and end apart: 21, of which 6 were waited for; matrix products, arithmetic and copies ran while one was open for 0% of the time, Pallas kernels for 28%

profile of v8, /device:TPU:0, one launch (start us, length us, event | category | flops | bytes accessed | tf_op | source)
XLA Modules:
  0.0 64.1 jit_solution(17288270564057863178)
XLA Ops:
  0.6 1.0 %copy-done.2 = bf16[4,4,9,1024]{3,1,2,0:T(4,128)(2,1)S(1)} copy-done((bf16[4,4,9,1024]{3,1,2,0:T(4,128)(2,1)S(1)}, bf16[4,4,9,1024]{3,1,2,0:T(4,128)(2,1)}, u32[]{:S(2)}) %copy-start.2) | copy-done | bytes 294936
  1.6 0.1 edge_rows.1
  1.7 0.5 collective-permute-start
  2.2 2.0 %collective-permute-start.1 = (bf16[36,1024]{1,0:T(8,128)(2,1)S(1)}, bf16[36,1024]{1,0:T(8,128)(2,1)S(1)}, u32[]{:S(2)}, u32[]{:S(2)}) collective-permute-start(bf16[36,1024]{1,0:T(8,128)(2,1)S(1)} %get-tuple-element.44), channel_id=1, source_target_pairs={{0,24},{8,0},{16,8},{24,16},{1,25},{9,1},{17,9},{25,17},{2,26},{10... | collective-permute-start | bytes 221192 | tf_op jit(solution)/shard_map/ppermute | solution.py:39
  4.2 0.1 pad_add_fusion.here_ref
  4.3 1.0 %copy-done.3 = f32[9,1024]{1,0:T(8,128)S(1)} copy-done((f32[9,1024]{1,0:T(8,128)S(1)}, f32[9,1024]{1,0:T(8,128)}, u32[]{:S(2)}) %copy-start.3) | copy-done | bytes 36888
  5.3 0.9 %conv_part.2 = (f32[8,144,128]{2,1,0:T(8,128)S(1)}, f32[8,9,128]{2,1,0:T(8,128)S(1)}) custom-call(bf16[4,9,4,1024]{3,2,1,0:T(4,128)(2,1)S(1)} %get-tuple-element.40.field_ref, f32[9,1024]{1,0:T(8,128)S(1)} %copy-done.3), custom_call_target="tpu_custom_call" | custom-call | flops 1100000000 | tf_op jit(solution)/shard_map/conv_part/pallas_call | solution.py:436
  6.2 0.1 collective-permute-done.north_ref
  6.3 0.7 %collective-permute-done.1.south_ref = bf16[36,1024]{1,0:T(8,128)(2,1)S(1)} collective-permute-done((bf16[36,1024]{1,0:T(8,128)(2,1)S(1)}, bf16[36,1024]{1,0:T(8,128)(2,1)S(1)}, u32[]{:S(2)}, u32[]{:S(2)}) %collective-permute-start.1) | collective-permute-done | bytes 73760 | tf_op jit(solution)/shard_map/ppermute | solution.py:39
  7.0 1.0 %conv_inner.1 = (bf16[112,1024]{1,0:T(8,128)(2,1)S(1)}, bf16[112,1024]{1,0:T(8,128)(2,1)S(1)}, bf16[24,1024]{1,0:T(8,128)(2,1)S(1)}, bf16[24,1024]{1,0:T(8,128)(2,1)S(1)}, s32[1,1024]{1,0:T(1,128)S(1)}) custom-call(s32[4]{0:T(128)S(1)} %pad_add_fusion.here_ref, f32[8,144,128]{2,1,0:T(8,128)S(1)} %get-tuple-element.41.part_ref, ...), custom_call_target="tpu_custom_call" | custom-call | flops 1100000000 | tf_op jit(solution)/shard_map/conv_inner/pallas_call | solution.py:436
  8.0 0.0 copy-start.5
  8.0 0.0 copy-start.6
  8.0 1.7 %collective-permute-start.4 = (bf16[112,1024]{1,0:T(8,128)(2,1)S(1)}, bf16[112,1024]{1,0:T(8,128)(2,1)S(1)}, u32[]{:S(2)}, u32[]{:S(2)}) collective-permute-start(bf16[112,1024]{1,0:T(8,128)(2,1)S(1)} %get-tuple-element.47.inner_ref), channel_id=1, source_target_pairs={{0,2},{2,4},{4,6},{6,7},{7,5},{5,3},{3,1},{1,0},{8,10},{10,12},{12... | collective-permute-start | bytes 688136 | tf_op jit(solution)/shard_map/ppermute | solution.py:518
  9.8 0.3 collective-permute-start.5
  10.7 4.7 %collective-permute-start.2 = (bf16[24,1024]{1,0:T(8,128)(2,1)S(1)}, bf16[24,1024]{1,0:T(8,128)(2,1)S(1)}, u32[]{:S(2)}, u32[]{:S(2)}) collective-permute-start(bf16[24,1024]{1,0:T(8,128)(2,1)S(1)} %get-tuple-element.45), channel_id=1, source_target_pairs={{1,2},{2,1},{3,4},{4,3},{5,6},{6,5},{7,0},{0,7},{9,10},{10,9},{11,... | collective-permute-start | bytes 147464 | tf_op jit(solution)/shard_map/ppermute | solution.py:452
  15.5 0.0 collective-permute-start.3
  15.5 0.4 weights_near.1
  15.9 0.8 %collective-permute-start.8 = (bf16[112,1024]{1,0:T(8,128)(2,1)S(1)}, bf16[112,1024]{1,0:T(8,128)(2,1)S(1)}, u32[]{:S(2)}, u32[]{:S(2)}) collective-permute-start(bf16[112,1024]{1,0:T(8,128)(2,1)S(1)} %get-tuple-element.57), channel_id=1, source_target_pairs={{0,8},{8,16},{16,24},{24,0},{1,9},{9,17},{17,25},{25,1},{2,10},{10... | collective-permute-start | bytes 688136 | tf_op jit(solution)/shard_map/ppermute | solution.py:39
  16.8 3.4 %collective-permute-done.2.across_ref = bf16[24,1024]{1,0:T(8,128)(2,1)S(1)} collective-permute-done((bf16[24,1024]{1,0:T(8,128)(2,1)S(1)}, bf16[24,1024]{1,0:T(8,128)(2,1)S(1)}, u32[]{:S(2)}, u32[]{:S(2)}) %collective-permute-start.2) | collective-permute-done | bytes 49184 | tf_op jit(solution)/shard_map/ppermute | solution.py:452
  20.1 1.3 %collective-permute-start.9 = (bf16[112,1024]{1,0:T(8,128)(2,1)S(1)}, bf16[112,1024]{1,0:T(8,128)(2,1)S(1)}, u32[]{:S(2)}, u32[]{:S(2)}) collective-permute-start(bf16[112,1024]{1,0:T(8,128)(2,1)S(1)} %get-tuple-element.57), channel_id=1, source_target_pairs={{0,24},{8,0},{16,8},{24,16},{1,25},{9,1},{17,9},{25,17},{2,26},{10... | collective-permute-start | bytes 688136 | tf_op jit(solution)/shard_map/ppermute | solution.py:39
  21.4 0.0 collective-permute-done.4.ahead_ref
  21.4 0.0 collective-permute-done.5.behind_ref
  21.4 1.1 %conv_edge.1 = (bf16[32,1024]{1,0:T(8,128)(2,1)S(1)}, bf16[32,1024]{1,0:T(8,128)(2,1)S(1)}, bf16[144,1024]{1,0:T(8,128)(2,1)S(1)}, bf16[144,1024]{1,0:T(8,128)(2,1)S(1)}, bf16[144,1024]{1,0:T(8,128)(2,1)S(1)}) custom-call(s32[4]{0:T(128)S(1)} %pad_add_fusion.here_ref, f32[8,144,128]{2,1,0:T(8,128)S(1)} %get-tuple-element.41.part_ref, ...), custom_call_target="tpu_custom_call" | custom-call | flops 1100000000 | tf_op jit(solution)/shard_map/conv_edge/pallas_call | solution.py:436
  22.5 0.1 collective-permute-start.6
  22.5 2.0 %collective-permute-start.7 = (bf16[144,1024]{1,0:T(8,128)(2,1)S(1)}, bf16[144,1024]{1,0:T(8,128)(2,1)S(1)}, u32[]{:S(2)}, u32[]{:S(2)}) collective-permute-start(bf16[144,1024]{1,0:T(8,128)(2,1)S(1)} %get-tuple-element.56), channel_id=1, source_target_pairs={{2,0},{4,2},{6,4},{7,6},{5,7},{3,5},{1,3},{0,1},{10,8},{12,10},{14... | collective-permute-start | bytes 884744 | tf_op jit(solution)/shard_map/ppermute | solution.py:576
  24.5 4.5 %own_block.1 = (bf16[32,1024]{1,0:T(8,128)(2,1)S(1)}, bf16[8,288,128]{2,1,0:T(8,128)(2,1)S(1)}, f32[144,1024]{1,0:T(8,128)S(1)}, f32[144,1024]{1,0:T(8,128)S(1)}, f32[144,1024]{1,0:T(8,128)S(1)}) custom-call(s32[4]{0:T(128)S(1)} %pad_add_fusion.here_ref, s32[8,8]{1,0:T(8,128)S(1)} %copy-done.6, s32[1,1,8]{2,1,0:T(1,128)S(1)} %copy-done.5, ...), custom_call_target="tpu_custom_call" | custom-call | flops 4400000000 | tf_op jit(solution)/shard_map/own_block/pallas_call | solution.py:436
  29.1 0.1 collective-permute-start.12
  29.1 1.7 %collective-permute-start.13 = (bf16[32,1024]{1,0:T(8,128)(2,1)S(1)}, bf16[32,1024]{1,0:T(8,128)(2,1)S(1)}, u32[]{:S(2)}, u32[]{:S(2)}) collective-permute-start(bf16[32,1024]{1,0:T(8,128)(2,1)S(1)} %get-tuple-element.61), channel_id=1, source_target_pairs={{0,24},{8,0},{16,8},{24,16},{1,25},{9,1},{17,9},{25,17},{2,26},{10... | collective-permute-start | bytes 196616 | tf_op jit(solution)/shard_map/ppermute | solution.py:39
  30.9 0.1 collective-permute-start.10
  31.0 0.0 collective-permute-done.7.refs_1_
  31.0 1.9 %collective-permute-start.11 = (bf16[144,1024]{1,0:T(8,128)(2,1)S(1)}, bf16[144,1024]{1,0:T(8,128)(2,1)S(1)}, u32[]{:S(2)}, u32[]{:S(2)}) collective-permute-start(bf16[144,1024]{1,0:T(8,128)(2,1)S(1)} %collective-permute-done.7.refs_1_), channel_id=1, source_target_pairs={{2,0},{4,2},{6,4},{7,6},{5,7},{3,5},{1,3},{0,1},{10,8},{12,10},{14... | collective-permute-start | bytes 884744 | tf_op jit(solution)/shard_map/ppermute | solution.py:576
  32.9 0.0 collective-permute-done.9.refs_3_
  32.9 4.6 %attend_batch.2 = (f32[144,1024]{1,0:T(8,128)S(1)}, f32[144,1024]{1,0:T(8,128)S(1)}, f32[144,1024]{1,0:T(8,128)S(1)}, bf16[32,1024]{1,0:T(8,128)(2,1)S(1)}) custom-call(s32[4]{0:T(128)S(1)} %pad_add_fusion.here_ref, s32[8,8]{1,0:T(8,128)S(1)} %copy-done.6, s32[1,1,8]{2,1,0:T(1,128)S(1)} %copy-done.5, s32[1,1]{1,0:T(1,128)S(6)} %copy.10.count_ref, ...), custom_call_target="tpu_custom_call" | custom-call | flops 6380000256 | tf_op jit(solution)/shard_map/attend_batch/pallas_call | solution.py:436
  37.5 2.7 %collective-permute-start.16 = (bf16[32,1024]{1,0:T(8,128)(2,1)S(1)}, bf16[32,1024]{1,0:T(8,128)(2,1)S(1)}, u32[]{:S(2)}, u32[]{:S(2)}) collective-permute-start(bf16[32,1024]{1,0:T(8,128)(2,1)S(1)} %get-tuple-element.67), channel_id=1, source_target_pairs={{0,7},{2,5},{4,3},{6,1},{7,0},{5,2},{3,4},{1,6},{8,15},{10,13},{12... | collective-permute-start | bytes 196616 | tf_op jit(solution)/shard_map/ppermute | solution.py:581
  40.3 0.0 collective-permute-done.10.refs_0_
  40.3 0.2 collective-permute-start.14
  40.5 0.0 collective-permute-done.11.refs_1_
  40.5 2.1 %collective-permute-start.15 = (bf16[80,1024]{1,0:T(8,128)(2,1)S(1)}, bf16[80,1024]{1,0:T(8,128)(2,1)S(1)}, u32[]{:S(2)}, u32[]{:S(2)}) collective-permute-start(bf16[80,1024]{1,0:T(8,128)(2,1)S(1)} %slice.30), channel_id=1, source_target_pairs={{2,0},{4,2},{6,4},{7,6},{5,7},{3,5},{1,3},{0,1},{10,8},{12,10},{14... | collective-permute-start | bytes 491528 | tf_op jit(solution)/shard_map/ppermute | solution.py:590
  42.7 4.4 %attend_batch.3 = (f32[144,1024]{1,0:T(8,128)S(1)}, f32[144,1024]{1,0:T(8,128)S(1)}, f32[144,1024]{1,0:T(8,128)S(1)}, bf16[32,1024]{1,0:T(8,128)(2,1)}) custom-call(s32[4]{0:T(128)S(1)} %pad_add_fusion.here_ref, s32[8,8]{1,0:T(8,128)S(1)} %copy-done.6, s32[1,1,8]{2,1,0:T(1,128)S(1)} %copy-done.5, s32[1,1]{1,0:T(1,128)S(6)} %copy.10.count_ref, ...), custom_call_target="tpu_custom_call" | custom-call | flops 6380000256 | tf_op jit(solution)/shard_map/attend_batch/pallas_call | solution.py:436
  47.1 0.2 collective-permute-done.14.refs_0_
  47.3 3.4 %attend_last.1 = (f32[144,1024]{1,0:T(8,128)S(1)}, f32[8,144,128]{2,1,0:T(8,128)S(1)}, bf16[36,1024]{1,0:T(8,128)(2,1)S(1)}, bf16[36,1024]{1,0:T(8,128)(2,1)S(1)...) custom-call(s32[4]{0:T(128)S(1)} %pad_add_fusion.here_ref, s32[8,8]{1,0:T(8,128)S(1)} %copy-done.6, ...), custom_call_target="tpu_custom_call" | custom-call | flops 5500000256 | tf_op jit(solution)/shard_map/attend_last/pallas_call | solution.py:436
  50.7 2.3 %collective-permute-start.17 = (bf16[16,1024]{1,0:T(8,128)(2,1)S(1)}, bf16[16,1024]{1,0:T(8,128)(2,1)S(1)}, u32[]{:S(2)}, u32[]{:S(2)}) collective-permute-start(bf16[16,1024]{1,0:T(8,128)(2,1)S(1)} %get-tuple-element.70), channel_id=1, source_target_pairs={{1,2},{2,1},{3,4},{4,3},{5,6},{6,5},{7,0},{0,7},{9,10},{10,9},{11,... | collective-permute-start | bytes 98312 | tf_op jit(solution)/shard_map/ppermute | solution.py:452
  53.0 4.4 %collective-permute-done.17.across_ref = bf16[16,1024]{1,0:T(8,128)(2,1)S(1)} collective-permute-done((bf16[16,1024]{1,0:T(8,128)(2,1)S(1)}, bf16[16,1024]{1,0:T(8,128)(2,1)S(1)}, u32[]{:S(2)}, u32[]{:S(2)}) %collective-permute-start.17) | collective-permute-done | bytes 32800 | tf_op jit(solution)/shard_map/ppermute | solution.py:452
  57.5 0.1 collective-permute-start.20
  57.6 0.5 collective-permute-start.19
  58.2 2.2 %conv_part.3 = (f32[8,144,128]{2,1,0:T(8,128)S(1)}, f32[8,9,128]{2,1,0:T(8,128)S(1)}, bf16[4,9,4,1024]{3,2,1,0:T(4,128)(2,1)}) custom-call(s32[4]{0:T(128)S(1)} %pad_add_fusion.here_ref, f32[8,144,128]{2,1,0:T(8,128)S(1)} %get-tuple-element.68.field_ref, f32[9,1024]{1,0:T(8,128)S(1)} %copy-done.4, f32[144,1024]{1,0:T(8,128)S(1)} %get-tuple-element.69.dense_ref, ...), custom_call_target="tpu_custom_call" | custom-call | flops 2200000000 | tf_op jit(solution)/shard_map/conv_part/pallas_call | solution.py:436
  60.4 2.0 %collective-permute-done.19.north_ref = bf16[44,1024]{1,0:T(8,128)(2,1)S(1)} collective-permute-done((bf16[44,1024]{1,0:T(8,128)(2,1)S(1)}, bf16[44,1024]{1,0:T(8,128)(2,1)S(1)}, u32[]{:S(2)}, u32[]{:S(2)}) %collective-permute-start.19) | collective-permute-done | bytes 90144 | tf_op jit(solution)/shard_map/ppermute | solution.py:39
  62.3 1.6 %conv_second.1 = bf16[4,9,4,1024]{3,2,1,0:T(4,128)(2,1)} custom-call(s32[4]{0:T(128)S(1)} %pad_add_fusion.here_ref, f32[8,144,128]{2,1,0:T(8,128)S(1)} %get-tuple-element.73.part_ref, f32[8,9,128]{2,1,0:T(8,128)S(1)} %get-tuple-element.74.taps_ref, bf16[44,1024]{1,0:T(8,128)(2,1)S(1)} %collective-permute-done.19.north_ref, ...), custom_call_target="tpu_custom_call" | custom-call | flops 2000000000 | tf_op jit(solution)/shard_map/conv_second/pallas_call | solution.py:617
  (32 shorter events, 0.3 us)
Async XLA Ops:
  0.6 1.0 %copy-start.2 = (bf16[4,4,9,1024]{3,1,2,0:T(4,128)(2,1)S(1)}, bf16[4,4,9,1024]{3,1,2,0:T(4,128)(2,1)}, u32[]{:S(2)}) copy-start(bf16[4,4,9,1024]{3,1,2,0:T(4,128)(2,1)} %param.8) | copy-start | bytes 884740
  1.7 4.6 %collective-permute-start = (bf16[36,1024]{1,0:T(8,128)(2,1)S(1)}, bf16[36,1024]{1,0:T(8,128)(2,1)S(1)}, u32[]{:S(2)}, u32[]{:S(2)}) collective-permute-start(bf16[36,1024]{1,0:T(8,128)(2,1)S(1)} %get-tuple-element.43), channel_id=1, source_target_pairs={{0,8},{8,16},{16,24},{24,0},{1,9},{9,17},{17,25},{25,1},{2,10},{10... | collective-permute-start | bytes 221192 | tf_op jit(solution)/shard_map/ppermute | solution.py:39
  2.2 4.7 %collective-permute-start.1 = (bf16[36,1024]{1,0:T(8,128)(2,1)S(1)}, bf16[36,1024]{1,0:T(8,128)(2,1)S(1)}, u32[]{:S(2)}, u32[]{:S(2)}) collective-permute-start(bf16[36,1024]{1,0:T(8,128)(2,1)S(1)} %get-tuple-element.44), channel_id=1, source_target_pairs={{0,24},{8,0},{16,8},{24,16},{1,25},{9,1},{17,9},{25,17},{2,26},{10... | collective-permute-start | bytes 221192 | tf_op jit(solution)/shard_map/ppermute | solution.py:39
  4.2 11.3 %copy-start = (bf16[1024,3072]{1,0:T(8,128)(2,1)S(1)}, bf16[1024,3072]{1,0:T(8,128)(2,1)}, u32[]{:S(2)}) copy-start(bf16[1024,3072]{1,0:T(8,128)(2,1)} %far_ref.1) | copy-start | bytes 18874372
  4.3 1.0 %copy-start.3 = (f32[9,1024]{1,0:T(8,128)S(1)}, f32[9,1024]{1,0:T(8,128)}, u32[]{:S(2)}) copy-start(f32[9,1024]{1,0:T(8,128)} %weights_ref.2) | copy-start | bytes 110596
  8.0 16.6 %copy-start.5 = (s32[1,1,8]{2,1,0:T(1,128)S(1)}, s32[1,1,8]{2,1,0:T(1,128)}, u32[]{:S(2)}) copy-start(s32[1,1,8]{2,1,0:T(1,128)} %list_ref.7) | copy-start | bytes 100
  8.0 16.6 %copy-start.6 = (s32[8,8]{1,0:T(8,128)S(1)}, s32[8,8]{1,0:T(8,128)}, u32[]{:S(2)}) copy-start(s32[8,8]{1,0:T(8,128)} %constant.27.clone.sources_ref) | copy-start | bytes 772
  8.0 13.4 %collective-permute-start.4 = (bf16[112,1024]{1,0:T(8,128)(2,1)S(1)}, bf16[112,1024]{1,0:T(8,128)(2,1)S(1)}, u32[]{:S(2)}, u32[]{:S(2)}) collective-permute-start(bf16[112,1024]{1,0:T(8,128)(2,1)S(1)} %get-tuple-element.47.inner_ref), channel_id=1, source_target_pairs={{0,2},{2,4},{4,6},{6,7},{7,5},{5,3},{3,1},{1,0},{8,10},{10,12},{12... | collective-permute-start | bytes 688136 | tf_op jit(solution)/shard_map/ppermute | solution.py:518
  9.8 11.6 %collective-permute-start.5 = (bf16[112,1024]{1,0:T(8,128)(2,1)S(1)}, bf16[112,1024]{1,0:T(8,128)(2,1)S(1)}, u32[]{:S(2)}, u32[]{:S(2)}) collective-permute-start(bf16[112,1024]{1,0:T(8,128)(2,1)S(1)} %get-tuple-element.47.inner_ref), channel_id=1, source_target_pairs={{2,0},{4,2},{6,4},{7,6},{5,7},{3,5},{1,3},{0,1},{10,8},{12,10},{14... | collective-permute-start | bytes 688136 | tf_op jit(solution)/shard_map/ppermute | solution.py:519
  10.7 9.4 %collective-permute-start.2 = (bf16[24,1024]{1,0:T(8,128)(2,1)S(1)}, bf16[24,1024]{1,0:T(8,128)(2,1)S(1)}, u32[]{:S(2)}, u32[]{:S(2)}) collective-permute-start(bf16[24,1024]{1,0:T(8,128)(2,1)S(1)} %get-tuple-element.45), channel_id=1, source_target_pairs={{1,2},{2,1},{3,4},{4,3},{5,6},{6,5},{7,0},{0,7},{9,10},{10,9},{11,... | collective-permute-start | bytes 147464 | tf_op jit(solution)/shard_map/ppermute | solution.py:452
  15.5 5.9 %collective-permute-start.3 = (bf16[24,1024]{1,0:T(8,128)(2,1)S(1)}, bf16[24,1024]{1,0:T(8,128)(2,1)S(1)}, u32[]{:S(2)}, u32[]{:S(2)}) collective-permute-start(bf16[24,1024]{1,0:T(8,128)(2,1)S(1)} %get-tuple-element.46), channel_id=1, source_target_pairs={{0,1},{1,0},{2,3},{3,2},{4,5},{5,4},{6,7},{7,6},{8,9},{9,8},{10,11... | collective-permute-start | bytes 147464 | tf_op jit(solution)/shard_map/ppermute | solution.py:452
  15.9 13.2 %collective-permute-start.8 = (bf16[112,1024]{1,0:T(8,128)(2,1)S(1)}, bf16[112,1024]{1,0:T(8,128)(2,1)S(1)}, u32[]{:S(2)}, u32[]{:S(2)}) collective-permute-start(bf16[112,1024]{1,0:T(8,128)(2,1)S(1)} %get-tuple-element.57), channel_id=1, source_target_pairs={{0,8},{8,16},{16,24},{24,0},{1,9},{9,17},{17,25},{25,1},{2,10},{10... | collective-permute-start | bytes 688136 | tf_op jit(solution)/shard_map/ppermute | solution.py:39
  20.1 12.8 %collective-permute-start.9 = (bf16[112,1024]{1,0:T(8,128)(2,1)S(1)}, bf16[112,1024]{1,0:T(8,128)(2,1)S(1)}, u32[]{:S(2)}, u32[]{:S(2)}) collective-permute-start(bf16[112,1024]{1,0:T(8,128)(2,1)S(1)} %get-tuple-element.57), channel_id=1, source_target_pairs={{0,24},{8,0},{16,8},{24,16},{1,25},{9,1},{17,9},{25,17},{2,26},{10... | collective-permute-start | bytes 688136 | tf_op jit(solution)/shard_map/ppermute | solution.py:39
  22.5 8.4 %collective-permute-start.6 = (bf16[144,1024]{1,0:T(8,128)(2,1)S(1)}, bf16[144,1024]{1,0:T(8,128)(2,1)S(1)}, u32[]{:S(2)}, u32[]{:S(2)}) collective-permute-start(bf16[144,1024]{1,0:T(8,128)(2,1)S(1)} %get-tuple-element.55), channel_id=1, source_target_pairs={{0,2},{2,4},{4,6},{6,7},{7,5},{5,3},{3,1},{1,0},{8,10},{10,12},{12... | collective-permute-start | bytes 884744 | tf_op jit(solution)/shard_map/ppermute | solution.py:575
  22.5 8.5 %collective-permute-start.7 = (bf16[144,1024]{1,0:T(8,128)(2,1)S(1)}, bf16[144,1024]{1,0:T(8,128)(2,1)S(1)}, u32[]{:S(2)}, u32[]{:S(2)}) collective-permute-start(bf16[144,1024]{1,0:T(8,128)(2,1)S(1)} %get-tuple-element.56), channel_id=1, source_target_pairs={{2,0},{4,2},{6,4},{7,6},{5,7},{3,5},{1,3},{0,1},{10,8},{12,10},{14... | collective-permute-start | bytes 884744 | tf_op jit(solution)/shard_map/ppermute | solution.py:576
  29.1 13.6 %collective-permute-start.12 = (bf16[32,1024]{1,0:T(8,128)(2,1)S(1)}, bf16[32,1024]{1,0:T(8,128)(2,1)S(1)}, u32[]{:S(2)}, u32[]{:S(2)}) collective-permute-start(bf16[32,1024]{1,0:T(8,128)(2,1)S(1)} %get-tuple-element.61), channel_id=1, source_target_pairs={{0,8},{8,16},{16,24},{24,0},{1,9},{9,17},{17,25},{25,1},{2,10},{10... | collective-permute-start | bytes 196616 | tf_op jit(solution)/shard_map/ppermute | solution.py:39
  29.1 13.5 %collective-permute-start.13 = (bf16[32,1024]{1,0:T(8,128)(2,1)S(1)}, bf16[32,1024]{1,0:T(8,128)(2,1)S(1)}, u32[]{:S(2)}, u32[]{:S(2)}) collective-permute-start(bf16[32,1024]{1,0:T(8,128)(2,1)S(1)} %get-tuple-element.61), channel_id=1, source_target_pairs={{0,24},{8,0},{16,8},{24,16},{1,25},{9,1},{17,9},{25,17},{2,26},{10... | collective-permute-start | bytes 196616 | tf_op jit(solution)/shard_map/ppermute | solution.py:39
  30.9 9.4 %collective-permute-start.10 = (bf16[144,1024]{1,0:T(8,128)(2,1)S(1)}, bf16[144,1024]{1,0:T(8,128)(2,1)S(1)}, u32[]{:S(2)}, u32[]{:S(2)}) collective-permute-start(bf16[144,1024]{1,0:T(8,128)(2,1)S(1)} %collective-permute-done.6.refs_0_), channel_id=1, source_target_pairs={{0,2},{2,4},{4,6},{6,7},{7,5},{5,3},{3,1},{1,0},{8,10},{10,12},{12... | collective-permute-start | bytes 884744 | tf_op jit(solution)/shard_map/ppermute | solution.py:575
  31.0 9.5 %collective-permute-start.11 = (bf16[144,1024]{1,0:T(8,128)(2,1)S(1)}, bf16[144,1024]{1,0:T(8,128)(2,1)S(1)}, u32[]{:S(2)}, u32[]{:S(2)}) collective-permute-start(bf16[144,1024]{1,0:T(8,128)(2,1)S(1)} %collective-permute-done.7.refs_1_), channel_id=1, source_target_pairs={{2,0},{4,2},{6,4},{7,6},{5,7},{3,5},{1,3},{0,1},{10,8},{12,10},{14... | collective-permute-start | bytes 884744 | tf_op jit(solution)/shard_map/ppermute | solution.py:576
  37.5 9.6 %collective-permute-start.16 = (bf16[32,1024]{1,0:T(8,128)(2,1)S(1)}, bf16[32,1024]{1,0:T(8,128)(2,1)S(1)}, u32[]{:S(2)}, u32[]{:S(2)}) collective-permute-start(bf16[32,1024]{1,0:T(8,128)(2,1)S(1)} %get-tuple-element.67), channel_id=1, source_target_pairs={{0,7},{2,5},{4,3},{6,1},{7,0},{5,2},{3,4},{1,6},{8,15},{10,13},{12... | collective-permute-start | bytes 196616 | tf_op jit(solution)/shard_map/ppermute | solution.py:581
  40.3 7.0 %collective-permute-start.14 = (bf16[96,1024]{1,0:T(8,128)(2,1)S(1)}, bf16[96,1024]{1,0:T(8,128)(2,1)S(1)}, u32[]{:S(2)}, u32[]{:S(2)}) collective-permute-start(bf16[96,1024]{1,0:T(8,128)(2,1)S(1)} %pad_maximum_fusion), channel_id=1, source_target_pairs={{0,2},{2,4},{4,6},{6,7},{7,5},{5,3},{3,1},{1,0},{8,10},{10,12},{12... | collective-permute-start | bytes 589832 | tf_op jit(solution)/shard_map/ppermute | solution.py:589
  40.5 6.6 %collective-permute-start.15 = (bf16[80,1024]{1,0:T(8,128)(2,1)S(1)}, bf16[80,1024]{1,0:T(8,128)(2,1)S(1)}, u32[]{:S(2)}, u32[]{:S(2)}) collective-permute-start(bf16[80,1024]{1,0:T(8,128)(2,1)S(1)} %slice.30), channel_id=1, source_target_pairs={{2,0},{4,2},{6,4},{7,6},{5,7},{3,5},{1,3},{0,1},{10,8},{12,10},{14... | collective-permute-start | bytes 491528 | tf_op jit(solution)/shard_map/ppermute | solution.py:590
  42.6 4.7 %copy-start.1 = (bf16[1024,1024]{1,0:T(8,128)(2,1)S(1)}, bf16[1024,1024]{1,0:T(8,128)(2,1)}, u32[]{:S(2)}) copy-start(bf16[1024,1024]{1,0:T(8,128)(2,1)} %wo_ref.1) | copy-start | bytes 6291460
  47.3 10.8 %copy-start.4 = (f32[9,1024]{1,0:T(8,128)S(1)}, f32[9,1024]{1,0:T(8,128)}, u32[]{:S(2)}) copy-start(f32[9,1024]{1,0:T(8,128)} %weights_ref.3) | copy-start | bytes 110596
  50.7 6.7 %collective-permute-start.17 = (bf16[16,1024]{1,0:T(8,128)(2,1)S(1)}, bf16[16,1024]{1,0:T(8,128)(2,1)S(1)}, u32[]{:S(2)}, u32[]{:S(2)}) collective-permute-start(bf16[16,1024]{1,0:T(8,128)(2,1)S(1)} %get-tuple-element.70), channel_id=1, source_target_pairs={{1,2},{2,1},{3,4},{4,3},{5,6},{6,5},{7,0},{0,7},{9,10},{10,9},{11,... | collective-permute-start | bytes 98312 | tf_op jit(solution)/shard_map/ppermute | solution.py:452
  53.0 4.4 %collective-permute-start.18 = (bf16[16,1024]{1,0:T(8,128)(2,1)S(1)}, bf16[16,1024]{1,0:T(8,128)(2,1)S(1)}, u32[]{:S(2)}, u32[]{:S(2)}) collective-permute-start(bf16[16,1024]{1,0:T(8,128)(2,1)S(1)} %get-tuple-element.71), channel_id=1, source_target_pairs={{0,1},{1,0},{2,3},{3,2},{4,5},{5,4},{6,7},{7,6},{8,9},{9,8},{10,11... | collective-permute-start | bytes 98312 | tf_op jit(solution)/shard_map/ppermute | solution.py:452
  57.5 2.8 %collective-permute-start.20 = (bf16[44,1024]{1,0:T(8,128)(2,1)S(1)}, bf16[44,1024]{1,0:T(8,128)(2,1)S(1)}, u32[]{:S(2)}, u32[]{:S(2)}) collective-permute-start(bf16[44,1024]{1,0:T(8,128)(2,1)S(1)} %pad_maximum_fusion.2), channel_id=1, source_target_pairs={{0,24},{8,0},{16,8},{24,16},{1,25},{9,1},{17,9},{25,17},{2,26},{10... | collective-permute-start | bytes 270344 | tf_op jit(solution)/shard_map/ppermute | solution.py:39
  57.6 4.7 %collective-permute-start.19 = (bf16[44,1024]{1,0:T(8,128)(2,1)S(1)}, bf16[44,1024]{1,0:T(8,128)(2,1)S(1)}, u32[]{:S(2)}, u32[]{:S(2)}) collective-permute-start(bf16[44,1024]{1,0:T(8,128)(2,1)S(1)} %pad_maximum_fusion.1), channel_id=1, source_target_pairs={{0,8},{8,16},{16,24},{24,0},{1,9},{9,17},{17,25},{25,1},{2,10},{10... | collective-permute-start | bytes 270344 | tf_op jit(solution)/shard_map/ppermute | solution.py:39
